TPU v7x, 32 devices: a whole 2x2x4 slice. The times are simulated.
32 devices in a mesh: runs: 2 (over y), gx: 4 (over z), gy: 4 (over x, core).
Axes of the slice: x: 2, y: 2, z: 4, core: 2. Of those that a mesh axis runs over, the one named last changes fastest.
Arguments:
- melt_flow: float32 [3, 32, 512, 128], P(None, ('runs', 'gx'), 'gy'), parts along dimension 1, may hold values from -6 to 6
- thermal_state: float32 [32, 512, 128], P(('runs', 'gx'), 'gy'), parts along dimension 0, may hold values from -6 to 6
- powder_flag: int32 [32, 512, 128], P(('runs', 'gx'), 'gy'), parts along dimension 0, may hold values 0 or 1
- spot_lateral_a_cell: int32 [16], P('runs'), parts along dimension 0, may hold values from 0 to 15
- spot_lateral_b_cell: int32 [16], P('runs'), parts along dimension 0, may hold values from 0 to 511
Outputs:
- corrected_flow: float32 [3, 32, 512, 128], P(None, ('runs', 'gx'), 'gy'), parts along dimension 1
- advected_thermal_state: float32 [32, 512, 128], P(('runs', 'gx'), 'gy'), parts along dimension 0
- pressure_iterate: float32 [32, 512, 128], P(('runs', 'gx'), 'gy'), parts along dimension 0
There are 2 independent parts, one for each index of `runs`. A program takes and returns all parts, laid end to end along the dimension named above; each array names one. Nothing has to cross between parts.
All inputs are finite; a program needn't handle non-finite values. No bound on the sum of `powder_flag` on one device may be relied on, other than what follows from the above.
Results may differ from a plain program's by a relative error of at most 0.0003.
Values sent between devices are 32-bit elements; how exact they have to be, the bound alone decides.
No kernel may reach another device: no remote copies, remote signals or barrier semaphores. Data moves between devices by JAX's collectives and lax.ppermute only.
A program may use at most 64 MiB of HBM per device.

v0:
```python
import math

import jax
import jax.numpy as jnp
from jax import lax
from jax.sharding import PartitionSpec as P

BLOCK = 128
ITERS = 2


TIME_INCREMENT = 0.2
MARANGONI = 1.5
DRAG_RATE = 4.0
LASER_POWER = 3.0
SPOT_RADIUS = 5.0


def extended(cells, sides, width):
    for axis, dim in sides:
        count = lax.axis_size(axis)
        head = lax.slice_in_dim(cells, 0, width, axis=dim)
        tail = lax.slice_in_dim(cells, cells.shape[dim] - width, cells.shape[dim], axis=dim)
        cells = jnp.concatenate(
            [
                lax.ppermute(tail, axis, [(i, (i + 1) % count) for i in range(count)]),
                cells,
                lax.ppermute(head, axis, [((i + 1) % count, i) for i in range(count)]),
            ],
            axis=dim,
        )
    return cells


def passed_along(array, axis, by):
    length = lax.axis_size(axis)
    return lax.ppermute(array, axis, [(i, (i + by) % length) for i in range(length)])


def sine_table(length):
    positions = jnp.arange(length, dtype=jnp.float32) + 1.0
    phase_step = math.pi / (length + 1)
    sine_rows = jnp.sqrt(2.0 / (length + 1)) * jnp.sin(
        phase_step * positions[:, None] * positions[None, :]
    )
    eigen_values = 2.0 - 2.0 * jnp.cos(phase_step * positions)
    return (sine_rows, eigen_values)


def depth_shift(source, offset):
    vertical_plane_number = source.shape[-1]
    padded = jnp.pad(source, [(0, 0)] * (source.ndim - 1) + [(2, 2)])
    return padded[..., 2 + offset : 2 + offset + vertical_plane_number]


def laser_heat(
    start_x,
    start_y,
    span_lateral_a,
    span_lateral_b,
    total_x,
    total_y,
    spot_lateral_a_cell,
    spot_lateral_b_cell,
):
    cells_x = start_x + jnp.arange(span_lateral_a, dtype=jnp.int32)
    cells_y = start_y + jnp.arange(span_lateral_b, dtype=jnp.int32)
    dist_x = (
        (cells_x[:, None] - spot_lateral_a_cell[None, :] + total_x // 2) % total_x - total_x // 2
    ).astype(jnp.float32)
    dist_y = (
        (cells_y[:, None] - spot_lateral_b_cell[None, :] + total_y // 2) % total_y - total_y // 2
    ).astype(jnp.float32)
    spot_x = jnp.exp(-(dist_x * dist_x) / (SPOT_RADIUS * SPOT_RADIUS))
    spot_y = jnp.exp(-(dist_y * dist_y) / (SPOT_RADIUS * SPOT_RADIUS))
    return LASER_POWER * jnp.dot(spot_x, spot_y.T, precision=lax.Precision.HIGHEST)


def window(widened_block, margin, keep_rim, off_x, off_y):
    inner_x = widened_block.shape[-3] - 2 * margin
    inner_y = widened_block.shape[-2] - 2 * margin
    low_x = margin - keep_rim + off_x
    low_y = margin - keep_rim + off_y
    return widened_block[
        ..., low_x : low_x + inner_x + 2 * keep_rim, low_y : low_y + inner_y + 2 * keep_rim, :
    ]


def march_forward(widened_block, margin, keep_rim, solid_fraction):
    middle_entry = window(widened_block, margin, keep_rim, 0, 0)
    speed_x = middle_entry[0][None]
    speed_y = middle_entry[1][None]
    speed_z = middle_entry[2][None]
    behind = (
        1.5 * middle_entry
        - 2.0 * window(widened_block, margin, keep_rim, -1, 0)
        + 0.5 * window(widened_block, margin, keep_rim, -2, 0)
    )
    forward = (
        -1.5 * middle_entry
        + 2.0 * window(widened_block, margin, keep_rim, 1, 0)
        - 0.5 * window(widened_block, margin, keep_rim, 2, 0)
    )
    along_x = jnp.where(speed_x >= 0.0, behind, forward)
    behind = (
        1.5 * middle_entry
        - 2.0 * window(widened_block, margin, keep_rim, 0, -1)
        + 0.5 * window(widened_block, margin, keep_rim, 0, -2)
    )
    forward = (
        -1.5 * middle_entry
        + 2.0 * window(widened_block, margin, keep_rim, 0, 1)
        - 0.5 * window(widened_block, margin, keep_rim, 0, 2)
    )
    along_y = jnp.where(speed_y >= 0.0, behind, forward)
    behind = (
        1.5 * middle_entry
        - 2.0 * depth_shift(middle_entry, -1)
        + 0.5 * depth_shift(middle_entry, -2)
    )
    forward = (
        -1.5 * middle_entry
        + 2.0 * depth_shift(middle_entry, 1)
        - 0.5 * depth_shift(middle_entry, 2)
    )
    along_z = jnp.where(speed_z >= 0.0, behind, forward)
    time_derivative = speed_x * along_x + speed_y * along_y + speed_z * along_z
    vertical_plane_number = middle_entry.shape[-1]
    upper_boundary = (jnp.arange(vertical_plane_number) == vertical_plane_number - 1).astype(
        jnp.float32
    )
    slope_lateral_a = 0.5 * (
        window(widened_block, margin, keep_rim, 1, 0)[3]
        - window(widened_block, margin, keep_rim, -1, 0)[3]
    )
    slope_lateral_b = 0.5 * (
        window(widened_block, margin, keep_rim, 0, 1)[3]
        - window(widened_block, margin, keep_rim, 0, -1)[3]
    )
    traction = jnp.stack(
        [
            -MARANGONI * slope_lateral_a * upper_boundary,
            -MARANGONI * slope_lateral_b * upper_boundary,
            jnp.zeros_like(slope_lateral_a),
        ]
    )
    provisional_flow = (
        middle_entry[:3] - TIME_INCREMENT * time_derivative[:3] + TIME_INCREMENT * traction
    ) / (1.0 + TIME_INCREMENT * DRAG_RATE * solid_fraction)[None]
    thermal_subblock = middle_entry[3] - TIME_INCREMENT * time_derivative[3]
    return (provisional_flow, thermal_subblock, upper_boundary)


def local_solve(source):
    highest = lax.Precision.HIGHEST
    span_lateral_a, span_lateral_b, vertical_plane_number = source.shape
    table_y, values_y = sine_table(span_lateral_b)
    table_z, values_z = sine_table(vertical_plane_number)
    spectrum = jnp.einsum("jb,ijk->ibk", table_y, source, precision=highest)
    spectrum = jnp.einsum("kc,ibk->ibc", table_z, spectrum, precision=highest)
    flat = spectrum.reshape(span_lateral_a, span_lateral_b * vertical_plane_number)
    pencil = lax.all_to_all(flat, "gx", split_axis=1, concat_axis=0, tiled=True)
    total_x, width_cols = pencil.shape
    block_x = span_lateral_a * min(lax.axis_size("gx"), BLOCK // span_lateral_a)
    table_x, values_x = sine_table(block_x)
    grouped = pencil.reshape(total_x // block_x, block_x, width_cols)
    grouped = jnp.einsum("ia,gic->gac", table_x, grouped, precision=highest)
    columns = lax.axis_index("gx") * width_cols + jnp.arange(width_cols, dtype=jnp.int32)
    index_y = (columns // vertical_plane_number).astype(jnp.float32) + 1.0
    index_z = (columns % vertical_plane_number).astype(jnp.float32) + 1.0
    lam_y = 2.0 - 2.0 * jnp.cos(math.pi / (span_lateral_b + 1) * index_y)
    lam_z = 2.0 - 2.0 * jnp.cos(math.pi / (vertical_plane_number + 1) * index_z)
    denominator = values_x[None, :, None] + (lam_y + lam_z)[None, None, :]
    grouped = grouped / denominator
    grouped = jnp.einsum("ia,gac->gic", table_x, grouped, precision=highest)
    back = lax.all_to_all(
        grouped.reshape(total_x, width_cols), "gx", split_axis=0, concat_axis=1, tiled=True
    )
    spectrum = back.reshape(span_lateral_a, span_lateral_b, vertical_plane_number)
    spectrum = jnp.einsum("kc,ibc->ibk", table_z, spectrum, precision=highest)
    return jnp.einsum("jb,ibk->ijk", table_y, spectrum, precision=highest)


def extend(source):
    return extended(source, (("gx", 0), ("gy", 1)), 1)


def operate(widened_block):
    middle_entry = widened_block[1:-1, 1:-1]
    beside = widened_block[2:, 1:-1] + widened_block[:-2, 1:-1]
    beside = beside + widened_block[1:-1, 2:] + widened_block[1:-1, :-2]
    beside = beside + depth_shift(middle_entry, 1) + depth_shift(middle_entry, -1)
    return 6.0 * middle_entry - beside


def energy_sum(residual, precond):
    return lax.psum(jnp.sum(residual * precond), ("gx", "gy"))


def per_device(melt_flow, thermal_state, powder_flag, spot_lateral_a_cell, spot_lateral_b_cell):
    span_lateral_a, span_lateral_b, vertical_plane_number = thermal_state.shape
    combined_states = jnp.concatenate([melt_flow, thermal_state[None]], 0)
    widened_block = extended(combined_states, (("gx", 1), ("gy", 2)), 2)
    solid_fraction = powder_flag.astype(jnp.float32)
    provisional_flow, thermal_subblock, upper_boundary = march_forward(
        widened_block, 2, 0, solid_fraction
    )
    lower_x = passed_along(provisional_flow[0, -1:], "gx", 1)
    prev_x = jnp.concatenate([lower_x, provisional_flow[0, :-1]], 0)
    lower_y = passed_along(provisional_flow[1, :, -1:], "gy", 1)
    prev_y = jnp.concatenate([lower_y, provisional_flow[1, :, :-1]], 1)
    total_x = span_lateral_a * lax.axis_size("gx")
    total_y = span_lateral_b * lax.axis_size("gy")
    laser_power_input = laser_heat(
        lax.axis_index("gx") * span_lateral_a,
        lax.axis_index("gy") * span_lateral_b,
        span_lateral_a,
        span_lateral_b,
        total_x,
        total_y,
        spot_lateral_a_cell,
        spot_lateral_b_cell,
    )
    advected_thermal_state = (
        thermal_subblock + TIME_INCREMENT * laser_power_input[:, :, None] * upper_boundary
    )
    divergence = (
        provisional_flow[0]
        - prev_x
        + (provisional_flow[1] - prev_y)
        + (provisional_flow[2] - depth_shift(provisional_flow[2], -1))
    )
    residual = -divergence
    pressure_iterate = jnp.zeros_like(residual)
    precond = local_solve(residual)
    direction = precond
    energy_now = energy_sum(residual, precond)
    for iteration in range(ITERS):
        direction_rim = extend(direction)
        applied = operate(direction_rim)
        step_size = energy_now / lax.psum(jnp.sum(direction * applied), ("gx", "gy"))
        pressure_iterate = pressure_iterate + step_size * direction
        residual = residual - step_size * applied
        if iteration + 1 < ITERS:
            precond = local_solve(residual)
            energy_next = energy_sum(residual, precond)
            direction = precond + energy_next / energy_now * direction
            energy_now = energy_next
    upper_x = passed_along(pressure_iterate[:1], "gx", -1)
    ahead_x = jnp.concatenate([pressure_iterate[1:], upper_x], 0)
    upper_y = passed_along(pressure_iterate[:, :1], "gy", -1)
    ahead_y = jnp.concatenate([pressure_iterate[:, 1:], upper_y], 1)
    gradient = jnp.stack(
        [
            ahead_x - pressure_iterate,
            ahead_y - pressure_iterate,
            depth_shift(pressure_iterate, 1) - pressure_iterate,
        ]
    )
    corrected_flow = provisional_flow - gradient
    return (corrected_flow, advected_thermal_state, pressure_iterate)


def solution(mesh):
    placed = (
        P(None, ("runs", "gx"), "gy", None),
        P(("runs", "gx"), "gy", None),
        P(("runs", "gx"), "gy", None),
        P("runs"),
        P("runs"),
    )
    return jax.shard_map(
        per_device,
        mesh=mesh,
        in_specs=placed,
        out_specs=(
            P(None, ("runs", "gx"), "gy", None),
            P(("runs", "gx"), "gy", None),
            P(("runs", "gx"), "gy", None),
        ),
        check_vma=False,
    )
```

profile of v0, /device:TPU:0, one launch (start us, length us, event | category | flops | bytes accessed | tf_op | source)
XLA Modules:
  0.0 222.4 jit_solution(6776429194633802086)
XLA Ops:
  2.0 3.1 %collective-permute-start = (f32[4,2,128,128]{3,2,1,0:T(8,128)S(1)}, f32[4,2,128,128]{3,2,1,0:T(8,128)S(1)}, u32[]{:S(2)}, u32[]{:S(2)}) collective-permute-start(f32[4,2,128,128]{3,2,1,0:T(8,128)S(1)} %get-tuple-element.16), channel_id=1, source_target_pairs={{0,4},{4,8},{8,12},{12,0},{1,5},{5,9},{9,13},{13,1},{2,6},{6,10},{... | collective-permute-start | bytes 1572872 | tf_op jit(solution)/shard_map/ppermute | solution.py:26
  5.1 2.1 collective-permute-start.1
  7.5 12.4 %collective-permute-done = f32[4,2,128,128]{3,2,1,0:T(8,128)S(1)} collective-permute-done((f32[4,2,128,128]{3,2,1,0:T(8,128)S(1)}, f32[4,2,128,128]{3,2,1,0:T(8,128)S(1)}, u32[]{:S(2)}, u32[]{:S(2)}) %collective-permute-start) | collective-permute-done | bytes 524320 | tf_op jit(solution)/shard_map/ppermute | solution.py:26
  19.9 9.8 %collective-permute-done.1 = f32[4,2,128,128]{3,2,1,0:T(8,128)S(1)} collective-permute-done((f32[4,2,128,128]{3,2,1,0:T(8,128)S(1)}, f32[4,2,128,128]{3,2,1,0:T(8,128)S(1)}, u32[]{:S(2)}, u32[]{:S(2)}) %collective-permute-start.1) | collective-permute-done | bytes 524320 | tf_op jit(solution)/shard_map/ppermute | solution.py:28
  29.8 1.7 collective-permute-start.3
  33.6 1.7 fusion.9
  39.9 2.0 collective-permute-done.4
  44.6 3.4 %all-to-all-start = ((f32[4,4,4096]{2,0,1:T(4,128)}), f32[4,4,4096]{2,0,1:T(4,128)S(1)}, u32[]{:S(2)}, u32[]{:S(2)}) async-start(f32[4,4,4096]{2,0,1:T(4,128)} %copy.26), calls=%async_computation | async-start | bytes 524288 | tf_op jit(solution)/shard_map/all_to_all | solution.py:162
  48.2 9.5 %all-to-all-done = f32[4,4,4096]{2,0,1:T(4,128)S(1)} async-done(((f32[4,4,4096]{2,0,1:T(4,128)}), f32[4,4,4096]{2,0,1:T(4,128)S(1)}, u32[]{:S(2)}, u32[]{:S(2)}) %all-to-all-start) | async-done | bytes 262176 | tf_op jit(solution)/shard_map/all_to_all | solution.py:162
  58.9 11.2 %all_to_all.64 = f32[4,4,4096]{2,1,0:T(4,128)S(1)} all-to-all(f32[4,4,4096]{2,1,0:T(4,128)S(1)} %all_to_all.51), channel_id=1, replica_groups=mesh['runs'=2,'gx'=4,'gy'=4] {'gx'}, dimensions={0} | all-to-all | bytes 524288 | tf_op jit(solution)/shard_map/all_to_all | solution.py:176
  73.9 2.2 %collective-permute-done.6 = f32[1,128,128]{2,1,0:T(8,128)S(1)} collective-permute-done((f32[1,128,128]{2,1,0:T(8,128)S(1)}, f32[1,128,128]{2,1,0:T(8,128)S(1)}, u32[]{:S(2)}, u32[]{:S(2)}) %collective-permute-start.6) | collective-permute-done | bytes 65568 | tf_op jit(solution)/shard_map/ppermute | solution.py:28
  76.1 3.3 %collective-permute-done.7 = f32[1,128,128]{2,1,0:T(8,128)S(1)} collective-permute-done((f32[1,128,128]{2,1,0:T(8,128)S(1)}, f32[1,128,128]{2,1,0:T(8,128)S(1)}, u32[]{:S(2)}, u32[]{:S(2)}) %collective-permute-start.7) | collective-permute-done | bytes 65568 | tf_op jit(solution)/shard_map/ppermute | solution.py:26
  80.7 1.8 collective-permute-done.9
  83.3 30.1 %all-reduce.5 = (f32[]{:T(128)}, f32[]{:T(128)}) all-reduce(f32[]{:T(128)} %get-tuple-element.4, f32[]{:T(128)} %get-tuple-element.3), channel_id=1, replica_groups=mesh['runs'=2,'gx'=4,'gy'=4] {'gx','gy'}, use_global_device_ids=true, to_apply=%region_1.2 | all-reduce | flops 2 | bytes 16 | tf_op jit(solution)/shard_map/psum | solution.py:197
  116.6 11.6 %all_to_all.65 = f32[4,4,4096]{2,0,1:T(4,128)S(1)} all-to-all(f32[4,4,4096]{2,0,1:T(4,128)S(1)} %copy.30), channel_id=1, replica_groups=mesh['runs'=2,'gx'=4,'gy'=4] {'gx'}, dimensions={1} | all-to-all | bytes 524288 | tf_op jit(solution)/shard_map/all_to_all | solution.py:162
  130.0 3.7 %all-to-all-start.3 = ((f32[4,4,4096]{2,1,0:T(4,128)}), f32[4,4,4096]{2,1,0:T(4,128)S(1)}, u32[]{:S(2)}, u32[]{:S(2)}) async-start(f32[4,4,4096]{2,1,0:T(4,128)} %all_to_all.57), calls=%async_computation.3 | async-start | bytes 524288 | tf_op jit(solution)/shard_map/all_to_all | solution.py:176
  133.8 7.8 %all-to-all-done.3 = f32[4,4,4096]{2,1,0:T(4,128)S(1)} async-done(((f32[4,4,4096]{2,1,0:T(4,128)}), f32[4,4,4096]{2,1,0:T(4,128)S(1)}, u32[]{:S(2)}, u32[]{:S(2)}) %all-to-all-start.3) | async-done | bytes 262176 | tf_op jit(solution)/shard_map/all_to_all | solution.py:176
  143.8 30.1 %psum.30 = f32[]{:T(128)} all-reduce(f32[]{:T(128)} %get-tuple-element.34), channel_id=1, replica_groups=mesh['runs'=2,'gx'=4,'gy'=4] {'gx','gy'}, use_global_device_ids=true, to_apply=%region_5.6 | all-reduce | flops 1 | bytes 8 | tf_op jit(solution)/shard_map/psum | solution.py:197
  175.4 2.0 collective-permute-start.11
  177.4 2.2 %collective-permute-done.10 = f32[1,128,128]{2,1,0:T(8,128)S(1)} collective-permute-done((f32[1,128,128]{2,1,0:T(8,128)S(1)}, f32[1,128,128]{2,1,0:T(8,128)S(1)}, u32[]{:S(2)}, u32[]{:S(2)}) %collective-permute-start.10) | collective-permute-done | bytes 65568 | tf_op jit(solution)/shard_map/ppermute | solution.py:28
  179.7 1.9 collective-permute-done.11
  182.8 1.8 collective-permute-done.13
  185.4 30.1 %psum.31 = f32[]{:T(128)} all-reduce(f32[]{:T(128)} %fusion.45), channel_id=1, replica_groups=mesh['runs'=2,'gx'=4,'gy'=4] {'gx','gy'}, use_global_device_ids=true, to_apply=%region_7.8 | all-reduce | flops 1 | bytes 8 | tf_op jit(solution)/shard_map/psum | solution.py:241
  218.4 2.9 %collective-permute-done.14 = f32[1,128,128]{2,1,0:T(8,128)S(1)} collective-permute-done((f32[1,128,128]{2,1,0:T(8,128)S(1)}, f32[1,128,128]{2,1,0:T(8,128)S(1)}, u32[]{:S(2)}, u32[]{:S(2)}) %collective-permute-start.14) | collective-permute-done | bytes 65568 | tf_op jit(solution)/shard_map/ppermute | solution.py:37
  (95 shorter events, 28.9 us)
Async XLA Ops:
  0.6 6.6 %copy-start.1 = (f32[4,128,128]{2,1,0:T(8,128)S(1)}, f32[4,128,128]{2,1,0:T(8,128)}, u32[]{:S(2)}) copy-start(f32[4,128,128]{2,1,0:T(8,128)} %param.6) | copy-start | bytes 786436
  0.6 6.5 %copy-start = (f32[3,4,128,128]{3,2,1,0:T(8,128)S(1)}, f32[3,4,128,128]{3,2,1,0:T(8,128)}, u32[]{:S(2)}) copy-start(f32[3,4,128,128]{3,2,1,0:T(8,128)} %param.5) | copy-start | bytes 2359300
  2.0 5.4 %copy-start.3 = (s32[4,128,128]{2,1,0:T(8,128)S(1)}, s32[4,128,128]{2,1,0:T(8,128)}, u32[]{:S(2)}) copy-start(s32[4,128,128]{2,1,0:T(8,128)} %param.7) | copy-start | bytes 786436
  2.0 17.9 %collective-permute-start = (f32[4,2,128,128]{3,2,1,0:T(8,128)S(1)}, f32[4,2,128,128]{3,2,1,0:T(8,128)S(1)}, u32[]{:S(2)}, u32[]{:S(2)}) collective-permute-start(f32[4,2,128,128]{3,2,1,0:T(8,128)S(1)} %get-tuple-element.16), channel_id=1, source_target_pairs={{0,4},{4,8},{8,12},{12,0},{1,5},{5,9},{9,13},{13,1},{2,6},{6,10},{... | collective-permute-start | bytes 1572872 | tf_op jit(solution)/shard_map/ppermute | solution.py:26
  5.1 24.6 %collective-permute-start.1 = (f32[4,2,128,128]{3,2,1,0:T(8,128)S(1)}, f32[4,2,128,128]{3,2,1,0:T(8,128)S(1)}, u32[]{:S(2)}, u32[]{:S(2)}) collective-permute-start(f32[4,2,128,128]{3,2,1,0:T(8,128)S(1)} %get-tuple-element.17), channel_id=1, source_target_pairs={{4,0},{8,4},{12,8},{0,12},{5,1},{9,5},{13,9},{1,13},{6,2},{10,6},{... | collective-permute-start | bytes 1572872 | tf_op jit(solution)/shard_map/ppermute | solution.py:28
  29.7 3.4 %collective-permute-start.2 = (f32[4,8,2,128]{3,2,1,0:T(2,128)S(1)}, f32[4,8,2,128]{3,2,1,0:T(2,128)S(1)}, u32[]{:S(2)}, u32[]{:S(2)}) collective-permute-start(f32[4,8,2,128]{3,2,1,0:T(2,128)S(1)} %get-tuple-element.12), channel_id=1, source_target_pairs={{0,1},{1,2},{2,3},{3,0},{4,5},{5,6},{6,7},{7,4},{8,9},{9,10},{10,1... | collective-permute-start | bytes 98312 | tf_op jit(solution)/shard_map/ppermute | solution.py:26
  29.8 3.3 %collective-permute-start.3 = (f32[4,8,2,128]{3,2,1,0:T(2,128)S(1)}, f32[4,8,2,128]{3,2,1,0:T(2,128)S(1)}, u32[]{:S(2)}, u32[]{:S(2)}) collective-permute-start(f32[4,8,2,128]{3,2,1,0:T(2,128)S(1)} %get-tuple-element.13), channel_id=1, source_target_pairs={{1,0},{2,1},{3,2},{0,3},{5,4},{6,5},{7,6},{4,7},{9,8},{10,9},{11,1... | collective-permute-start | bytes 98312 | tf_op jit(solution)/shard_map/ppermute | solution.py:28
  35.7 6.2 %collective-permute-start.4 = (f32[1,128,128]{2,1,0:T(8,128)S(1)}, f32[1,128,128]{2,1,0:T(8,128)S(1)}, u32[]{:S(2)}, u32[]{:S(2)}) collective-permute-start(f32[1,128,128]{2,1,0:T(8,128)S(1)} %slice_bitcast_fusion.8), channel_id=1, source_target_pairs={{0,4},{4,8},{8,12},{12,0},{1,5},{5,9},{9,13},{13,1},{2,6},{6,10},{... | collective-permute-start | bytes 196616 | tf_op jit(solution)/shard_map/ppermute | solution.py:37
  36.9 3.0 %collective-permute-start.5 = (f32[4,1,128]{2,1,0:T(1,128)S(1)}, f32[4,1,128]{2,1,0:T(1,128)S(1)}, u32[]{:S(2)}, u32[]{:S(2)}) collective-permute-start(f32[4,1,128]{2,1,0:T(1,128)S(1)} %slice_bitcast_fusion.9), channel_id=1, source_target_pairs={{0,1},{1,2},{2,3},{3,0},{4,5},{5,6},{6,7},{7,4},{8,9},{9,10},{10,1... | collective-permute-start | bytes 6152 | tf_op jit(solution)/shard_map/ppermute | solution.py:37
  44.6 13.1 %all-to-all-start = ((f32[4,4,4096]{2,0,1:T(4,128)}), f32[4,4,4096]{2,0,1:T(4,128)S(1)}, u32[]{:S(2)}, u32[]{:S(2)}) async-start(f32[4,4,4096]{2,0,1:T(4,128)} %copy.26), calls=%async_computation | async-start | bytes 524288 | tf_op jit(solution)/shard_map/all_to_all | solution.py:162
  71.8 4.3 %collective-permute-start.6 = (f32[1,128,128]{2,1,0:T(8,128)S(1)}, f32[1,128,128]{2,1,0:T(8,128)S(1)}, u32[]{:S(2)}, u32[]{:S(2)}) collective-permute-start(f32[1,128,128]{2,1,0:T(8,128)S(1)} %get-tuple-element.33), channel_id=1, source_target_pairs={{4,0},{8,4},{12,8},{0,12},{5,1},{9,5},{13,9},{1,13},{6,2},{10,6},{... | collective-permute-start | bytes 196616 | tf_op jit(solution)/shard_map/ppermute | solution.py:28
  73.3 6.1 %collective-permute-start.7 = (f32[1,128,128]{2,1,0:T(8,128)S(1)}, f32[1,128,128]{2,1,0:T(8,128)S(1)}, u32[]{:S(2)}, u32[]{:S(2)}) collective-permute-start(f32[1,128,128]{2,1,0:T(8,128)S(1)} %get-tuple-element.32), channel_id=1, source_target_pairs={{0,4},{4,8},{8,12},{12,0},{1,5},{5,9},{9,13},{13,1},{2,6},{6,10},{... | collective-permute-start | bytes 196616 | tf_op jit(solution)/shard_map/ppermute | solution.py:26
  79.4 1.3 collective-permute-start.8
  79.4 3.1 %collective-permute-start.9 = (f32[6,1,128]{2,1,0:T(1,128)S(1)}, f32[6,1,128]{2,1,0:T(1,128)S(1)}, u32[]{:S(2)}, u32[]{:S(2)}) collective-permute-start(f32[6,1,128]{2,1,0:T(1,128)S(1)} %get-tuple-element.26), channel_id=1, source_target_pairs={{0,1},{1,2},{2,3},{3,0},{4,5},{5,6},{6,7},{7,4},{8,9},{9,10},{10,1... | collective-permute-start | bytes 9224 | tf_op jit(solution)/shard_map/ppermute | solution.py:26
  130.0 52.0 %copy-start.4 = (s32[8]{0:T(128)S(1)}, s32[8]{0:T(128)}, u32[]{:S(2)}) copy-start(s32[8]{0:T(128)} %param.9) | copy-start | bytes 100
  130.0 52.0 %copy-start.5 = (s32[8]{0:T(128)S(1)}, s32[8]{0:T(128)}, u32[]{:S(2)}) copy-start(s32[8]{0:T(128)} %param.8) | copy-start | bytes 100
  130.0 11.5 %all-to-all-start.3 = ((f32[4,4,4096]{2,1,0:T(4,128)}), f32[4,4,4096]{2,1,0:T(4,128)S(1)}, u32[]{:S(2)}, u32[]{:S(2)}) async-start(f32[4,4,4096]{2,1,0:T(4,128)} %all_to_all.57), calls=%async_computation.3 | async-start | bytes 524288 | tf_op jit(solution)/shard_map/all_to_all | solution.py:176
  175.3 4.3 %collective-permute-start.10 = (f32[1,128,128]{2,1,0:T(8,128)S(1)}, f32[1,128,128]{2,1,0:T(8,128)S(1)}, u32[]{:S(2)}, u32[]{:S(2)}) collective-permute-start(f32[1,128,128]{2,1,0:T(8,128)S(1)} %get-tuple-element.31), channel_id=1, source_target_pairs={{4,0},{8,4},{12,8},{0,12},{5,1},{9,5},{13,9},{1,13},{6,2},{10,6},{... | collective-permute-start | bytes 196616 | tf_op jit(solution)/shard_map/ppermute | solution.py:28
  175.4 6.1 %collective-permute-start.11 = (f32[1,128,128]{2,1,0:T(8,128)S(1)}, f32[1,128,128]{2,1,0:T(8,128)S(1)}, u32[]{:S(2)}, u32[]{:S(2)}) collective-permute-start(f32[1,128,128]{2,1,0:T(8,128)S(1)} %get-tuple-element.30), channel_id=1, source_target_pairs={{0,4},{4,8},{8,12},{12,0},{1,5},{5,9},{9,13},{13,1},{2,6},{6,10},{... | collective-permute-start | bytes 196616 | tf_op jit(solution)/shard_map/ppermute | solution.py:26
  181.5 1.3 collective-permute-start.12
  181.5 3.1 %collective-permute-start.13 = (f32[6,1,128]{2,1,0:T(1,128)S(1)}, f32[6,1,128]{2,1,0:T(1,128)S(1)}, u32[]{:S(2)}, u32[]{:S(2)}) collective-permute-start(f32[6,1,128]{2,1,0:T(1,128)S(1)} %get-tuple-element.24), channel_id=1, source_target_pairs={{0,1},{1,2},{2,3},{3,0},{4,5},{5,6},{6,7},{7,4},{8,9},{9,10},{10,1... | collective-permute-start | bytes 9224 | tf_op jit(solution)/shard_map/ppermute | solution.py:26
  216.9 5.5 %copy-start.2 = (f32[4,128,128]{2,1,0:T(8,128)}, f32[4,128,128]{2,1,0:T(8,128)S(1)}, u32[]{:S(2)}) copy-start(f32[4,128,128]{2,1,0:T(8,128)S(1)} %multiply_add_fusion) | copy-start | bytes 786436
  216.9 4.3 %collective-permute-start.14 = (f32[1,128,128]{2,1,0:T(8,128)S(1)}, f32[1,128,128]{2,1,0:T(8,128)S(1)}, u32[]{:S(2)}, u32[]{:S(2)}) collective-permute-start(f32[1,128,128]{2,1,0:T(8,128)S(1)} %slice.282), channel_id=1, source_target_pairs={{0,12},{4,0},{8,4},{12,8},{1,13},{5,1},{9,5},{13,9},{2,14},{6,2},{... | collective-permute-start | bytes 196616 | tf_op jit(solution)/shard_map/ppermute | solution.py:37
  217.0 1.4 collective-permute-start.15
where the time goes:
time: 223 us; the launch traced here: 222 us
  blocking collectives  113 us (51%)
  waiting for transfers between devices  62.2 us (28%)
  starting transfers between devices  21.9 us (10%)
  matrix products  8.48 us (4%)
  other arithmetic  8.44 us (4%)
  between operations  5.12 us (2%)
  local copies, waits for them, and re-layouts  3.17 us (1%)
    psum x2, blocking collectives, energy_sum(): return lax.psum(jnp.sum(residual * precond), ('gx', 'gy'))  60.2 us
    psum x1, blocking collectives, per_device(): lax.psum(jnp.sum(direction * applied), ('gx', 'gy'))  30.1 us
    ppermute x6, waiting for transfers between devices, extended(): lax.ppermute(tail, axis, [(i, (i + 1) % count) for i in range(count)])  22.3 us
    ppermute x6, waiting for transfers between devices, extended(): lax.ppermute(head, axis, [((i + 1) % count, i) for i in range(count)])  15.7 us
    all_to_all x1, blocking collectives, local_solve(): pencil = lax.all_to_all(flat, 'gx', split_axis=1, concat_axis=0, tiled=True)  11.6 us
    all_to_all x1, blocking collectives, local_solve(): lax.all_to_all(grouped.reshape(total_x, width_cols), 'gx', split_axis=0,...  11.2 us
    all_to_all x1, waiting for transfers between devices, local_solve(): pencil = lax.all_to_all(flat, 'gx', split_axis=1, concat_axis=0, tiled=True)  9.49 us
    all_to_all x1, waiting for transfers between devices, local_solve(): lax.all_to_all(grouped.reshape(total_x, width_cols), 'gx', split_axis=0,...  7.75 us
  transfers between devices with their start and end apart: 18, of which 17 were waited for; matrix products, arithmetic and copies ran while one was open for 1% of the time, Pallas kernels for 0%

commit v1 on v0

v1 whole, which is shorter than its diff:
```python
import functools
import math

import jax
import jax.numpy as jnp
import numpy as np
from jax import lax
from jax.experimental import pallas as pl
from jax.experimental.pallas import tpu as pltpu
from jax.sharding import PartitionSpec as P

BLOCK = 128

TIME_INCREMENT = 0.2
MARANGONI = 1.5
DRAG_RATE = 4.0
LASER_POWER = 3.0
SPOT_RADIUS = 5.0

F32 = jnp.float32
VMEM = pl.BlockSpec(memory_space=pltpu.VMEM)
SMEM = pl.BlockSpec(memory_space=pltpu.SMEM)


def call(body, operands, shapes, scratch=(), scalars=1, flops=1 << 20):
    out_shape = [jax.ShapeDtypeStruct(shape, F32) for shape in shapes]
    moved = 4 * sum(math.prod(shape) for shape in shapes)
    return pl.pallas_call(
        body,
        out_shape=out_shape,
        in_specs=[SMEM] * scalars + [VMEM] * (len(operands) - scalars),
        out_specs=[VMEM] * len(shapes),
        scratch_shapes=list(scratch),
        compiler_params=pltpu.CompilerParams(vmem_limit_bytes=44 << 20),
        cost_estimate=pl.CostEstimate(flops=flops, bytes_accessed=2 * moved, transcendentals=0),
    )(*operands)


def dot(left, right):
    return jnp.dot(left, right, precision=lax.Precision.HIGHEST, preferred_element_type=F32)


def total(cells):
    return jnp.sum(jnp.sum(cells, axis=0, keepdims=True), axis=1, keepdims=True)


def loop(low, high, body, start):
    if isinstance(high, int) and isinstance(low, int) and high - low <= 24:
        carry = start
        for index in range(low, high):
            carry = body(index, carry)
        return carry
    return lax.fori_loop(low, high, body, start)


def sines(length):
    positions = np.arange(length) + 1.0
    step = math.pi / (length + 1)
    table = np.sqrt(2.0 / (length + 1)) * np.sin(step * positions[:, None] * positions[None, :])
    return table, 2.0 - 2.0 * np.cos(step * positions)


def lane_shift(cells, offset):
    width = cells.shape[1]
    lane = lax.broadcasted_iota(jnp.int32, cells.shape, 1)
    moved = pltpu.roll(cells, (-offset) % width, 1)
    keep = lane < width - offset if offset > 0 else lane >= -offset
    return jnp.where(keep, moved, 0.0)


def column(row):
    length = row.shape[1]
    shape = (length, length)
    same = lax.broadcasted_iota(jnp.int32, shape, 0) == lax.broadcasted_iota(jnp.int32, shape, 1)
    return jnp.sum(jnp.where(same, row, 0.0), axis=1, keepdims=True)


def advance(layers, padded, index, speed):
    middle = layers[2]
    rows = middle.shape[0]
    speed_x, speed_y, speed_z = speed
    ahead = speed_x >= 0.0
    near = jnp.where(ahead, layers[1], layers[3])
    far = jnp.where(ahead, layers[0], layers[4])
    rate = jnp.abs(speed_x) * (1.5 * middle - 2.0 * near + 0.5 * far)
    ahead = speed_y >= 0.0
    near = jnp.where(ahead, padded[index, pl.ds(7, rows), :], padded[index, pl.ds(9, rows), :])
    far = jnp.where(ahead, padded[index, pl.ds(6, rows), :], padded[index, pl.ds(10, rows), :])
    rate = rate + jnp.abs(speed_y) * (1.5 * middle - 2.0 * near + 0.5 * far)
    ahead = speed_z >= 0.0
    near = jnp.where(ahead, lane_shift(middle, -1), lane_shift(middle, 1))
    far = jnp.where(ahead, lane_shift(middle, -2), lane_shift(middle, 2))
    rate = rate + jnp.abs(speed_z) * (1.5 * middle - 2.0 * near + 0.5 * far)
    return middle - TIME_INCREMENT * rate


def pad_rows(padded, index, before, middle, after):
    rows = middle.shape[0]
    padded[index, pl.ds(8, rows), :] = middle
    padded[index, pl.ds(6, 2), :] = before
    padded[index, pl.ds(8 + rows, 2), :] = after


def march_kernel(flow, low_x, high_x, low_y, high_y, thermal, low_t, high_t, flag, star, padded):
    _, layers, rows, depth = flow.shape
    top = lax.broadcasted_iota(jnp.int32, (rows, depth), 1) == depth - 1
    for index in range(layers):
        for part in range(3):
            pad_rows(
                padded, part, low_y[part, index], flow[part, index], high_y[part, index]
            )
        pad_rows(padded, 3, low_y[3, index], thermal[index], high_y[3, index])
        speed = [flow[part, index] for part in range(3)]
        behind = thermal[index - 1] if index > 0 else column(low_t[...])
        before = thermal[index + 1] if index + 1 < layers else column(high_t[...])
        pull = -MARANGONI * 0.5 * TIME_INCREMENT
        drive_x = jnp.where(top, pull * (before - behind), 0.0)
        drive_y = jnp.where(
            top, pull * (padded[3, pl.ds(9, rows), :] - padded[3, pl.ds(7, rows), :]), 0.0
        )
        drag = 1.0 / (1.0 + TIME_INCREMENT * DRAG_RATE * flag[index].astype(F32))
        for part in range(3):
            around = []
            for other in range(index - 2, index + 3):
                if other < 0:
                    around.append(low_x[part, other + 2])
                elif other >= layers:
                    around.append(high_x[part, other - layers])
                else:
                    around.append(flow[part, other])
            moved = advance(around, padded, part, speed)
            if part == 0:
                moved = moved + drive_x
            if part == 1:
                moved = moved + drive_y
            star[part, index] = moved * drag


def heat_kernel(thermal, low_x, high_x, low_y, high_y, flow, heat, warmed, padded):
    layers, rows, depth = thermal.shape
    top = lax.broadcasted_iota(jnp.int32, (rows, depth), 1) == depth - 1
    for index in range(layers):
        pad_rows(padded, 0, low_y[index], thermal[index], high_y[index])
        around = []
        for other in range(index - 2, index + 3):
            if other < 0:
                around.append(low_x[other + 2])
            elif other >= layers:
                around.append(high_x[other - layers])
            else:
                around.append(thermal[other])
        speed = [flow[part, index] for part in range(3)]
        gain = TIME_INCREMENT * column(heat[pl.ds(index, 1), :])
        warmed[index] = advance(around, padded, 0, speed) + jnp.where(top, gain, 0.0)


def laser_heat(start_x, start_y, span_x, span_y, total_x, total_y, spots_a, spots_b):
    cells_x = start_x + jnp.arange(span_x, dtype=jnp.int32)
    cells_y = start_y + jnp.arange(span_y, dtype=jnp.int32)
    dist_x = (
        (cells_x[:, None] - spots_a[None, :] + total_x // 2) % total_x - total_x // 2
    ).astype(F32)
    dist_y = (
        (cells_y[:, None] - spots_b[None, :] + total_y // 2) % total_y - total_y // 2
    ).astype(F32)
    spot_x = jnp.exp(-(dist_x * dist_x) / (SPOT_RADIUS * SPOT_RADIUS))
    spot_y = jnp.exp(-(dist_y * dist_y) / (SPOT_RADIUS * SPOT_RADIUS))
    return LASER_POWER * jnp.dot(spot_x, spot_y.T, precision=lax.Precision.HIGHEST)


def tables_kernel(group, layers, place, diagonal, ratio, weight):
    length = group * layers
    mine = place[0]
    first = mine * layers
    diag = diagonal[...]
    ratio[0] = jnp.zeros_like(diag)

    def step(index, previous):
        current = 1.0 / (diag - previous)
        ratio[index] = current
        return current

    loop(1, length + 1, step, jnp.zeros_like(diag))

    def decay(low, high):
        return lax.fori_loop(
            low + 1, high + 1, lambda index, value: value * ratio[index], jnp.ones_like(diag)
        )

    def green(index):
        return 1.0 / (diag - ratio[index] - ratio[jnp.maximum(length - 1 - index, 0)])

    rounds = group.bit_length() - 1
    for turn in range(rounds):
        half = 1 << turn
        right = ((mine >> turn) & 1) == 1
        start = (mine >> (turn + 1)) << (turn + 1)
        cut = (start + half) * layers
        end = (start + 2 * half) * layers
        weight[4 * turn] = decay(cut - 1, end - 1)
        weight[4 * turn + 1] = decay(length - 1 - cut, length - 1 - start * layers)
        low = jnp.where(right, cut - 1, length - 1 - cut)
        high = jnp.where(right, first - 1, length - 1 - first - layers)
        weight[4 * turn + 2] = decay(low, high)
        weight[4 * turn + 3] = green(cut) * ratio[cut]
    inner = jnp.where(mine == group - 1, 0.0, 1.0)
    weight[4 * rounds] = inner * green(first + layers)


def source_kernel(
    length, place, star, before_x, before_y, table_y, table_z, ratio, source, ends, rows_
):
    _, layers, rows, depth = star.shape
    first = place[0] * layers
    for index in range(layers):
        rows_[pl.ds(8, rows), :] = star[1, index]
        rows_[pl.ds(7, 1), :] = before_y[pl.ds(index, 1), :]
        behind = star[0, index - 1] if index > 0 else before_x[...]
        sink = star[0, index] - behind
        sink = sink + (star[1, index] - rows_[pl.ds(7, rows), :])
        sink = sink + (star[2, index] - lane_shift(star[2, index], -1))
        source[index] = dot(dot(table_y[...], -sink), table_z[...])
    forward = source[0]
    for index in range(1, layers):
        forward = source[index] + ratio[first + index] * forward
    ends[0] = forward
    backward = source[layers - 1]
    for index in range(layers - 2, -1, -1):
        backward = source[index] + ratio[length - 1 - first - index] * backward
    ends[1] = backward


def face_rows(plane, edge):
    return (
        jnp.sum(plane * edge[0], axis=0, keepdims=True),
        jnp.sum(plane * edge[1], axis=0, keepdims=True),
    )


def faces_kernel(length, place, source, ratio, edge, faces, sweep):
    layers, rows, depth = source.shape
    first = place[0] * layers
    inside = lambda index: (index >= first) & (index < first + layers)
    zero = jnp.zeros((rows, depth), F32)

    def own(index):
        value = source[jnp.clip(index - first, 0, layers - 1)]
        return jnp.where(inside(index), value, 0.0)

    def down(index, previous):
        current = own(index) + ratio[index] * previous
        sweep[index] = current
        return current

    loop(0, length, down, zero)

    def up(back, carry):
        following, energy = carry
        index = length - 1 - back
        value = ratio[index + 1] * (sweep[index] + following)
        low, high = face_rows(value, edge)
        faces[pl.ds(index, 1), :] = low
        faces[pl.ds(length + index, 1), :] = high
        return value, energy + own(index) * value

    _, energy = loop(0, length, up, (zero, zero))
    faces[pl.ds(2 * length, 8), :] = jnp.broadcast_to(total(energy), (8, depth))


def merge_kernel(
    turn, last, length, place, ends, other, sums, faces, other_faces, weight, ratio,
    new_ends, new_sums, new_faces,
):
    count = faces.shape[0] - 8
    right = ((place[0] >> turn) & 1) == 1
    left_s = jnp.where(right, other[0], ends[0])
    right_s = jnp.where(right, ends[0], other[0])
    left_t = jnp.where(right, other[1], ends[1])
    right_t = jnp.where(right, ends[1], other[1])
    own = weight[4 * turn + 2]
    new_sums[0] = sums[0] + jnp.where(right, left_s * own, 0.0)
    new_sums[1] = sums[1] + jnp.where(right, 0.0, right_t * own)
    scale = ratio[length] if last else 1.0
    new_ends[0] = scale * (right_s + left_s * weight[4 * turn])
    new_ends[1] = scale * (left_t + right_t * weight[4 * turn + 1])
    new_faces[...] = faces[...] + other_faces[...]
    cross = 2.0 * total(left_s * right_t * weight[4 * turn + 3])
    new_faces[pl.ds(count, 8), :] = new_faces[pl.ds(count, 8), :] + cross


def coarse_kernel(
    length, place, source, ends, beyond, sums, faces, weight, ratio, edge,
    precond, image, report, sweep,
):
    layers, rows, depth = source.shape
    mine = place[0]
    first = mine * layers
    lone = weight.shape[0] - 1
    count = faces.shape[0] - 8
    forward = sums[0]
    for index in range(layers):
        forward = source[index] + ratio[first + index] * forward
        sweep[index] = forward
    value = weight[lone] * (sums[1] + ratio[first + layers] * forward)
    is_last = first + layers == length
    precond[layers] = jnp.where(is_last, beyond[1], value)
    for index in range(layers - 1, -1, -1):
        value = ratio[first + index + 1] * (sweep[index] + value)
        precond[index] = value
    lead, trail = edge[0], edge[1]

    def pull(index):
        below = faces[pl.ds(length + index, 1), :]
        above = faces[pl.ds(2 * length + index, 1), :]
        return below, above

    def down(index, previous):
        below, above = pull(index)
        current = lead * below + trail * above + ratio[index] * previous
        if isinstance(index, int):
            if index == 0:
                current = current + beyond[0]
            if index == length - 1:
                current = current + beyond[1]
        else:
            current = current + jnp.where(index == 0, beyond[0], 0.0)
            current = current + jnp.where(index == length - 1, beyond[1], 0.0)
        sweep[index] = current
        return current

    zero = jnp.zeros((rows, depth), F32)
    loop(0, length, down, zero)
    line = jnp.zeros((1, depth), F32)

    def up(back, carry):
        following, linked, squared = carry
        index = length - 1 - back
        value = ratio[index + 1] * (sweep[index] + following)
        sweep[index] = value
        low, high = face_rows(value, edge)
        report[pl.ds(index, 1), :] = low
        report[pl.ds(length + index, 1), :] = high
        below, above = pull(index)
        linked = linked + faces[pl.ds(index, 1), :] * below
        squared = squared + low * below + high * above
        return value, linked, squared

    _, linked, squared = loop(0, length, up, (zero, line, line))
    sweep[length] = sweep[0]
    for index in range(layers + 1):
        image[index] = sweep[first + index]
    head, tail = sweep[0], sweep[length - 1]
    linked = 2.0 * total(linked) + total(ends[1] * beyond[0] + ends[0] * beyond[1])
    squared = total(squared) + total(head * beyond[0] + tail * beyond[1])
    crossing = 2.0 * total(head * tail)
    where = 2 * length
    report[pl.ds(where, 1), :] = faces[pl.ds(count, 1), :]
    report[pl.ds(where + 1, 1), :] = jnp.broadcast_to(linked, (1, depth))
    report[pl.ds(where + 2, 1), :] = jnp.broadcast_to(squared, (1, depth))
    report[pl.ds(where + 3, 1), :] = jnp.broadcast_to(crossing, (1, depth))
    report[pl.ds(where + 4, 4), :] = jnp.zeros((4, depth), F32)


def physical_kernel(precond, image, table_y, table_z, precond_out, image_out):
    for index in range(precond.shape[0]):
        precond_out[index] = dot(dot(table_y[...], precond[index]), table_z[...])
        image_out[index] = dot(dot(table_y[...], image[index]), table_z[...])


def project_kernel(
    length, paired, place, star, precond, image, faces, table_z, *refs
):
    reports, (flow, pressure, field, rows_) = refs[:-4], refs[-4:]
    _, layers, rows, depth = star.shape
    first = place[0] * layers
    where = 2 * length
    sums = reports[0][pl.ds(where, 8), :]
    for other in reports[1:]:
        sums = sums + other[pl.ds(where, 8), :]
    pairs = jnp.zeros((1, depth), F32)
    for index in range(len(reports)):
        upper, lower = reports[index], reports[(index + 1) % len(reports)]
        pairs = pairs + jnp.sum(
            upper[pl.ds(0, length), :] * lower[pl.ds(length, length), :], axis=0, keepdims=True
        )
    energy, linked, squared, crossing = (sums[k : k + 1, 0:1] for k in range(4))
    if not paired:
        crossing = crossing + 2.0 * total(pairs)
    first_image = energy - linked
    step = energy / first_image
    beta = (energy * squared - linked * linked) / (first_image * first_image)
    rest = -linked / first_image
    second_image = (
        rest * rest * first_image
        + 2.0 * rest * step * (linked - squared)
        + step * step * (squared - crossing)
        - beta * beta * first_image
    )
    second_step = beta * energy / second_image
    alpha = step + second_step * (rest + beta)
    gamma = second_step * step
    for index in range(layers + 1):
        field[index] = alpha * precond[index] + gamma * image[index]
    own = pl.ds(2 * length + first, layers)
    following = alpha * faces[own, :] + gamma * reports[-1][pl.ds(first, layers), :]
    following = dot(following, table_z[...])
    for index in range(layers):
        value = field[index]
        pressure[index] = value
        rows_[pl.ds(0, rows), :] = value
        rows_[pl.ds(rows, 1), :] = following[index : index + 1]
        flow[0, index] = star[0, index] - (field[index + 1] - value)
        flow[1, index] = star[1, index] - (rows_[pl.ds(1, rows), :] - value)
        flow[2, index] = star[2, index] - (lane_shift(value, 1) - value)


def along(array, axis, by):
    length = lax.axis_size(axis)
    return lax.ppermute(array, axis, [(i, (i + by) % length) for i in range(length)])


def swapped(array, axis, bit):
    return lax.ppermute(array, axis, [(i, i ^ bit) for i in range(lax.axis_size(axis))])


def per_device(melt_flow, thermal_state, powder_flag, spot_lateral_a_cell, spot_lateral_b_cell):
    layers, rows, depth = thermal_state.shape
    count_x, count_y = lax.axis_size("gx"), lax.axis_size("gy")
    group = min(count_x, BLOCK // layers)
    blocks = count_x // group
    length = group * layers
    rounds = group.bit_length() - 1
    sine_y, values_y = sines(rows)
    sine_z, values_z = sines(depth)
    table_y = jnp.asarray(sine_y, F32)
    table_z = jnp.asarray(sine_z, F32)
    edge = jnp.asarray(
        np.broadcast_to(sine_y[[0, rows - 1]][:, :, None], (2, rows, depth)), F32
    )
    diagonal = jnp.asarray(2.0 + values_y[:, None] + values_z[None, :], F32)
    place = (lax.axis_index("gx") % group).astype(jnp.int32).reshape(1)
    plane = (rows, depth)

    states = jnp.concatenate([melt_flow, thermal_state[None]], 0)
    low_x = along(melt_flow[:, -2:], "gx", 1)
    high_x = along(melt_flow[:, :2], "gx", -1)
    low_t = along(thermal_state[-1, :, -1].reshape(1, rows), "gx", 1)
    high_t = along(thermal_state[0, :, -1].reshape(1, rows), "gx", -1)
    low_y = along(states[:, :, -2:], "gy", 1)
    high_y = along(states[:, :, :2], "gy", -1)
    far_low = along(thermal_state[-2:], "gx", 1)
    far_high = along(thermal_state[:2], "gx", -1)

    ratio, weight = call(
        functools.partial(tables_kernel, group, layers),
        [place, diagonal],
        [(length + 1,) + plane, (4 * rounds + 1,) + plane],
    )
    (star,) = call(
        march_kernel,
        [
            melt_flow, low_x, high_x, low_y, high_y, thermal_state, low_t, high_t,
            powder_flag.astype(jnp.int32),
        ],
        [(3, layers) + plane],
        [pltpu.VMEM((4, rows + 16, depth), F32)],
        scalars=0,
    )
    before_x = along(star[0, -1], "gx", 1)
    before_y = along(star[1, :, -1], "gy", 1)
    source, ends = call(
        functools.partial(source_kernel, length),
        [place, star, before_x, before_y, table_y, table_z, ratio],
        [(layers,) + plane, (2,) + plane],
        [pltpu.VMEM((rows + 16, depth), F32)],
    )
    (faces,) = call(
        functools.partial(faces_kernel, length),
        [place, source, ratio, edge],
        [(2 * length + 8, depth)],
        [pltpu.VMEM((length,) + plane, F32)],
    )
    below = along(faces[length : 2 * length], "gy", 1)
    above = along(faces[:length], "gy", -1)
    faces = jnp.concatenate([faces[:length], below, above, faces[2 * length :]], 0)
    sums = jnp.zeros((2,) + plane, F32)
    for turn in range(rounds):
        other = swapped(ends, "gx", 1 << turn)
        other_faces = swapped(faces, "gx", 1 << turn)
        ends, sums, faces = call(
            functools.partial(merge_kernel, turn, turn + 1 == rounds, length),
            [place, ends, other, sums, faces, other_faces, weight, ratio],
            [(2,) + plane, (2,) + plane, faces.shape],
        )
    if blocks == 1:
        beyond = ends
    else:
        beyond = jnp.stack([along(ends[0], "gx", group), along(ends[1], "gx", -group)])
    precond, image, report = call(
        functools.partial(coarse_kernel, length),
        [place, source, ends, beyond, sums, faces, weight, ratio, edge],
        [(layers + 1,) + plane, (layers + 1,) + plane, (2 * length + 8, depth)],
        [pltpu.VMEM((length + 1,) + plane, F32)],
    )
    if blocks > 1:
        ahead = along(image[0], "gx", -1)
        tail = place[0] == group - 1
        image = image.at[layers].set(jnp.where(tail, ahead, image[layers]))
        upper = along(report[:length], "gy", -1)
        crossing = jnp.sum(ahead * image[layers - 1]) + jnp.sum(upper * report[length : 2 * length])
        crossing = jnp.where(tail, 2.0 * crossing, 0.0)
        numbers = report[2 * length :]
        numbers = jnp.where(place[0] == group - 1, numbers, 0.0).at[3].set(crossing)
        report = report.at[2 * length :].set(lax.psum(numbers, "gx"))
    reports = [report] + [along(report, "gy", by) for by in range(1, count_y)]
    precond, image = call(
        physical_kernel,
        [precond, image, table_y, table_z],
        [(layers + 1,) + plane, (layers + 1,) + plane],
        scalars=0,
    )
    heat = laser_heat(
        lax.axis_index("gx") * layers,
        lax.axis_index("gy") * rows,
        layers,
        rows,
        layers * count_x,
        rows * count_y,
        spot_lateral_a_cell,
        spot_lateral_b_cell,
    )
    (warmed,) = call(
        heat_kernel,
        [thermal_state, far_low, far_high, low_y[3], high_y[3], melt_flow, heat],
        [(layers,) + plane],
        [pltpu.VMEM((1, rows + 16, depth), F32)],
        scalars=0,
    )
    flow, pressure = call(
        functools.partial(project_kernel, length, blocks > 1),
        [place, star, precond, image, faces, table_z] + reports,
        [(3, layers) + plane, (layers,) + plane],
        [pltpu.VMEM((layers + 1,) + plane, F32), pltpu.VMEM((rows + 16, depth), F32)],
    )
    return (flow, warmed, pressure)


def solution(mesh):
    placed = (
        P(None, ("runs", "gx"), "gy", None),
        P(("runs", "gx"), "gy", None),
        P(("runs", "gx"), "gy", None),
        P("runs"),
        P("runs"),
    )
    return jax.shard_map(
        per_device,
        mesh=mesh,
        in_specs=placed,
        out_specs=(
            P(None, ("runs", "gx"), "gy", None),
            P(("runs", "gx"), "gy", None),
            P(("runs", "gx"), "gy", None),
        ),
        check_vma=False,
    )
```

time: 223 us -> 65.5 us (0.29)
  blocking collectives: 113 us -> 0 us
  waiting for transfers between devices: 62.2 us -> 35.8 us
  other arithmetic: 8.44 us -> 0.03 us
  matrix products: 8.48 us -> 0.21 us
  Pallas kernels: 0 us -> 8.05 us
  between operations: 5.12 us -> 0.91 us
  starting transfers between devices: 21.9 us -> 18.2 us
    psum x3 -> x0, blocking collectives: 90.3 us -> none  [the longest x2 60.2 us: energy_sum(): return lax.psum(jnp.sum(residual * precond), ('gx', 'gy'))]
    all_to_all x2 -> x0, blocking collectives: 22.8 us -> none  [the longest x1 11.6 us: local_solve(): pencil = lax.all_to_all(flat, 'gx', split_axis=1, concat_axis=0, tiled=True)]
    all_to_all x2 -> x0, waiting for transfers between devices: 17.2 us -> none  [the longest x1 9.49 us: local_solve(): pencil = lax.all_to_all(flat, 'gx', split_axis=1, concat_axis=0, tiled=True)]
    ppermute x16 -> x19, waiting for transfers between devices: 45 us -> 35.8 us  [the longest x15 24.8 us: along(): lax.ppermute(array, axis, [(i, (i + by) % length) for i in range(length)])]
    dot_general x12 -> x0, matrix products: 8.27 us -> none  [the longest x2 1.97 us: local_solve(): return jnp.einsum('jb,ibk->ijk', table_y, spectrum, precision=highest)]
    pallas_call x0 -> x10, Pallas kernels: none -> 8.05 us  [call(): pl.pallas_call(body, out_shape=out_shape, in_specs=[SMEM] * scalars + [VM...]
    all_to_all x2 -> x0, starting transfers between devices: 7.13 us -> none  [the longest x1 3.72 us: local_solve(): lax.all_to_all(grouped.reshape(total_x, width_cols), 'gx', split_axis=0,...]
    ppermute x16 -> x19, starting transfers between devices: 14.7 us -> 18.2 us  [the longest x15 15.3 us: along(): lax.ppermute(array, axis, [(i, (i + by) % length) for i in range(length)])]
  transfers between devices with their start and end apart: 18 -> 19, of which waited for: 17 -> 8; matrix products, arithmetic and copies ran while one was open for 1% -> 2% of each run, Pallas kernels for 0% -> 10%
where the time goes in v1:
time: 65.5 us; the launch traced here: 65.4 us
  waiting for transfers between devices  35.8 us (55%)
  starting transfers between devices  18.2 us (28%)
  Pallas kernels  8.05 us (12%)
  local copies, waits for them, and re-layouts  2.18 us (3%)
  between operations  0.91 us (1%)
    ppermute x15, waiting for transfers between devices, along(): lax.ppermute(array, axis, [(i, (i + by) % length) for i in range(length)])  24.8 us
    ppermute x15, starting transfers between devices, along(): lax.ppermute(array, axis, [(i, (i + by) % length) for i in range(length)])  15.3 us
    ppermute x4, waiting for transfers between devices, swapped(): lax.ppermute(array, axis, [(i, i ^ bit) for i in range(lax.axis_size(axis...  11 us
    pallas_call x10, Pallas kernels, call(): pl.pallas_call(body, out_shape=out_shape, in_specs=[SMEM] * scalars + [VM...  8.05 us
    ppermute x4, starting transfers between devices, swapped(): lax.ppermute(array, axis, [(i, i ^ bit) for i in range(lax.axis_size(axis...  2.93 us
  transfers between devices with their start and end apart: 19, of which 8 were waited for; matrix products, arithmetic and copies ran while one was open for 2% of the time, Pallas kernels for 10%

profile of v1, /device:TPU:0, one launch (start us, length us, event | category | flops | bytes accessed | tf_op | source)
XLA Modules:
  0.0 65.4 jit_solution(3746776496390954459)
XLA Ops:
  0.6 1.3 %fusion.48 = (f32[3,2,128,128]{3,2,1,0:T(8,128)S(1)}, f32[3,2,128,128]{3,2,1,0:T(8,128)S(1)}) fusion(f32[3,4,128,128]{3,2,1,0:T(8,128)} %flow.3), kind=kLoop, calls=%fused_computation.63 | loop fusion | bytes 1572864 | tf_op jit(solution)/shard_map/slice | solution.py:446
  1.9 3.1 %collective-permute-start = (f32[3,2,128,128]{3,2,1,0:T(8,128)S(1)}, f32[3,2,128,128]{3,2,1,0:T(8,128)S(1)}, u32[]{:S(2)}, u32[]{:S(2)}) collective-permute-start(f32[3,2,128,128]{3,2,1,0:T(8,128)S(1)} %get-tuple-element.42), channel_id=1, source_target_pairs={{0,4},{4,8},{8,12},{12,0},{1,5},{5,9},{9,13},{13,1},{2,6},{6,10},{... | collective-permute-start | bytes 1179656 | tf_op jit(solution)/shard_map/ppermute | solution.py:419
  5.0 2.1 %collective-permute-start.1 = (f32[3,2,128,128]{3,2,1,0:T(8,128)S(1)}, f32[3,2,128,128]{3,2,1,0:T(8,128)S(1)}, u32[]{:S(2)}, u32[]{:S(2)}) collective-permute-start(f32[3,2,128,128]{3,2,1,0:T(8,128)S(1)} %get-tuple-element.41), channel_id=1, source_target_pairs={{0,12},{4,0},{8,4},{12,8},{1,13},{5,1},{9,5},{13,9},{2,14},{6,2},{... | collective-permute-start | bytes 1179656 | tf_op jit(solution)/shard_map/ppermute | solution.py:419
  7.4 1.7 %collective-permute-start.3 = (f32[4,4,2,128]{3,2,1,0:T(2,128)S(1)}, f32[4,4,2,128]{3,2,1,0:T(2,128)S(1)}, u32[]{:S(2)}, u32[]{:S(2)}) collective-permute-start(f32[4,4,2,128]{3,2,1,0:T(2,128)S(1)} %get-tuple-element.39), channel_id=1, source_target_pairs={{0,3},{1,0},{2,1},{3,2},{4,7},{5,4},{6,5},{7,6},{8,11},{9,8},{10,9... | collective-permute-start | bytes 49160 | tf_op jit(solution)/shard_map/ppermute | solution.py:419
  9.2 15.4 %collective-permute-done.4.low_t = f32[1,128]{1,0:T(1,128)S(1)} collective-permute-done((f32[1,128]{1,0:T(1,128)S(1)}, f32[1,128]{1,0:T(1,128)S(1)}, u32[]{:S(2)}, u32[]{:S(2)}) %collective-permute-start.4) | collective-permute-done | bytes 544 | tf_op jit(solution)/shard_map/ppermute | solution.py:419
  24.6 1.8 %collective-permute-start.5 = (f32[1,128]{1,0:T(1,128)S(1)}, f32[1,128]{1,0:T(1,128)S(1)}, u32[]{:S(2)}, u32[]{:S(2)}) collective-permute-start(f32[1,128]{1,0:T(1,128)S(1)} %bitcast.15), channel_id=1, source_target_pairs={{0,12},{4,0},{8,4},{12,8},{1,13},{5,1},{9,5},{13,9},{2,14},{6,2},{... | collective-permute-start | bytes 1544 | tf_op jit(solution)/shard_map/ppermute | solution.py:419
  26.4 0.7 %fusion.49 = (f32[2,128,128]{2,1,0:T(8,128)S(1)}, f32[2,128,128]{2,1,0:T(8,128)}) fusion(f32[4,128,128]{2,1,0:T(8,128)S(1)} %copy-done.1), kind=kLoop, calls=%fused_computation.64 | loop fusion | bytes 524288 | tf_op jit(solution)/shard_map/slice | solution.py:452
  27.0 1.1 %collective-permute-done.5.high_t = f32[1,128]{1,0:T(1,128)S(1)} collective-permute-done((f32[1,128]{1,0:T(1,128)S(1)}, f32[1,128]{1,0:T(1,128)S(1)}, u32[]{:S(2)}, u32[]{:S(2)}) %collective-permute-start.5) | collective-permute-done | bytes 544 | tf_op jit(solution)/shard_map/ppermute | solution.py:419
  28.2 3.8 %collective-permute-start.18 = (f32[2,128,128]{2,1,0:T(8,128)S(1)}, f32[2,128,128]{2,1,0:T(8,128)S(1)}, u32[]{:S(2)}, u32[]{:S(2)}) collective-permute-start(f32[2,128,128]{2,1,0:T(8,128)S(1)} %get-tuple-element.43), channel_id=1, source_target_pairs={{0,12},{4,0},{8,4},{12,8},{1,13},{5,1},{9,5},{13,9},{2,14},{6,2},{... | collective-permute-start | bytes 393224 | tf_op jit(solution)/shard_map/ppermute | solution.py:419
  32.0 1.3 %shard_map.112.star = f32[3,4,128,128]{3,2,1,0:T(8,128)S(1)} custom-call(f32[3,4,128,128]{3,2,1,0:T(8,128)S(1)} %copy-done, f32[3,2,128,128]{3,2,1,0:T(8,128)S(1)} %collective-permute-done.low_x, f32[3,2,128,128]{3,2,1,0:T(8,128)S(1)} %collective-permute-done.1.high_x, f32[4,4,2,128]{3,2,1,0:T(2,128)S(1)} %collective-permute-done.2.low_y, ...), custom_call_target="tpu_custom_call" | custom-call | flops 1048576 | bytes 1572864 | tf_op jit(solution)/shard_map/pallas_call | solution.py:28
  33.9 2.6 %collective-permute-done.7.before_y = f32[4,128]{1,0:T(4,128)S(1)} collective-permute-done((f32[4,128]{1,0:T(4,128)S(1)}, f32[4,128]{1,0:T(4,128)S(1)}, u32[]{:S(2)}, u32[]{:S(2)}) %collective-permute-start.7) | collective-permute-done | bytes 2080 | tf_op jit(solution)/shard_map/ppermute | solution.py:419
  36.5 3.0 %collective-permute-done.6.before_x = f32[128,128]{1,0:T(8,128)S(1)} collective-permute-done((f32[128,128]{1,0:T(8,128)S(1)}, f32[128,128]{1,0:T(8,128)S(1)}, u32[]{:S(2)}, u32[]{:S(2)}) %collective-permute-start.6) | collective-permute-done | bytes 65568 | tf_op jit(solution)/shard_map/ppermute | solution.py:419
  39.5 0.8 %shard_map.114 = (f32[4,128,128]{2,1,0:T(8,128)S(1)}, f32[2,128,128]{2,1,0:T(8,128)S(1)}) custom-call(s32[1]{0:T(128)} %bitcast.place, f32[3,4,128,128]{3,2,1,0:T(8,128)S(1)} %shard_map.112.star, f32[128,128]{1,0:T(8,128)S(1)} %collective-permute-done.6.before_x, f32[4,128]{1,0:T(4,128)S(1)} %collective-permute-done.7.before_y, f32[128,128]{1,0:T(8,128)S(1)} %copy-done.2, ...), custom_call_target="tpu_custom_call" | custom-call | flops 1048576 | bytes 786432 | tf_op jit(solution)/shard_map/pallas_call | solution.py:28
  41.5 0.8 %collective-permute-done.10 = f32[16,128]{1,0:T(8,128)S(1)} collective-permute-done((f32[16,128]{1,0:T(8,128)S(1)}, f32[16,128]{1,0:T(8,128)S(1)}, u32[]{:S(2)}, u32[]{:S(2)}) %collective-permute-start.10) | collective-permute-done | bytes 8224 | tf_op jit(solution)/shard_map/ppermute | solution.py:419
  42.3 1.8 %collective-permute-done.9 = f32[16,128]{1,0:T(8,128)S(1)} collective-permute-done((f32[16,128]{1,0:T(8,128)S(1)}, f32[16,128]{1,0:T(8,128)S(1)}, u32[]{:S(2)}, u32[]{:S(2)}) %collective-permute-start.9) | collective-permute-done | bytes 8224 | tf_op jit(solution)/shard_map/ppermute | solution.py:419
  44.4 4.0 %collective-permute-done.11.other_faces = f32[56,128]{1,0:T(8,128)S(1)} collective-permute-done((f32[56,128]{1,0:T(8,128)S(1)}, f32[56,128]{1,0:T(8,128)S(1)}, u32[]{:S(2)}, u32[]{:S(2)}) %collective-permute-start.11) | collective-permute-done | bytes 28704 | tf_op jit(solution)/shard_map/ppermute | solution.py:423
  48.6 2.9 %collective-permute-start.13 = (f32[56,128]{1,0:T(8,128)S(1)}, f32[56,128]{1,0:T(8,128)S(1)}, u32[]{:S(2)}, u32[]{:S(2)}) collective-permute-start(f32[56,128]{1,0:T(8,128)S(1)} %get-tuple-element.26.faces), channel_id=1, source_target_pairs={{0,8},{4,12},{8,0},{12,4},{1,9},{5,13},{9,1},{13,5},{2,10},{6,14},... | collective-permute-start | bytes 86024 | tf_op jit(solution)/shard_map/ppermute | solution.py:423
  51.5 7.0 %collective-permute-done.13.other_faces = f32[56,128]{1,0:T(8,128)S(1)} collective-permute-done((f32[56,128]{1,0:T(8,128)S(1)}, f32[56,128]{1,0:T(8,128)S(1)}, u32[]{:S(2)}, u32[]{:S(2)}) %collective-permute-start.13) | collective-permute-done | bytes 28704 | tf_op jit(solution)/shard_map/ppermute | solution.py:423
  58.7 0.6 shard_map.118
  59.4 0.6 collective-permute-start.15
  60.0 1.4 %collective-permute-start.16 = (f32[40,128]{1,0:T(8,128)S(1)}, f32[40,128]{1,0:T(8,128)S(1)}, u32[]{:S(2)}, u32[]{:S(2)}) collective-permute-start(f32[40,128]{1,0:T(8,128)S(1)} %get-tuple-element.34.refs_0_), channel_id=1, source_target_pairs={{0,3},{1,0},{2,1},{3,2},{4,7},{5,4},{6,5},{7,6},{8,11},{9,8},{10,9... | collective-permute-start | bytes 61448 | tf_op jit(solution)/shard_map/ppermute | solution.py:419
  61.4 1.3 %shard_map.121 = f32[4,128,128]{2,1,0:T(8,128)} custom-call(f32[4,128,128]{2,1,0:T(8,128)S(1)} %copy-done.1, f32[2,128,128]{2,1,0:T(8,128)S(1)} %collective-permute-done.17.low_x, f32[2,128,128]{2,1,0:T(8,128)S(1)} %collective-permute-done.18.high_x, f32[4,2,128]{2,1,0:T(2,128)S(1)} %slice_bitcast_fusion.2.low_y, ...), custom_call_target="tpu_custom_call" | custom-call | flops 1048576 | bytes 524288 | tf_op jit(solution)/shard_map/pallas_call | solution.py:28
  62.7 1.4 %shard_map.119 = (f32[5,128,128]{2,1,0:T(8,128)S(1)}, f32[5,128,128]{2,1,0:T(8,128)S(1)}) custom-call(f32[5,128,128]{2,1,0:T(8,128)S(1)} %get-tuple-element.30.precond, f32[5,128,128]{2,1,0:T(8,128)S(1)} %get-tuple-element.31.image, f32[128,128]{1,0:T(8,128)S(1)} %copy-done.2, f32[128,128]{1,0:T(8,128)S(1)} %copy-done.2), custom_call_target="tpu_custom_call" | custom-call | flops 1048576 | bytes 1310720 | tf_op jit(solution)/shard_map/pallas_call | solution.py:28
  64.1 1.2 %shard_map.120 = (f32[3,4,128,128]{3,2,1,0:T(8,128)}, f32[4,128,128]{2,1,0:T(8,128)}) custom-call(s32[1]{0:T(128)} %bitcast.place, f32[3,4,128,128]{3,2,1,0:T(8,128)S(1)} %shard_map.112.star, f32[5,128,128]{2,1,0:T(8,128)S(1)} %get-tuple-element.32.precond, f32[5,128,128]{2,1,0:T(8,128)S(1)} %get-tuple-element.33.image, ...), custom_call_target="tpu_custom_call" | custom-call | flops 1048576 | bytes 2097152 | tf_op jit(solution)/shard_map/pallas_call | solution.py:28
  (55 shorter events, 2.7 us)
Async XLA Ops:
  0.6 6.7 %copy-start = (f32[3,4,128,128]{3,2,1,0:T(8,128)S(1)}, f32[3,4,128,128]{3,2,1,0:T(8,128)}, u32[]{:S(2)}) copy-start(f32[3,4,128,128]{3,2,1,0:T(8,128)} %flow.3) | copy-start | bytes 2359300
  0.6 6.5 %copy-start.1 = (f32[4,128,128]{2,1,0:T(8,128)S(1)}, f32[4,128,128]{2,1,0:T(8,128)}, u32[]{:S(2)}) copy-start(f32[4,128,128]{2,1,0:T(8,128)} %thermal.3) | copy-start | bytes 786436
  1.9 30.1 %copy-start.4 = (s32[4,128,128]{2,1,0:T(8,128)S(1)}, s32[4,128,128]{2,1,0:T(8,128)}, u32[]{:S(2)}) copy-start(s32[4,128,128]{2,1,0:T(8,128)} %flag.1) | copy-start | bytes 786436
  1.9 30.1 %collective-permute-start = (f32[3,2,128,128]{3,2,1,0:T(8,128)S(1)}, f32[3,2,128,128]{3,2,1,0:T(8,128)S(1)}, u32[]{:S(2)}, u32[]{:S(2)}) collective-permute-start(f32[3,2,128,128]{3,2,1,0:T(8,128)S(1)} %get-tuple-element.42), channel_id=1, source_target_pairs={{0,4},{4,8},{8,12},{12,0},{1,5},{5,9},{9,13},{13,1},{2,6},{6,10},{... | collective-permute-start | bytes 1179656 | tf_op jit(solution)/shard_map/ppermute | solution.py:419
  5.0 27.0 %collective-permute-start.1 = (f32[3,2,128,128]{3,2,1,0:T(8,128)S(1)}, f32[3,2,128,128]{3,2,1,0:T(8,128)S(1)}, u32[]{:S(2)}, u32[]{:S(2)}) collective-permute-start(f32[3,2,128,128]{3,2,1,0:T(8,128)S(1)} %get-tuple-element.41), channel_id=1, source_target_pairs={{0,12},{4,0},{8,4},{12,8},{1,13},{5,1},{9,5},{13,9},{2,14},{6,2},{... | collective-permute-start | bytes 1179656 | tf_op jit(solution)/shard_map/ppermute | solution.py:419
  7.3 17.3 %collective-permute-start.4 = (f32[1,128]{1,0:T(1,128)S(1)}, f32[1,128]{1,0:T(1,128)S(1)}, u32[]{:S(2)}, u32[]{:S(2)}) collective-permute-start(f32[1,128]{1,0:T(1,128)S(1)} %bitcast.16), channel_id=1, source_target_pairs={{0,4},{4,8},{8,12},{12,0},{1,5},{5,9},{9,13},{13,1},{2,6},{6,10},{... | collective-permute-start | bytes 1544 | tf_op jit(solution)/shard_map/ppermute | solution.py:419
  7.4 20.8 %collective-permute-start.2 = (f32[4,4,2,128]{3,2,1,0:T(2,128)S(1)}, f32[4,4,2,128]{3,2,1,0:T(2,128)S(1)}, u32[]{:S(2)}, u32[]{:S(2)}) collective-permute-start(f32[4,4,2,128]{3,2,1,0:T(2,128)S(1)} %get-tuple-element.40), channel_id=1, source_target_pairs={{0,1},{1,2},{2,3},{3,0},{4,5},{5,6},{6,7},{7,4},{8,9},{9,10},{10,1... | collective-permute-start | bytes 49160 | tf_op jit(solution)/shard_map/ppermute | solution.py:419
  7.4 24.5 %collective-permute-start.3 = (f32[4,4,2,128]{3,2,1,0:T(2,128)S(1)}, f32[4,4,2,128]{3,2,1,0:T(2,128)S(1)}, u32[]{:S(2)}, u32[]{:S(2)}) collective-permute-start(f32[4,4,2,128]{3,2,1,0:T(2,128)S(1)} %get-tuple-element.39), channel_id=1, source_target_pairs={{0,3},{1,0},{2,1},{3,2},{4,7},{5,4},{6,5},{7,6},{8,11},{9,8},{10,9... | collective-permute-start | bytes 49160 | tf_op jit(solution)/shard_map/ppermute | solution.py:419
  24.6 3.5 %collective-permute-start.5 = (f32[1,128]{1,0:T(1,128)S(1)}, f32[1,128]{1,0:T(1,128)S(1)}, u32[]{:S(2)}, u32[]{:S(2)}) collective-permute-start(f32[1,128]{1,0:T(1,128)S(1)} %bitcast.15), channel_id=1, source_target_pairs={{0,12},{4,0},{8,4},{12,8},{1,13},{5,1},{9,5},{13,9},{2,14},{6,2},{... | collective-permute-start | bytes 1544 | tf_op jit(solution)/shard_map/ppermute | solution.py:419
  28.1 33.3 %collective-permute-start.17 = (f32[2,128,128]{2,1,0:T(8,128)}, f32[2,128,128]{2,1,0:T(8,128)S(1)}, u32[]{:S(2)}, u32[]{:S(2)}) collective-permute-start(f32[2,128,128]{2,1,0:T(8,128)} %get-tuple-element.44), channel_id=1, source_target_pairs={{0,4},{4,8},{8,12},{12,0},{1,5},{5,9},{9,13},{13,1},{2,6},{6,10},{... | collective-permute-start | bytes 393224 | tf_op jit(solution)/shard_map/ppermute | solution.py:419
  28.1 11.3 %copy-start.2 = (f32[128,128]{1,0:T(8,128)S(1)}, f32[128,128]{1,0:T(8,128)}, u32[]{:S(2)}) copy-start(f32[128,128]{1,0:T(8,128)} %constant.73.clone.table_y.table_z) | copy-start | bytes 196612
  28.2 33.2 %collective-permute-start.18 = (f32[2,128,128]{2,1,0:T(8,128)S(1)}, f32[2,128,128]{2,1,0:T(8,128)S(1)}, u32[]{:S(2)}, u32[]{:S(2)}) collective-permute-start(f32[2,128,128]{2,1,0:T(8,128)S(1)} %get-tuple-element.43), channel_id=1, source_target_pairs={{0,12},{4,0},{8,4},{12,8},{1,13},{5,1},{9,5},{13,9},{2,14},{6,2},{... | collective-permute-start | bytes 393224 | tf_op jit(solution)/shard_map/ppermute | solution.py:419
  33.3 7.0 %copy-start.3 = (f32[2,128,128]{2,1,0:T(8,128)S(1)}, f32[2,128,128]{2,1,0:T(8,128)}, u32[]{:S(2)}) copy-start(f32[2,128,128]{2,1,0:T(8,128)} %constant.74.clone.edge) | copy-start | bytes 393220
  33.4 6.1 %collective-permute-start.6 = (f32[128,128]{1,0:T(8,128)S(1)}, f32[128,128]{1,0:T(8,128)S(1)}, u32[]{:S(2)}, u32[]{:S(2)}) collective-permute-start(f32[128,128]{1,0:T(8,128)S(1)} %slice_bitcast_fusion), channel_id=1, source_target_pairs={{0,4},{4,8},{8,12},{12,0},{1,5},{5,9},{9,13},{13,1},{2,6},{6,10},{... | collective-permute-start | bytes 196616 | tf_op jit(solution)/shard_map/ppermute | solution.py:419
  33.4 3.1 %collective-permute-start.7 = (f32[4,128]{1,0:T(4,128)S(1)}, f32[4,128]{1,0:T(4,128)S(1)}, u32[]{:S(2)}, u32[]{:S(2)}) collective-permute-start(f32[4,128]{1,0:T(4,128)S(1)} %bitcast.14), channel_id=1, source_target_pairs={{0,1},{1,2},{2,3},{3,0},{4,5},{5,6},{6,7},{7,4},{8,9},{9,10},{10,1... | collective-permute-start | bytes 6152 | tf_op jit(solution)/shard_map/ppermute | solution.py:419
  41.0 1.4 %collective-permute-start.10 = (f32[16,128]{1,0:T(8,128)S(1)}, f32[16,128]{1,0:T(8,128)S(1)}, u32[]{:S(2)}, u32[]{:S(2)}) collective-permute-start(f32[16,128]{1,0:T(8,128)S(1)} %get-tuple-element.46), channel_id=1, source_target_pairs={{0,3},{1,0},{2,1},{3,2},{4,7},{5,4},{6,5},{7,6},{8,11},{9,8},{10,9... | collective-permute-start | bytes 24584 | tf_op jit(solution)/shard_map/ppermute | solution.py:419
  41.0 3.2 %collective-permute-start.9 = (f32[16,128]{1,0:T(8,128)S(1)}, f32[16,128]{1,0:T(8,128)S(1)}, u32[]{:S(2)}, u32[]{:S(2)}) collective-permute-start(f32[16,128]{1,0:T(8,128)S(1)} %get-tuple-element.45), channel_id=1, source_target_pairs={{0,1},{1,2},{2,3},{3,0},{4,5},{5,6},{6,7},{7,4},{8,9},{9,10},{10,1... | collective-permute-start | bytes 24584 | tf_op jit(solution)/shard_map/ppermute | solution.py:419
  41.5 6.9 %collective-permute-start.8 = (f32[2,128,128]{2,1,0:T(8,128)S(1)}, f32[2,128,128]{2,1,0:T(8,128)S(1)}, u32[]{:S(2)}, u32[]{:S(2)}) collective-permute-start(f32[2,128,128]{2,1,0:T(8,128)S(1)} %get-tuple-element.22.ends), channel_id=1, source_target_pairs={{0,4},{4,0},{8,12},{12,8},{1,5},{5,1},{9,13},{13,9},{2,6},{6,2},{1... | collective-permute-start | bytes 393224 | tf_op jit(solution)/shard_map/ppermute | solution.py:423
  44.2 4.2 %collective-permute-start.11 = (f32[56,128]{1,0:T(8,128)S(1)}, f32[56,128]{1,0:T(8,128)S(1)}, u32[]{:S(2)}, u32[]{:S(2)}) collective-permute-start(f32[56,128]{1,0:T(8,128)S(1)} %pad_maximum_fusion.faces), channel_id=1, source_target_pairs={{0,4},{4,0},{8,12},{12,8},{1,5},{5,1},{9,13},{13,9},{2,6},{6,2},{1... | collective-permute-start | bytes 86024 | tf_op jit(solution)/shard_map/ppermute | solution.py:423
  48.6 9.9 %collective-permute-start.12 = (f32[2,128,128]{2,1,0:T(8,128)S(1)}, f32[2,128,128]{2,1,0:T(8,128)S(1)}, u32[]{:S(2)}, u32[]{:S(2)}) collective-permute-start(f32[2,128,128]{2,1,0:T(8,128)S(1)} %get-tuple-element.24.ends), channel_id=1, source_target_pairs={{0,8},{4,12},{8,0},{12,4},{1,9},{5,13},{9,1},{13,5},{2,10},{6,14},... | collective-permute-start | bytes 393224 | tf_op jit(solution)/shard_map/ppermute | solution.py:423
  48.6 9.9 %collective-permute-start.13 = (f32[56,128]{1,0:T(8,128)S(1)}, f32[56,128]{1,0:T(8,128)S(1)}, u32[]{:S(2)}, u32[]{:S(2)}) collective-permute-start(f32[56,128]{1,0:T(8,128)S(1)} %get-tuple-element.26.faces), channel_id=1, source_target_pairs={{0,8},{4,12},{8,0},{12,4},{1,9},{5,13},{9,1},{13,5},{2,10},{6,14},... | collective-permute-start | bytes 86024 | tf_op jit(solution)/shard_map/ppermute | solution.py:423
  59.3 4.8 %collective-permute-start.14 = (f32[40,128]{1,0:T(8,128)S(1)}, f32[40,128]{1,0:T(8,128)S(1)}, u32[]{:S(2)}, u32[]{:S(2)}) collective-permute-start(f32[40,128]{1,0:T(8,128)S(1)} %get-tuple-element.34.refs_0_), channel_id=1, source_target_pairs={{0,1},{1,2},{2,3},{3,0},{4,5},{5,6},{6,7},{7,4},{8,9},{9,10},{10,1... | collective-permute-start | bytes 61448 | tf_op jit(solution)/shard_map/ppermute | solution.py:419
  59.4 4.7 %collective-permute-start.15 = (f32[40,128]{1,0:T(8,128)S(1)}, f32[40,128]{1,0:T(8,128)S(1)}, u32[]{:S(2)}, u32[]{:S(2)}) collective-permute-start(f32[40,128]{1,0:T(8,128)S(1)} %get-tuple-element.34.refs_0_), channel_id=1, source_target_pairs={{0,2},{1,3},{2,0},{3,1},{4,6},{5,7},{6,4},{7,5},{8,10},{9,11},{10,... | collective-permute-start | bytes 61448 | tf_op jit(solution)/shard_map/ppermute | solution.py:419
  60.0 4.1 %collective-permute-start.16 = (f32[40,128]{1,0:T(8,128)S(1)}, f32[40,128]{1,0:T(8,128)S(1)}, u32[]{:S(2)}, u32[]{:S(2)}) collective-permute-start(f32[40,128]{1,0:T(8,128)S(1)} %get-tuple-element.34.refs_0_), channel_id=1, source_target_pairs={{0,3},{1,0},{2,1},{3,2},{4,7},{5,4},{6,5},{7,6},{8,11},{9,8},{10,9... | collective-permute-start | bytes 61448 | tf_op jit(solution)/shard_map/ppermute | solution.py:419
  (3 other events, 13.1 us)

commit v2 on v1

--- a/solution.py
+++ b/solution.py
@@ -75,7 +75,7 @@
     return jnp.sum(jnp.where(same, row, 0.0), axis=1, keepdims=True)
 
 
-def advance(layers, padded, index, speed):
+def advance(layers, padded, index, speed, start=0):
     middle = layers[2]
     rows = middle.shape[0]
     speed_x, speed_y, speed_z = speed
@@ -84,8 +84,8 @@
     far = jnp.where(ahead, layers[0], layers[4])
     rate = jnp.abs(speed_x) * (1.5 * middle - 2.0 * near + 0.5 * far)
     ahead = speed_y >= 0.0
-    near = jnp.where(ahead, padded[index, pl.ds(7, rows), :], padded[index, pl.ds(9, rows), :])
-    far = jnp.where(ahead, padded[index, pl.ds(6, rows), :], padded[index, pl.ds(10, rows), :])
+    near = jnp.where(ahead, padded[index, pl.ds(7 + start, rows), :], padded[index, pl.ds(9 + start, rows), :])
+    far = jnp.where(ahead, padded[index, pl.ds(6 + start, rows), :], padded[index, pl.ds(10 + start, rows), :])
     rate = rate + jnp.abs(speed_y) * (1.5 * middle - 2.0 * near + 0.5 * far)
     ahead = speed_z >= 0.0
     near = jnp.where(ahead, lane_shift(middle, -1), lane_shift(middle, 1))
@@ -101,57 +101,135 @@
     padded[index, pl.ds(8 + rows, 2), :] = after
 
 
-def march_kernel(flow, low_x, high_x, low_y, high_y, thermal, low_t, high_t, flag, star, padded):
+def march_layer(refs, padded, index, parts, start, count):
+    flow, low_x, high_x, thermal, flag = refs
     _, layers, rows, depth = flow.shape
-    top = lax.broadcasted_iota(jnp.int32, (rows, depth), 1) == depth - 1
-    for index in range(layers):
-        for part in range(3):
-            pad_rows(
-                padded, part, low_y[part, index], flow[part, index], high_y[part, index]
-            )
-        pad_rows(padded, 3, low_y[3, index], thermal[index], high_y[3, index])
-        speed = [flow[part, index] for part in range(3)]
-        behind = thermal[index - 1] if index > 0 else column(low_t[...])
-        before = thermal[index + 1] if index + 1 < layers else column(high_t[...])
-        pull = -MARANGONI * 0.5 * TIME_INCREMENT
-        drive_x = jnp.where(top, pull * (before - behind), 0.0)
-        drive_y = jnp.where(
-            top, pull * (padded[3, pl.ds(9, rows), :] - padded[3, pl.ds(7, rows), :]), 0.0
-        )
-        drag = 1.0 / (1.0 + TIME_INCREMENT * DRAG_RATE * flag[index].astype(F32))
-        for part in range(3):
-            around = []
-            for other in range(index - 2, index + 3):
-                if other < 0:
-                    around.append(low_x[part, other + 2])
-                elif other >= layers:
-                    around.append(high_x[part, other - layers])
-                else:
-                    around.append(flow[part, other])
-            moved = advance(around, padded, part, speed)
-            if part == 0:
-                moved = moved + drive_x
-            if part == 1:
-                moved = moved + drive_y
-            star[part, index] = moved * drag
-
-
-def heat_kernel(thermal, low_x, high_x, low_y, high_y, flow, heat, warmed, padded):
-    layers, rows, depth = thermal.shape
-    top = lax.broadcasted_iota(jnp.int32, (rows, depth), 1) == depth - 1
-    for index in range(layers):
-        pad_rows(padded, 0, low_y[index], thermal[index], high_y[index])
+    span = pl.ds(start, count)
+    surface = 6 * rows
+    speed = [flow[part, index, span, :] for part in range(3)]
+    drag = 1.0 / (1.0 + TIME_INCREMENT * DRAG_RATE * flag[index, span, :].astype(F32))
+    top = lax.broadcasted_iota(jnp.int32, (count, depth), 1) == depth - 1
+    pull = -MARANGONI * 0.5 * TIME_INCREMENT
+    out = []
+    for part in parts:
         around = []
         for other in range(index - 2, index + 3):
             if other < 0:
-                around.append(low_x[other + 2])
+                first = (2 * part + other + 2) * rows + start
+                around.append(low_x[pl.ds(first, count), :])
             elif other >= layers:
-                around.append(high_x[other - layers])
+                first = (2 * part + other - layers) * rows + start
+                around.append(high_x[pl.ds(first, count), :])
+            else:
+                around.append(flow[part, other, span, :])
+        moved = advance(around, padded, part, speed, start)
+        if part == 0:
+            edge = lambda halo: column(halo[pl.ds(surface, 1), pl.ds(0, rows)])
+            behind = thermal[index - 1] if index > 0 else edge(low_x)
+            before = thermal[index + 1] if index + 1 < layers else edge(high_x)
+            moved = moved + jnp.where(top, pull * (before - behind), 0.0)
+        if part == 1:
+            slope = padded[3, pl.ds(9 + start, count), :] - padded[3, pl.ds(7 + start, count), :]
+            moved = moved + jnp.where(top, pull * slope, 0.0)
+        out.append(moved * drag)
+    return out
+
+
+def pad_layer(refs, low_y, high_y, padded, index):
+    flow, _, _, thermal, _ = refs
+    for part in range(3):
+        pad_rows(padded, part, low_y[part, index], flow[part, index], high_y[part, index])
+    pad_rows(padded, 3, low_y[3, index], thermal[index], high_y[3, index])
+
+
+def rim_kernel(
+    flow, low_x, high_x, thermal, flag, low_y, high_y, weight, star, side_x, side_y, padded
+):
+    refs = (flow, low_x, high_x, thermal, flag)
+    _, layers, rows, depth = flow.shape
+    for index in range(layers):
+        pad_layer(refs, low_y, high_y, padded, index)
+        if index == layers - 1:
+            for part, value in enumerate(march_layer(refs, padded, index, range(3), 0, rows)):
+                star[part] = value
+                if part == 0:
+                    side_x[...] = value
+                if part == 1:
+                    side_y[pl.ds(index, 1), :] = value[rows - 1 :, :]
+        else:
+            (value,) = march_layer(refs, padded, index, [1], rows - 8, 8)
+            side_y[pl.ds(index, 1), :] = value[7:, :]
+
+
+def march_kernel(
+    flow, low_x, high_x, thermal, flag, low_y, high_y, rim, table_y, table_z,
+    star, source, padded,
+):
+    refs = (flow, low_x, high_x, thermal, flag)
+    _, layers, rows, depth = flow.shape
+    top = lax.broadcasted_iota(jnp.int32, (rows, depth), 0) == 0
+    for index in range(layers):
+        if index == layers - 1:
+            value = [rim[part] for part in range(3)]
+        else:
+            pad_layer(refs, low_y, high_y, padded, index)
+            value = march_layer(refs, padded, index, range(3), 0, rows)
+        for part in range(3):
+            star[part, index] = value[part]
+        sink = value[0]
+        if index > 0:
+            sink = sink - star[0, index - 1]
+        sink = sink + (value[1] - jnp.where(top, 0.0, pltpu.roll(value[1], 1, 0)))
+        sink = sink + (value[2] - lane_shift(value[2], -1))
+        source[index] = dot(dot(table_y[...], -sink), table_z[...])
+
+
+def pack_kernel(flow, thermal, ahead, behind, planes, sems):
+    parts, layers, rows, depth = flow.shape
+    copies = []
+    for part in range(parts):
+        for layer in range(2):
+            for target, source in ((ahead, layers - 2 + layer), (behind, layer)):
+                copies.append(
+                    (flow.at[part, source], target.at[pl.ds((2 * part + layer) * rows, rows), :])
+                )
+    copies.append((thermal.at[layers - 1], planes.at[0]))
+    copies.append((thermal.at[0], planes.at[1]))
+    copies = [
+        pltpu.make_async_copy(source, target, sems.at[index])
+        for index, (source, target) in enumerate(copies)
+    ]
+    for copy in copies:
+        copy.start()
+    shape = (rows, rows)
+    same = lax.broadcasted_iota(jnp.int32, shape, 0) == lax.broadcasted_iota(jnp.int32, shape, 1)
+    for copy in copies[-2:]:
+        copy.wait()
+    for side, target in enumerate((ahead, behind)):
+        tops = planes[side][:, depth - 1 :]
+        row = jnp.sum(jnp.where(same, tops, 0.0), axis=0, keepdims=True)
+        target[pl.ds(2 * parts * rows, 8), pl.ds(0, rows)] = jnp.broadcast_to(row, (8, rows))
+    for copy in copies[:-2]:
+        copy.wait()
+
+
+def heat_kernel(span, thermal, halo, low_y, high_y, flow, heat, warmed, padded):
+    layers, rows, depth = thermal.shape
+    top = lax.broadcasted_iota(jnp.int32, (rows, depth), 1) == depth - 1
+    for index in span:
+        pad_rows(padded, 0, low_y[3, index], thermal[index], high_y[3, index])
+        around = []
+        for other in range(index - 2, index + 3):
+            if other < 0:
+                around.append(halo[other + 2])
+            elif other >= layers:
+                around.append(halo[other - layers])
             else:
                 around.append(thermal[other])
         speed = [flow[part, index] for part in range(3)]
         gain = TIME_INCREMENT * column(heat[pl.ds(index, 1), :])
-        warmed[index] = advance(around, padded, 0, speed) + jnp.where(top, gain, 0.0)
+        moved = advance(around, padded, 0, speed) + jnp.where(top, gain, 0.0)
+        warmed[index - span[0]] = moved
 
 
 def laser_heat(start_x, start_y, span_x, span_y, total_x, total_y, spots_a, spots_b):
@@ -207,29 +285,6 @@
     weight[4 * rounds] = inner * green(first + layers)
 
 
-def source_kernel(
-    length, place, star, before_x, before_y, table_y, table_z, ratio, source, ends, rows_
-):
-    _, layers, rows, depth = star.shape
-    first = place[0] * layers
-    for index in range(layers):
-        rows_[pl.ds(8, rows), :] = star[1, index]
-        rows_[pl.ds(7, 1), :] = before_y[pl.ds(index, 1), :]
-        behind = star[0, index - 1] if index > 0 else before_x[...]
-        sink = star[0, index] - behind
-        sink = sink + (star[1, index] - rows_[pl.ds(7, rows), :])
-        sink = sink + (star[2, index] - lane_shift(star[2, index], -1))
-        source[index] = dot(dot(table_y[...], -sink), table_z[...])
-    forward = source[0]
-    for index in range(1, layers):
-        forward = source[index] + ratio[first + index] * forward
-    ends[0] = forward
-    backward = source[layers - 1]
-    for index in range(layers - 2, -1, -1):
-        backward = source[index] + ratio[length - 1 - first - index] * backward
-    ends[1] = backward
-
-
 def face_rows(plane, edge):
     return (
         jnp.sum(plane * edge[0], axis=0, keepdims=True),
@@ -237,11 +292,29 @@
     )
 
 
-def faces_kernel(length, place, source, ratio, edge, faces, sweep):
-    layers, rows, depth = source.shape
+def source_kernel(
+    length, place, partial, before_x, before_y, table_y, table_z, ratio, edge, thermal,
+    source, message, head, tail, late, sweep,
+):
+    layers, rows, depth = partial.shape
     first = place[0] * layers
     inside = lambda index: (index >= first) & (index < first + layers)
     zero = jnp.zeros((rows, depth), F32)
+    late[...] = thermal[layers - 2 :]
+    extra = dot(before_y[...], table_z[...])
+    for index in range(layers):
+        value = partial[index] + edge[0] * extra[index : index + 1]
+        if index == 0:
+            value = value + dot(dot(table_y[...], before_x[...]), table_z[...])
+        source[index] = value
+    forward = source[0]
+    for index in range(1, layers):
+        forward = source[index] + ratio[first + index] * forward
+    message[pl.ds(0, rows), :] = forward
+    backward = source[layers - 1]
+    for index in range(layers - 2, -1, -1):
+        backward = source[index] + ratio[length - 1 - first - index] * backward
+    message[pl.ds(rows, rows), :] = backward
 
     def own(index):
         value = source[jnp.clip(index - first, 0, layers - 1)]
@@ -259,33 +332,64 @@
         index = length - 1 - back
         value = ratio[index + 1] * (sweep[index] + following)
         low, high = face_rows(value, edge)
-        faces[pl.ds(index, 1), :] = low
-        faces[pl.ds(length + index, 1), :] = high
+        head[pl.ds(index, 1), :] = low
+        tail[pl.ds(index, 1), :] = high
         return value, energy + own(index) * value
 
     _, energy = loop(0, length, up, (zero, zero))
-    faces[pl.ds(2 * length, 8), :] = jnp.broadcast_to(total(energy), (8, depth))
-
-
-def merge_kernel(
-    turn, last, length, place, ends, other, sums, faces, other_faces, weight, ratio,
-    new_ends, new_sums, new_faces,
-):
-    count = faces.shape[0] - 8
+    message[pl.ds(2 * rows, length), :] = head[...]
+    message[pl.ds(2 * rows + length, length), :] = tail[...]
+    energy = jnp.broadcast_to(total(energy), (8, depth))
+    message[pl.ds(2 * rows + 2 * length, 8), :] = energy
+
+
+def joined(turn, place, message, other, sums, weight, new_sums):
+    rows, depth = weight.shape[1:]
     right = ((place[0] >> turn) & 1) == 1
-    left_s = jnp.where(right, other[0], ends[0])
-    right_s = jnp.where(right, ends[0], other[0])
-    left_t = jnp.where(right, other[1], ends[1])
-    right_t = jnp.where(right, ends[1], other[1])
+    upper, lower = pl.ds(0, rows), pl.ds(rows, rows)
+    left_s = jnp.where(right, other[upper, :], message[upper, :])
+    right_s = jnp.where(right, message[upper, :], other[upper, :])
+    left_t = jnp.where(right, other[lower, :], message[lower, :])
+    right_t = jnp.where(right, message[lower, :], other[lower, :])
     own = weight[4 * turn + 2]
     new_sums[0] = sums[0] + jnp.where(right, left_s * own, 0.0)
     new_sums[1] = sums[1] + jnp.where(right, 0.0, right_t * own)
-    scale = ratio[length] if last else 1.0
-    new_ends[0] = scale * (right_s + left_s * weight[4 * turn])
-    new_ends[1] = scale * (left_t + right_t * weight[4 * turn + 1])
-    new_faces[...] = faces[...] + other_faces[...]
-    cross = 2.0 * total(left_s * right_t * weight[4 * turn + 3])
-    new_faces[pl.ds(count, 8), :] = new_faces[pl.ds(count, 8), :] + cross
+    forward = right_s + left_s * weight[4 * turn]
+    backward = left_t + right_t * weight[4 * turn + 1]
+    energy = 2.0 * total(left_s * right_t * weight[4 * turn + 3])
+    where = pl.ds(message.shape[0] - 8, 8)
+    return forward, backward, message[where, :] + other[where, :] + energy
+
+
+def merge_kernel(
+    turn, length, place, message, other, sums, weight, thermal,
+    new_message, new_sums, head, tail, late,
+):
+    rows, depth = weight.shape[1:]
+    late[...] = thermal[:2]
+    forward, backward, energy = joined(turn, place, message, other, sums, weight, new_sums)
+    new_message[pl.ds(0, rows), :] = forward
+    new_message[pl.ds(rows, rows), :] = backward
+    both = pl.ds(2 * rows, 2 * length)
+    new_message[both, :] = message[both, :] + other[both, :]
+    new_message[pl.ds(2 * rows + 2 * length, 8), :] = energy
+    head[...] = new_message[pl.ds(2 * rows, length), :]
+    tail[...] = new_message[pl.ds(2 * rows + length, length), :]
+
+
+def close_kernel(
+    turn, length, place, message, other, sums, weight, ratio, below, below_far, above, above_far,
+    ends, new_sums, faces,
+):
+    rows, depth = weight.shape[1:]
+    forward, backward, energy = joined(turn, place, message, other, sums, weight, new_sums)
+    ends[0] = ratio[length] * forward
+    ends[1] = ratio[length] * backward
+    own = pl.ds(2 * rows, length)
+    faces[pl.ds(0, length), :] = message[own, :] + other[own, :]
+    faces[pl.ds(length, length), :] = below[...] + below_far[...]
+    faces[pl.ds(2 * length, length), :] = above[...] + above_far[...]
+    faces[pl.ds(3 * length, 8), :] = energy
 
 
 def coarse_kernel(
@@ -368,9 +472,11 @@
 
 
 def project_kernel(
-    length, paired, place, star, precond, image, faces, table_z, *refs
+    length, paired, place, star, precond, image, faces, table_z, warm_low, warm_high, *refs
 ):
-    reports, (flow, pressure, field, rows_) = refs[:-4], refs[-4:]
+    reports, (flow, pressure, warmed, field, rows_) = refs[:-5], refs[-5:]
+    warmed[:2] = warm_low[...]
+    warmed[2:] = warm_high[...]
     _, layers, rows, depth = star.shape
     first = place[0] * layers
     where = 2 * length
@@ -419,8 +525,29 @@
     return lax.ppermute(array, axis, [(i, (i + by) % length) for i in range(length)])
 
 
-def swapped(array, axis, bit):
-    return lax.ppermute(array, axis, [(i, i ^ bit) for i in range(lax.axis_size(axis))])
+def swapped(array, bit, by=0):
+    count_x, count_y = lax.axis_size("gx"), lax.axis_size("gy")
+    pairs = [
+        (x * count_y + y, (x ^ bit) * count_y + (y + by) % count_y)
+        for x in range(count_x)
+        for y in range(count_y)
+    ]
+    return lax.ppermute(array, ("gx", "gy"), pairs)
+
+
+def pack(melt_flow, thermal_state):
+    parts, layers, rows, depth = melt_flow.shape
+    shape = jax.ShapeDtypeStruct((2 * parts * rows + 8, max(rows, depth)), F32)
+    return pl.pallas_call(
+        pack_kernel,
+        out_shape=[shape, shape],
+        in_specs=[pl.BlockSpec(memory_space=pl.ANY)] * 2,
+        out_specs=[VMEM, VMEM],
+        scratch_shapes=[
+            pltpu.VMEM((2, rows, depth), F32),
+            pltpu.SemaphoreType.DMA((4 * parts + 2,)),
+        ],
+    )(melt_flow, thermal_state)
 
 
 def per_device(melt_flow, thermal_state, powder_flag, spot_lateral_a_cell, spot_lateral_b_cell):
@@ -440,58 +567,60 @@
     diagonal = jnp.asarray(2.0 + values_y[:, None] + values_z[None, :], F32)
     place = (lax.axis_index("gx") % group).astype(jnp.int32).reshape(1)
     plane = (rows, depth)
-
+    line = (length, depth)
+    padded = pltpu.VMEM((4, rows + 16, depth), F32)
+
+    ahead, behind = pack(melt_flow, thermal_state)
+    low_x = along(ahead, "gx", 1)
+    high_x = along(behind, "gx", -1)
     states = jnp.concatenate([melt_flow, thermal_state[None]], 0)
-    low_x = along(melt_flow[:, -2:], "gx", 1)
-    high_x = along(melt_flow[:, :2], "gx", -1)
-    low_t = along(thermal_state[-1, :, -1].reshape(1, rows), "gx", 1)
-    high_t = along(thermal_state[0, :, -1].reshape(1, rows), "gx", -1)
     low_y = along(states[:, :, -2:], "gy", 1)
     high_y = along(states[:, :, :2], "gy", -1)
-    far_low = along(thermal_state[-2:], "gx", 1)
-    far_high = along(thermal_state[:2], "gx", -1)
-
     ratio, weight = call(
         functools.partial(tables_kernel, group, layers),
         [place, diagonal],
         [(length + 1,) + plane, (4 * rounds + 1,) + plane],
     )
-    (star,) = call(
+    marched = [melt_flow, low_x, high_x, thermal_state, powder_flag, low_y, high_y]
+    rim, side_x, side_y = call(
+        rim_kernel, marched + [weight], [(3,) + plane, plane, (layers, depth)], [padded], scalars=0
+    )
+    before_x = along(side_x, "gx", 1)
+    before_y = along(side_y, "gy", 1)
+    star, partial = call(
         march_kernel,
+        marched + [rim, table_y, table_z],
+        [(3, layers) + plane, (layers,) + plane],
+        [padded],
+        scalars=0,
+    )
+    tall = (2 * rows + 2 * length + 8, depth)
+    source, message, head, tail, late_low = call(
+        functools.partial(source_kernel, length),
+        [place, partial, before_x, before_y, table_y, table_z, ratio, edge, thermal_state],
+        [(layers,) + plane, tall, line, line, (2,) + plane],
+        [pltpu.VMEM((length,) + plane, F32)],
+    )
+    sums = jnp.zeros((2,) + plane, F32)
+    late_high = thermal_state[:2]
+    for turn in range(rounds - 1):
+        other = swapped(message, 1 << turn)
+        message, sums, head, tail, late_high = call(
+            functools.partial(merge_kernel, turn, length),
+            [place, message, other, sums, weight, thermal_state],
+            [tall, (2,) + plane, line, line, (2,) + plane],
+        )
+    bit = group >> 1
+    other = swapped(message, bit)
+    ends, sums, faces = call(
+        functools.partial(close_kernel, rounds - 1, length),
         [
-            melt_flow, low_x, high_x, low_y, high_y, thermal_state, low_t, high_t,
-            powder_flag.astype(jnp.int32),
+            place, message, other, sums, weight, ratio,
+            swapped(tail, 0, 1), swapped(tail, bit, 1),
+            swapped(head, 0, -1), swapped(head, bit, -1),
         ],
-        [(3, layers) + plane],
-        [pltpu.VMEM((4, rows + 16, depth), F32)],
-        scalars=0,
-    )
-    before_x = along(star[0, -1], "gx", 1)
-    before_y = along(star[1, :, -1], "gy", 1)
-    source, ends = call(
-        functools.partial(source_kernel, length),
-        [place, star, before_x, before_y, table_y, table_z, ratio],
-        [(layers,) + plane, (2,) + plane],
-        [pltpu.VMEM((rows + 16, depth), F32)],
-    )
-    (faces,) = call(
-        functools.partial(faces_kernel, length),
-        [place, source, ratio, edge],
-        [(2 * length + 8, depth)],
-        [pltpu.VMEM((length,) + plane, F32)],
-    )
-    below = along(faces[length : 2 * length], "gy", 1)
-    above = along(faces[:length], "gy", -1)
-    faces = jnp.concatenate([faces[:length], below, above, faces[2 * length :]], 0)
-    sums = jnp.zeros((2,) + plane, F32)
-    for turn in range(rounds):
-        other = swapped(ends, "gx", 1 << turn)
-        other_faces = swapped(faces, "gx", 1 << turn)
-        ends, sums, faces = call(
-            functools.partial(merge_kernel, turn, turn + 1 == rounds, length),
-            [place, ends, other, sums, faces, other_faces, weight, ratio],
-            [(2,) + plane, (2,) + plane, faces.shape],
-        )
+        [(2,) + plane, (2,) + plane, (3 * length + 8, depth)],
+    )
     if blocks == 1:
         beyond = ends
     else:
@@ -503,15 +632,15 @@
         [pltpu.VMEM((length + 1,) + plane, F32)],
     )
     if blocks > 1:
-        ahead = along(image[0], "gx", -1)
-        tail = place[0] == group - 1
-        image = image.at[layers].set(jnp.where(tail, ahead, image[layers]))
+        onward = along(image[0], "gx", -1)
+        at_end = place[0] == group - 1
+        image = image.at[layers].set(jnp.where(at_end, onward, image[layers]))
         upper = along(report[:length], "gy", -1)
-        crossing = jnp.sum(ahead * image[layers - 1]) + jnp.sum(upper * report[length : 2 * length])
-        crossing = jnp.where(tail, 2.0 * crossing, 0.0)
-        numbers = report[2 * length :]
-        numbers = jnp.where(place[0] == group - 1, numbers, 0.0).at[3].set(crossing)
-        report = report.at[2 * length :].set(lax.psum(numbers, "gx"))
+        crossing = jnp.sum(onward * image[layers - 1])
+        crossing = crossing + jnp.sum(upper * report[length : 2 * length])
+        numbers = report[2 * length :].at[3].set(2.0 * crossing)
+        numbers = lax.psum(jnp.where(at_end, numbers, 0.0), "gx")
+        report = report.at[2 * length :].set(numbers)
     reports = [report] + [along(report, "gy", by) for by in range(1, count_y)]
     precond, image = call(
         physical_kernel,
@@ -529,17 +658,20 @@
         spot_lateral_a_cell,
         spot_lateral_b_cell,
     )
-    (warmed,) = call(
-        heat_kernel,
-        [thermal_state, far_low, far_high, low_y[3], high_y[3], melt_flow, heat],
-        [(layers,) + plane],
-        [pltpu.VMEM((1, rows + 16, depth), F32)],
-        scalars=0,
-    )
-    flow, pressure = call(
+    warmed = []
+    late = (along(late_low, "gx", 1), along(late_high, "gx", -1))
+    for halo, span in zip(late, (range(0, 2), range(2, layers))):
+        warmed += call(
+            functools.partial(heat_kernel, span),
+            [thermal_state, halo, low_y, high_y, melt_flow, heat],
+            [(len(span),) + plane],
+            [pltpu.VMEM((1, rows + 16, depth), F32)],
+            scalars=0,
+        )
+    flow, pressure, warmed = call(
         functools.partial(project_kernel, length, blocks > 1),
-        [place, star, precond, image, faces, table_z] + reports,
-        [(3, layers) + plane, (layers,) + plane],
+        [place, star, precond, image, faces, table_z] + warmed + reports,
+        [(3, layers) + plane, (layers,) + plane, (layers,) + plane],
         [pltpu.VMEM((layers + 1,) + plane, F32), pltpu.VMEM((rows + 16, depth), F32)],
     )
     return (flow, warmed, pressure)

time: 65.5 us -> 67 us (1.023)
  waiting for transfers between devices: 35.8 us -> 27.4 us
  Pallas kernels: 8.05 us -> 14.7 us
  local copies, waits for them, and re-layouts: 2.18 us -> 4.7 us
  starting transfers between devices: 18.2 us -> 18.9 us
    ppermute x15 -> x11, waiting for transfers between devices: 24.8 us -> 18.4 us  [along(): lax.ppermute(array, axis, [(i, (i + by) % length) for i in range(length)])]
    unnamed x16 -> x32, local copies, waits for them, and re-layouts: 0.04 us -> 4.69 us
    pallas_call x10 -> x11, Pallas kernels: 8.05 us -> 12.3 us  [call(): pl.pallas_call(body, out_shape=out_shape, in_specs=[SMEM] * scalars + [VM...]
    pallas_call x0 -> x1, Pallas kernels: none -> 2.41 us  [pack(): pl.pallas_call(pack_kernel, out_shape=[shape, shape], in_specs=[pl.BlockS...]
    slice x6 -> x0, local copies, waits for them, and re-layouts: 2.11 us -> none  [the longest x1 1.26 us: per_device(): high_x = along(melt_flow[:, :2], 'gx', -1)]
    ppermute x4 -> x6, waiting for transfers between devices: 11 us -> 9.01 us  [swapped(): return lax.ppermute(array, ('gx', 'gy'), pairs)]
    ppermute x4 -> x6, starting transfers between devices: 2.93 us -> 4.68 us  [swapped(): return lax.ppermute(array, ('gx', 'gy'), pairs)]
    ppermute x15 -> x11, starting transfers between devices: 15.3 us -> 14.3 us  [along(): lax.ppermute(array, axis, [(i, (i + by) % length) for i in range(length)])]
  transfers between devices with their start and end apart: 19 -> 17, of which waited for: 8 -> 9; matrix products, arithmetic and copies ran while one was open for 2% -> 0% of each run, Pallas kernels for 10% -> 10%
where the time goes in v2:
time: 67 us; the launch traced here: 66.8 us
  waiting for transfers between devices  27.4 us (41%)
  starting transfers between devices  18.9 us (28%)
  Pallas kernels  14.7 us (22%)
  local copies, waits for them, and re-layouts  4.7 us (7%)
  between operations  0.81 us (1%)
    ppermute x11, waiting for transfers between devices, along(): lax.ppermute(array, axis, [(i, (i + by) % length) for i in range(length)])  18.4 us
    ppermute x11, starting transfers between devices, along(): lax.ppermute(array, axis, [(i, (i + by) % length) for i in range(length)])  14.3 us
    pallas_call x11, Pallas kernels, call(): pl.pallas_call(body, out_shape=out_shape, in_specs=[SMEM] * scalars + [VM...  12.3 us
    ppermute x6, waiting for transfers between devices, swapped(): return lax.ppermute(array, ('gx', 'gy'), pairs)  9.01 us
    unnamed x32, local copies, waits for them, and re-layouts  4.69 us
    ppermute x6, starting transfers between devices, swapped(): return lax.ppermute(array, ('gx', 'gy'), pairs)  4.68 us
    pallas_call x1, Pallas kernels, pack(): pl.pallas_call(pack_kernel, out_shape=[shape, shape], in_specs=[pl.BlockS...  2.41 us
  transfers between devices with their start and end apart: 17, of which 9 were waited for; matrix products, arithmetic and copies ran while one was open for 0% of the time, Pallas kernels for 10%

profile of v2, /device:TPU:0, one launch (start us, length us, event | category | flops | bytes accessed | tf_op | source)
XLA Modules:
  0.0 66.8 jit_solution(10153181800852997676)
XLA Ops:
  0.7 2.4 %shard_map.112 = (f32[776,128]{1,0:T(8,128)}, f32[776,128]{1,0:T(8,128)}) custom-call(f32[3,4,128,128]{3,2,1,0:T(8,128)} %flow.9, f32[4,128,128]{2,1,0:T(8,128)} %thermal.13), custom_call_target="tpu_custom_call" | custom-call | tf_op jit(solution)/shard_map/pallas_call | solution.py:541
  3.1 3.1 %collective-permute-start = (f32[776,128]{1,0:T(8,128)}, f32[776,128]{1,0:T(8,128)S(1)}, u32[]{:S(2)}, u32[]{:S(2)}) collective-permute-start(f32[776,128]{1,0:T(8,128)} %get-tuple-element.31), channel_id=1, source_target_pairs={{0,4},{4,8},{8,12},{12,0},{1,5},{5,9},{9,13},{13,1},{2,6},{6,10},{... | collective-permute-start | bytes 1191944 | tf_op jit(solution)/shard_map/ppermute | solution.py:525
  6.2 2.1 %collective-permute-start.1 = (f32[776,128]{1,0:T(8,128)}, f32[776,128]{1,0:T(8,128)}, u32[]{:S(2)}, u32[]{:S(2)}) collective-permute-start(f32[776,128]{1,0:T(8,128)} %get-tuple-element.32), channel_id=1, source_target_pairs={{0,12},{4,0},{8,4},{12,8},{1,13},{5,1},{9,5},{13,9},{2,14},{6,2},{... | collective-permute-start | bytes 1191944 | tf_op jit(solution)/shard_map/ppermute | solution.py:525
  9.4 1.0 %collective-permute-done.3.high_y = f32[4,4,2,128]{3,2,1,0:T(2,128)S(1)} collective-permute-done((f32[4,4,2,128]{3,2,1,0:T(2,128)S(1)}, f32[4,4,2,128]{3,2,1,0:T(2,128)S(1)}, u32[]{:S(2)}, u32[]{:S(2)}) %collective-permute-start.3) | collective-permute-done | bytes 16416 | tf_op jit(solution)/shard_map/ppermute | solution.py:525
  10.4 1.7 %collective-permute-done.2.low_y = f32[4,4,2,128]{3,2,1,0:T(2,128)S(1)} collective-permute-done((f32[4,4,2,128]{3,2,1,0:T(2,128)S(1)}, f32[4,4,2,128]{3,2,1,0:T(2,128)S(1)}, u32[]{:S(2)}, u32[]{:S(2)}) %collective-permute-start.2) | collective-permute-done | bytes 16416 | tf_op jit(solution)/shard_map/ppermute | solution.py:525
  12.2 6.3 %collective-permute-done.low_x = f32[776,128]{1,0:T(8,128)S(1)} collective-permute-done((f32[776,128]{1,0:T(8,128)}, f32[776,128]{1,0:T(8,128)S(1)}, u32[]{:S(2)}, u32[]{:S(2)}) %collective-permute-start) | collective-permute-done | bytes 397344 | tf_op jit(solution)/shard_map/ppermute | solution.py:525
  18.5 7.2 %collective-permute-done.1.high_x = f32[776,128]{1,0:T(8,128)} collective-permute-done((f32[776,128]{1,0:T(8,128)}, f32[776,128]{1,0:T(8,128)}, u32[]{:S(2)}, u32[]{:S(2)}) %collective-permute-start.1) | collective-permute-done | bytes 397344 | tf_op jit(solution)/shard_map/ppermute | solution.py:525
  25.7 1.4 %shard_map.114 = (f32[3,128,128]{2,1,0:T(8,128)S(1)}, f32[128,128]{1,0:T(8,128)S(1)}, f32[4,128]{1,0:T(4,128)S(1)}) custom-call(f32[3,4,128,128]{3,2,1,0:T(8,128)S(1)} %copy-done, f32[776,128]{1,0:T(8,128)S(1)} %collective-permute-done.low_x, f32[776,128]{1,0:T(8,128)} %collective-permute-done.1.high_x, f32[4,128,128]{2,1,0:T(8,128)S(1)} %copy-done.1, ...), custom_call_target="tpu_custom_call" | custom-call | flops 1048576 | bytes 528384 | tf_op jit(solution)/shard_map/pallas_call | solution.py:28
  27.1 1.2 %collective-permute-start.4 = (f32[128,128]{1,0:T(8,128)S(1)}, f32[128,128]{1,0:T(8,128)S(1)}, u32[]{:S(2)}, u32[]{:S(2)}) collective-permute-start(f32[128,128]{1,0:T(8,128)S(1)} %get-tuple-element.37), channel_id=1, source_target_pairs={{0,4},{4,8},{8,12},{12,0},{1,5},{5,9},{9,13},{13,1},{2,6},{6,10},{... | collective-permute-start | bytes 196616 | tf_op jit(solution)/shard_map/ppermute | solution.py:525
  28.3 2.8 %shard_map.115 = (f32[3,4,128,128]{3,2,1,0:T(8,128)S(1)}, f32[4,128,128]{2,1,0:T(8,128)S(1)}) custom-call(f32[3,4,128,128]{3,2,1,0:T(8,128)S(1)} %copy-done, f32[776,128]{1,0:T(8,128)S(1)} %collective-permute-done.low_x, f32[776,128]{1,0:T(8,128)} %collective-permute-done.1.high_x, f32[4,128,128]{2,1,0:T(8,128)S(1)} %copy-done.1, ...), custom_call_target="tpu_custom_call" | custom-call | flops 1048576 | bytes 2097152 | tf_op jit(solution)/shard_map/pallas_call | solution.py:28
  32.0 1.2 %collective-permute-done.4.before_x = f32[128,128]{1,0:T(8,128)S(1)} collective-permute-done((f32[128,128]{1,0:T(8,128)S(1)}, f32[128,128]{1,0:T(8,128)S(1)}, u32[]{:S(2)}, u32[]{:S(2)}) %collective-permute-start.4) | collective-permute-done | bytes 65568 | tf_op jit(solution)/shard_map/ppermute | solution.py:525
  33.2 1.5 %shard_map.116 = (f32[4,128,128]{2,1,0:T(8,128)S(1)}, f32[296,128]{1,0:T(8,128)S(1)}, f32[16,128]{1,0:T(8,128)}, f32[16,128]{1,0:T(8,128)}, f32[2,128,128]{2,1,0:T(8,128)S(1)}) custom-call(s32[1]{0:T(128)} %bitcast.place, f32[4,128,128]{2,1,0:T(8,128)S(1)} %get-tuple-element.36.partial, f32[128,128]{1,0:T(8,128)S(1)} %collective-permute-done.4.before_x, ...), custom_call_target="tpu_custom_call" | custom-call | flops 1048576 | bytes 1122304 | tf_op jit(solution)/shard_map/pallas_call | solution.py:28
  35.4 5.7 %collective-permute-done.6.other = f32[296,128]{1,0:T(8,128)} collective-permute-done((f32[296,128]{1,0:T(8,128)S(1)}, f32[296,128]{1,0:T(8,128)}, u32[]{:S(2)}, u32[]{:S(2)}) %collective-permute-start.6) | collective-permute-done | bytes 151584 | tf_op jit(solution)/shard_map/ppermute | solution.py:535
  42.0 1.1 %shard_map.117 = (f32[296,128]{1,0:T(8,128)S(1)}, f32[2,128,128]{2,1,0:T(8,128)S(1)}, f32[16,128]{1,0:T(8,128)S(1)}, f32[16,128]{1,0:T(8,128)S(1)}, f32[2,128,128]{2,1,0:T(8,128)S(1)}) custom-call(s32[1]{0:T(128)} %bitcast.place, f32[296,128]{1,0:T(8,128)S(1)} %copy-done.9, f32[296,128]{1,0:T(8,128)} %collective-permute-done.6.other, ...), custom_call_target="tpu_custom_call" | custom-call | flops 1048576 | bytes 860160 | tf_op jit(solution)/shard_map/pallas_call | solution.py:28
  44.9 1.3 %collective-permute-start.9 = (f32[16,128]{1,0:T(8,128)S(1)}, f32[16,128]{1,0:T(8,128)S(1)}, u32[]{:S(2)}, u32[]{:S(2)}) collective-permute-start(f32[16,128]{1,0:T(8,128)S(1)} %get-tuple-element.44), channel_id=1, source_target_pairs={{0,9},{1,10},{2,11},{3,8},{4,13},{5,14},{6,15},{7,12},{8,1},{9,2},... | collective-permute-start | bytes 24584 | tf_op jit(solution)/shard_map/ppermute | solution.py:535
  46.2 1.2 %collective-permute-start.8 = (f32[16,128]{1,0:T(8,128)S(1)}, f32[16,128]{1,0:T(8,128)S(1)}, u32[]{:S(2)}, u32[]{:S(2)}) collective-permute-start(f32[16,128]{1,0:T(8,128)S(1)} %get-tuple-element.44), channel_id=1, source_target_pairs={{0,1},{1,2},{2,3},{3,0},{4,5},{5,6},{6,7},{7,4},{8,9},{9,10},{10,1... | collective-permute-start | bytes 24584 | tf_op jit(solution)/shard_map/ppermute | solution.py:535
  47.4 1.3 %collective-permute-start.11 = (f32[16,128]{1,0:T(8,128)S(1)}, f32[16,128]{1,0:T(8,128)S(1)}, u32[]{:S(2)}, u32[]{:S(2)}) collective-permute-start(f32[16,128]{1,0:T(8,128)S(1)} %get-tuple-element.45), channel_id=1, source_target_pairs={{0,11},{1,8},{2,9},{3,10},{4,15},{5,12},{6,13},{7,14},{8,3},{9,0},... | collective-permute-start | bytes 24584 | tf_op jit(solution)/shard_map/ppermute | solution.py:535
  49.1 3.3 %collective-permute-done.9.below_far = f32[16,128]{1,0:T(8,128)S(1)} collective-permute-done((f32[16,128]{1,0:T(8,128)S(1)}, f32[16,128]{1,0:T(8,128)S(1)}, u32[]{:S(2)}, u32[]{:S(2)}) %collective-permute-start.9) | collective-permute-done | bytes 8224 | tf_op jit(solution)/shard_map/ppermute | solution.py:535
  52.4 1.5 %collective-permute-start.12 = (f32[2,128,128]{2,1,0:T(8,128)S(1)}, f32[2,128,128]{2,1,0:T(8,128)S(1)}, u32[]{:S(2)}, u32[]{:S(2)}) collective-permute-start(f32[2,128,128]{2,1,0:T(8,128)S(1)} %get-tuple-element.53), channel_id=1, source_target_pairs={{0,4},{4,8},{8,12},{12,0},{1,5},{5,9},{9,13},{13,1},{2,6},{6,10},{... | collective-permute-start | bytes 393224 | tf_op jit(solution)/shard_map/ppermute | solution.py:525
  53.9 3.2 %collective-permute-start.13 = (f32[2,128,128]{2,1,0:T(8,128)}, f32[2,128,128]{2,1,0:T(8,128)S(1)}, u32[]{:S(2)}, u32[]{:S(2)}) collective-permute-start(f32[2,128,128]{2,1,0:T(8,128)} %copy-done.13), channel_id=1, source_target_pairs={{0,12},{4,0},{8,4},{12,8},{1,13},{5,1},{9,5},{13,9},{2,14},{6,2},{... | collective-permute-start | bytes 393224 | tf_op jit(solution)/shard_map/ppermute | solution.py:525
  58.1 1.1 %shard_map.118 = (f32[2,128,128]{2,1,0:T(8,128)S(1)}, f32[2,128,128]{2,1,0:T(8,128)S(1)}, f32[56,128]{1,0:T(8,128)S(1)}) custom-call(s32[1]{0:T(128)} %bitcast.place, f32[296,128]{1,0:T(8,128)S(1)} %get-tuple-element.42.message, f32[296,128]{1,0:T(8,128)} %collective-permute-done.7.other, f32[2,128,128]{2,1,0:T(8,128)S(1)} %copy-done.11, ...), custom_call_target="tpu_custom_call" | custom-call | flops 1048576 | bytes 581632 | tf_op jit(solution)/shard_map/pallas_call | solution.py:28
  60.0 2.2 %collective-permute-start.15 = (f32[40,128]{1,0:T(8,128)S(1)}, f32[40,128]{1,0:T(8,128)S(1)}, u32[]{:S(2)}, u32[]{:S(2)}) collective-permute-start(f32[40,128]{1,0:T(8,128)S(1)} %get-tuple-element.55.refs_0_), channel_id=1, source_target_pairs={{0,2},{1,3},{2,0},{3,1},{4,6},{5,7},{6,4},{7,5},{8,10},{9,11},{10,... | collective-permute-start | bytes 61448 | tf_op jit(solution)/shard_map/ppermute | solution.py:525
  63.4 1.4 %shard_map.120 = (f32[5,128,128]{2,1,0:T(8,128)S(1)}, f32[5,128,128]{2,1,0:T(8,128)S(1)}) custom-call(f32[5,128,128]{2,1,0:T(8,128)S(1)} %get-tuple-element.49.precond, f32[5,128,128]{2,1,0:T(8,128)S(1)} %get-tuple-element.50.image, f32[128,128]{1,0:T(8,128)S(1)} %copy-done.2, f32[128,128]{1,0:T(8,128)S(1)} %copy-done.2), custom_call_target="tpu_custom_call" | custom-call | flops 1048576 | bytes 1310720 | tf_op jit(solution)/shard_map/pallas_call | solution.py:28
  65.5 1.3 %shard_map.123 = (f32[3,4,128,128]{3,2,1,0:T(8,128)}, f32[4,128,128]{2,1,0:T(8,128)}, f32[4,128,128]{2,1,0:T(8,128)}) custom-call(s32[1]{0:T(128)} %bitcast.place, f32[3,4,128,128]{3,2,1,0:T(8,128)S(1)} %copy-done.5, f32[5,128,128]{2,1,0:T(8,128)S(1)} %get-tuple-element.51.precond, f32[5,128,128]{2,1,0:T(8,128)S(1)} %get-tuple-element.52.image, ...), custom_call_target="tpu_custom_call" | custom-call | flops 1048576 | bytes 2621440 | tf_op jit(solution)/shard_map/pallas_call | solution.py:28
  (59 shorter events, 9.2 us)
Async XLA Ops:
  0.6 7.6 %copy-start.1 = (f32[4,128,128]{2,1,0:T(8,128)S(1)}, f32[4,128,128]{2,1,0:T(8,128)}, u32[]{:S(2)}) copy-start(f32[4,128,128]{2,1,0:T(8,128)} %thermal.13) | copy-start | bytes 786436
  0.6 7.6 %copy-start = (f32[3,4,128,128]{3,2,1,0:T(8,128)S(1)}, f32[3,4,128,128]{3,2,1,0:T(8,128)}, u32[]{:S(2)}) copy-start(f32[3,4,128,128]{3,2,1,0:T(8,128)} %flow.9) | copy-start | bytes 2359300
  0.7 8.3 %copy-start.12 = (f32[128,128]{1,0:T(8,128)S(1)}, f32[128,128]{1,0:T(8,128)}, u32[]{:S(2)}) copy-start(f32[128,128]{1,0:T(8,128)} %constant.75.clone.diagonal) | copy-start | bytes 196612
  0.7 25.0 %copy-start.3 = (s32[4,128,128]{2,1,0:T(8,128)S(1)}, s32[4,128,128]{2,1,0:T(8,128)}, u32[]{:S(2)}) copy-start(s32[4,128,128]{2,1,0:T(8,128)} %flag.3) | copy-start | bytes 786436
  3.1 15.4 %collective-permute-start = (f32[776,128]{1,0:T(8,128)}, f32[776,128]{1,0:T(8,128)S(1)}, u32[]{:S(2)}, u32[]{:S(2)}) collective-permute-start(f32[776,128]{1,0:T(8,128)} %get-tuple-element.31), channel_id=1, source_target_pairs={{0,4},{4,8},{8,12},{12,0},{1,5},{5,9},{9,13},{13,1},{2,6},{6,10},{... | collective-permute-start | bytes 1191944 | tf_op jit(solution)/shard_map/ppermute | solution.py:525
  6.2 19.5 %collective-permute-start.1 = (f32[776,128]{1,0:T(8,128)}, f32[776,128]{1,0:T(8,128)}, u32[]{:S(2)}, u32[]{:S(2)}) collective-permute-start(f32[776,128]{1,0:T(8,128)} %get-tuple-element.32), channel_id=1, source_target_pairs={{0,12},{4,0},{8,4},{12,8},{1,13},{5,1},{9,5},{13,9},{2,14},{6,2},{... | collective-permute-start | bytes 1191944 | tf_op jit(solution)/shard_map/ppermute | solution.py:525
  8.3 2.1 %collective-permute-start.3 = (f32[4,4,2,128]{3,2,1,0:T(2,128)S(1)}, f32[4,4,2,128]{3,2,1,0:T(2,128)S(1)}, u32[]{:S(2)}, u32[]{:S(2)}) collective-permute-start(f32[4,4,2,128]{3,2,1,0:T(2,128)S(1)} %get-tuple-element.59), channel_id=1, source_target_pairs={{0,3},{1,0},{2,1},{3,2},{4,7},{5,4},{6,5},{7,6},{8,11},{9,8},{10,9... | collective-permute-start | bytes 49160 | tf_op jit(solution)/shard_map/ppermute | solution.py:525
  9.0 3.2 %collective-permute-start.2 = (f32[4,4,2,128]{3,2,1,0:T(2,128)S(1)}, f32[4,4,2,128]{3,2,1,0:T(2,128)S(1)}, u32[]{:S(2)}, u32[]{:S(2)}) collective-permute-start(f32[4,4,2,128]{3,2,1,0:T(2,128)S(1)} %get-tuple-element.60), channel_id=1, source_target_pairs={{0,1},{1,2},{2,3},{3,0},{4,5},{5,6},{6,7},{7,4},{8,9},{9,10},{10,1... | collective-permute-start | bytes 49160 | tf_op jit(solution)/shard_map/ppermute | solution.py:525
  27.1 6.1 %collective-permute-start.4 = (f32[128,128]{1,0:T(8,128)S(1)}, f32[128,128]{1,0:T(8,128)S(1)}, u32[]{:S(2)}, u32[]{:S(2)}) collective-permute-start(f32[128,128]{1,0:T(8,128)S(1)} %get-tuple-element.37), channel_id=1, source_target_pairs={{0,4},{4,8},{8,12},{12,0},{1,5},{5,9},{9,13},{13,1},{2,6},{6,10},{... | collective-permute-start | bytes 196616 | tf_op jit(solution)/shard_map/ppermute | solution.py:525
  28.3 3.7 %collective-permute-start.5 = (f32[4,128]{1,0:T(4,128)S(1)}, f32[4,128]{1,0:T(4,128)S(1)}, u32[]{:S(2)}, u32[]{:S(2)}) collective-permute-start(f32[4,128]{1,0:T(4,128)S(1)} %get-tuple-element.38), channel_id=1, source_target_pairs={{0,1},{1,2},{2,3},{3,0},{4,5},{5,6},{6,7},{7,4},{8,9},{9,10},{10,1... | collective-permute-start | bytes 6152 | tf_op jit(solution)/shard_map/ppermute | solution.py:525
  28.3 4.9 %copy-start.6 = (f32[2,128,128]{2,1,0:T(8,128)S(1)}, f32[2,128,128]{2,1,0:T(8,128)}, u32[]{:S(2)}) copy-start(f32[2,128,128]{2,1,0:T(8,128)} %constant.74.clone.edge) | copy-start | bytes 393220
  34.8 6.3 %collective-permute-start.6 = (f32[296,128]{1,0:T(8,128)S(1)}, f32[296,128]{1,0:T(8,128)}, u32[]{:S(2)}, u32[]{:S(2)}) collective-permute-start(f32[296,128]{1,0:T(8,128)S(1)} %get-tuple-element.41.message), channel_id=1, source_target_pairs={{0,4},{1,5},{2,6},{3,7},{4,0},{5,1},{6,2},{7,3},{8,12},{9,13},{10,... | collective-permute-start | bytes 454664 | tf_op jit(solution)/shard_map/ppermute | solution.py:535
  44.4 14.8 %copy-start.7 = (f32[2,128,128]{2,1,0:T(8,128)S(1)}, f32[2,128,128]{2,1,0:T(8,128)}, u32[]{:S(2)}) copy-start(f32[2,128,128]{2,1,0:T(8,128)} %constant.74.clone.edge) | copy-start | bytes 393220
  44.4 12.8 %collective-permute-start.7 = (f32[296,128]{1,0:T(8,128)S(1)}, f32[296,128]{1,0:T(8,128)}, u32[]{:S(2)}, u32[]{:S(2)}) collective-permute-start(f32[296,128]{1,0:T(8,128)S(1)} %get-tuple-element.42.message), channel_id=1, source_target_pairs={{0,8},{1,9},{2,10},{3,11},{4,12},{5,13},{6,14},{7,15},{8,0},{9,1},... | collective-permute-start | bytes 454664 | tf_op jit(solution)/shard_map/ppermute | solution.py:535
  44.9 7.6 %collective-permute-start.9 = (f32[16,128]{1,0:T(8,128)S(1)}, f32[16,128]{1,0:T(8,128)S(1)}, u32[]{:S(2)}, u32[]{:S(2)}) collective-permute-start(f32[16,128]{1,0:T(8,128)S(1)} %get-tuple-element.44), channel_id=1, source_target_pairs={{0,9},{1,10},{2,11},{3,8},{4,13},{5,14},{6,15},{7,12},{8,1},{9,2},... | collective-permute-start | bytes 24584 | tf_op jit(solution)/shard_map/ppermute | solution.py:535
  46.2 7.7 %collective-permute-start.8 = (f32[16,128]{1,0:T(8,128)S(1)}, f32[16,128]{1,0:T(8,128)S(1)}, u32[]{:S(2)}, u32[]{:S(2)}) collective-permute-start(f32[16,128]{1,0:T(8,128)S(1)} %get-tuple-element.44), channel_id=1, source_target_pairs={{0,1},{1,2},{2,3},{3,0},{4,5},{5,6},{6,7},{7,4},{8,9},{9,10},{10,1... | collective-permute-start | bytes 24584 | tf_op jit(solution)/shard_map/ppermute | solution.py:535
  47.4 9.7 %collective-permute-start.11 = (f32[16,128]{1,0:T(8,128)S(1)}, f32[16,128]{1,0:T(8,128)S(1)}, u32[]{:S(2)}, u32[]{:S(2)}) collective-permute-start(f32[16,128]{1,0:T(8,128)S(1)} %get-tuple-element.45), channel_id=1, source_target_pairs={{0,11},{1,8},{2,9},{3,10},{4,15},{5,12},{6,13},{7,14},{8,3},{9,0},... | collective-permute-start | bytes 24584 | tf_op jit(solution)/shard_map/ppermute | solution.py:535
  48.7 8.4 %collective-permute-start.10 = (f32[16,128]{1,0:T(8,128)S(1)}, f32[16,128]{1,0:T(8,128)S(1)}, u32[]{:S(2)}, u32[]{:S(2)}) collective-permute-start(f32[16,128]{1,0:T(8,128)S(1)} %get-tuple-element.45), channel_id=1, source_target_pairs={{0,3},{1,0},{2,1},{3,2},{4,7},{5,4},{6,5},{7,6},{8,11},{9,8},{10,9... | collective-permute-start | bytes 24584 | tf_op jit(solution)/shard_map/ppermute | solution.py:535
  52.4 10.0 %collective-permute-start.12 = (f32[2,128,128]{2,1,0:T(8,128)S(1)}, f32[2,128,128]{2,1,0:T(8,128)S(1)}, u32[]{:S(2)}, u32[]{:S(2)}) collective-permute-start(f32[2,128,128]{2,1,0:T(8,128)S(1)} %get-tuple-element.53), channel_id=1, source_target_pairs={{0,4},{4,8},{8,12},{12,0},{1,5},{5,9},{9,13},{13,1},{2,6},{6,10},{... | collective-permute-start | bytes 393224 | tf_op jit(solution)/shard_map/ppermute | solution.py:525
  53.9 9.2 %collective-permute-start.13 = (f32[2,128,128]{2,1,0:T(8,128)}, f32[2,128,128]{2,1,0:T(8,128)S(1)}, u32[]{:S(2)}, u32[]{:S(2)}) collective-permute-start(f32[2,128,128]{2,1,0:T(8,128)} %copy-done.13), channel_id=1, source_target_pairs={{0,12},{4,0},{8,4},{12,8},{1,13},{5,1},{9,5},{13,9},{2,14},{6,2},{... | collective-permute-start | bytes 393224 | tf_op jit(solution)/shard_map/ppermute | solution.py:525
  59.2 3.1 %copy-start.15 = (s32[8]{0:T(128)S(1)}, s32[8]{0:T(128)}, u32[]{:S(2)}) copy-start(s32[8]{0:T(128)} %param.12) | copy-start | bytes 100
  59.8 5.1 %collective-permute-start.16 = (f32[40,128]{1,0:T(8,128)S(1)}, f32[40,128]{1,0:T(8,128)S(1)}, u32[]{:S(2)}, u32[]{:S(2)}) collective-permute-start(f32[40,128]{1,0:T(8,128)S(1)} %get-tuple-element.55.refs_0_), channel_id=1, source_target_pairs={{0,3},{1,0},{2,1},{3,2},{4,7},{5,4},{6,5},{7,6},{8,11},{9,8},{10,9... | collective-permute-start | bytes 61448 | tf_op jit(solution)/shard_map/ppermute | solution.py:525
  60.0 4.9 %collective-permute-start.15 = (f32[40,128]{1,0:T(8,128)S(1)}, f32[40,128]{1,0:T(8,128)S(1)}, u32[]{:S(2)}, u32[]{:S(2)}) collective-permute-start(f32[40,128]{1,0:T(8,128)S(1)} %get-tuple-element.55.refs_0_), channel_id=1, source_target_pairs={{0,2},{1,3},{2,0},{3,1},{4,6},{5,7},{6,4},{7,5},{8,10},{9,11},{10,... | collective-permute-start | bytes 61448 | tf_op jit(solution)/shard_map/ppermute | solution.py:525
  62.2 3.2 %collective-permute-start.14 = (f32[40,128]{1,0:T(8,128)S(1)}, f32[40,128]{1,0:T(8,128)S(1)}, u32[]{:S(2)}, u32[]{:S(2)}) collective-permute-start(f32[40,128]{1,0:T(8,128)S(1)} %get-tuple-element.55.refs_0_), channel_id=1, source_target_pairs={{0,1},{1,2},{2,3},{3,0},{4,5},{5,6},{6,7},{7,4},{8,9},{9,10},{10,1... | collective-permute-start | bytes 61448 | tf_op jit(solution)/shard_map/ppermute | solution.py:525
  (9 other events, 13.1 us)

commit v3 on v2

--- a/solution.py
+++ b/solution.py
@@ -25,13 +25,15 @@
 def call(body, operands, shapes, scratch=(), scalars=1, flops=1 << 20):
     out_shape = [jax.ShapeDtypeStruct(shape, F32) for shape in shapes]
     moved = 4 * sum(math.prod(shape) for shape in shapes)
+    held = moved + 4 * sum(operand.size for operand in operands)
+    held += 4 * sum(math.prod(space.shape) for space in scratch)
     return pl.pallas_call(
         body,
         out_shape=out_shape,
         in_specs=[SMEM] * scalars + [VMEM] * (len(operands) - scalars),
         out_specs=[VMEM] * len(shapes),
         scratch_shapes=list(scratch),
-        compiler_params=pltpu.CompilerParams(vmem_limit_bytes=44 << 20),
+        compiler_params=pltpu.CompilerParams(vmem_limit_bytes=held + (4 << 20)),
         cost_estimate=pl.CostEstimate(flops=flops, bytes_accessed=2 * moved, transcendentals=0),
     )(*operands)
 
@@ -142,45 +144,31 @@
     pad_rows(padded, 3, low_y[3, index], thermal[index], high_y[3, index])
 
 
-def rim_kernel(
+def march_kernel(
     flow, low_x, high_x, thermal, flag, low_y, high_y, weight, star, side_x, side_y, padded
 ):
     refs = (flow, low_x, high_x, thermal, flag)
     _, layers, rows, depth = flow.shape
     for index in range(layers):
         pad_layer(refs, low_y, high_y, padded, index)
-        if index == layers - 1:
-            for part, value in enumerate(march_layer(refs, padded, index, range(3), 0, rows)):
-                star[part] = value
-                if part == 0:
-                    side_x[...] = value
-                if part == 1:
-                    side_y[pl.ds(index, 1), :] = value[rows - 1 :, :]
-        else:
-            (value,) = march_layer(refs, padded, index, [1], rows - 8, 8)
-            side_y[pl.ds(index, 1), :] = value[7:, :]
-
-
-def march_kernel(
-    flow, low_x, high_x, thermal, flag, low_y, high_y, rim, table_y, table_z,
-    star, source, padded,
-):
-    refs = (flow, low_x, high_x, thermal, flag)
-    _, layers, rows, depth = flow.shape
-    top = lax.broadcasted_iota(jnp.int32, (rows, depth), 0) == 0
-    for index in range(layers):
-        if index == layers - 1:
-            value = [rim[part] for part in range(3)]
-        else:
-            pad_layer(refs, low_y, high_y, padded, index)
-            value = march_layer(refs, padded, index, range(3), 0, rows)
+        value = march_layer(refs, padded, index, range(3), 0, rows)
         for part in range(3):
             star[part, index] = value[part]
-        sink = value[0]
+        side_y[pl.ds(index, 1), :] = value[1][rows - 1 :, :]
+        if index == layers - 1:
+            side_x[...] = value[0]
+
+
+def transform_kernel(star, table_y, table_z, source, rows_):
+    _, layers, rows, depth = star.shape
+    rows_[pl.ds(0, 8), :] = jnp.zeros((8, depth), F32)
+    for index in range(layers):
+        rows_[pl.ds(8, rows), :] = star[1, index]
+        sink = star[0, index]
         if index > 0:
             sink = sink - star[0, index - 1]
-        sink = sink + (value[1] - jnp.where(top, 0.0, pltpu.roll(value[1], 1, 0)))
-        sink = sink + (value[2] - lane_shift(value[2], -1))
+        sink = sink + (star[1, index] - rows_[pl.ds(7, rows), :])
+        sink = sink + (star[2, index] - lane_shift(star[2, index], -1))
         source[index] = dot(dot(table_y[...], -sink), table_z[...])
 
 
@@ -293,14 +281,12 @@
 
 
 def source_kernel(
-    length, place, partial, before_x, before_y, table_y, table_z, ratio, edge, thermal,
-    source, message, head, tail, late, sweep,
+    length, place, partial, before_x, before_y, table_y, table_z, ratio, edge, early, thermal,
+    source, message, late,
 ):
     layers, rows, depth = partial.shape
     first = place[0] * layers
-    inside = lambda index: (index >= first) & (index < first + layers)
-    zero = jnp.zeros((rows, depth), F32)
-    late[...] = thermal[layers - 2 :]
+    late[...] = thermal[:2]
     extra = dot(before_y[...], table_z[...])
     for index in range(layers):
         value = partial[index] + edge[0] * extra[index : index + 1]
@@ -316,6 +302,13 @@
         backward = source[index] + ratio[length - 1 - first - index] * backward
     message[pl.ds(rows, rows), :] = backward
 
+
+def faces_kernel(length, place, source, ratio, edge, faces, sweep):
+    layers, rows, depth = source.shape
+    first = place[0] * layers
+    inside = lambda index: (index >= first) & (index < first + layers)
+    zero = jnp.zeros((rows, depth), F32)
+
     def own(index):
         value = source[jnp.clip(index - first, 0, layers - 1)]
         return jnp.where(inside(index), value, 0.0)
@@ -332,18 +325,15 @@
         index = length - 1 - back
         value = ratio[index + 1] * (sweep[index] + following)
         low, high = face_rows(value, edge)
-        head[pl.ds(index, 1), :] = low
-        tail[pl.ds(index, 1), :] = high
+        faces[pl.ds(index, 1), :] = low
+        faces[pl.ds(length + index, 1), :] = high
         return value, energy + own(index) * value
 
     _, energy = loop(0, length, up, (zero, zero))
-    message[pl.ds(2 * rows, length), :] = head[...]
-    message[pl.ds(2 * rows + length, length), :] = tail[...]
-    energy = jnp.broadcast_to(total(energy), (8, depth))
-    message[pl.ds(2 * rows + 2 * length, 8), :] = energy
-
-
-def joined(turn, place, message, other, sums, weight, new_sums):
+    faces[pl.ds(2 * length, 8), :] = jnp.broadcast_to(total(energy), (8, depth))
+
+
+def joined(turn, place, message, other, sums, weight):
     rows, depth = weight.shape[1:]
     right = ((place[0] >> turn) & 1) == 1
     upper, lower = pl.ds(0, rows), pl.ds(rows, rows)
@@ -352,60 +342,62 @@
     left_t = jnp.where(right, other[lower, :], message[lower, :])
     right_t = jnp.where(right, message[lower, :], other[lower, :])
     own = weight[4 * turn + 2]
-    new_sums[0] = sums[0] + jnp.where(right, left_s * own, 0.0)
-    new_sums[1] = sums[1] + jnp.where(right, 0.0, right_t * own)
+    before = sums[0] + jnp.where(right, left_s * own, 0.0)
+    after = sums[1] + jnp.where(right, 0.0, right_t * own)
     forward = right_s + left_s * weight[4 * turn]
     backward = left_t + right_t * weight[4 * turn + 1]
     energy = 2.0 * total(left_s * right_t * weight[4 * turn + 3])
-    where = pl.ds(message.shape[0] - 8, 8)
-    return forward, backward, message[where, :] + other[where, :] + energy
+    return forward, backward, before, after, energy
 
 
 def merge_kernel(
-    turn, length, place, message, other, sums, weight, thermal,
-    new_message, new_sums, head, tail, late,
+    turn, length, place, message, other, faces, other_faces, sums, weight,
+    new_message, new_sums, head, tail,
 ):
     rows, depth = weight.shape[1:]
-    late[...] = thermal[:2]
-    forward, backward, energy = joined(turn, place, message, other, sums, weight, new_sums)
+    forward, backward, before, after, energy = joined(turn, place, message, other, sums, weight)
+    new_sums[0] = before
+    new_sums[1] = after
     new_message[pl.ds(0, rows), :] = forward
     new_message[pl.ds(rows, rows), :] = backward
-    both = pl.ds(2 * rows, 2 * length)
-    new_message[both, :] = message[both, :] + other[both, :]
-    new_message[pl.ds(2 * rows + 2 * length, 8), :] = energy
-    head[...] = new_message[pl.ds(2 * rows, length), :]
-    tail[...] = new_message[pl.ds(2 * rows + length, length), :]
-
-
-def close_kernel(
-    turn, length, place, message, other, sums, weight, ratio, below, below_far, above, above_far,
-    ends, new_sums, faces,
-):
-    rows, depth = weight.shape[1:]
-    forward, backward, energy = joined(turn, place, message, other, sums, weight, new_sums)
+    low, high, number = pl.ds(0, length), pl.ds(length, length), pl.ds(2 * length, 8)
+    head[...] = faces[low, :] + other_faces[low, :]
+    tail[...] = faces[high, :] + other_faces[high, :]
+    new_message[pl.ds(2 * rows, length), :] = head[...]
+    new_message[pl.ds(2 * rows + length, 8), :] = faces[number, :] + other_faces[number, :] + energy
+
+
+def close_kernel(turn, length, place, message, other, sums, weight, ratio, ends, new_sums):
+    forward, backward, before, after, energy = joined(turn, place, message, other, sums, weight)
     ends[0] = ratio[length] * forward
     ends[1] = ratio[length] * backward
+    new_sums[0] = before
+    new_sums[1] = after
+
+
+def coarse_kernel(
+    turn, length, lone, place, source, message, other, sums, faces_in, weight, ratio, edge, *refs
+):
+    outer, (precond, image, report, faces, sweep, ends) = refs[:-6], refs[-6:]
+    layers, rows, depth = source.shape
+    mine = place[0]
+    first = mine * layers
+    below, below_far, above, above_far = faces_in
+    forward, backward, before, after, energy = joined(turn, place, message, other, sums, weight)
+    ends[0] = ratio[length] * forward
+    ends[1] = ratio[length] * backward
+    beyond = outer[0] if outer else ends
     own = pl.ds(2 * rows, length)
     faces[pl.ds(0, length), :] = message[own, :] + other[own, :]
     faces[pl.ds(length, length), :] = below[...] + below_far[...]
     faces[pl.ds(2 * length, length), :] = above[...] + above_far[...]
-    faces[pl.ds(3 * length, 8), :] = energy
-
-
-def coarse_kernel(
-    length, place, source, ends, beyond, sums, faces, weight, ratio, edge,
-    precond, image, report, sweep,
-):
-    layers, rows, depth = source.shape
-    mine = place[0]
-    first = mine * layers
-    lone = weight.shape[0] - 1
-    count = faces.shape[0] - 8
-    forward = sums[0]
+    number = pl.ds(2 * rows + length, 8)
+    energy = message[number, :] + other[number, :] + energy
+    forward = before
     for index in range(layers):
         forward = source[index] + ratio[first + index] * forward
         sweep[index] = forward
-    value = weight[lone] * (sums[1] + ratio[first + layers] * forward)
+    value = weight[lone] * (after + ratio[first + layers] * forward)
     is_last = first + layers == length
     precond[layers] = jnp.where(is_last, beyond[1], value)
     for index in range(layers - 1, -1, -1):
@@ -458,7 +450,7 @@
     squared = total(squared) + total(head * beyond[0] + tail * beyond[1])
     crossing = 2.0 * total(head * tail)
     where = 2 * length
-    report[pl.ds(where, 1), :] = faces[pl.ds(count, 1), :]
+    report[pl.ds(where, 1), :] = energy[0:1]
     report[pl.ds(where + 1, 1), :] = jnp.broadcast_to(linked, (1, depth))
     report[pl.ds(where + 2, 1), :] = jnp.broadcast_to(squared, (1, depth))
     report[pl.ds(where + 3, 1), :] = jnp.broadcast_to(crossing, (1, depth))
@@ -547,6 +539,7 @@
             pltpu.VMEM((2, rows, depth), F32),
             pltpu.SemaphoreType.DMA((4 * parts + 2,)),
         ],
+        compiler_params=pltpu.CompilerParams(vmem_limit_bytes=4 << 20),
     )(melt_flow, thermal_state)
 
 
@@ -568,7 +561,6 @@
     place = (lax.axis_index("gx") % group).astype(jnp.int32).reshape(1)
     plane = (rows, depth)
     line = (length, depth)
-    padded = pltpu.VMEM((4, rows + 16, depth), F32)
 
     ahead, behind = pack(melt_flow, thermal_state)
     low_x = along(ahead, "gx", 1)
@@ -581,55 +573,76 @@
         [place, diagonal],
         [(length + 1,) + plane, (4 * rounds + 1,) + plane],
     )
-    marched = [melt_flow, low_x, high_x, thermal_state, powder_flag, low_y, high_y]
-    rim, side_x, side_y = call(
-        rim_kernel, marched + [weight], [(3,) + plane, plane, (layers, depth)], [padded], scalars=0
+    star, side_x, side_y = call(
+        march_kernel,
+        [melt_flow, low_x, high_x, thermal_state, powder_flag, low_y, high_y, weight],
+        [(3, layers) + plane, plane, (layers, depth)],
+        [pltpu.VMEM((4, rows + 16, depth), F32)],
+        scalars=0,
     )
     before_x = along(side_x, "gx", 1)
     before_y = along(side_y, "gy", 1)
-    star, partial = call(
-        march_kernel,
-        marched + [rim, table_y, table_z],
-        [(3, layers) + plane, (layers,) + plane],
-        [padded],
+    early = along(thermal_state[-2:], "gx", 1)
+    (partial,) = call(
+        transform_kernel,
+        [star, table_y, table_z],
+        [(layers,) + plane],
+        [pltpu.VMEM((rows + 16, depth), F32)],
         scalars=0,
     )
-    tall = (2 * rows + 2 * length + 8, depth)
-    source, message, head, tail, late_low = call(
+    source, message, late = call(
         functools.partial(source_kernel, length),
-        [place, partial, before_x, before_y, table_y, table_z, ratio, edge, thermal_state],
-        [(layers,) + plane, tall, line, line, (2,) + plane],
+        [
+            place, partial, before_x, before_y, table_y, table_z, ratio, edge, early,
+            thermal_state,
+        ],
+        [(layers,) + plane, (2 * rows, depth), (2,) + plane],
+    )
+    late = along(late, "gx", -1)
+    (faces,) = call(
+        functools.partial(faces_kernel, length),
+        [place, source, ratio, edge],
+        [(2 * length + 8, depth)],
         [pltpu.VMEM((length,) + plane, F32)],
     )
     sums = jnp.zeros((2,) + plane, F32)
-    late_high = thermal_state[:2]
     for turn in range(rounds - 1):
-        other = swapped(message, 1 << turn)
-        message, sums, head, tail, late_high = call(
+        message, sums, head, tail = call(
             functools.partial(merge_kernel, turn, length),
-            [place, message, other, sums, weight, thermal_state],
-            [tall, (2,) + plane, line, line, (2,) + plane],
+            [
+                place, message, swapped(message, 1 << turn), faces, swapped(faces, 1 << turn),
+                sums, weight,
+            ],
+            [(2 * rows + length + 8, depth), (2,) + plane, line, line],
         )
+        if turn + 2 < rounds:
+            number = message[2 * rows + length :]
+            message, faces = message[: 2 * rows], jnp.concatenate([head, tail, number], 0)
     bit = group >> 1
     other = swapped(message, bit)
-    ends, sums, faces = call(
-        functools.partial(close_kernel, rounds - 1, length),
-        [
-            place, message, other, sums, weight, ratio,
-            swapped(tail, 0, 1), swapped(tail, bit, 1),
-            swapped(head, 0, -1), swapped(head, bit, -1),
-        ],
-        [(2,) + plane, (2,) + plane, (3 * length + 8, depth)],
-    )
-    if blocks == 1:
-        beyond = ends
-    else:
-        beyond = jnp.stack([along(ends[0], "gx", group), along(ends[1], "gx", -group)])
-    precond, image, report = call(
-        functools.partial(coarse_kernel, length),
-        [place, source, ends, beyond, sums, faces, weight, ratio, edge],
-        [(layers + 1,) + plane, (layers + 1,) + plane, (2 * length + 8, depth)],
-        [pltpu.VMEM((length + 1,) + plane, F32)],
+    rim = [
+        swapped(tail, 0, 1), swapped(tail, bit, 1), swapped(head, 0, -1), swapped(head, bit, -1)
+    ]
+    outer = []
+    if blocks > 1:
+        ends, _ = call(
+            functools.partial(close_kernel, rounds - 1, length),
+            [place, message, other, sums, weight, ratio],
+            [(2,) + plane, (2,) + plane],
+        )
+        outer = [jnp.stack([along(ends[0], "gx", group), along(ends[1], "gx", -group)])]
+    operands = [place, source, message, other, sums] + rim + [weight, ratio, edge] + outer
+
+    def coarse(*refs):
+        return coarse_kernel(
+            rounds - 1, length, 4 * rounds, *refs[:5], refs[5:9], *refs[9:]
+        )
+
+    precond, image, report, faces = call(
+        coarse,
+        operands,
+        [(layers + 1,) + plane, (layers + 1,) + plane, (2 * length + 8, depth), (3 * length, depth)],
+        [pltpu.VMEM((length + 1,) + plane, F32), pltpu.VMEM((2,) + plane, F32)],
     )
     if blocks > 1:
         onward = along(image[0], "gx", -1)
@@ -659,8 +672,7 @@
         spot_lateral_b_cell,
     )
     warmed = []
-    late = (along(late_low, "gx", 1), along(late_high, "gx", -1))
-    for halo, span in zip(late, (range(0, 2), range(2, layers))):
+    for halo, span in ((early, range(0, 2)), (late, range(2, layers))):
         warmed += call(
             functools.partial(heat_kernel, span),
             [thermal_state, halo, low_y, high_y, melt_flow, heat],

time: 67 us -> 66.8 us (level)
  local copies, waits for them, and re-layouts: 4.7 us -> 7.94 us
  waiting for transfers between devices: 27.4 us -> 25.2 us
  Pallas kernels: 14.7 us -> 13 us
    ppermute x6 -> x7, waiting for transfers between devices: 9.01 us -> 4.94 us  [swapped(): return lax.ppermute(array, ('gx', 'gy'), pairs)]
    ppermute x6 -> x7, starting transfers between devices: 4.68 us -> 7.96 us  [swapped(): return lax.ppermute(array, ('gx', 'gy'), pairs)]
    unnamed x32 -> x38, local copies, waits for them, and re-layouts: 4.69 us -> 7.92 us
    ppermute x11, starting transfers between devices: 14.3 us -> 11.1 us  [along(): lax.ppermute(array, axis, [(i, (i + by) % length) for i in range(length)])]
    ppermute x11, waiting for transfers between devices: 18.4 us -> 20.3 us  [along(): lax.ppermute(array, axis, [(i, (i + by) % length) for i in range(length)])]
    pallas_call x11, Pallas kernels: 12.3 us -> 10.7 us  [call(): pl.pallas_call(body, out_shape=out_shape, in_specs=[SMEM] * scalars + [VM...]
  transfers between devices with their start and end apart: 17 -> 18, of which waited for: 9 -> 9; matrix products, arithmetic and copies ran while one was open for 0% -> 0% of each run, Pallas kernels for 10% -> 12%
where the time goes in v3:
time: 66.8 us; the launch traced here: 66.3 us
  waiting for transfers between devices  25.2 us (38%)
  starting transfers between devices  19 us (28%)
  Pallas kernels  13 us (19%)
  local copies, waits for them, and re-layouts  7.94 us (12%)
  between operations  0.85 us (1%)
    ppermute x11, waiting for transfers between devices, along(): lax.ppermute(array, axis, [(i, (i + by) % length) for i in range(length)])  20.3 us
    ppermute x11, starting transfers between devices, along(): lax.ppermute(array, axis, [(i, (i + by) % length) for i in range(length)])  11.1 us
    pallas_call x11, Pallas kernels, call(): pl.pallas_call(body, out_shape=out_shape, in_specs=[SMEM] * scalars + [VM...  10.7 us
    ppermute x7, starting transfers between devices, swapped(): return lax.ppermute(array, ('gx', 'gy'), pairs)  7.96 us
    unnamed x38, local copies, waits for them, and re-layouts  7.92 us
    ppermute x7, waiting for transfers between devices, swapped(): return lax.ppermute(array, ('gx', 'gy'), pairs)  4.94 us
    pallas_call x1, Pallas kernels, pack(): pl.pallas_call(pack_kernel, out_shape=[shape, shape], in_specs=[pl.BlockS...  2.33 us
  transfers between devices with their start and end apart: 18, of which 9 were waited for; matrix products, arithmetic and copies ran while one was open for 0% of the time, Pallas kernels for 12%

profile of v3, /device:TPU:0, one launch (start us, length us, event | category | flops | bytes accessed | tf_op | source)
XLA Modules:
  0.0 66.3 jit_solution(14004913371337756120)
XLA Ops:
  0.6 1.1 %copy-done = f32[3,4,128,128]{3,2,1,0:T(8,128)S(1)} copy-done((f32[3,4,128,128]{3,2,1,0:T(8,128)S(1)}, f32[3,4,128,128]{3,2,1,0:T(8,128)}, u32[]{:S(2)}) %copy-start) | copy-done | bytes 786456
  2.7 2.3 %shard_map.112 = (f32[776,128]{1,0:T(8,128)}, f32[776,128]{1,0:T(8,128)}) custom-call(f32[3,4,128,128]{3,2,1,0:T(8,128)S(1)} %copy-done, f32[4,128,128]{2,1,0:T(8,128)S(1)} %copy-done.2), custom_call_target="tpu_custom_call" | custom-call | tf_op jit(solution)/shard_map/pallas_call | solution.py:533
  5.1 3.1 %collective-permute-start = (f32[776,128]{1,0:T(8,128)}, f32[776,128]{1,0:T(8,128)S(1)}, u32[]{:S(2)}, u32[]{:S(2)}) collective-permute-start(f32[776,128]{1,0:T(8,128)} %get-tuple-element.26), channel_id=1, source_target_pairs={{0,4},{4,8},{8,12},{12,0},{1,5},{5,9},{9,13},{13,1},{2,6},{6,10},{... | collective-permute-start | bytes 1191944 | tf_op jit(solution)/shard_map/ppermute | solution.py:517
  8.1 2.1 %collective-permute-start.1 = (f32[776,128]{1,0:T(8,128)}, f32[776,128]{1,0:T(8,128)}, u32[]{:S(2)}, u32[]{:S(2)}) collective-permute-start(f32[776,128]{1,0:T(8,128)} %get-tuple-element.27), channel_id=1, source_target_pairs={{0,12},{4,0},{8,4},{12,8},{1,13},{5,1},{9,5},{13,9},{2,14},{6,2},{... | collective-permute-start | bytes 1191944 | tf_op jit(solution)/shard_map/ppermute | solution.py:517
  12.5 1.7 %collective-permute-done.2.low_y = f32[4,4,2,128]{3,2,1,0:T(2,128)S(1)} collective-permute-done((f32[4,4,2,128]{3,2,1,0:T(2,128)S(1)}, f32[4,4,2,128]{3,2,1,0:T(2,128)S(1)}, u32[]{:S(2)}, u32[]{:S(2)}) %collective-permute-start.2) | collective-permute-done | bytes 16416 | tf_op jit(solution)/shard_map/ppermute | solution.py:517
  14.2 6.2 %collective-permute-done.low_x = f32[776,128]{1,0:T(8,128)S(1)} collective-permute-done((f32[776,128]{1,0:T(8,128)}, f32[776,128]{1,0:T(8,128)S(1)}, u32[]{:S(2)}, u32[]{:S(2)}) %collective-permute-start) | collective-permute-done | bytes 397344 | tf_op jit(solution)/shard_map/ppermute | solution.py:517
  21.2 6.7 %collective-permute-done.1.high_x = f32[776,128]{1,0:T(8,128)} collective-permute-done((f32[776,128]{1,0:T(8,128)}, f32[776,128]{1,0:T(8,128)}, u32[]{:S(2)}, u32[]{:S(2)}) %collective-permute-start.1) | collective-permute-done | bytes 397344 | tf_op jit(solution)/shard_map/ppermute | solution.py:517
  29.8 2.4 %shard_map.114 = (f32[3,4,128,128]{3,2,1,0:T(8,128)S(1)}, f32[128,128]{1,0:T(8,128)S(1)}, f32[4,128]{1,0:T(4,128)S(1)}) custom-call(f32[3,4,128,128]{3,2,1,0:T(8,128)S(1)} %copy-done.1, f32[776,128]{1,0:T(8,128)S(1)} %copy-done.9, f32[776,128]{1,0:T(8,128)} %collective-permute-done.1.high_x, f32[4,128,128]{2,1,0:T(8,128)S(1)} %copy-done.3, ...), custom_call_target="tpu_custom_call" | custom-call | flops 1048576 | bytes 1708032 | tf_op jit(solution)/shard_map/pallas_call | solution.py:30
  32.2 1.7 %collective-permute-start.4 = (f32[128,128]{1,0:T(8,128)S(1)}, f32[128,128]{1,0:T(8,128)S(1)}, u32[]{:S(2)}, u32[]{:S(2)}) collective-permute-start(f32[128,128]{1,0:T(8,128)S(1)} %get-tuple-element.30), channel_id=1, source_target_pairs={{0,4},{4,8},{8,12},{12,0},{1,5},{5,9},{9,13},{13,1},{2,6},{6,10},{... | collective-permute-start | bytes 196616 | tf_op jit(solution)/shard_map/ppermute | solution.py:517
  34.8 2.1 %collective-permute-done.5.before_y = f32[4,128]{1,0:T(4,128)S(1)} collective-permute-done((f32[4,128]{1,0:T(4,128)S(1)}, f32[4,128]{1,0:T(4,128)S(1)}, u32[]{:S(2)}, u32[]{:S(2)}) %collective-permute-start.5) | collective-permute-done | bytes 2080 | tf_op jit(solution)/shard_map/ppermute | solution.py:517
  37.0 1.4 %collective-permute-done.4.before_x = f32[128,128]{1,0:T(8,128)S(1)} collective-permute-done((f32[128,128]{1,0:T(8,128)S(1)}, f32[128,128]{1,0:T(8,128)S(1)}, u32[]{:S(2)}, u32[]{:S(2)}) %collective-permute-start.4) | collective-permute-done | bytes 65568 | tf_op jit(solution)/shard_map/ppermute | solution.py:517
  40.4 1.7 %collective-permute-start.8 = (f32[40,128]{1,0:T(8,128)S(1)}, f32[40,128]{1,0:T(8,128)}, u32[]{:S(2)}, u32[]{:S(2)}) collective-permute-start(f32[40,128]{1,0:T(8,128)S(1)} %shard_map.117.faces), channel_id=1, source_target_pairs={{0,4},{1,5},{2,6},{3,7},{4,0},{5,1},{6,2},{7,3},{8,12},{9,13},{10,... | collective-permute-start | bytes 61448 | tf_op jit(solution)/shard_map/ppermute | solution.py:527
  42.1 2.7 %collective-permute-done.8.other_faces = f32[40,128]{1,0:T(8,128)} collective-permute-done((f32[40,128]{1,0:T(8,128)S(1)}, f32[40,128]{1,0:T(8,128)}, u32[]{:S(2)}, u32[]{:S(2)}) %collective-permute-start.8) | collective-permute-done | bytes 20512 | tf_op jit(solution)/shard_map/ppermute | solution.py:527
  45.8 1.1 %shard_map.118 = (f32[280,128]{1,0:T(8,128)S(1)}, f32[2,128,128]{2,1,0:T(8,128)S(1)}, f32[16,128]{1,0:T(8,128)S(1)}, f32[16,128]{1,0:T(8,128)S(1)}) custom-call(s32[1]{0:T(128)} %bitcast.place.refs_0_, f32[256,128]{1,0:T(8,128)S(1)} %copy-done.14, f32[256,128]{1,0:T(8,128)} %collective-permute-done.7.other, f32[40,128]{1,0:T(8,128)S(1)} %shard_map.117.faces, ...), custom_call_target="tpu_custom_call" | custom-call | flops 1048576 | bytes 581632 | tf_op jit(solution)/shard_map/pallas_call | solution.py:30
  47.5 1.7 %collective-permute-start.9 = (f32[280,128]{1,0:T(8,128)S(1)}, f32[280,128]{1,0:T(8,128)}, u32[]{:S(2)}, u32[]{:S(2)}) collective-permute-start(f32[280,128]{1,0:T(8,128)S(1)} %get-tuple-element.35.refs_2_), channel_id=1, source_target_pairs={{0,8},{1,9},{2,10},{3,11},{4,12},{5,13},{6,14},{7,15},{8,0},{9,1},... | collective-permute-start | bytes 430088 | tf_op jit(solution)/shard_map/ppermute | solution.py:527
  49.2 2.4 %collective-permute-start.10 = (f32[16,128]{1,0:T(8,128)S(1)}, f32[16,128]{1,0:T(8,128)S(1)}, u32[]{:S(2)}, u32[]{:S(2)}) collective-permute-start(f32[16,128]{1,0:T(8,128)S(1)} %get-tuple-element.37), channel_id=1, source_target_pairs={{0,1},{1,2},{2,3},{3,0},{4,5},{5,6},{6,7},{7,4},{8,9},{9,10},{10,1... | collective-permute-start | bytes 24584 | tf_op jit(solution)/shard_map/ppermute | solution.py:527
  51.7 1.1 %collective-permute-start.13 = (f32[16,128]{1,0:T(8,128)S(1)}, f32[16,128]{1,0:T(8,128)S(1)}, u32[]{:S(2)}, u32[]{:S(2)}) collective-permute-start(f32[16,128]{1,0:T(8,128)S(1)} %get-tuple-element.38), channel_id=1, source_target_pairs={{0,11},{1,8},{2,9},{3,10},{4,15},{5,12},{6,13},{7,14},{8,3},{9,0},... | collective-permute-start | bytes 24584 | tf_op jit(solution)/shard_map/ppermute | solution.py:527
  53.4 2.2 %collective-permute-done.11.refs_6_ = f32[16,128]{1,0:T(8,128)S(1)} collective-permute-done((f32[16,128]{1,0:T(8,128)S(1)}, f32[16,128]{1,0:T(8,128)S(1)}, u32[]{:S(2)}, u32[]{:S(2)}) %collective-permute-start.11) | collective-permute-done | bytes 8224 | tf_op jit(solution)/shard_map/ppermute | solution.py:527
  55.6 1.8 %collective-permute-start.14 = (f32[2,128,128]{2,1,0:T(8,128)}, f32[2,128,128]{2,1,0:T(8,128)S(1)}, u32[]{:S(2)}, u32[]{:S(2)}) collective-permute-start(f32[2,128,128]{2,1,0:T(8,128)} %copy-done.16), channel_id=1, source_target_pairs={{0,12},{4,0},{8,4},{12,8},{1,13},{5,1},{9,5},{13,9},{2,14},{6,2},{... | collective-permute-start | bytes 393224 | tf_op jit(solution)/shard_map/ppermute | solution.py:517
  58.4 1.6 %shard_map.119 = (f32[5,128,128]{2,1,0:T(8,128)S(1)}, f32[5,128,128]{2,1,0:T(8,128)S(1)}, f32[40,128]{1,0:T(8,128)S(1)}, f32[48,128]{1,0:T(8,128)S(1)}) custom-call(s32[1]{0:T(128)} %bitcast.place.refs_0_, f32[4,128,128]{2,1,0:T(8,128)S(1)} %get-tuple-element.33.source.refs_1_, f32[280,128]{1,0:T(8,128)S(1)} %get-tuple-element.35.refs_2_, ...), custom_call_target="tpu_custom_call" | custom-call | flops 1048576 | bytes 1400832 | tf_op jit(solution)/shard_map/pallas_call | solution.py:30
  60.0 1.1 %collective-permute-start.17 = (f32[40,128]{1,0:T(8,128)S(1)}, f32[40,128]{1,0:T(8,128)S(1)}, u32[]{:S(2)}, u32[]{:S(2)}) collective-permute-start(f32[40,128]{1,0:T(8,128)S(1)} %get-tuple-element.45.refs_0_), channel_id=1, source_target_pairs={{0,3},{1,0},{2,1},{3,2},{4,7},{5,4},{6,5},{7,6},{8,11},{9,8},{10,9... | collective-permute-start | bytes 61448 | tf_op jit(solution)/shard_map/ppermute | solution.py:517
  62.5 1.4 %shard_map.120 = (f32[5,128,128]{2,1,0:T(8,128)S(1)}, f32[5,128,128]{2,1,0:T(8,128)S(1)}) custom-call(f32[5,128,128]{2,1,0:T(8,128)S(1)} %get-tuple-element.39.precond, f32[5,128,128]{2,1,0:T(8,128)S(1)} %get-tuple-element.40.image, f32[128,128]{1,0:T(8,128)S(1)} %copy-done.4, f32[128,128]{1,0:T(8,128)S(1)} %copy-done.4), custom_call_target="tpu_custom_call" | custom-call | flops 1048576 | bytes 1310720 | tf_op jit(solution)/shard_map/pallas_call | solution.py:30
  63.9 1.1 %collective-permute-done.16.refs_2_ = f32[40,128]{1,0:T(8,128)S(1)} collective-permute-done((f32[40,128]{1,0:T(8,128)S(1)}, f32[40,128]{1,0:T(8,128)S(1)}, u32[]{:S(2)}, u32[]{:S(2)}) %collective-permute-start.16) | collective-permute-done | bytes 20512 | tf_op jit(solution)/shard_map/ppermute | solution.py:517
  65.0 1.3 %shard_map.123 = (f32[3,4,128,128]{3,2,1,0:T(8,128)}, f32[4,128,128]{2,1,0:T(8,128)}, f32[4,128,128]{2,1,0:T(8,128)}) custom-call(s32[1]{0:T(128)} %bitcast.place.refs_0_, f32[3,4,128,128]{3,2,1,0:T(8,128)S(1)} %copy-done.6, f32[5,128,128]{2,1,0:T(8,128)S(1)} %get-tuple-element.41.precond, f32[5,128,128]{2,1,0:T(8,128)S(1)} %get-tuple-element.42.image, ...), custom_call_target="tpu_custom_call" | custom-call | flops 1048576 | bytes 2621440 | tf_op jit(solution)/shard_map/pallas_call | solution.py:30
  (68 shorter events, 13.2 us)
Async XLA Ops:
  2.7 7.5 %copy-start.3 = (f32[4,128,128]{2,1,0:T(8,128)S(1)}, f32[4,128,128]{2,1,0:T(8,128)}, u32[]{:S(2)}) copy-start(f32[4,128,128]{2,1,0:T(8,128)} %thermal.9) | copy-start | bytes 786436
  2.7 7.6 %copy-start.1 = (f32[3,4,128,128]{3,2,1,0:T(8,128)S(1)}, f32[3,4,128,128]{3,2,1,0:T(8,128)}, u32[]{:S(2)}) copy-start(f32[3,4,128,128]{3,2,1,0:T(8,128)} %flow.7) | copy-start | bytes 2359300
  2.7 8.3 %copy-start.15 = (f32[128,128]{1,0:T(8,128)S(1)}, f32[128,128]{1,0:T(8,128)}, u32[]{:S(2)}) copy-start(f32[128,128]{1,0:T(8,128)} %constant.75.clone.diagonal) | copy-start | bytes 196612
  5.1 15.4 %collective-permute-start = (f32[776,128]{1,0:T(8,128)}, f32[776,128]{1,0:T(8,128)S(1)}, u32[]{:S(2)}, u32[]{:S(2)}) collective-permute-start(f32[776,128]{1,0:T(8,128)} %get-tuple-element.26), channel_id=1, source_target_pairs={{0,4},{4,8},{8,12},{12,0},{1,5},{5,9},{9,13},{13,1},{2,6},{6,10},{... | collective-permute-start | bytes 1191944 | tf_op jit(solution)/shard_map/ppermute | solution.py:517
  8.1 19.7 %collective-permute-start.1 = (f32[776,128]{1,0:T(8,128)}, f32[776,128]{1,0:T(8,128)}, u32[]{:S(2)}, u32[]{:S(2)}) collective-permute-start(f32[776,128]{1,0:T(8,128)} %get-tuple-element.27), channel_id=1, source_target_pairs={{0,12},{4,0},{8,4},{12,8},{1,13},{5,1},{9,5},{13,9},{2,14},{6,2},{... | collective-permute-start | bytes 1191944 | tf_op jit(solution)/shard_map/ppermute | solution.py:517
  10.2 24.6 %collective-permute-start.6 = (f32[2,128,128]{2,1,0:T(8,128)S(1)}, f32[2,128,128]{2,1,0:T(8,128)S(1)}, u32[]{:S(2)}, u32[]{:S(2)}) collective-permute-start(f32[2,128,128]{2,1,0:T(8,128)S(1)} %slice.11), channel_id=1, source_target_pairs={{0,4},{4,8},{8,12},{12,0},{1,5},{5,9},{9,13},{13,1},{2,6},{6,10},{... | collective-permute-start | bytes 393224 | tf_op jit(solution)/shard_map/ppermute | solution.py:517
  10.3 2.1 %collective-permute-start.3 = (f32[4,4,2,128]{3,2,1,0:T(2,128)S(1)}, f32[4,4,2,128]{3,2,1,0:T(2,128)S(1)}, u32[]{:S(2)}, u32[]{:S(2)}) collective-permute-start(f32[4,4,2,128]{3,2,1,0:T(2,128)S(1)} %get-tuple-element.49), channel_id=1, source_target_pairs={{0,3},{1,0},{2,1},{3,2},{4,7},{5,4},{6,5},{7,6},{8,11},{9,8},{10,9... | collective-permute-start | bytes 49160 | tf_op jit(solution)/shard_map/ppermute | solution.py:517
  11.0 3.2 %collective-permute-start.2 = (f32[4,4,2,128]{3,2,1,0:T(2,128)S(1)}, f32[4,4,2,128]{3,2,1,0:T(2,128)S(1)}, u32[]{:S(2)}, u32[]{:S(2)}) collective-permute-start(f32[4,4,2,128]{3,2,1,0:T(2,128)S(1)} %get-tuple-element.50), channel_id=1, source_target_pairs={{0,1},{1,2},{2,3},{3,0},{4,5},{5,6},{6,7},{7,4},{8,9},{9,10},{10,1... | collective-permute-start | bytes 49160 | tf_op jit(solution)/shard_map/ppermute | solution.py:517
  32.2 6.7 %copy-start.5 = (f32[3,4,128,128]{3,2,1,0:T(8,128)}, f32[3,4,128,128]{3,2,1,0:T(8,128)S(1)}, u32[]{:S(2)}) copy-start(f32[3,4,128,128]{3,2,1,0:T(8,128)S(1)} %get-tuple-element.29.star) | copy-start | bytes 2359300
  32.2 6.2 %copy-start.7 = (f32[2,128,128]{2,1,0:T(8,128)S(1)}, f32[2,128,128]{2,1,0:T(8,128)}, u32[]{:S(2)}) copy-start(f32[2,128,128]{2,1,0:T(8,128)} %constant.74.clone.edge.refs_11_) | copy-start | bytes 393220
  32.2 6.2 %collective-permute-start.4 = (f32[128,128]{1,0:T(8,128)S(1)}, f32[128,128]{1,0:T(8,128)S(1)}, u32[]{:S(2)}, u32[]{:S(2)}) collective-permute-start(f32[128,128]{1,0:T(8,128)S(1)} %get-tuple-element.30), channel_id=1, source_target_pairs={{0,4},{4,8},{8,12},{12,0},{1,5},{5,9},{9,13},{13,1},{2,6},{6,10},{... | collective-permute-start | bytes 196616 | tf_op jit(solution)/shard_map/ppermute | solution.py:517
  33.9 3.0 %collective-permute-start.5 = (f32[4,128]{1,0:T(4,128)S(1)}, f32[4,128]{1,0:T(4,128)S(1)}, u32[]{:S(2)}, u32[]{:S(2)}) collective-permute-start(f32[4,128]{1,0:T(4,128)S(1)} %get-tuple-element.31), channel_id=1, source_target_pairs={{0,1},{1,2},{2,3},{3,0},{4,5},{5,6},{6,7},{7,4},{8,9},{9,10},{10,1... | collective-permute-start | bytes 6152 | tf_op jit(solution)/shard_map/ppermute | solution.py:517
  39.6 5.3 %copy-start.13 = (f32[256,128]{1,0:T(8,128)}, f32[256,128]{1,0:T(8,128)S(1)}, u32[]{:S(2)}) copy-start(f32[256,128]{1,0:T(8,128)S(1)} %get-tuple-element.34.message) | copy-start | bytes 393220
  39.6 5.3 %collective-permute-start.7 = (f32[256,128]{1,0:T(8,128)S(1)}, f32[256,128]{1,0:T(8,128)}, u32[]{:S(2)}, u32[]{:S(2)}) collective-permute-start(f32[256,128]{1,0:T(8,128)S(1)} %get-tuple-element.34.message), channel_id=1, source_target_pairs={{0,4},{1,5},{2,6},{3,7},{4,0},{5,1},{6,2},{7,3},{8,12},{9,13},{10,... | collective-permute-start | bytes 393224 | tf_op jit(solution)/shard_map/ppermute | solution.py:527
  40.4 4.4 %collective-permute-start.8 = (f32[40,128]{1,0:T(8,128)S(1)}, f32[40,128]{1,0:T(8,128)}, u32[]{:S(2)}, u32[]{:S(2)}) collective-permute-start(f32[40,128]{1,0:T(8,128)S(1)} %shard_map.117.faces), channel_id=1, source_target_pairs={{0,4},{1,5},{2,6},{3,7},{4,0},{5,1},{6,2},{7,3},{8,12},{9,13},{10,... | collective-permute-start | bytes 61448 | tf_op jit(solution)/shard_map/ppermute | solution.py:527
  47.5 10.0 %collective-permute-start.9 = (f32[280,128]{1,0:T(8,128)S(1)}, f32[280,128]{1,0:T(8,128)}, u32[]{:S(2)}, u32[]{:S(2)}) collective-permute-start(f32[280,128]{1,0:T(8,128)S(1)} %get-tuple-element.35.refs_2_), channel_id=1, source_target_pairs={{0,8},{1,9},{2,10},{3,11},{4,12},{5,13},{6,14},{7,15},{8,0},{9,1},... | collective-permute-start | bytes 430088 | tf_op jit(solution)/shard_map/ppermute | solution.py:527
  49.2 6.4 %collective-permute-start.11 = (f32[16,128]{1,0:T(8,128)S(1)}, f32[16,128]{1,0:T(8,128)S(1)}, u32[]{:S(2)}, u32[]{:S(2)}) collective-permute-start(f32[16,128]{1,0:T(8,128)S(1)} %get-tuple-element.37), channel_id=1, source_target_pairs={{0,9},{1,10},{2,11},{3,8},{4,13},{5,14},{6,15},{7,12},{8,1},{9,2},... | collective-permute-start | bytes 24584 | tf_op jit(solution)/shard_map/ppermute | solution.py:527
  49.2 8.3 %collective-permute-start.10 = (f32[16,128]{1,0:T(8,128)S(1)}, f32[16,128]{1,0:T(8,128)S(1)}, u32[]{:S(2)}, u32[]{:S(2)}) collective-permute-start(f32[16,128]{1,0:T(8,128)S(1)} %get-tuple-element.37), channel_id=1, source_target_pairs={{0,1},{1,2},{2,3},{3,0},{4,5},{5,6},{6,7},{7,4},{8,9},{9,10},{10,1... | collective-permute-start | bytes 24584 | tf_op jit(solution)/shard_map/ppermute | solution.py:527
  51.7 5.8 %collective-permute-start.13 = (f32[16,128]{1,0:T(8,128)S(1)}, f32[16,128]{1,0:T(8,128)S(1)}, u32[]{:S(2)}, u32[]{:S(2)}) collective-permute-start(f32[16,128]{1,0:T(8,128)S(1)} %get-tuple-element.38), channel_id=1, source_target_pairs={{0,11},{1,8},{2,9},{3,10},{4,15},{5,12},{6,13},{7,14},{8,3},{9,0},... | collective-permute-start | bytes 24584 | tf_op jit(solution)/shard_map/ppermute | solution.py:527
  52.8 4.7 %collective-permute-start.12 = (f32[16,128]{1,0:T(8,128)S(1)}, f32[16,128]{1,0:T(8,128)S(1)}, u32[]{:S(2)}, u32[]{:S(2)}) collective-permute-start(f32[16,128]{1,0:T(8,128)S(1)} %get-tuple-element.38), channel_id=1, source_target_pairs={{0,3},{1,0},{2,1},{3,2},{4,7},{5,4},{6,5},{7,6},{8,11},{9,8},{10,9... | collective-permute-start | bytes 24584 | tf_op jit(solution)/shard_map/ppermute | solution.py:527
  55.6 6.5 %collective-permute-start.14 = (f32[2,128,128]{2,1,0:T(8,128)}, f32[2,128,128]{2,1,0:T(8,128)S(1)}, u32[]{:S(2)}, u32[]{:S(2)}) collective-permute-start(f32[2,128,128]{2,1,0:T(8,128)} %copy-done.16), channel_id=1, source_target_pairs={{0,12},{4,0},{8,4},{12,8},{1,13},{5,1},{9,5},{13,9},{2,14},{6,2},{... | collective-permute-start | bytes 393224 | tf_op jit(solution)/shard_map/ppermute | solution.py:517
  60.0 3.9 %collective-permute-start.17 = (f32[40,128]{1,0:T(8,128)S(1)}, f32[40,128]{1,0:T(8,128)S(1)}, u32[]{:S(2)}, u32[]{:S(2)}) collective-permute-start(f32[40,128]{1,0:T(8,128)S(1)} %get-tuple-element.45.refs_0_), channel_id=1, source_target_pairs={{0,3},{1,0},{2,1},{3,2},{4,7},{5,4},{6,5},{7,6},{8,11},{9,8},{10,9... | collective-permute-start | bytes 61448 | tf_op jit(solution)/shard_map/ppermute | solution.py:517
  61.1 3.9 %collective-permute-start.16 = (f32[40,128]{1,0:T(8,128)S(1)}, f32[40,128]{1,0:T(8,128)S(1)}, u32[]{:S(2)}, u32[]{:S(2)}) collective-permute-start(f32[40,128]{1,0:T(8,128)S(1)} %get-tuple-element.45.refs_0_), channel_id=1, source_target_pairs={{0,2},{1,3},{2,0},{3,1},{4,6},{5,7},{6,4},{7,5},{8,10},{9,11},{10,... | collective-permute-start | bytes 61448 | tf_op jit(solution)/shard_map/ppermute | solution.py:517
  61.6 3.4 %collective-permute-start.15 = (f32[40,128]{1,0:T(8,128)S(1)}, f32[40,128]{1,0:T(8,128)S(1)}, u32[]{:S(2)}, u32[]{:S(2)}) collective-permute-start(f32[40,128]{1,0:T(8,128)S(1)} %get-tuple-element.45.refs_0_), channel_id=1, source_target_pairs={{0,1},{1,2},{2,3},{3,0},{4,5},{5,6},{6,7},{7,4},{8,9},{9,10},{10,1... | collective-permute-start | bytes 61448 | tf_op jit(solution)/shard_map/ppermute | solution.py:517
  (13 other events, 21.3 us)

commit v4 on v3

--- a/solution.py
+++ b/solution.py
@@ -22,7 +22,7 @@
 SMEM = pl.BlockSpec(memory_space=pltpu.SMEM)
 
 
-def call(body, operands, shapes, scratch=(), scalars=1, flops=1 << 20):
+def call(body, operands, shapes, scratch=(), scalars=0, flops=1 << 20):
     out_shape = [jax.ShapeDtypeStruct(shape, F32) for shape in shapes]
     moved = 4 * sum(math.prod(shape) for shape in shapes)
     held = moved + 4 * sum(operand.size for operand in operands)
@@ -53,6 +53,10 @@
             carry = body(index, carry)
         return carry
     return lax.fori_loop(low, high, body, start)
+
+
+def position(group):
+    return lax.rem(lax.axis_index("gx"), group)
 
 
 def sines(length):
@@ -201,7 +205,28 @@
         copy.wait()
 
 
-def heat_kernel(span, thermal, halo, low_y, high_y, flow, heat, warmed, padded):
+def wrapped(distance, span):
+    moved = distance + span // 2
+    moved = jnp.where(moved < 0, moved + span, moved)
+    moved = jnp.where(moved >= span, moved - span, moved)
+    return (moved - span // 2).astype(F32)
+
+
+def laser_row(index, layers, rows, spots_a, spots_b):
+    total_x = layers * lax.axis_size("gx")
+    total_y = rows * lax.axis_size("gy")
+    cell_x = lax.axis_index("gx") * layers + index
+    cells_y = lax.broadcasted_iota(jnp.int32, (1, rows), 1) + lax.axis_index("gy") * rows
+    heat = jnp.zeros((1, rows), F32)
+    for spot in range(spots_a.shape[0]):
+        dist_x = wrapped(jnp.full((1, rows), cell_x - spots_a[spot], jnp.int32), total_x)
+        dist_y = wrapped(cells_y - spots_b[spot], total_y)
+        square = dist_x * dist_x + dist_y * dist_y
+        heat = heat + jnp.exp(square * (-1.0 / (SPOT_RADIUS * SPOT_RADIUS)))
+    return LASER_POWER * heat
+
+
+def heat_kernel(span, spots_a, spots_b, thermal, halo, low_y, high_y, flow, warmed, padded):
     layers, rows, depth = thermal.shape
     top = lax.broadcasted_iota(jnp.int32, (rows, depth), 1) == depth - 1
     for index in span:
@@ -215,28 +240,14 @@
             else:
                 around.append(thermal[other])
         speed = [flow[part, index] for part in range(3)]
-        gain = TIME_INCREMENT * column(heat[pl.ds(index, 1), :])
+        gain = TIME_INCREMENT * column(laser_row(index, layers, rows, spots_a, spots_b))
         moved = advance(around, padded, 0, speed) + jnp.where(top, gain, 0.0)
         warmed[index - span[0]] = moved
 
 
-def laser_heat(start_x, start_y, span_x, span_y, total_x, total_y, spots_a, spots_b):
-    cells_x = start_x + jnp.arange(span_x, dtype=jnp.int32)
-    cells_y = start_y + jnp.arange(span_y, dtype=jnp.int32)
-    dist_x = (
-        (cells_x[:, None] - spots_a[None, :] + total_x // 2) % total_x - total_x // 2
-    ).astype(F32)
-    dist_y = (
-        (cells_y[:, None] - spots_b[None, :] + total_y // 2) % total_y - total_y // 2
-    ).astype(F32)
-    spot_x = jnp.exp(-(dist_x * dist_x) / (SPOT_RADIUS * SPOT_RADIUS))
-    spot_y = jnp.exp(-(dist_y * dist_y) / (SPOT_RADIUS * SPOT_RADIUS))
-    return LASER_POWER * jnp.dot(spot_x, spot_y.T, precision=lax.Precision.HIGHEST)
-
-
-def tables_kernel(group, layers, place, diagonal, ratio, weight):
+def tables_kernel(group, layers, diagonal, ratio, weight):
     length = group * layers
-    mine = place[0]
+    mine = position(group)
     first = mine * layers
     diag = diagonal[...]
     ratio[0] = jnp.zeros_like(diag)
@@ -281,12 +292,11 @@
 
 
 def source_kernel(
-    length, place, partial, before_x, before_y, table_y, table_z, ratio, edge, early, thermal,
-    source, message, late,
+    group, length, partial, before_x, before_y, table_y, table_z, ratio, edge, early,
+    source, message,
 ):
     layers, rows, depth = partial.shape
-    first = place[0] * layers
-    late[...] = thermal[:2]
+    first = position(group) * layers
     extra = dot(before_y[...], table_z[...])
     for index in range(layers):
         value = partial[index] + edge[0] * extra[index : index + 1]
@@ -303,9 +313,9 @@
     message[pl.ds(rows, rows), :] = backward
 
 
-def faces_kernel(length, place, source, ratio, edge, faces, sweep):
+def faces_kernel(group, length, source, ratio, edge, faces, sweep):
     layers, rows, depth = source.shape
-    first = place[0] * layers
+    first = position(group) * layers
     inside = lambda index: (index >= first) & (index < first + layers)
     zero = jnp.zeros((rows, depth), F32)
 
@@ -333,9 +343,9 @@
     faces[pl.ds(2 * length, 8), :] = jnp.broadcast_to(total(energy), (8, depth))
 
 
-def joined(turn, place, message, other, sums, weight):
+def joined(turn, group, message, other, sums, weight):
     rows, depth = weight.shape[1:]
-    right = ((place[0] >> turn) & 1) == 1
+    right = ((position(group) >> turn) & 1) == 1
     upper, lower = pl.ds(0, rows), pl.ds(rows, rows)
     left_s = jnp.where(right, other[upper, :], message[upper, :])
     right_s = jnp.where(right, message[upper, :], other[upper, :])
@@ -351,11 +361,11 @@
 
 
 def merge_kernel(
-    turn, length, place, message, other, faces, other_faces, sums, weight,
+    turn, group, length, message, other, faces, other_faces, sums, weight,
     new_message, new_sums, head, tail,
 ):
     rows, depth = weight.shape[1:]
-    forward, backward, before, after, energy = joined(turn, place, message, other, sums, weight)
+    forward, backward, before, after, energy = joined(turn, group, message, other, sums, weight)
     new_sums[0] = before
     new_sums[1] = after
     new_message[pl.ds(0, rows), :] = forward
@@ -367,8 +377,8 @@
     new_message[pl.ds(2 * rows + length, 8), :] = faces[number, :] + other_faces[number, :] + energy
 
 
-def close_kernel(turn, length, place, message, other, sums, weight, ratio, ends, new_sums):
-    forward, backward, before, after, energy = joined(turn, place, message, other, sums, weight)
+def close_kernel(turn, group, length, message, other, sums, weight, ratio, ends, new_sums):
+    forward, backward, before, after, energy = joined(turn, group, message, other, sums, weight)
     ends[0] = ratio[length] * forward
     ends[1] = ratio[length] * backward
     new_sums[0] = before
@@ -376,14 +386,16 @@
 
 
 def coarse_kernel(
-    turn, length, lone, place, source, message, other, sums, faces_in, weight, ratio, edge, *refs
+    turn, group, length, lone, source, message, other, sums, faces_in, weight, ratio, edge,
+    thermal, *refs
 ):
-    outer, (precond, image, report, faces, sweep, ends) = refs[:-6], refs[-6:]
+    outer, (precond, image, report, faces, late, sweep, ends) = refs[:-7], refs[-7:]
+    late[...] = thermal[:2]
     layers, rows, depth = source.shape
-    mine = place[0]
+    mine = position(group)
     first = mine * layers
     below, below_far, above, above_far = faces_in
-    forward, backward, before, after, energy = joined(turn, place, message, other, sums, weight)
+    forward, backward, before, after, energy = joined(turn, group, message, other, sums, weight)
     ends[0] = ratio[length] * forward
     ends[1] = ratio[length] * backward
     beyond = outer[0] if outer else ends
@@ -464,13 +476,13 @@
 
 
 def project_kernel(
-    length, paired, place, star, precond, image, faces, table_z, warm_low, warm_high, *refs
+    group, length, paired, star, precond, image, faces, table_z, warm_low, warm_high, *refs
 ):
     reports, (flow, pressure, warmed, field, rows_) = refs[:-5], refs[-5:]
     warmed[:2] = warm_low[...]
     warmed[2:] = warm_high[...]
     _, layers, rows, depth = star.shape
-    first = place[0] * layers
+    first = position(group) * layers
     where = 2 * length
     sums = reports[0][pl.ds(where, 8), :]
     for other in reports[1:]:
@@ -558,7 +570,6 @@
         np.broadcast_to(sine_y[[0, rows - 1]][:, :, None], (2, rows, depth)), F32
     )
     diagonal = jnp.asarray(2.0 + values_y[:, None] + values_z[None, :], F32)
-    place = (lax.axis_index("gx") % group).astype(jnp.int32).reshape(1)
     plane = (rows, depth)
     line = (length, depth)
 
@@ -570,7 +581,7 @@
     high_y = along(states[:, :, :2], "gy", -1)
     ratio, weight = call(
         functools.partial(tables_kernel, group, layers),
-        [place, diagonal],
+        [diagonal],
         [(length + 1,) + plane, (4 * rounds + 1,) + plane],
     )
     star, side_x, side_y = call(
@@ -578,7 +589,6 @@
         [melt_flow, low_x, high_x, thermal_state, powder_flag, low_y, high_y, weight],
         [(3, layers) + plane, plane, (layers, depth)],
         [pltpu.VMEM((4, rows + 16, depth), F32)],
-        scalars=0,
     )
     before_x = along(side_x, "gx", 1)
     before_y = along(side_y, "gy", 1)
@@ -588,29 +598,26 @@
         [star, table_y, table_z],
         [(layers,) + plane],
         [pltpu.VMEM((rows + 16, depth), F32)],
-        scalars=0,
-    )
-    source, message, late = call(
-        functools.partial(source_kernel, length),
+    )
+    source, message = call(
+        functools.partial(source_kernel, group, length),
         [
-            place, partial, before_x, before_y, table_y, table_z, ratio, edge, early,
-            thermal_state,
+            partial, before_x, before_y, table_y, table_z, ratio, edge, early,
         ],
-        [(layers,) + plane, (2 * rows, depth), (2,) + plane],
-    )
-    late = along(late, "gx", -1)
+        [(layers,) + plane, (2 * rows, depth)],
+    )
     (faces,) = call(
-        functools.partial(faces_kernel, length),
-        [place, source, ratio, edge],
+        functools.partial(faces_kernel, group, length),
+        [source, ratio, edge],
         [(2 * length + 8, depth)],
         [pltpu.VMEM((length,) + plane, F32)],
     )
     sums = jnp.zeros((2,) + plane, F32)
     for turn in range(rounds - 1):
         message, sums, head, tail = call(
-            functools.partial(merge_kernel, turn, length),
+            functools.partial(merge_kernel, turn, group, length),
             [
-                place, message, swapped(message, 1 << turn), faces, swapped(faces, 1 << turn),
+                message, swapped(message, 1 << turn), faces, swapped(faces, 1 << turn),
                 sums, weight,
             ],
             [(2 * rows + length + 8, depth), (2,) + plane, line, line],
@@ -626,27 +633,30 @@
     outer = []
     if blocks > 1:
         ends, _ = call(
-            functools.partial(close_kernel, rounds - 1, length),
-            [place, message, other, sums, weight, ratio],
+            functools.partial(close_kernel, rounds - 1, group, length),
+            [message, other, sums, weight, ratio],
             [(2,) + plane, (2,) + plane],
         )
         outer = [jnp.stack([along(ends[0], "gx", group), along(ends[1], "gx", -group)])]
-    operands = [place, source, message, other, sums] + rim + [weight, ratio, edge] + outer
+    operands = [source, message, other, sums] + rim + [weight, ratio, edge, thermal_state] + outer
 
     def coarse(*refs):
         return coarse_kernel(
-            rounds - 1, length, 4 * rounds, *refs[:5], refs[5:9], *refs[9:]
+            rounds - 1, group, length, 4 * rounds, *refs[:4], refs[4:8], *refs[8:]
         )
 
-    precond, image, report, faces = call(
+    precond, image, report, faces, late = call(
         coarse,
         operands,
-        [(layers + 1,) + plane, (layers + 1,) + plane, (2 * length + 8, depth), (3 * length, depth)],
+        [
+            (layers + 1,) + plane, (layers + 1,) + plane, (2 * length + 8, depth),
+            (3 * length, depth), (2,) + plane,
+        ],
         [pltpu.VMEM((length + 1,) + plane, F32), pltpu.VMEM((2,) + plane, F32)],
     )
     if blocks > 1:
         onward = along(image[0], "gx", -1)
-        at_end = place[0] == group - 1
+        at_end = position(group) == group - 1
         image = image.at[layers].set(jnp.where(at_end, onward, image[layers]))
         upper = along(report[:length], "gy", -1)
         crossing = jnp.sum(onward * image[layers - 1])
@@ -659,30 +669,19 @@
         physical_kernel,
         [precond, image, table_y, table_z],
         [(layers + 1,) + plane, (layers + 1,) + plane],
-        scalars=0,
-    )
-    heat = laser_heat(
-        lax.axis_index("gx") * layers,
-        lax.axis_index("gy") * rows,
-        layers,
-        rows,
-        layers * count_x,
-        rows * count_y,
-        spot_lateral_a_cell,
-        spot_lateral_b_cell,
-    )
+    )
+    late = along(late, "gx", -1)
     warmed = []
     for halo, span in ((early, range(0, 2)), (late, range(2, layers))):
         warmed += call(
             functools.partial(heat_kernel, span),
-            [thermal_state, halo, low_y, high_y, melt_flow, heat],
+            [spot_lateral_a_cell, spot_lateral_b_cell, thermal_state, halo, low_y, high_y, melt_flow],
             [(len(span),) + plane],
             [pltpu.VMEM((1, rows + 16, depth), F32)],
-            scalars=0,
-        )
+            )
     flow, pressure, warmed = call(
-        functools.partial(project_kernel, length, blocks > 1),
-        [place, star, precond, image, faces, table_z] + warmed + reports,
+        functools.partial(project_kernel, group, length, blocks > 1),
+        [star, precond, image, faces, table_z] + warmed + reports,
         [(3, layers) + plane, (layers,) + plane, (layers,) + plane],
         [pltpu.VMEM((layers + 1,) + plane, F32), pltpu.VMEM((rows + 16, depth), F32)],
     )

time: 66.8 us -> 58.5 us (0.88)
  local copies, waits for them, and re-layouts: 7.94 us -> 2.13 us
  Pallas kernels: 13 us -> 10.1 us
    unnamed x38 -> x20, local copies, waits for them, and re-layouts: 7.92 us -> 2.11 us
    pallas_call x11, Pallas kernels: 10.7 us -> 8.61 us  [call(): pl.pallas_call(body, out_shape=out_shape, in_specs=[SMEM] * scalars + [VM...]
    ppermute x11, starting transfers between devices: 11.1 us -> 12 us  [along(): lax.ppermute(array, axis, [(i, (i + by) % length) for i in range(length)])]
    pallas_call x1, Pallas kernels: 2.33 us -> 1.45 us  [pack(): pl.pallas_call(pack_kernel, out_shape=[shape, shape], in_specs=[pl.BlockS...]
  transfers between devices with their start and end apart: 18 -> 18, of which waited for: 9 -> 11; matrix products, arithmetic and copies ran while one was open for 0% -> 0% of each run, Pallas kernels for 12% -> 10%
where the time goes in v4:
time: 58.5 us; the launch traced here: 58.3 us
  waiting for transfers between devices  25.7 us (44%)
  starting transfers between devices  19.5 us (33%)
  Pallas kernels  10.1 us (17%)
  local copies, waits for them, and re-layouts  2.13 us (4%)
  between operations  0.81 us (1%)
    ppermute x11, waiting for transfers between devices, along(): lax.ppermute(array, axis, [(i, (i + by) % length) for i in range(length)])  20.3 us
    ppermute x11, starting transfers between devices, along(): lax.ppermute(array, axis, [(i, (i + by) % length) for i in range(length)])  12 us
    pallas_call x11, Pallas kernels, call(): pl.pallas_call(body, out_shape=out_shape, in_specs=[SMEM] * scalars + [VM...  8.61 us
    ppermute x7, starting transfers between devices, swapped(): return lax.ppermute(array, ('gx', 'gy'), pairs)  7.46 us
    ppermute x7, waiting for transfers between devices, swapped(): return lax.ppermute(array, ('gx', 'gy'), pairs)  5.4 us
    unnamed x20, local copies, waits for them, and re-layouts  2.11 us
    pallas_call x1, Pallas kernels, pack(): pl.pallas_call(pack_kernel, out_shape=[shape, shape], in_specs=[pl.BlockS...  1.45 us
  transfers between devices with their start and end apart: 18, of which 11 were waited for; matrix products, arithmetic and copies ran while one was open for 0% of the time, Pallas kernels for 10%

profile of v4, /device:TPU:0, one launch (start us, length us, event | category | flops | bytes accessed | tf_op | source)
XLA Modules:
  0.0 58.3 jit_solution(4602733289694422528)
XLA Ops:
  0.6 1.1 %copy-done = f32[3,4,128,128]{3,2,1,0:T(8,128)S(1)} copy-done((f32[3,4,128,128]{3,2,1,0:T(8,128)S(1)}, f32[3,4,128,128]{3,2,1,0:T(8,128)}, u32[]{:S(2)}) %copy-start) | copy-done | bytes 786456
  1.8 0.9 %copy-done.2 = f32[4,128,128]{2,1,0:T(8,128)S(1)} copy-done((f32[4,128,128]{2,1,0:T(8,128)S(1)}, f32[4,128,128]{2,1,0:T(8,128)}, u32[]{:S(2)}) %copy-start.2) | copy-done | bytes 262168
  2.7 1.4 %shard_map.112 = (f32[776,128]{1,0:T(8,128)S(1)}, f32[776,128]{1,0:T(8,128)S(1)}) custom-call(f32[3,4,128,128]{3,2,1,0:T(8,128)S(1)} %copy-done, f32[4,128,128]{2,1,0:T(8,128)S(1)} %copy-done.2), custom_call_target="tpu_custom_call" | custom-call | tf_op jit(solution)/shard_map/pallas_call | solution.py:545
  4.2 3.1 %collective-permute-start = (f32[776,128]{1,0:T(8,128)S(1)}, f32[776,128]{1,0:T(8,128)S(1)}, u32[]{:S(2)}, u32[]{:S(2)}) collective-permute-start(f32[776,128]{1,0:T(8,128)S(1)} %get-tuple-element.26), channel_id=1, source_target_pairs={{0,4},{4,8},{8,12},{12,0},{1,5},{5,9},{9,13},{13,1},{2,6},{6,10},{... | collective-permute-start | bytes 1191944 | tf_op jit(solution)/shard_map/ppermute | solution.py:529
  7.3 2.1 %collective-permute-start.1 = (f32[776,128]{1,0:T(8,128)S(1)}, f32[776,128]{1,0:T(8,128)S(1)}, u32[]{:S(2)}, u32[]{:S(2)}) collective-permute-start(f32[776,128]{1,0:T(8,128)S(1)} %get-tuple-element.27), channel_id=1, source_target_pairs={{0,12},{4,0},{8,4},{12,8},{1,13},{5,1},{9,5},{13,9},{2,14},{6,2},{... | collective-permute-start | bytes 1191944 | tf_op jit(solution)/shard_map/ppermute | solution.py:529
  10.6 1.0 %collective-permute-done.3.high_y = f32[4,4,2,128]{3,2,1,0:T(2,128)S(1)} collective-permute-done((f32[4,4,2,128]{3,2,1,0:T(2,128)S(1)}, f32[4,4,2,128]{3,2,1,0:T(2,128)S(1)}, u32[]{:S(2)}, u32[]{:S(2)}) %collective-permute-start.3) | collective-permute-done | bytes 16416 | tf_op jit(solution)/shard_map/ppermute | solution.py:529
  11.6 1.7 %collective-permute-done.2.low_y = f32[4,4,2,128]{3,2,1,0:T(2,128)S(1)} collective-permute-done((f32[4,4,2,128]{3,2,1,0:T(2,128)S(1)}, f32[4,4,2,128]{3,2,1,0:T(2,128)S(1)}, u32[]{:S(2)}, u32[]{:S(2)}) %collective-permute-start.2) | collective-permute-done | bytes 16416 | tf_op jit(solution)/shard_map/ppermute | solution.py:529
  13.3 6.0 %collective-permute-done.low_x = f32[776,128]{1,0:T(8,128)S(1)} collective-permute-done((f32[776,128]{1,0:T(8,128)S(1)}, f32[776,128]{1,0:T(8,128)S(1)}, u32[]{:S(2)}, u32[]{:S(2)}) %collective-permute-start) | collective-permute-done | bytes 397344 | tf_op jit(solution)/shard_map/ppermute | solution.py:529
  19.4 7.3 %collective-permute-done.1.high_x = f32[776,128]{1,0:T(8,128)S(1)} collective-permute-done((f32[776,128]{1,0:T(8,128)S(1)}, f32[776,128]{1,0:T(8,128)S(1)}, u32[]{:S(2)}, u32[]{:S(2)}) %collective-permute-start.1) | collective-permute-done | bytes 397344 | tf_op jit(solution)/shard_map/ppermute | solution.py:529
  26.7 1.7 %shard_map.114 = (f32[3,4,128,128]{3,2,1,0:T(8,128)S(1)}, f32[128,128]{1,0:T(8,128)S(1)}, f32[4,128]{1,0:T(4,128)S(1)}) custom-call(f32[3,4,128,128]{3,2,1,0:T(8,128)S(1)} %copy-done.1, f32[776,128]{1,0:T(8,128)S(1)} %collective-permute-done.low_x, f32[776,128]{1,0:T(8,128)S(1)} %collective-permute-done.1.high_x, f32[4,128,128]{2,1,0:T(8,128)S(1)} %copy-done.3, ...), custom_call_target="tpu_custom_call" | custom-call | flops 1048576 | bytes 1708032 | tf_op jit(solution)/shard_map/pallas_call | solution.py:30
  28.4 1.7 %collective-permute-start.4 = (f32[128,128]{1,0:T(8,128)S(1)}, f32[128,128]{1,0:T(8,128)S(1)}, u32[]{:S(2)}, u32[]{:S(2)}) collective-permute-start(f32[128,128]{1,0:T(8,128)S(1)} %get-tuple-element.30), channel_id=1, source_target_pairs={{0,4},{4,8},{8,12},{12,0},{1,5},{5,9},{9,13},{13,1},{2,6},{6,10},{... | collective-permute-start | bytes 196616 | tf_op jit(solution)/shard_map/ppermute | solution.py:529
  30.1 0.9 %shard_map.115.partial = f32[4,128,128]{2,1,0:T(8,128)S(1)} custom-call(f32[3,4,128,128]{3,2,1,0:T(8,128)S(1)} %get-tuple-element.29.star, f32[128,128]{1,0:T(8,128)S(1)} %copy-done.4, f32[128,128]{1,0:T(8,128)S(1)} %copy-done.4), custom_call_target="tpu_custom_call" | custom-call | flops 1048576 | bytes 524288 | tf_op jit(solution)/shard_map/pallas_call | solution.py:30
  31.0 2.1 %collective-permute-done.5.before_y = f32[4,128]{1,0:T(4,128)S(1)} collective-permute-done((f32[4,128]{1,0:T(4,128)S(1)}, f32[4,128]{1,0:T(4,128)S(1)}, u32[]{:S(2)}, u32[]{:S(2)}) %collective-permute-start.5) | collective-permute-done | bytes 2080 | tf_op jit(solution)/shard_map/ppermute | solution.py:529
  33.1 1.4 %collective-permute-done.4.before_x = f32[128,128]{1,0:T(8,128)S(1)} collective-permute-done((f32[128,128]{1,0:T(8,128)S(1)}, f32[128,128]{1,0:T(8,128)S(1)}, u32[]{:S(2)}, u32[]{:S(2)}) %collective-permute-start.4) | collective-permute-done | bytes 65568 | tf_op jit(solution)/shard_map/ppermute | solution.py:529
  35.7 2.0 %collective-permute-start.8 = (f32[40,128]{1,0:T(8,128)S(1)}, f32[40,128]{1,0:T(8,128)S(1)}, u32[]{:S(2)}, u32[]{:S(2)}) collective-permute-start(f32[40,128]{1,0:T(8,128)S(1)} %shard_map.117.faces), channel_id=1, source_target_pairs={{0,4},{1,5},{2,6},{3,7},{4,0},{5,1},{6,2},{7,3},{8,12},{9,13},{10,... | collective-permute-start | bytes 61448 | tf_op jit(solution)/shard_map/ppermute | solution.py:539
  37.7 2.6 %collective-permute-done.8.other_faces = f32[40,128]{1,0:T(8,128)S(1)} collective-permute-done((f32[40,128]{1,0:T(8,128)S(1)}, f32[40,128]{1,0:T(8,128)S(1)}, u32[]{:S(2)}, u32[]{:S(2)}) %collective-permute-start.8) | collective-permute-done | bytes 20512 | tf_op jit(solution)/shard_map/ppermute | solution.py:539
  40.4 1.2 %collective-permute-start.9 = (f32[280,128]{1,0:T(8,128)S(1)}, f32[280,128]{1,0:T(8,128)S(1)}, u32[]{:S(2)}, u32[]{:S(2)}) collective-permute-start(f32[280,128]{1,0:T(8,128)S(1)} %get-tuple-element.35.refs_1_), channel_id=1, source_target_pairs={{0,8},{1,9},{2,10},{3,11},{4,12},{5,13},{6,14},{7,15},{8,0},{9,1},... | collective-permute-start | bytes 430088 | tf_op jit(solution)/shard_map/ppermute | solution.py:539
  41.6 3.0 %collective-permute-start.10 = (f32[16,128]{1,0:T(8,128)S(1)}, f32[16,128]{1,0:T(8,128)S(1)}, u32[]{:S(2)}, u32[]{:S(2)}) collective-permute-start(f32[16,128]{1,0:T(8,128)S(1)} %get-tuple-element.37), channel_id=1, source_target_pairs={{0,1},{1,2},{2,3},{3,0},{4,5},{5,6},{6,7},{7,4},{8,9},{9,10},{10,1... | collective-permute-start | bytes 24584 | tf_op jit(solution)/shard_map/ppermute | solution.py:539
  46.6 2.1 %collective-permute-done.13.refs_7_ = f32[16,128]{1,0:T(8,128)S(1)} collective-permute-done((f32[16,128]{1,0:T(8,128)S(1)}, f32[16,128]{1,0:T(8,128)S(1)}, u32[]{:S(2)}, u32[]{:S(2)}) %collective-permute-start.13) | collective-permute-done | bytes 8224 | tf_op jit(solution)/shard_map/ppermute | solution.py:539
  49.4 1.4 %collective-permute-start.14 = (f32[2,128,128]{2,1,0:T(8,128)S(1)}, f32[2,128,128]{2,1,0:T(8,128)S(1)}, u32[]{:S(2)}, u32[]{:S(2)}) collective-permute-start(f32[2,128,128]{2,1,0:T(8,128)S(1)} %get-tuple-element.44), channel_id=1, source_target_pairs={{0,12},{4,0},{8,4},{12,8},{1,13},{5,1},{9,5},{13,9},{2,14},{6,2},{... | collective-permute-start | bytes 393224 | tf_op jit(solution)/shard_map/ppermute | solution.py:529
  50.8 1.0 %collective-permute-start.17 = (f32[40,128]{1,0:T(8,128)S(1)}, f32[40,128]{1,0:T(8,128)S(1)}, u32[]{:S(2)}, u32[]{:S(2)}) collective-permute-start(f32[40,128]{1,0:T(8,128)S(1)} %get-tuple-element.45.refs_0_), channel_id=1, source_target_pairs={{0,3},{1,0},{2,1},{3,2},{4,7},{5,4},{6,5},{7,6},{8,11},{9,8},{10,9... | collective-permute-start | bytes 61448 | tf_op jit(solution)/shard_map/ppermute | solution.py:529
  51.8 2.0 %collective-permute-start.16 = (f32[40,128]{1,0:T(8,128)S(1)}, f32[40,128]{1,0:T(8,128)S(1)}, u32[]{:S(2)}, u32[]{:S(2)}) collective-permute-start(f32[40,128]{1,0:T(8,128)S(1)} %get-tuple-element.45.refs_0_), channel_id=1, source_target_pairs={{0,2},{1,3},{2,0},{3,1},{4,6},{5,7},{6,4},{7,5},{8,10},{9,11},{10,... | collective-permute-start | bytes 61448 | tf_op jit(solution)/shard_map/ppermute | solution.py:529
  54.2 1.5 %shard_map.120 = (f32[5,128,128]{2,1,0:T(8,128)S(1)}, f32[5,128,128]{2,1,0:T(8,128)S(1)}) custom-call(f32[5,128,128]{2,1,0:T(8,128)S(1)} %get-tuple-element.39.precond, f32[5,128,128]{2,1,0:T(8,128)S(1)} %get-tuple-element.40.image, f32[128,128]{1,0:T(8,128)S(1)} %copy-done.4, f32[128,128]{1,0:T(8,128)S(1)} %copy-done.4), custom_call_target="tpu_custom_call" | custom-call | flops 1048576 | bytes 1310720 | tf_op jit(solution)/shard_map/pallas_call | solution.py:30
  56.9 1.3 %shard_map.123 = (f32[3,4,128,128]{3,2,1,0:T(8,128)}, f32[4,128,128]{2,1,0:T(8,128)}, f32[4,128,128]{2,1,0:T(8,128)}) custom-call(f32[3,4,128,128]{3,2,1,0:T(8,128)S(1)} %get-tuple-element.29.star, f32[5,128,128]{2,1,0:T(8,128)S(1)} %get-tuple-element.41.precond, f32[5,128,128]{2,1,0:T(8,128)S(1)} %get-tuple-element.42.image, ...), custom_call_target="tpu_custom_call" | custom-call | flops 1048576 | bytes 2621440 | tf_op jit(solution)/shard_map/pallas_call | solution.py:30
  (47 shorter events, 6.9 us)
Async XLA Ops:
  2.7 6.6 %copy-start.3 = (f32[4,128,128]{2,1,0:T(8,128)S(1)}, f32[4,128,128]{2,1,0:T(8,128)}, u32[]{:S(2)}) copy-start(f32[4,128,128]{2,1,0:T(8,128)} %thermal.7) | copy-start | bytes 786436
  2.7 6.7 %copy-start.1 = (f32[3,4,128,128]{3,2,1,0:T(8,128)S(1)}, f32[3,4,128,128]{3,2,1,0:T(8,128)}, u32[]{:S(2)}) copy-start(f32[3,4,128,128]{3,2,1,0:T(8,128)} %flow.7) | copy-start | bytes 2359300
  2.7 7.5 %copy-start.7 = (f32[128,128]{1,0:T(8,128)S(1)}, f32[128,128]{1,0:T(8,128)}, u32[]{:S(2)}) copy-start(f32[128,128]{1,0:T(8,128)} %constant.10.clone.diagonal) | copy-start | bytes 196612
  2.7 23.9 %copy-start.6 = (s32[4,128,128]{2,1,0:T(8,128)S(1)}, s32[4,128,128]{2,1,0:T(8,128)}, u32[]{:S(2)}) copy-start(s32[4,128,128]{2,1,0:T(8,128)} %flag.1) | copy-start | bytes 786436
  4.2 15.2 %collective-permute-start = (f32[776,128]{1,0:T(8,128)S(1)}, f32[776,128]{1,0:T(8,128)S(1)}, u32[]{:S(2)}, u32[]{:S(2)}) collective-permute-start(f32[776,128]{1,0:T(8,128)S(1)} %get-tuple-element.26), channel_id=1, source_target_pairs={{0,4},{4,8},{8,12},{12,0},{1,5},{5,9},{9,13},{13,1},{2,6},{6,10},{... | collective-permute-start | bytes 1191944 | tf_op jit(solution)/shard_map/ppermute | solution.py:529
  7.3 19.4 %collective-permute-start.1 = (f32[776,128]{1,0:T(8,128)S(1)}, f32[776,128]{1,0:T(8,128)S(1)}, u32[]{:S(2)}, u32[]{:S(2)}) collective-permute-start(f32[776,128]{1,0:T(8,128)S(1)} %get-tuple-element.27), channel_id=1, source_target_pairs={{0,12},{4,0},{8,4},{12,8},{1,13},{5,1},{9,5},{13,9},{2,14},{6,2},{... | collective-permute-start | bytes 1191944 | tf_op jit(solution)/shard_map/ppermute | solution.py:529
  9.4 21.6 %collective-permute-start.6 = (f32[2,128,128]{2,1,0:T(8,128)S(1)}, f32[2,128,128]{2,1,0:T(8,128)S(1)}, u32[]{:S(2)}, u32[]{:S(2)}) collective-permute-start(f32[2,128,128]{2,1,0:T(8,128)S(1)} %slice.11), channel_id=1, source_target_pairs={{0,4},{4,8},{8,12},{12,0},{1,5},{5,9},{9,13},{13,1},{2,6},{6,10},{... | collective-permute-start | bytes 393224 | tf_op jit(solution)/shard_map/ppermute | solution.py:529
  9.5 2.1 %collective-permute-start.3 = (f32[4,4,2,128]{3,2,1,0:T(2,128)S(1)}, f32[4,4,2,128]{3,2,1,0:T(2,128)S(1)}, u32[]{:S(2)}, u32[]{:S(2)}) collective-permute-start(f32[4,4,2,128]{3,2,1,0:T(2,128)S(1)} %get-tuple-element.49), channel_id=1, source_target_pairs={{0,3},{1,0},{2,1},{3,2},{4,7},{5,4},{6,5},{7,6},{8,11},{9,8},{10,9... | collective-permute-start | bytes 49160 | tf_op jit(solution)/shard_map/ppermute | solution.py:529
  10.2 3.2 %collective-permute-start.2 = (f32[4,4,2,128]{3,2,1,0:T(2,128)S(1)}, f32[4,4,2,128]{3,2,1,0:T(2,128)S(1)}, u32[]{:S(2)}, u32[]{:S(2)}) collective-permute-start(f32[4,4,2,128]{3,2,1,0:T(2,128)S(1)} %get-tuple-element.50), channel_id=1, source_target_pairs={{0,1},{1,2},{2,3},{3,0},{4,5},{5,6},{6,7},{7,4},{8,9},{9,10},{10,1... | collective-permute-start | bytes 49160 | tf_op jit(solution)/shard_map/ppermute | solution.py:529
  28.4 6.1 %copy-start.5 = (f32[2,128,128]{2,1,0:T(8,128)S(1)}, f32[2,128,128]{2,1,0:T(8,128)}, u32[]{:S(2)}) copy-start(f32[2,128,128]{2,1,0:T(8,128)} %constant.9.clone.edge.refs_10_) | copy-start | bytes 393220
  28.4 6.1 %collective-permute-start.4 = (f32[128,128]{1,0:T(8,128)S(1)}, f32[128,128]{1,0:T(8,128)S(1)}, u32[]{:S(2)}, u32[]{:S(2)}) collective-permute-start(f32[128,128]{1,0:T(8,128)S(1)} %get-tuple-element.30), channel_id=1, source_target_pairs={{0,4},{4,8},{8,12},{12,0},{1,5},{5,9},{9,13},{13,1},{2,6},{6,10},{... | collective-permute-start | bytes 196616 | tf_op jit(solution)/shard_map/ppermute | solution.py:529
  30.1 3.0 %collective-permute-start.5 = (f32[4,128]{1,0:T(4,128)S(1)}, f32[4,128]{1,0:T(4,128)S(1)}, u32[]{:S(2)}, u32[]{:S(2)}) collective-permute-start(f32[4,128]{1,0:T(4,128)S(1)} %get-tuple-element.31), channel_id=1, source_target_pairs={{0,1},{1,2},{2,3},{3,0},{4,5},{5,6},{6,7},{7,4},{8,9},{9,10},{10,1... | collective-permute-start | bytes 6152 | tf_op jit(solution)/shard_map/ppermute | solution.py:529
  35.0 5.3 %collective-permute-start.7 = (f32[256,128]{1,0:T(8,128)S(1)}, f32[256,128]{1,0:T(8,128)S(1)}, u32[]{:S(2)}, u32[]{:S(2)}) collective-permute-start(f32[256,128]{1,0:T(8,128)S(1)} %get-tuple-element.34.message), channel_id=1, source_target_pairs={{0,4},{1,5},{2,6},{3,7},{4,0},{5,1},{6,2},{7,3},{8,12},{9,13},{10,... | collective-permute-start | bytes 393224 | tf_op jit(solution)/shard_map/ppermute | solution.py:539
  35.7 4.6 %collective-permute-start.8 = (f32[40,128]{1,0:T(8,128)S(1)}, f32[40,128]{1,0:T(8,128)S(1)}, u32[]{:S(2)}, u32[]{:S(2)}) collective-permute-start(f32[40,128]{1,0:T(8,128)S(1)} %shard_map.117.faces), channel_id=1, source_target_pairs={{0,4},{1,5},{2,6},{3,7},{4,0},{5,1},{6,2},{7,3},{8,12},{9,13},{10,... | collective-permute-start | bytes 61448 | tf_op jit(solution)/shard_map/ppermute | solution.py:539
  40.4 8.2 %collective-permute-start.9 = (f32[280,128]{1,0:T(8,128)S(1)}, f32[280,128]{1,0:T(8,128)S(1)}, u32[]{:S(2)}, u32[]{:S(2)}) collective-permute-start(f32[280,128]{1,0:T(8,128)S(1)} %get-tuple-element.35.refs_1_), channel_id=1, source_target_pairs={{0,8},{1,9},{2,10},{3,11},{4,12},{5,13},{6,14},{7,15},{8,0},{9,1},... | collective-permute-start | bytes 430088 | tf_op jit(solution)/shard_map/ppermute | solution.py:539
  41.6 5.0 %collective-permute-start.11 = (f32[16,128]{1,0:T(8,128)S(1)}, f32[16,128]{1,0:T(8,128)S(1)}, u32[]{:S(2)}, u32[]{:S(2)}) collective-permute-start(f32[16,128]{1,0:T(8,128)S(1)} %get-tuple-element.37), channel_id=1, source_target_pairs={{0,9},{1,10},{2,11},{3,8},{4,13},{5,14},{6,15},{7,12},{8,1},{9,2},... | collective-permute-start | bytes 24584 | tf_op jit(solution)/shard_map/ppermute | solution.py:539
  41.6 5.0 %collective-permute-start.10 = (f32[16,128]{1,0:T(8,128)S(1)}, f32[16,128]{1,0:T(8,128)S(1)}, u32[]{:S(2)}, u32[]{:S(2)}) collective-permute-start(f32[16,128]{1,0:T(8,128)S(1)} %get-tuple-element.37), channel_id=1, source_target_pairs={{0,1},{1,2},{2,3},{3,0},{4,5},{5,6},{6,7},{7,4},{8,9},{9,10},{10,1... | collective-permute-start | bytes 24584 | tf_op jit(solution)/shard_map/ppermute | solution.py:539
  44.7 4.0 %collective-permute-start.13 = (f32[16,128]{1,0:T(8,128)S(1)}, f32[16,128]{1,0:T(8,128)S(1)}, u32[]{:S(2)}, u32[]{:S(2)}) collective-permute-start(f32[16,128]{1,0:T(8,128)S(1)} %get-tuple-element.38), channel_id=1, source_target_pairs={{0,11},{1,8},{2,9},{3,10},{4,15},{5,12},{6,13},{7,14},{8,3},{9,0},... | collective-permute-start | bytes 24584 | tf_op jit(solution)/shard_map/ppermute | solution.py:539
  45.2 3.5 %collective-permute-start.12 = (f32[16,128]{1,0:T(8,128)S(1)}, f32[16,128]{1,0:T(8,128)S(1)}, u32[]{:S(2)}, u32[]{:S(2)}) collective-permute-start(f32[16,128]{1,0:T(8,128)S(1)} %get-tuple-element.38), channel_id=1, source_target_pairs={{0,3},{1,0},{2,1},{3,2},{4,7},{5,4},{6,5},{7,6},{8,11},{9,8},{10,9... | collective-permute-start | bytes 24584 | tf_op jit(solution)/shard_map/ppermute | solution.py:539
  48.6 5.1 %copy-start.8 = (s32[8]{0:T(128)S(1)}, s32[8]{0:T(128)}, u32[]{:S(2)}) copy-start(s32[8]{0:T(128)} %spots_a.3) | copy-start | bytes 100
  49.4 6.4 %collective-permute-start.14 = (f32[2,128,128]{2,1,0:T(8,128)S(1)}, f32[2,128,128]{2,1,0:T(8,128)S(1)}, u32[]{:S(2)}, u32[]{:S(2)}) collective-permute-start(f32[2,128,128]{2,1,0:T(8,128)S(1)} %get-tuple-element.44), channel_id=1, source_target_pairs={{0,12},{4,0},{8,4},{12,8},{1,13},{5,1},{9,5},{13,9},{2,14},{6,2},{... | collective-permute-start | bytes 393224 | tf_op jit(solution)/shard_map/ppermute | solution.py:529
  50.8 5.5 %collective-permute-start.17 = (f32[40,128]{1,0:T(8,128)S(1)}, f32[40,128]{1,0:T(8,128)S(1)}, u32[]{:S(2)}, u32[]{:S(2)}) collective-permute-start(f32[40,128]{1,0:T(8,128)S(1)} %get-tuple-element.45.refs_0_), channel_id=1, source_target_pairs={{0,3},{1,0},{2,1},{3,2},{4,7},{5,4},{6,5},{7,6},{8,11},{9,8},{10,9... | collective-permute-start | bytes 61448 | tf_op jit(solution)/shard_map/ppermute | solution.py:529
  51.8 4.5 %collective-permute-start.16 = (f32[40,128]{1,0:T(8,128)S(1)}, f32[40,128]{1,0:T(8,128)S(1)}, u32[]{:S(2)}, u32[]{:S(2)}) collective-permute-start(f32[40,128]{1,0:T(8,128)S(1)} %get-tuple-element.45.refs_0_), channel_id=1, source_target_pairs={{0,2},{1,3},{2,0},{3,1},{4,6},{5,7},{6,4},{7,5},{8,10},{9,11},{10,... | collective-permute-start | bytes 61448 | tf_op jit(solution)/shard_map/ppermute | solution.py:529
  53.7 3.2 %collective-permute-start.15 = (f32[40,128]{1,0:T(8,128)S(1)}, f32[40,128]{1,0:T(8,128)S(1)}, u32[]{:S(2)}, u32[]{:S(2)}) collective-permute-start(f32[40,128]{1,0:T(8,128)S(1)} %get-tuple-element.45.refs_0_), channel_id=1, source_target_pairs={{0,1},{1,2},{2,3},{3,0},{4,5},{5,6},{6,7},{7,4},{8,9},{9,10},{10,1... | collective-permute-start | bytes 61448 | tf_op jit(solution)/shard_map/ppermute | solution.py:529
  (4 other events, 10.7 us)

commit v5 on v4

--- a/solution.py
+++ b/solution.py
@@ -149,7 +149,7 @@
 
 
 def march_kernel(
-    flow, low_x, high_x, thermal, flag, low_y, high_y, weight, star, side_x, side_y, padded
+    flow, low_x, high_x, thermal, flag, low_y, high_y, weight, star, side_y, padded
 ):
     refs = (flow, low_x, high_x, thermal, flag)
     _, layers, rows, depth = flow.shape
@@ -159,12 +159,12 @@
         for part in range(3):
             star[part, index] = value[part]
         side_y[pl.ds(index, 1), :] = value[1][rows - 1 :, :]
-        if index == layers - 1:
-            side_x[...] = value[0]
-
-
-def transform_kernel(star, table_y, table_z, source, rows_):
+
+
+def transform_kernel(group, length, star, table_y, table_z, ratio, source, message, side, rows_):
     _, layers, rows, depth = star.shape
+    first = position(group) * layers
+    inner = jnp.where(first + layers == length, 0.0, 1.0)
     rows_[pl.ds(0, 8), :] = jnp.zeros((8, depth), F32)
     for index in range(layers):
         rows_[pl.ds(8, rows), :] = star[1, index]
@@ -174,6 +174,18 @@
         sink = sink + (star[1, index] - rows_[pl.ds(7, rows), :])
         sink = sink + (star[2, index] - lane_shift(star[2, index], -1))
         source[index] = dot(dot(table_y[...], -sink), table_z[...])
+    onward = dot(dot(table_y[...], star[0, layers - 1]), table_z[...])
+    side[...] = onward
+    onward = inner * onward
+    source[layers] = onward
+    forward = source[0]
+    for index in range(1, layers):
+        forward = source[index] + ratio[first + index] * forward
+    message[pl.ds(0, rows), :] = forward + onward / ratio[first + layers]
+    backward = onward
+    for index in range(layers - 1, -1, -1):
+        backward = source[index] + ratio[length - 1 - first - index] * backward
+    message[pl.ds(rows, rows), :] = backward
 
 
 def pack_kernel(flow, thermal, ahead, behind, planes, sems):
@@ -291,37 +303,37 @@
     )
 
 
-def source_kernel(
-    group, length, partial, before_x, before_y, table_y, table_z, ratio, edge, early,
-    source, message,
+def faces_kernel(
+    group, length, alone, source, wrap, before_y, table_z, ratio, weight, edge, early,
+    faces, sweep,
 ):
-    layers, rows, depth = partial.shape
-    first = position(group) * layers
+    layers, rows, depth = source.shape[0] - 1, *source.shape[1:]
+    mine = position(group)
+    first = mine * layers
+    zero = jnp.zeros((rows, depth), F32)
+    keep = jnp.where(mine == (group - 1 if alone else 0), 1.0, 0.0)
     extra = dot(before_y[...], table_z[...])
+    faces[...] = jnp.zeros(faces.shape, F32)
     for index in range(layers):
-        value = partial[index] + edge[0] * extra[index : index + 1]
-        if index == 0:
-            value = value + dot(dot(table_y[...], before_x[...]), table_z[...])
-        source[index] = value
-    forward = source[0]
-    for index in range(1, layers):
+        faces[pl.ds(2 * length + first + index, 1), :] = extra[index : index + 1]
+    forward = zero
+    for index in range(layers):
         forward = source[index] + ratio[first + index] * forward
-    message[pl.ds(0, rows), :] = forward
-    backward = source[layers - 1]
-    for index in range(layers - 2, -1, -1):
-        backward = source[index] + ratio[length - 1 - first - index] * backward
-    message[pl.ds(rows, rows), :] = backward
-
-
-def faces_kernel(group, length, source, ratio, edge, faces, sweep):
-    layers, rows, depth = source.shape
-    first = position(group) * layers
-    inside = lambda index: (index >= first) & (index < first + layers)
-    zero = jnp.zeros((rows, depth), F32)
+        sweep[index] = forward
+    value = weight[weight.shape[0] - 1] * (source[layers] + ratio[first + layers] * forward)
+    energy = source[layers] * value
+    for index in range(layers - 1, -1, -1):
+        value = ratio[first + index + 1] * (sweep[index] + value)
+        energy = energy + source[index] * value
+    faces[pl.ds(3 * length, 8), :] = jnp.broadcast_to(total(energy), (8, depth))
 
     def own(index):
-        value = source[jnp.clip(index - first, 0, layers - 1)]
-        return jnp.where(inside(index), value, 0.0)
+        value = source[jnp.clip(index - first, 0, layers)]
+        inside = (index >= first) & (index <= first + layers)
+        value = jnp.where(inside, value, 0.0) + edge[0] * faces[pl.ds(2 * length + index, 1), :]
+        if isinstance(index, int):
+            return value + keep * wrap[...] if index == 0 else value
+        return value + jnp.where(index == 0, keep * wrap[...], 0.0)
 
     def down(index, previous):
         current = own(index) + ratio[index] * previous
@@ -330,17 +342,15 @@
 
     loop(0, length, down, zero)
 
-    def up(back, carry):
-        following, energy = carry
+    def up(back, following):
         index = length - 1 - back
         value = ratio[index + 1] * (sweep[index] + following)
         low, high = face_rows(value, edge)
         faces[pl.ds(index, 1), :] = low
         faces[pl.ds(length + index, 1), :] = high
-        return value, energy + own(index) * value
-
-    _, energy = loop(0, length, up, (zero, zero))
-    faces[pl.ds(2 * length, 8), :] = jnp.broadcast_to(total(energy), (8, depth))
+        return value
+
+    loop(0, length, up, zero)
 
 
 def joined(turn, group, message, other, sums, weight):
@@ -370,51 +380,99 @@
     new_sums[1] = after
     new_message[pl.ds(0, rows), :] = forward
     new_message[pl.ds(rows, rows), :] = backward
-    low, high, number = pl.ds(0, length), pl.ds(length, length), pl.ds(2 * length, 8)
+    low, high = pl.ds(0, length), pl.ds(length, length)
+    late, number = pl.ds(2 * length, length), pl.ds(3 * length, 8)
     head[...] = faces[low, :] + other_faces[low, :]
     tail[...] = faces[high, :] + other_faces[high, :]
     new_message[pl.ds(2 * rows, length), :] = head[...]
-    new_message[pl.ds(2 * rows + length, 8), :] = faces[number, :] + other_faces[number, :] + energy
-
-
-def close_kernel(turn, group, length, message, other, sums, weight, ratio, ends, new_sums):
-    forward, backward, before, after, energy = joined(turn, group, message, other, sums, weight)
-    ends[0] = ratio[length] * forward
-    ends[1] = ratio[length] * backward
-    new_sums[0] = before
-    new_sums[1] = after
+    new_message[pl.ds(2 * rows + length, length), :] = faces[late, :] + other_faces[late, :]
+    energy = faces[number, :] + other_faces[number, :] + energy
+    new_message[pl.ds(2 * rows + 2 * length, 8), :] = energy
+
+
+def late_solve(length, message, other, wrap, ratio, edge, late, sweep):
+    rows, depth = wrap.shape
+    own = pl.ds(2 * rows + length, length)
+    late[pl.ds(0, length), :] = message[own, :] + other[own, :]
+
+    def down(index, previous):
+        current = edge[0] * late[pl.ds(index, 1), :] + ratio[index] * previous
+        if isinstance(index, int):
+            current = current + wrap if index == 0 else current
+        else:
+            current = current + jnp.where(index == 0, wrap, 0.0)
+        sweep[index] = current
+        return current
+
+    zero = jnp.zeros((rows, depth), F32)
+    loop(0, length, down, zero)
+
+    def up(back, following):
+        index = length - 1 - back
+        value = ratio[index + 1] * (sweep[index] + following)
+        sweep[index] = value
+        late[pl.ds(length + index, 1), :] = jnp.sum(value * edge[0], axis=0, keepdims=True)
+        return value
+
+    loop(0, length, up, zero)
+    sweep[length] = zero
+
+
+def wrap_kernel(group, alone, side, *refs):
+    wraps, wrap = refs[:-1], refs[-1]
+    here = position(group) == group - 1
+    value = jnp.where(here, side[...], 0.0) if alone else jnp.zeros(side.shape, F32)
+    for part in wraps:
+        value = value + part[...]
+    wrap[...] = value
+
+
+def close_kernel(
+    turn, group, length, message, other, sums, weight, ratio, edge, wrap, ends, late, sweep
+):
+    forward, backward, _, _, _ = joined(turn, group, message, other, sums, weight)
+    late_solve(length, message, other, wrap[...], ratio, edge, late, sweep)
+    ends[0] = ratio[length] * forward + sweep[length - 1]
+    ends[1] = ratio[length] * backward + sweep[0]
 
 
 def coarse_kernel(
-    turn, group, length, lone, source, message, other, sums, faces_in, weight, ratio, edge,
-    thermal, *refs
+    turn, group, length, source, message, other, sums, faces_in, weight, ratio, edge, thermal,
+    wrap, *refs
 ):
-    outer, (precond, image, report, faces, late, sweep, ends) = refs[:-7], refs[-7:]
-    late[...] = thermal[:2]
-    layers, rows, depth = source.shape
-    mine = position(group)
-    first = mine * layers
+    layers, rows, depth = source.shape[0] - 1, *source.shape[1:]
+    outer, (precond, image, report, faces, after_heat, late, sweep, ends) = refs[:-8], refs[-8:]
+    after_heat[...] = thermal[:2]
+    first = position(group) * layers
+    wrap = wrap[...]
     below, below_far, above, above_far = faces_in
     forward, backward, before, after, energy = joined(turn, group, message, other, sums, weight)
-    ends[0] = ratio[length] * forward
-    ends[1] = ratio[length] * backward
+    late_solve(length, message, other, wrap, ratio, edge, late, sweep)
+    ends[0] = ratio[length] * forward + sweep[length - 1]
+    ends[1] = ratio[length] * backward + sweep[0]
     beyond = outer[0] if outer else ends
     own = pl.ds(2 * rows, length)
     faces[pl.ds(0, length), :] = message[own, :] + other[own, :]
     faces[pl.ds(length, length), :] = below[...] + below_far[...]
     faces[pl.ds(2 * length, length), :] = above[...] + above_far[...]
-    number = pl.ds(2 * rows + length, 8)
+    number = pl.ds(2 * rows + 2 * length, 8)
     energy = message[number, :] + other[number, :] + energy
+    late_rows = late[pl.ds(0, length), :]
+    energy = energy + total(
+        late_rows * (2.0 * faces[pl.ds(0, length), :] - late[pl.ds(length, length), :])
+    )
+    energy = energy + total(wrap * (2.0 * ratio[length] * backward + sweep[0]))
     forward = before
     for index in range(layers):
         forward = source[index] + ratio[first + index] * forward
-        sweep[index] = forward
-    value = weight[lone] * (after + ratio[first + layers] * forward)
+        precond[index] = forward
+    lone = weight[weight.shape[0] - 1]
+    value = lone * (after + source[layers] + ratio[first + layers] * forward)
     is_last = first + layers == length
-    precond[layers] = jnp.where(is_last, beyond[1], value)
+    precond[layers] = jnp.where(is_last, beyond[1], value + sweep[first + layers])
     for index in range(layers - 1, -1, -1):
-        value = ratio[first + index + 1] * (sweep[index] + value)
-        precond[index] = value
+        value = ratio[first + index + 1] * (precond[index] + value)
+        precond[index] = value + sweep[first + index]
     lead, trail = edge[0], edge[1]
 
     def pull(index):
@@ -545,7 +603,7 @@
     return pl.pallas_call(
         pack_kernel,
         out_shape=[shape, shape],
-        in_specs=[pl.BlockSpec(memory_space=pl.ANY)] * 2,
+        in_specs=[pl.BlockSpec(memory_space=pltpu.HBM)] * 2,
         out_specs=[VMEM, VMEM],
         scratch_shapes=[
             pltpu.VMEM((2, rows, depth), F32),
@@ -584,33 +642,39 @@
         [diagonal],
         [(length + 1,) + plane, (4 * rounds + 1,) + plane],
     )
-    star, side_x, side_y = call(
+    star, side_y = call(
         march_kernel,
         [melt_flow, low_x, high_x, thermal_state, powder_flag, low_y, high_y, weight],
-        [(3, layers) + plane, plane, (layers, depth)],
+        [(3, layers) + plane, (layers, depth)],
         [pltpu.VMEM((4, rows + 16, depth), F32)],
     )
-    before_x = along(side_x, "gx", 1)
     before_y = along(side_y, "gy", 1)
     early = along(thermal_state[-2:], "gx", 1)
-    (partial,) = call(
-        transform_kernel,
-        [star, table_y, table_z],
-        [(layers,) + plane],
+    source, message, side = call(
+        functools.partial(transform_kernel, group, length),
+        [star, table_y, table_z, ratio],
+        [(layers + 1,) + plane, (2 * rows, depth), plane],
         [pltpu.VMEM((rows + 16, depth), F32)],
     )
-    source, message = call(
-        functools.partial(source_kernel, group, length),
+    alone = blocks == 1
+    (faces,) = call(
+        functools.partial(faces_kernel, group, length, alone),
         [
-            partial, before_x, before_y, table_y, table_z, ratio, edge, early,
+            source, side if alone else along(side, "gx", 1), before_y, table_z, ratio, weight,
+            edge, early,
         ],
-        [(layers,) + plane, (2 * rows, depth)],
-    )
-    (faces,) = call(
-        functools.partial(faces_kernel, group, length),
-        [source, ratio, edge],
-        [(2 * length + 8, depth)],
-        [pltpu.VMEM((length,) + plane, F32)],
+        [(3 * length + 8, depth)],
+        [pltpu.VMEM((max(length, layers + 1),) + plane, F32)],
+    )
+    wraps = []
+    for target in range(group - 1 if alone else group):
+        pairs = [
+            (block * group + group - 1, (block + 1) % blocks * group + target)
+            for block in range(blocks)
+        ]
+        wraps.append(lax.ppermute(side, "gx", pairs))
+    (wrap,) = call(
+        functools.partial(wrap_kernel, group, alone), [side] + wraps, [plane], flops=1 << 30
     )
     sums = jnp.zeros((2,) + plane, F32)
     for turn in range(rounds - 1):
@@ -620,30 +684,31 @@
                 message, swapped(message, 1 << turn), faces, swapped(faces, 1 << turn),
                 sums, weight,
             ],
-            [(2 * rows + length + 8, depth), (2,) + plane, line, line],
+            [(2 * rows + 2 * length + 8, depth), (2,) + plane, line, line],
         )
         if turn + 2 < rounds:
-            number = message[2 * rows + length :]
-            message, faces = message[: 2 * rows], jnp.concatenate([head, tail, number], 0)
+            rest = message[2 * rows + length :]
+            message, faces = message[: 2 * rows], jnp.concatenate([head, tail, rest], 0)
     bit = group >> 1
     other = swapped(message, bit)
     rim = [
         swapped(tail, 0, 1), swapped(tail, bit, 1), swapped(head, 0, -1), swapped(head, bit, -1)
     ]
     outer = []
-    if blocks > 1:
-        ends, _ = call(
+    scratch = [pltpu.VMEM((2 * length, depth), F32), pltpu.VMEM((length + 1,) + plane, F32)]
+    if not alone:
+        (ends,) = call(
             functools.partial(close_kernel, rounds - 1, group, length),
-            [message, other, sums, weight, ratio],
-            [(2,) + plane, (2,) + plane],
+            [message, other, sums, weight, ratio, edge, wrap],
+            [(2,) + plane],
+            scratch,
         )
         outer = [jnp.stack([along(ends[0], "gx", group), along(ends[1], "gx", -group)])]
-    operands = [source, message, other, sums] + rim + [weight, ratio, edge, thermal_state] + outer
+    operands = [source, message, other, sums] + rim
+    operands += [weight, ratio, edge, thermal_state, wrap] + outer
 
     def coarse(*refs):
-        return coarse_kernel(
-            rounds - 1, group, length, 4 * rounds, *refs[:4], refs[4:8], *refs[8:]
-        )
+        coarse_kernel(rounds - 1, group, length, *refs[:4], refs[4:8], *refs[8:])
 
     precond, image, report, faces, late = call(
         coarse,
@@ -652,7 +717,7 @@
             (layers + 1,) + plane, (layers + 1,) + plane, (2 * length + 8, depth),
             (3 * length, depth), (2,) + plane,
         ],
-        [pltpu.VMEM((length + 1,) + plane, F32), pltpu.VMEM((2,) + plane, F32)],
+        scratch + [pltpu.VMEM((2,) + plane, F32)],
     )
     if blocks > 1:
         onward = along(image[0], "gx", -1)

time: 58.5 us -> 59.9 us (1.024)
  waiting for transfers between devices: 25.7 us -> 26.4 us
    ppermute x11 -> x10, starting transfers between devices: 12 us -> 9.2 us  [along(): lax.ppermute(array, axis, [(i, (i + by) % length) for i in range(length)])]
    ppermute x0 -> x3, starting transfers between devices: none -> 2.61 us  [per_device(): wraps.append(lax.ppermute(side, 'gx', pairs))]
    ppermute x0 -> x3, waiting for transfers between devices: none -> 1.37 us  [per_device(): wraps.append(lax.ppermute(side, 'gx', pairs))]
    ppermute x7, starting transfers between devices: 7.46 us -> 8.15 us  [swapped(): return lax.ppermute(array, ('gx', 'gy'), pairs)]
    ppermute x11 -> x10, waiting for transfers between devices: 20.3 us -> 19.9 us  [along(): lax.ppermute(array, axis, [(i, (i + by) % length) for i in range(length)])]
  transfers between devices with their start and end apart: 18 -> 20, of which waited for: 11 -> 10; matrix products, arithmetic and copies ran while one was open for 0% -> 0% of each run, Pallas kernels for 10% -> 11%
where the time goes in v5:
time: 59.9 us; the launch traced here: 59.7 us
  waiting for transfers between devices  26.4 us (44%)
  starting transfers between devices  20 us (33%)
  Pallas kernels  10.4 us (17%)
  local copies, waits for them, and re-layouts  2.13 us (4%)
  between operations  0.82 us (1%)
    ppermute x10, waiting for transfers between devices, along(): lax.ppermute(array, axis, [(i, (i + by) % length) for i in range(length)])  19.9 us
    ppermute x10, starting transfers between devices, along(): lax.ppermute(array, axis, [(i, (i + by) % length) for i in range(length)])  9.2 us
    pallas_call x11, Pallas kernels, call(): pl.pallas_call(body, out_shape=out_shape, in_specs=[SMEM] * scalars + [VM...  8.9 us
    ppermute x7, starting transfers between devices, swapped(): return lax.ppermute(array, ('gx', 'gy'), pairs)  8.15 us
    ppermute x7, waiting for transfers between devices, swapped(): return lax.ppermute(array, ('gx', 'gy'), pairs)  5.19 us
    ppermute x3, starting transfers between devices, per_device(): wraps.append(lax.ppermute(side, 'gx', pairs))  2.61 us
    unnamed x20, local copies, waits for them, and re-layouts  2.11 us
    pallas_call x1, Pallas kernels, pack(): pl.pallas_call(pack_kernel, out_shape=[shape, shape], in_specs=[pl.BlockS...  1.45 us
  transfers between devices with their start and end apart: 20, of which 10 were waited for; matrix products, arithmetic and copies ran while one was open for 0% of the time, Pallas kernels for 11%

profile of v5, /device:TPU:0, one launch (start us, length us, event | category | flops | bytes accessed | tf_op | source)
XLA Modules:
  0.0 59.7 jit_solution(2720535770972094304)
XLA Ops:
  0.6 1.1 %copy-done = f32[3,4,128,128]{3,2,1,0:T(8,128)S(1)} copy-done((f32[3,4,128,128]{3,2,1,0:T(8,128)S(1)}, f32[3,4,128,128]{3,2,1,0:T(8,128)}, u32[]{:S(2)}) %copy-start) | copy-done | bytes 786456
  2.7 1.4 %shard_map.112 = (f32[776,128]{1,0:T(8,128)S(1)}, f32[776,128]{1,0:T(8,128)S(1)}) custom-call(f32[3,4,128,128]{3,2,1,0:T(8,128)S(1)} %copy-done, f32[4,128,128]{2,1,0:T(8,128)S(1)} %copy-done.2), custom_call_target="tpu_custom_call" | custom-call | tf_op jit(solution)/shard_map/pallas_call | solution.py:603
  4.2 3.1 %collective-permute-start = (f32[776,128]{1,0:T(8,128)S(1)}, f32[776,128]{1,0:T(8,128)S(1)}, u32[]{:S(2)}, u32[]{:S(2)}) collective-permute-start(f32[776,128]{1,0:T(8,128)S(1)} %get-tuple-element.26), channel_id=1, source_target_pairs={{0,4},{4,8},{8,12},{12,0},{1,5},{5,9},{9,13},{13,1},{2,6},{6,10},{... | collective-permute-start | bytes 1191944 | tf_op jit(solution)/shard_map/ppermute | solution.py:587
  7.3 2.1 %collective-permute-start.1 = (f32[776,128]{1,0:T(8,128)S(1)}, f32[776,128]{1,0:T(8,128)S(1)}, u32[]{:S(2)}, u32[]{:S(2)}) collective-permute-start(f32[776,128]{1,0:T(8,128)S(1)} %get-tuple-element.27), channel_id=1, source_target_pairs={{0,12},{4,0},{8,4},{12,8},{1,13},{5,1},{9,5},{13,9},{2,14},{6,2},{... | collective-permute-start | bytes 1191944 | tf_op jit(solution)/shard_map/ppermute | solution.py:587
  10.6 1.0 %collective-permute-done.3.high_y = f32[4,4,2,128]{3,2,1,0:T(2,128)S(1)} collective-permute-done((f32[4,4,2,128]{3,2,1,0:T(2,128)S(1)}, f32[4,4,2,128]{3,2,1,0:T(2,128)S(1)}, u32[]{:S(2)}, u32[]{:S(2)}) %collective-permute-start.3) | collective-permute-done | bytes 16416 | tf_op jit(solution)/shard_map/ppermute | solution.py:587
  11.6 1.7 %collective-permute-done.2.low_y = f32[4,4,2,128]{3,2,1,0:T(2,128)S(1)} collective-permute-done((f32[4,4,2,128]{3,2,1,0:T(2,128)S(1)}, f32[4,4,2,128]{3,2,1,0:T(2,128)S(1)}, u32[]{:S(2)}, u32[]{:S(2)}) %collective-permute-start.2) | collective-permute-done | bytes 16416 | tf_op jit(solution)/shard_map/ppermute | solution.py:587
  13.3 6.0 %collective-permute-done.low_x = f32[776,128]{1,0:T(8,128)S(1)} collective-permute-done((f32[776,128]{1,0:T(8,128)S(1)}, f32[776,128]{1,0:T(8,128)S(1)}, u32[]{:S(2)}, u32[]{:S(2)}) %collective-permute-start) | collective-permute-done | bytes 397344 | tf_op jit(solution)/shard_map/ppermute | solution.py:587
  19.4 7.3 %collective-permute-done.1.high_x = f32[776,128]{1,0:T(8,128)S(1)} collective-permute-done((f32[776,128]{1,0:T(8,128)S(1)}, f32[776,128]{1,0:T(8,128)S(1)}, u32[]{:S(2)}, u32[]{:S(2)}) %collective-permute-start.1) | collective-permute-done | bytes 397344 | tf_op jit(solution)/shard_map/ppermute | solution.py:587
  26.7 1.7 %shard_map.114 = (f32[3,4,128,128]{3,2,1,0:T(8,128)S(1)}, f32[4,128]{1,0:T(4,128)S(1)}) custom-call(f32[3,4,128,128]{3,2,1,0:T(8,128)S(1)} %copy-done.1, f32[776,128]{1,0:T(8,128)S(1)} %collective-permute-done.low_x, f32[776,128]{1,0:T(8,128)S(1)} %collective-permute-done.1.high_x, f32[4,128,128]{2,1,0:T(8,128)S(1)} %copy-done.3, ...), custom_call_target="tpu_custom_call" | custom-call | flops 1048576 | bytes 1576960 | tf_op jit(solution)/shard_map/pallas_call | solution.py:30
  28.4 1.0 %shard_map.115 = (f32[5,128,128]{2,1,0:T(8,128)S(1)}, f32[256,128]{1,0:T(8,128)S(1)}, f32[128,128]{1,0:T(8,128)S(1)}) custom-call(f32[3,4,128,128]{3,2,1,0:T(8,128)S(1)} %get-tuple-element.29.star, f32[128,128]{1,0:T(8,128)S(1)} %copy-done.4, f32[128,128]{1,0:T(8,128)S(1)} %copy-done.4, f32[17,128,128]{2,1,0:T(8,128)S(1)} %get-tuple-element.30.ratio.refs_9_), custom_call_target="tpu_custom_call" | custom-call | flops 1048576 | bytes 1048576 | tf_op jit(solution)/shard_map/pallas_call | solution.py:30
  29.4 1.8 %collective-permute-start.4 = (f32[256,128]{1,0:T(8,128)S(1)}, f32[256,128]{1,0:T(8,128)S(1)}, u32[]{:S(2)}, u32[]{:S(2)}) collective-permute-start(f32[256,128]{1,0:T(8,128)S(1)} %get-tuple-element.32.message), channel_id=1, source_target_pairs={{0,4},{1,5},{2,6},{3,7},{4,0},{5,1},{6,2},{7,3},{8,12},{9,13},{10,... | collective-permute-start | bytes 393224 | tf_op jit(solution)/shard_map/ppermute | solution.py:597
  31.2 3.0 %collective-permute-done.5.before_y = f32[4,128]{1,0:T(4,128)S(1)} collective-permute-done((f32[4,128]{1,0:T(4,128)S(1)}, f32[4,128]{1,0:T(4,128)S(1)}, u32[]{:S(2)}, u32[]{:S(2)}) %collective-permute-start.5) | collective-permute-done | bytes 2080 | tf_op jit(solution)/shard_map/ppermute | solution.py:587
  36.6 1.3 %collective-permute-start.13 = (f32[128,128]{1,0:T(8,128)S(1)}, f32[128,128]{1,0:T(8,128)S(1)}, u32[]{:S(2)}, u32[]{:S(2)}) collective-permute-start(f32[128,128]{1,0:T(8,128)S(1)} %get-tuple-element.33.wrap.side), channel_id=1, source_target_pairs={{12,0},{13,1},{14,2},{15,3},{28,16},{29,17},{30,18},{31,19}} | collective-permute-start | bytes 196616 | tf_op jit(solution)/shard_map/ppermute | solution.py:675
  39.0 2.1 %collective-permute-start.8 = (f32[296,128]{1,0:T(8,128)S(1)}, f32[296,128]{1,0:T(8,128)S(1)}, u32[]{:S(2)}, u32[]{:S(2)}) collective-permute-start(f32[296,128]{1,0:T(8,128)S(1)} %get-tuple-element.35.refs_1_), channel_id=1, source_target_pairs={{0,8},{1,9},{2,10},{3,11},{4,12},{5,13},{6,14},{7,15},{8,0},{9,1},... | collective-permute-start | bytes 454664 | tf_op jit(solution)/shard_map/ppermute | solution.py:597
  41.1 2.1 %collective-permute-start.9 = (f32[16,128]{1,0:T(8,128)S(1)}, f32[16,128]{1,0:T(8,128)S(1)}, u32[]{:S(2)}, u32[]{:S(2)}) collective-permute-start(f32[16,128]{1,0:T(8,128)S(1)} %get-tuple-element.37), channel_id=1, source_target_pairs={{0,1},{1,2},{2,3},{3,0},{4,5},{5,6},{6,7},{7,4},{8,9},{9,10},{10,1... | collective-permute-start | bytes 24584 | tf_op jit(solution)/shard_map/ppermute | solution.py:597
  43.2 1.8 %collective-permute-start.12 = (f32[16,128]{1,0:T(8,128)S(1)}, f32[16,128]{1,0:T(8,128)S(1)}, u32[]{:S(2)}, u32[]{:S(2)}) collective-permute-start(f32[16,128]{1,0:T(8,128)S(1)} %get-tuple-element.38), channel_id=1, source_target_pairs={{0,11},{1,8},{2,9},{3,10},{4,15},{5,12},{6,13},{7,14},{8,3},{9,0},... | collective-permute-start | bytes 24584 | tf_op jit(solution)/shard_map/ppermute | solution.py:597
  45.1 1.4 %collective-permute-done.13.refs_0_ = f32[128,128]{1,0:T(8,128)S(1)} collective-permute-done((f32[128,128]{1,0:T(8,128)S(1)}, f32[128,128]{1,0:T(8,128)S(1)}, u32[]{:S(2)}, u32[]{:S(2)}) %collective-permute-start.13) | collective-permute-done | bytes 65568 | tf_op jit(solution)/shard_map/ppermute | solution.py:675
  46.5 3.1 %collective-permute-done.10.refs_5_ = f32[16,128]{1,0:T(8,128)S(1)} collective-permute-done((f32[16,128]{1,0:T(8,128)S(1)}, f32[16,128]{1,0:T(8,128)S(1)}, u32[]{:S(2)}, u32[]{:S(2)}) %collective-permute-start.10) | collective-permute-done | bytes 8224 | tf_op jit(solution)/shard_map/ppermute | solution.py:597
  49.6 1.2 %collective-permute-done.8.refs_2_ = f32[296,128]{1,0:T(8,128)S(1)} collective-permute-done((f32[296,128]{1,0:T(8,128)S(1)}, f32[296,128]{1,0:T(8,128)S(1)}, u32[]{:S(2)}, u32[]{:S(2)}) %collective-permute-start.8) | collective-permute-done | bytes 151584 | tf_op jit(solution)/shard_map/ppermute | solution.py:597
  50.8 1.1 %shard_map.119 = (f32[5,128,128]{2,1,0:T(8,128)S(1)}, f32[5,128,128]{2,1,0:T(8,128)S(1)}, f32[40,128]{1,0:T(8,128)S(1)}, f32[48,128]{1,0:T(8,128)S(1)}, f32[2,128,128]{2,1,0:T(8,128)S(1)}) custom-call(f32[5,128,128]{2,1,0:T(8,128)S(1)} %get-tuple-element.31.source.refs_0_, f32[296,128]{1,0:T(8,128)S(1)} %get-tuple-element.35.refs_1_, ...), custom_call_target="tpu_custom_call" | custom-call | flops 1048576 | bytes 1662976 | tf_op jit(solution)/shard_map/pallas_call | solution.py:30
  51.9 1.0 %collective-permute-start.16 = (f32[2,128,128]{2,1,0:T(8,128)S(1)}, f32[2,128,128]{2,1,0:T(8,128)S(1)}, u32[]{:S(2)}, u32[]{:S(2)}) collective-permute-start(f32[2,128,128]{2,1,0:T(8,128)S(1)} %get-tuple-element.44), channel_id=1, source_target_pairs={{0,12},{4,0},{8,4},{12,8},{1,13},{5,1},{9,5},{13,9},{2,14},{6,2},{... | collective-permute-start | bytes 393224 | tf_op jit(solution)/shard_map/ppermute | solution.py:587
  53.7 1.5 %collective-permute-start.18 = (f32[40,128]{1,0:T(8,128)S(1)}, f32[40,128]{1,0:T(8,128)S(1)}, u32[]{:S(2)}, u32[]{:S(2)}) collective-permute-start(f32[40,128]{1,0:T(8,128)S(1)} %get-tuple-element.45.refs_0_), channel_id=1, source_target_pairs={{0,2},{1,3},{2,0},{3,1},{4,6},{5,7},{6,4},{7,5},{8,10},{9,11},{10,... | collective-permute-start | bytes 61448 | tf_op jit(solution)/shard_map/ppermute | solution.py:587
  55.7 1.5 %shard_map.120 = (f32[5,128,128]{2,1,0:T(8,128)S(1)}, f32[5,128,128]{2,1,0:T(8,128)S(1)}) custom-call(f32[5,128,128]{2,1,0:T(8,128)S(1)} %get-tuple-element.39.precond, f32[5,128,128]{2,1,0:T(8,128)S(1)} %get-tuple-element.40.image, f32[128,128]{1,0:T(8,128)S(1)} %copy-done.4, f32[128,128]{1,0:T(8,128)S(1)} %copy-done.4), custom_call_target="tpu_custom_call" | custom-call | flops 1048576 | bytes 1310720 | tf_op jit(solution)/shard_map/pallas_call | solution.py:30
  58.4 1.3 %shard_map.123 = (f32[3,4,128,128]{3,2,1,0:T(8,128)}, f32[4,128,128]{2,1,0:T(8,128)}, f32[4,128,128]{2,1,0:T(8,128)}) custom-call(f32[3,4,128,128]{3,2,1,0:T(8,128)S(1)} %get-tuple-element.29.star, f32[5,128,128]{2,1,0:T(8,128)S(1)} %get-tuple-element.41.precond, f32[5,128,128]{2,1,0:T(8,128)S(1)} %get-tuple-element.42.image, ...), custom_call_target="tpu_custom_call" | custom-call | flops 1048576 | bytes 2621440 | tf_op jit(solution)/shard_map/pallas_call | solution.py:30
  (51 shorter events, 8.3 us)
Async XLA Ops:
  2.7 6.6 %copy-start.3 = (f32[4,128,128]{2,1,0:T(8,128)S(1)}, f32[4,128,128]{2,1,0:T(8,128)}, u32[]{:S(2)}) copy-start(f32[4,128,128]{2,1,0:T(8,128)} %thermal.7) | copy-start | bytes 786436
  2.7 6.7 %copy-start.1 = (f32[3,4,128,128]{3,2,1,0:T(8,128)S(1)}, f32[3,4,128,128]{3,2,1,0:T(8,128)}, u32[]{:S(2)}) copy-start(f32[3,4,128,128]{3,2,1,0:T(8,128)} %flow.7) | copy-start | bytes 2359300
  2.7 7.5 %copy-start.7 = (f32[128,128]{1,0:T(8,128)S(1)}, f32[128,128]{1,0:T(8,128)}, u32[]{:S(2)}) copy-start(f32[128,128]{1,0:T(8,128)} %constant.10.clone.diagonal) | copy-start | bytes 196612
  2.7 23.9 %copy-start.6 = (s32[4,128,128]{2,1,0:T(8,128)S(1)}, s32[4,128,128]{2,1,0:T(8,128)}, u32[]{:S(2)}) copy-start(s32[4,128,128]{2,1,0:T(8,128)} %flag.1) | copy-start | bytes 786436
  4.2 15.2 %collective-permute-start = (f32[776,128]{1,0:T(8,128)S(1)}, f32[776,128]{1,0:T(8,128)S(1)}, u32[]{:S(2)}, u32[]{:S(2)}) collective-permute-start(f32[776,128]{1,0:T(8,128)S(1)} %get-tuple-element.26), channel_id=1, source_target_pairs={{0,4},{4,8},{8,12},{12,0},{1,5},{5,9},{9,13},{13,1},{2,6},{6,10},{... | collective-permute-start | bytes 1191944 | tf_op jit(solution)/shard_map/ppermute | solution.py:587
  7.3 19.4 %collective-permute-start.1 = (f32[776,128]{1,0:T(8,128)S(1)}, f32[776,128]{1,0:T(8,128)S(1)}, u32[]{:S(2)}, u32[]{:S(2)}) collective-permute-start(f32[776,128]{1,0:T(8,128)S(1)} %get-tuple-element.27), channel_id=1, source_target_pairs={{0,12},{4,0},{8,4},{12,8},{1,13},{5,1},{9,5},{13,9},{2,14},{6,2},{... | collective-permute-start | bytes 1191944 | tf_op jit(solution)/shard_map/ppermute | solution.py:587
  9.4 21.8 %collective-permute-start.6 = (f32[2,128,128]{2,1,0:T(8,128)S(1)}, f32[2,128,128]{2,1,0:T(8,128)S(1)}, u32[]{:S(2)}, u32[]{:S(2)}) collective-permute-start(f32[2,128,128]{2,1,0:T(8,128)S(1)} %slice.11), channel_id=1, source_target_pairs={{0,4},{4,8},{8,12},{12,0},{1,5},{5,9},{9,13},{13,1},{2,6},{6,10},{... | collective-permute-start | bytes 393224 | tf_op jit(solution)/shard_map/ppermute | solution.py:587
  9.5 2.1 %collective-permute-start.3 = (f32[4,4,2,128]{3,2,1,0:T(2,128)S(1)}, f32[4,4,2,128]{3,2,1,0:T(2,128)S(1)}, u32[]{:S(2)}, u32[]{:S(2)}) collective-permute-start(f32[4,4,2,128]{3,2,1,0:T(2,128)S(1)} %get-tuple-element.49), channel_id=1, source_target_pairs={{0,3},{1,0},{2,1},{3,2},{4,7},{5,4},{6,5},{7,6},{8,11},{9,8},{10,9... | collective-permute-start | bytes 49160 | tf_op jit(solution)/shard_map/ppermute | solution.py:587
  10.2 3.2 %collective-permute-start.2 = (f32[4,4,2,128]{3,2,1,0:T(2,128)S(1)}, f32[4,4,2,128]{3,2,1,0:T(2,128)S(1)}, u32[]{:S(2)}, u32[]{:S(2)}) collective-permute-start(f32[4,4,2,128]{3,2,1,0:T(2,128)S(1)} %get-tuple-element.50), channel_id=1, source_target_pairs={{0,1},{1,2},{2,3},{3,0},{4,5},{5,6},{6,7},{7,4},{8,9},{9,10},{10,1... | collective-permute-start | bytes 49160 | tf_op jit(solution)/shard_map/ppermute | solution.py:587
  29.4 9.4 %collective-permute-start.4 = (f32[256,128]{1,0:T(8,128)S(1)}, f32[256,128]{1,0:T(8,128)S(1)}, u32[]{:S(2)}, u32[]{:S(2)}) collective-permute-start(f32[256,128]{1,0:T(8,128)S(1)} %get-tuple-element.32.message), channel_id=1, source_target_pairs={{0,4},{1,5},{2,6},{3,7},{4,0},{5,1},{6,2},{7,3},{8,12},{9,13},{10,... | collective-permute-start | bytes 393224 | tf_op jit(solution)/shard_map/ppermute | solution.py:597
  31.1 3.0 %collective-permute-start.5 = (f32[4,128]{1,0:T(4,128)S(1)}, f32[4,128]{1,0:T(4,128)S(1)}, u32[]{:S(2)}, u32[]{:S(2)}) collective-permute-start(f32[4,128]{1,0:T(4,128)S(1)} %get-tuple-element.34), channel_id=1, source_target_pairs={{0,1},{1,2},{2,3},{3,0},{4,5},{5,6},{6,7},{7,4},{8,9},{9,10},{10,1... | collective-permute-start | bytes 6152 | tf_op jit(solution)/shard_map/ppermute | solution.py:587
  34.9 3.9 %collective-permute-start.7 = (f32[56,128]{1,0:T(8,128)S(1)}, f32[56,128]{1,0:T(8,128)S(1)}, u32[]{:S(2)}, u32[]{:S(2)}) collective-permute-start(f32[56,128]{1,0:T(8,128)S(1)} %shard_map.116.faces), channel_id=1, source_target_pairs={{0,4},{1,5},{2,6},{3,7},{4,0},{5,1},{6,2},{7,3},{8,12},{9,13},{10,... | collective-permute-start | bytes 86024 | tf_op jit(solution)/shard_map/ppermute | solution.py:597
  35.3 5.8 %collective-permute-start.15 = (f32[128,128]{1,0:T(8,128)S(1)}, f32[128,128]{1,0:T(8,128)S(1)}, u32[]{:S(2)}, u32[]{:S(2)}) collective-permute-start(f32[128,128]{1,0:T(8,128)S(1)} %get-tuple-element.33.wrap.side), channel_id=1, source_target_pairs={{12,8},{13,9},{14,10},{15,11},{28,24},{29,25},{30,26},{31,27}} | collective-permute-start | bytes 196616 | tf_op jit(solution)/shard_map/ppermute | solution.py:675
  35.9 7.3 %collective-permute-start.14 = (f32[128,128]{1,0:T(8,128)S(1)}, f32[128,128]{1,0:T(8,128)S(1)}, u32[]{:S(2)}, u32[]{:S(2)}) collective-permute-start(f32[128,128]{1,0:T(8,128)S(1)} %get-tuple-element.33.wrap.side), channel_id=1, source_target_pairs={{12,4},{13,5},{14,6},{15,7},{28,20},{29,21},{30,22},{31,23}} | collective-permute-start | bytes 196616 | tf_op jit(solution)/shard_map/ppermute | solution.py:675
  36.6 9.8 %collective-permute-start.13 = (f32[128,128]{1,0:T(8,128)S(1)}, f32[128,128]{1,0:T(8,128)S(1)}, u32[]{:S(2)}, u32[]{:S(2)}) collective-permute-start(f32[128,128]{1,0:T(8,128)S(1)} %get-tuple-element.33.wrap.side), channel_id=1, source_target_pairs={{12,0},{13,1},{14,2},{15,3},{28,16},{29,17},{30,18},{31,19}} | collective-permute-start | bytes 196616 | tf_op jit(solution)/shard_map/ppermute | solution.py:675
  39.0 11.8 %collective-permute-start.8 = (f32[296,128]{1,0:T(8,128)S(1)}, f32[296,128]{1,0:T(8,128)S(1)}, u32[]{:S(2)}, u32[]{:S(2)}) collective-permute-start(f32[296,128]{1,0:T(8,128)S(1)} %get-tuple-element.35.refs_1_), channel_id=1, source_target_pairs={{0,8},{1,9},{2,10},{3,11},{4,12},{5,13},{6,14},{7,15},{8,0},{9,1},... | collective-permute-start | bytes 454664 | tf_op jit(solution)/shard_map/ppermute | solution.py:597
  41.1 8.4 %collective-permute-start.10 = (f32[16,128]{1,0:T(8,128)S(1)}, f32[16,128]{1,0:T(8,128)S(1)}, u32[]{:S(2)}, u32[]{:S(2)}) collective-permute-start(f32[16,128]{1,0:T(8,128)S(1)} %get-tuple-element.37), channel_id=1, source_target_pairs={{0,9},{1,10},{2,11},{3,8},{4,13},{5,14},{6,15},{7,12},{8,1},{9,2},... | collective-permute-start | bytes 24584 | tf_op jit(solution)/shard_map/ppermute | solution.py:597
  41.1 8.4 %collective-permute-start.9 = (f32[16,128]{1,0:T(8,128)S(1)}, f32[16,128]{1,0:T(8,128)S(1)}, u32[]{:S(2)}, u32[]{:S(2)}) collective-permute-start(f32[16,128]{1,0:T(8,128)S(1)} %get-tuple-element.37), channel_id=1, source_target_pairs={{0,1},{1,2},{2,3},{3,0},{4,5},{5,6},{6,7},{7,4},{8,9},{9,10},{10,1... | collective-permute-start | bytes 24584 | tf_op jit(solution)/shard_map/ppermute | solution.py:597
  43.2 6.3 %collective-permute-start.12 = (f32[16,128]{1,0:T(8,128)S(1)}, f32[16,128]{1,0:T(8,128)S(1)}, u32[]{:S(2)}, u32[]{:S(2)}) collective-permute-start(f32[16,128]{1,0:T(8,128)S(1)} %get-tuple-element.38), channel_id=1, source_target_pairs={{0,11},{1,8},{2,9},{3,10},{4,15},{5,12},{6,13},{7,14},{8,3},{9,0},... | collective-permute-start | bytes 24584 | tf_op jit(solution)/shard_map/ppermute | solution.py:597
  46.4 3.1 %collective-permute-start.11 = (f32[16,128]{1,0:T(8,128)S(1)}, f32[16,128]{1,0:T(8,128)S(1)}, u32[]{:S(2)}, u32[]{:S(2)}) collective-permute-start(f32[16,128]{1,0:T(8,128)S(1)} %get-tuple-element.38), channel_id=1, source_target_pairs={{0,3},{1,0},{2,1},{3,2},{4,7},{5,4},{6,5},{7,6},{8,11},{9,8},{10,9... | collective-permute-start | bytes 24584 | tf_op jit(solution)/shard_map/ppermute | solution.py:597
  51.9 5.9 %collective-permute-start.16 = (f32[2,128,128]{2,1,0:T(8,128)S(1)}, f32[2,128,128]{2,1,0:T(8,128)S(1)}, u32[]{:S(2)}, u32[]{:S(2)}) collective-permute-start(f32[2,128,128]{2,1,0:T(8,128)S(1)} %get-tuple-element.44), channel_id=1, source_target_pairs={{0,12},{4,0},{8,4},{12,8},{1,13},{5,1},{9,5},{13,9},{2,14},{6,2},{... | collective-permute-start | bytes 393224 | tf_op jit(solution)/shard_map/ppermute | solution.py:587
  52.9 5.4 %collective-permute-start.19 = (f32[40,128]{1,0:T(8,128)S(1)}, f32[40,128]{1,0:T(8,128)S(1)}, u32[]{:S(2)}, u32[]{:S(2)}) collective-permute-start(f32[40,128]{1,0:T(8,128)S(1)} %get-tuple-element.45.refs_0_), channel_id=1, source_target_pairs={{0,3},{1,0},{2,1},{3,2},{4,7},{5,4},{6,5},{7,6},{8,11},{9,8},{10,9... | collective-permute-start | bytes 61448 | tf_op jit(solution)/shard_map/ppermute | solution.py:587
  53.7 4.6 %collective-permute-start.18 = (f32[40,128]{1,0:T(8,128)S(1)}, f32[40,128]{1,0:T(8,128)S(1)}, u32[]{:S(2)}, u32[]{:S(2)}) collective-permute-start(f32[40,128]{1,0:T(8,128)S(1)} %get-tuple-element.45.refs_0_), channel_id=1, source_target_pairs={{0,2},{1,3},{2,0},{3,1},{4,6},{5,7},{6,4},{7,5},{8,10},{9,11},{10,... | collective-permute-start | bytes 61448 | tf_op jit(solution)/shard_map/ppermute | solution.py:587
  55.2 3.2 %collective-permute-start.17 = (f32[40,128]{1,0:T(8,128)S(1)}, f32[40,128]{1,0:T(8,128)S(1)}, u32[]{:S(2)}, u32[]{:S(2)}) collective-permute-start(f32[40,128]{1,0:T(8,128)S(1)} %get-tuple-element.45.refs_0_), channel_id=1, source_target_pairs={{0,1},{1,2},{2,3},{3,0},{4,5},{5,6},{6,7},{7,4},{8,9},{9,10},{10,1... | collective-permute-start | bytes 61448 | tf_op jit(solution)/shard_map/ppermute | solution.py:587
  (6 other events, 18.5 us)

commit v6 on v5

--- a/solution.py
+++ b/solution.py
@@ -22,7 +22,7 @@
 SMEM = pl.BlockSpec(memory_space=pltpu.SMEM)
 
 
-def call(body, operands, shapes, scratch=(), scalars=0, flops=1 << 20):
+def call(body, operands, shapes, scratch=(), scalars=0, loose=0, flops=1 << 20):
     out_shape = [jax.ShapeDtypeStruct(shape, F32) for shape in shapes]
     moved = 4 * sum(math.prod(shape) for shape in shapes)
     held = moved + 4 * sum(operand.size for operand in operands)
@@ -30,7 +30,9 @@
     return pl.pallas_call(
         body,
         out_shape=out_shape,
-        in_specs=[SMEM] * scalars + [VMEM] * (len(operands) - scalars),
+        in_specs=[SMEM] * scalars
+        + [VMEM] * (len(operands) - scalars - loose)
+        + [pl.BlockSpec(memory_space=pl.ANY)] * loose,
         out_specs=[VMEM] * len(shapes),
         scratch_shapes=list(scratch),
         compiler_params=pltpu.CompilerParams(vmem_limit_bytes=held + (4 << 20)),
@@ -111,7 +113,6 @@
     flow, low_x, high_x, thermal, flag = refs
     _, layers, rows, depth = flow.shape
     span = pl.ds(start, count)
-    surface = 6 * rows
     speed = [flow[part, index, span, :] for part in range(3)]
     drag = 1.0 / (1.0 + TIME_INCREMENT * DRAG_RATE * flag[index, span, :].astype(F32))
     top = lax.broadcasted_iota(jnp.int32, (count, depth), 1) == depth - 1
@@ -130,7 +131,7 @@
                 around.append(flow[part, other, span, :])
         moved = advance(around, padded, part, speed, start)
         if part == 0:
-            edge = lambda halo: column(halo[pl.ds(surface, 1), pl.ds(0, rows)])
+            edge = lambda halo: column(halo[pl.ds(halo.shape[0] - 8, 1), pl.ds(0, rows)])
             behind = thermal[index - 1] if index > 0 else edge(low_x)
             before = thermal[index + 1] if index + 1 < layers else edge(high_x)
             moved = moved + jnp.where(top, pull * (before - behind), 0.0)
@@ -144,12 +145,15 @@
 def pad_layer(refs, low_y, high_y, padded, index):
     flow, _, _, thermal, _ = refs
     for part in range(3):
-        pad_rows(padded, part, low_y[part, index], flow[part, index], high_y[part, index])
-    pad_rows(padded, 3, low_y[3, index], thermal[index], high_y[3, index])
+        pad_rows(
+            padded, part, low_y[part, index, 6:], flow[part, index], high_y[part, index, :2]
+        )
+    pad_rows(padded, 3, low_y[3, index, 6:], thermal[index], high_y[3, index, :2])
 
 
 def march_kernel(
-    flow, low_x, high_x, thermal, flag, low_y, high_y, weight, star, side_y, padded
+    flow, low_x, high_x, thermal, flag, low_y, high_y, extra, weight,
+    star, side_x, side_y, padded,
 ):
     refs = (flow, low_x, high_x, thermal, flag)
     _, layers, rows, depth = flow.shape
@@ -159,61 +163,96 @@
         for part in range(3):
             star[part, index] = value[part]
         side_y[pl.ds(index, 1), :] = value[1][rows - 1 :, :]
-
-
-def transform_kernel(group, length, star, table_y, table_z, ratio, source, message, side, rows_):
+    plane = lambda index: low_x[pl.ds(index * rows, rows), pl.ds(0, depth)]
+    beside = extra[pl.ds(2 * rows, 8), pl.ds(0, depth)]
+    pad_rows(padded, 0, beside[2:4], plane(1), beside[4:6])
+    around = [extra[pl.ds(0, rows), pl.ds(0, depth)], plane(0), plane(1), flow[0, 0], flow[0, 1]]
+    moved = advance(around, padded, 0, [plane(1), plane(3), plane(5)])
+    top = lax.broadcasted_iota(jnp.int32, (rows, depth), 1) == depth - 1
+    pull = -MARANGONI * 0.5 * TIME_INCREMENT
+    behind = column(extra[pl.ds(2 * rows, 1), pl.ds(0, rows)])
+    moved = moved + jnp.where(top, pull * (thermal[0] - behind), 0.0)
+    drag = 1.0 + TIME_INCREMENT * DRAG_RATE * extra[pl.ds(rows, rows), pl.ds(0, depth)]
+    side_x[...] = moved / drag
+
+
+def transform_kernel(
+    group, length, star, side_x, table_y, table_z, ratio, source, message, rows_
+):
     _, layers, rows, depth = star.shape
     first = position(group) * layers
-    inner = jnp.where(first + layers == length, 0.0, 1.0)
     rows_[pl.ds(0, 8), :] = jnp.zeros((8, depth), F32)
     for index in range(layers):
         rows_[pl.ds(8, rows), :] = star[1, index]
-        sink = star[0, index]
-        if index > 0:
-            sink = sink - star[0, index - 1]
+        behind = star[0, index - 1] if index > 0 else side_x[...]
+        sink = star[0, index] - behind
         sink = sink + (star[1, index] - rows_[pl.ds(7, rows), :])
         sink = sink + (star[2, index] - lane_shift(star[2, index], -1))
         source[index] = dot(dot(table_y[...], -sink), table_z[...])
-    onward = dot(dot(table_y[...], star[0, layers - 1]), table_z[...])
-    side[...] = onward
-    onward = inner * onward
-    source[layers] = onward
     forward = source[0]
     for index in range(1, layers):
         forward = source[index] + ratio[first + index] * forward
-    message[pl.ds(0, rows), :] = forward + onward / ratio[first + layers]
-    backward = onward
-    for index in range(layers - 1, -1, -1):
+    message[pl.ds(0, rows), :] = forward
+    backward = source[layers - 1]
+    for index in range(layers - 2, -1, -1):
         backward = source[index] + ratio[length - 1 - first - index] * backward
     message[pl.ds(rows, rows), :] = backward
 
 
-def pack_kernel(flow, thermal, ahead, behind, planes, sems):
+def started(copies):
+    for copy in copies:
+        copy.start()
+    return copies
+
+
+def surface(plane):
+    rows, depth = plane.shape
+    shape = (rows, rows)
+    same = lax.broadcasted_iota(jnp.int32, shape, 0) == lax.broadcasted_iota(jnp.int32, shape, 1)
+    return jnp.sum(jnp.where(same, plane[:, depth - 1 :], 0.0), axis=0, keepdims=True)
+
+
+def halo_kernel(flow, thermal, ahead, behind, last_rows, first_rows, tops, sems):
     parts, layers, rows, depth = flow.shape
-    copies = []
+    pairs = [(thermal.at[layers - 1], tops.at[0]), (thermal.at[0], tops.at[1])]
+    for part in range(parts + 1):
+        for layer in range(layers):
+            source = thermal.at[layer] if part == parts else flow.at[part, layer]
+            pairs.append((source.at[pl.ds(rows - 8, 8), :], last_rows.at[part, layer]))
+            pairs.append((source.at[pl.ds(0, 8), :], first_rows.at[part, layer]))
     for part in range(parts):
         for layer in range(2):
-            for target, source in ((ahead, layers - 2 + layer), (behind, layer)):
-                copies.append(
-                    (flow.at[part, source], target.at[pl.ds((2 * part + layer) * rows, rows), :])
-                )
-    copies.append((thermal.at[layers - 1], planes.at[0]))
-    copies.append((thermal.at[0], planes.at[1]))
-    copies = [
-        pltpu.make_async_copy(source, target, sems.at[index])
-        for index, (source, target) in enumerate(copies)
-    ]
-    for copy in copies:
-        copy.start()
-    shape = (rows, rows)
-    same = lax.broadcasted_iota(jnp.int32, shape, 0) == lax.broadcasted_iota(jnp.int32, shape, 1)
-    for copy in copies[-2:]:
+            span = pl.ds((2 * part + layer) * rows, rows)
+            pairs.append((flow.at[part, layers - 2 + layer], ahead.at[span, :]))
+            pairs.append((flow.at[part, layer], behind.at[span, :]))
+    copies = started(
+        [pltpu.make_async_copy(*pair, sems.at[index]) for index, pair in enumerate(pairs)]
+    )
+    for side, message in enumerate((ahead, behind)):
+        copies[side].wait()
+        row = jnp.broadcast_to(surface(tops[side]), (8, rows))
+        message[pl.ds(2 * parts * rows, 8), pl.ds(0, rows)] = row
+    for copy in copies[2:]:
         copy.wait()
-    for side, target in enumerate((ahead, behind)):
-        tops = planes[side][:, depth - 1 :]
-        row = jnp.sum(jnp.where(same, tops, 0.0), axis=0, keepdims=True)
-        target[pl.ds(2 * parts * rows, 8), pl.ds(0, rows)] = jnp.broadcast_to(row, (8, rows))
-    for copy in copies[:-2]:
+
+
+def extra_kernel(flow, thermal, flag, low_y, high_y, extra, last, first, flags, sems):
+    _, layers, rows, depth = flow.shape
+    pairs = [(flag.at[layers - 1], flags), (thermal.at[pl.ds(layers - 2, 2)], last)]
+    pairs.append((thermal.at[pl.ds(0, 2)], first))
+    pairs.append((flow.at[0, layers - 3], extra.at[pl.ds(0, rows), :]))
+    copies = started(
+        [pltpu.make_async_copy(*pair, sems.at[index]) for index, pair in enumerate(pairs)]
+    )
+    base = 2 * rows
+    extra[pl.ds(base, 8), :] = jnp.zeros((8, extra.shape[1]), F32)
+    extra[pl.ds(base + 2, 2), pl.ds(0, depth)] = low_y[0, layers - 1, 6:, :]
+    extra[pl.ds(base + 4, 2), pl.ds(0, depth)] = high_y[0, layers - 1, :2, :]
+    for copy in copies[:2]:
+        copy.wait()
+    extra[pl.ds(rows, rows), :] = flags[...].astype(F32)
+    extra[pl.ds(base, 1), pl.ds(0, rows)] = surface(last[0])
+    for copy in copies[2:]:
         copy.wait()
 
 
@@ -238,23 +277,24 @@
     return LASER_POWER * heat
 
 
-def heat_kernel(span, spots_a, spots_b, thermal, halo, low_y, high_y, flow, warmed, padded):
+def heat_kernel(
+    spots_a, spots_b, thermal, low_x, high_x, low_y, high_y, flow, warmed, padded
+):
     layers, rows, depth = thermal.shape
     top = lax.broadcasted_iota(jnp.int32, (rows, depth), 1) == depth - 1
-    for index in span:
-        pad_rows(padded, 0, low_y[3, index], thermal[index], high_y[3, index])
+    for index in range(layers):
+        pad_rows(padded, 0, low_y[3, index, 6:], thermal[index], high_y[3, index, :2])
         around = []
         for other in range(index - 2, index + 3):
             if other < 0:
-                around.append(halo[other + 2])
+                around.append(low_x[other + 2])
             elif other >= layers:
-                around.append(halo[other - layers])
+                around.append(high_x[other - layers])
             else:
                 around.append(thermal[other])
         speed = [flow[part, index] for part in range(3)]
         gain = TIME_INCREMENT * column(laser_row(index, layers, rows, spots_a, spots_b))
-        moved = advance(around, padded, 0, speed) + jnp.where(top, gain, 0.0)
-        warmed[index - span[0]] = moved
+        warmed[index] = advance(around, padded, 0, speed) + jnp.where(top, gain, 0.0)
 
 
 def tables_kernel(group, layers, diagonal, ratio, weight):
@@ -304,14 +344,12 @@
 
 
 def faces_kernel(
-    group, length, alone, source, wrap, before_y, table_z, ratio, weight, edge, early,
-    faces, sweep,
+    group, length, source, before_y, table_z, ratio, weight, edge, *refs
 ):
-    layers, rows, depth = source.shape[0] - 1, *source.shape[1:]
-    mine = position(group)
-    first = mine * layers
+    faces, sweep = refs[-2:]
+    layers, rows, depth = source.shape
+    first = position(group) * layers
     zero = jnp.zeros((rows, depth), F32)
-    keep = jnp.where(mine == (group - 1 if alone else 0), 1.0, 0.0)
     extra = dot(before_y[...], table_z[...])
     faces[...] = jnp.zeros(faces.shape, F32)
     for index in range(layers):
@@ -320,23 +358,17 @@
     for index in range(layers):
         forward = source[index] + ratio[first + index] * forward
         sweep[index] = forward
-    value = weight[weight.shape[0] - 1] * (source[layers] + ratio[first + layers] * forward)
-    energy = source[layers] * value
+    value = weight[weight.shape[0] - 1] * (ratio[first + layers] * forward)
+    energy = zero
     for index in range(layers - 1, -1, -1):
         value = ratio[first + index + 1] * (sweep[index] + value)
         energy = energy + source[index] * value
     faces[pl.ds(3 * length, 8), :] = jnp.broadcast_to(total(energy), (8, depth))
 
-    def own(index):
-        value = source[jnp.clip(index - first, 0, layers)]
-        inside = (index >= first) & (index <= first + layers)
-        value = jnp.where(inside, value, 0.0) + edge[0] * faces[pl.ds(2 * length + index, 1), :]
-        if isinstance(index, int):
-            return value + keep * wrap[...] if index == 0 else value
-        return value + jnp.where(index == 0, keep * wrap[...], 0.0)
-
     def down(index, previous):
-        current = own(index) + ratio[index] * previous
+        inside = (index >= first) & (index < first + layers)
+        own = jnp.where(inside, source[jnp.clip(index - first, 0, layers - 1)], 0.0)
+        current = own + edge[0] * faces[pl.ds(2 * length + index, 1), :] + ratio[index] * previous
         sweep[index] = current
         return current
 
@@ -371,7 +403,7 @@
 
 
 def merge_kernel(
-    turn, group, length, message, other, faces, other_faces, sums, weight,
+    turn, group, length, message, other, faces, other_faces, sums, weight, _,
     new_message, new_sums, head, tail,
 ):
     rows, depth = weight.shape[1:]
@@ -390,17 +422,13 @@
     new_message[pl.ds(2 * rows + 2 * length, 8), :] = energy
 
 
-def late_solve(length, message, other, wrap, ratio, edge, late, sweep):
-    rows, depth = wrap.shape
+def late_solve(length, message, other, ratio, edge, late, sweep):
+    rows, depth = edge.shape[1:]
     own = pl.ds(2 * rows + length, length)
     late[pl.ds(0, length), :] = message[own, :] + other[own, :]
 
     def down(index, previous):
         current = edge[0] * late[pl.ds(index, 1), :] + ratio[index] * previous
-        if isinstance(index, int):
-            current = current + wrap if index == 0 else current
-        else:
-            current = current + jnp.where(index == 0, wrap, 0.0)
         sweep[index] = current
         return current
 
@@ -418,39 +446,27 @@
     sweep[length] = zero
 
 
-def wrap_kernel(group, alone, side, *refs):
-    wraps, wrap = refs[:-1], refs[-1]
-    here = position(group) == group - 1
-    value = jnp.where(here, side[...], 0.0) if alone else jnp.zeros(side.shape, F32)
-    for part in wraps:
-        value = value + part[...]
-    wrap[...] = value
-
-
 def close_kernel(
-    turn, group, length, message, other, sums, weight, ratio, edge, wrap, ends, late, sweep
+    turn, group, length, message, other, sums, weight, ratio, edge, ends, late, sweep
 ):
     forward, backward, _, _, _ = joined(turn, group, message, other, sums, weight)
-    late_solve(length, message, other, wrap[...], ratio, edge, late, sweep)
+    late_solve(length, message, other, ratio, edge, late, sweep)
     ends[0] = ratio[length] * forward + sweep[length - 1]
     ends[1] = ratio[length] * backward + sweep[0]
 
 
 def coarse_kernel(
-    turn, group, length, source, message, other, sums, faces_in, weight, ratio, edge, thermal,
-    wrap, *refs
+    turn, group, length, alone, source, message, other, sums, faces_in, weight, ratio, edge, *refs
 ):
-    layers, rows, depth = source.shape[0] - 1, *source.shape[1:]
-    outer, (precond, image, report, faces, after_heat, late, sweep, ends) = refs[:-8], refs[-8:]
-    after_heat[...] = thermal[:2]
+    precond, image, report, faces, late, sweep, ends = refs[-7:]
+    layers, rows, depth = source.shape
     first = position(group) * layers
-    wrap = wrap[...]
     below, below_far, above, above_far = faces_in
     forward, backward, before, after, energy = joined(turn, group, message, other, sums, weight)
-    late_solve(length, message, other, wrap, ratio, edge, late, sweep)
+    late_solve(length, message, other, ratio, edge, late, sweep)
     ends[0] = ratio[length] * forward + sweep[length - 1]
     ends[1] = ratio[length] * backward + sweep[0]
-    beyond = outer[0] if outer else ends
+    beyond = ends if alone else refs[0]
     own = pl.ds(2 * rows, length)
     faces[pl.ds(0, length), :] = message[own, :] + other[own, :]
     faces[pl.ds(length, length), :] = below[...] + below_far[...]
@@ -461,13 +477,11 @@
     energy = energy + total(
         late_rows * (2.0 * faces[pl.ds(0, length), :] - late[pl.ds(length, length), :])
     )
-    energy = energy + total(wrap * (2.0 * ratio[length] * backward + sweep[0]))
     forward = before
     for index in range(layers):
         forward = source[index] + ratio[first + index] * forward
         precond[index] = forward
-    lone = weight[weight.shape[0] - 1]
-    value = lone * (after + source[layers] + ratio[first + layers] * forward)
+    value = weight[weight.shape[0] - 1] * (after + ratio[first + layers] * forward)
     is_last = first + layers == length
     precond[layers] = jnp.where(is_last, beyond[1], value + sweep[first + layers])
     for index in range(layers - 1, -1, -1):
@@ -534,11 +548,9 @@
 
 
 def project_kernel(
-    group, length, paired, star, precond, image, faces, table_z, warm_low, warm_high, *refs
+    group, length, paired, star, precond, image, faces, table_z, *refs
 ):
-    reports, (flow, pressure, warmed, field, rows_) = refs[:-5], refs[-5:]
-    warmed[:2] = warm_low[...]
-    warmed[2:] = warm_high[...]
+    reports, (flow, pressure, field, rows_) = refs[:-4], refs[-4:]
     _, layers, rows, depth = star.shape
     first = position(group) * layers
     where = 2 * length
@@ -597,20 +609,16 @@
     return lax.ppermute(array, ("gx", "gy"), pairs)
 
 
-def pack(melt_flow, thermal_state):
-    parts, layers, rows, depth = melt_flow.shape
-    shape = jax.ShapeDtypeStruct((2 * parts * rows + 8, max(rows, depth)), F32)
+def pack(body, inputs, received, shapes, scratch, count):
+    inputs = [pltpu.with_memory_space_constraint(each, pltpu.HBM) for each in inputs]
     return pl.pallas_call(
-        pack_kernel,
-        out_shape=[shape, shape],
-        in_specs=[pl.BlockSpec(memory_space=pltpu.HBM)] * 2,
-        out_specs=[VMEM, VMEM],
-        scratch_shapes=[
-            pltpu.VMEM((2, rows, depth), F32),
-            pltpu.SemaphoreType.DMA((4 * parts + 2,)),
-        ],
+        body,
+        out_shape=[jax.ShapeDtypeStruct(shape, F32) for shape in shapes],
+        in_specs=[pl.BlockSpec(memory_space=pltpu.HBM)] * len(inputs) + [VMEM] * len(received),
+        out_specs=[VMEM] * len(shapes),
+        scratch_shapes=[scratch, pltpu.SemaphoreType.DMA((count,))],
         compiler_params=pltpu.CompilerParams(vmem_limit_bytes=4 << 20),
-    )(melt_flow, thermal_state)
+    )(*inputs, *received)
 
 
 def per_device(melt_flow, thermal_state, powder_flag, spot_lateral_a_cell, spot_lateral_b_cell):
@@ -631,50 +639,69 @@
     plane = (rows, depth)
     line = (length, depth)
 
-    ahead, behind = pack(melt_flow, thermal_state)
+    parts = melt_flow.shape[0]
+    width = max(rows, depth)
+    outer_planes = (2 * parts * rows + 8, width)
+    ahead, behind, last_rows, first_rows = pack(
+        halo_kernel,
+        [melt_flow, thermal_state],
+        [],
+        [outer_planes, outer_planes] + [(parts + 1, layers, 8, depth)] * 2,
+        pltpu.VMEM((2,) + plane, F32),
+        2 + 2 * layers * (parts + 1) + 4 * parts,
+    )
     low_x = along(ahead, "gx", 1)
     high_x = along(behind, "gx", -1)
-    states = jnp.concatenate([melt_flow, thermal_state[None]], 0)
-    low_y = along(states[:, :, -2:], "gy", 1)
-    high_y = along(states[:, :, :2], "gy", -1)
+    low_y = along(last_rows, "gy", 1)
+    high_y = along(first_rows, "gy", -1)
+    extra, last, first = pack(
+        extra_kernel,
+        [melt_flow, thermal_state, powder_flag],
+        [low_y, high_y],
+        [(2 * rows + 8, width), (2,) + plane, (2,) + plane],
+        pltpu.VMEM(plane, jnp.int32),
+        4,
+    )
+    extra = along(extra, "gx", 1)
     ratio, weight = call(
         functools.partial(tables_kernel, group, layers),
         [diagonal],
         [(length + 1,) + plane, (4 * rounds + 1,) + plane],
     )
-    star, side_y = call(
+    early_low = along(last, "gx", 1)
+    early_high = along(first, "gx", -1)
+    star, side_x, side_y = call(
         march_kernel,
-        [melt_flow, low_x, high_x, thermal_state, powder_flag, low_y, high_y, weight],
-        [(3, layers) + plane, (layers, depth)],
+        [
+            melt_flow, low_x, high_x, thermal_state, powder_flag, low_y, high_y, extra, weight,
+        ],
+        [(3, layers) + plane, plane, (layers, depth)],
         [pltpu.VMEM((4, rows + 16, depth), F32)],
     )
     before_y = along(side_y, "gy", 1)
-    early = along(thermal_state[-2:], "gx", 1)
-    source, message, side = call(
+    source, message = call(
         functools.partial(transform_kernel, group, length),
-        [star, table_y, table_z, ratio],
-        [(layers + 1,) + plane, (2 * rows, depth), plane],
+        [star, side_x, table_y, table_z, ratio],
+        [(layers,) + plane, (2 * rows, depth)],
         [pltpu.VMEM((rows + 16, depth), F32)],
     )
-    alone = blocks == 1
     (faces,) = call(
-        functools.partial(faces_kernel, group, length, alone),
-        [
-            source, side if alone else along(side, "gx", 1), before_y, table_z, ratio, weight,
-            edge, early,
-        ],
+        functools.partial(faces_kernel, group, length),
+        [source, before_y, table_z, ratio, weight, edge, early_low],
         [(3 * length + 8, depth)],
         [pltpu.VMEM((max(length, layers + 1),) + plane, F32)],
-    )
-    wraps = []
-    for target in range(group - 1 if alone else group):
-        pairs = [
-            (block * group + group - 1, (block + 1) % blocks * group + target)
-            for block in range(blocks)
-        ]
-        wraps.append(lax.ppermute(side, "gx", pairs))
-    (wrap,) = call(
-        functools.partial(wrap_kernel, group, alone), [side] + wraps, [plane], flops=1 << 30
+        loose=1,
+    )
+    alone = blocks == 1
+    (warmed,) = call(
+        heat_kernel,
+        [
+            spot_lateral_a_cell, spot_lateral_b_cell, thermal_state, early_low, early_high,
+            low_y, high_y, melt_flow,
+        ],
+        [(layers,) + plane],
+        [pltpu.VMEM((1, rows + 16, depth), F32)],
+        scalars=2,
     )
     sums = jnp.zeros((2,) + plane, F32)
     for turn in range(rounds - 1):
@@ -682,9 +709,10 @@
             functools.partial(merge_kernel, turn, group, length),
             [
                 message, swapped(message, 1 << turn), faces, swapped(faces, 1 << turn),
-                sums, weight,
+                sums, weight, early_high,
             ],
             [(2 * rows + 2 * length + 8, depth), (2,) + plane, line, line],
+            loose=1,
         )
         if turn + 2 < rounds:
             rest = message[2 * rows + length :]
@@ -699,25 +727,26 @@
     if not alone:
         (ends,) = call(
             functools.partial(close_kernel, rounds - 1, group, length),
-            [message, other, sums, weight, ratio, edge, wrap],
+            [message, other, sums, weight, ratio, edge],
             [(2,) + plane],
             scratch,
         )
         outer = [jnp.stack([along(ends[0], "gx", group), along(ends[1], "gx", -group)])]
     operands = [source, message, other, sums] + rim
-    operands += [weight, ratio, edge, thermal_state, wrap] + outer
+    operands += [weight, ratio, edge] + outer + [warmed]
 
     def coarse(*refs):
-        coarse_kernel(rounds - 1, group, length, *refs[:4], refs[4:8], *refs[8:])
-
-    precond, image, report, faces, late = call(
+        coarse_kernel(rounds - 1, group, length, alone, *refs[:4], refs[4:8], *refs[8:])
+
+    precond, image, report, faces = call(
         coarse,
         operands,
         [
             (layers + 1,) + plane, (layers + 1,) + plane, (2 * length + 8, depth),
-            (3 * length, depth), (2,) + plane,
+            (3 * length, depth),
         ],
         scratch + [pltpu.VMEM((2,) + plane, F32)],
+        loose=1,
     )
     if blocks > 1:
         onward = along(image[0], "gx", -1)
@@ -735,19 +764,10 @@
         [precond, image, table_y, table_z],
         [(layers + 1,) + plane, (layers + 1,) + plane],
     )
-    late = along(late, "gx", -1)
-    warmed = []
-    for halo, span in ((early, range(0, 2)), (late, range(2, layers))):
-        warmed += call(
-            functools.partial(heat_kernel, span),
-            [spot_lateral_a_cell, spot_lateral_b_cell, thermal_state, halo, low_y, high_y, melt_flow],
-            [(len(span),) + plane],
-            [pltpu.VMEM((1, rows + 16, depth), F32)],
-            )
-    flow, pressure, warmed = call(
+    flow, pressure = call(
         functools.partial(project_kernel, group, length, blocks > 1),
-        [star, precond, image, faces, table_z] + warmed + reports,
-        [(3, layers) + plane, (layers,) + plane, (layers,) + plane],
+        [star, precond, image, faces, table_z] + reports,
+        [(3, layers) + plane, (layers,) + plane],
         [pltpu.VMEM((layers + 1,) + plane, F32), pltpu.VMEM((rows + 16, depth), F32)],
     )
     return (flow, warmed, pressure)

time: 59.9 us -> 56.7 us (0.947)
  waiting for transfers between devices: 26.4 us -> 21.3 us
  Pallas kernels: 10.4 us -> 12.1 us
  starting transfers between devices: 20 us -> 21.3 us
  local copies, waits for them, and re-layouts: 2.13 us -> 1.01 us
    ppermute x10 -> x11, starting transfers between devices: 9.2 us -> 13.4 us  [along(): lax.ppermute(array, axis, [(i, (i + by) % length) for i in range(length)])]
    ppermute x3 -> x0, starting transfers between devices: 2.61 us -> none  [per_device(): wraps.append(lax.ppermute(side, 'gx', pairs))]
    ppermute x7, waiting for transfers between devices: 5.19 us -> 3.16 us  [swapped(): return lax.ppermute(array, ('gx', 'gy'), pairs)]
    ppermute x10 -> x11, waiting for transfers between devices: 19.9 us -> 18.1 us  [along(): lax.ppermute(array, axis, [(i, (i + by) % length) for i in range(length)])]
    pallas_call x1 -> x2, Pallas kernels: 1.45 us -> 2.92 us  [pack(): pl.pallas_call(body, out_shape=[jax.ShapeDtypeStruct(shape, F32) for shap...]
    ppermute x3 -> x0, waiting for transfers between devices: 1.37 us -> none  [per_device(): wraps.append(lax.ppermute(side, 'gx', pairs))]
    unnamed x20 -> x18, local copies, waits for them, and re-layouts: 2.11 us -> 1 us
    pallas_call x11 -> x9, Pallas kernels: 8.9 us -> 9.18 us  [call(): pl.pallas_call(body, out_shape=out_shape, in_specs=[SMEM] * scalars + [VM...]
  transfers between devices with their start and end apart: 20 -> 18, of which waited for: 10 -> 8; matrix products, arithmetic and copies ran while one was open for 0% -> 0% of each run, Pallas kernels for 11% -> 14%
where the time goes in v6:
time: 56.7 us; the launch traced here: 56.5 us
  starting transfers between devices  21.3 us (38%)
  waiting for transfers between devices  21.3 us (38%)
  Pallas kernels  12.1 us (21%)
  local copies, waits for them, and re-layouts  1.01 us (2%)
  between operations  0.82 us (1%)
    ppermute x11, waiting for transfers between devices, along(): lax.ppermute(array, axis, [(i, (i + by) % length) for i in range(length)])  18.1 us
    ppermute x11, starting transfers between devices, along(): lax.ppermute(array, axis, [(i, (i + by) % length) for i in range(length)])  13.4 us
    pallas_call x9, Pallas kernels, call(): pl.pallas_call(body, out_shape=out_shape, in_specs=[SMEM] * scalars + [VM...  9.18 us
    ppermute x7, starting transfers between devices, swapped(): return lax.ppermute(array, ('gx', 'gy'), pairs)  7.89 us
    ppermute x7, waiting for transfers between devices, swapped(): return lax.ppermute(array, ('gx', 'gy'), pairs)  3.16 us
    pallas_call x2, Pallas kernels, pack(): pl.pallas_call(body, out_shape=[jax.ShapeDtypeStruct(shape, F32) for shap...  2.92 us
  transfers between devices with their start and end apart: 18, of which 8 were waited for; matrix products, arithmetic and copies ran while one was open for 0% of the time, Pallas kernels for 14%

profile of v6, /device:TPU:0, one launch (start us, length us, event | category | flops | bytes accessed | tf_op | source)
XLA Modules:
  0.0 56.5 jit_solution(11534337313439862965)
XLA Ops:
  0.7 1.8 %shard_map.112 = (f32[776,128]{1,0:T(8,128)S(1)}, f32[776,128]{1,0:T(8,128)S(1)}, f32[4,4,8,128]{3,2,1,0:T(8,128)S(1)}, f32[4,4,8,128]{3,2,1,0:T(8,128)S(1)}) custom-call(f32[3,4,128,128]{3,2,1,0:T(8,128)} %flow.7, f32[4,128,128]{2,1,0:T(8,128)} %thermal.7), custom_call_target="tpu_custom_call" | custom-call | tf_op jit(solution)/shard_map/pallas_call | solution.py:614
  2.5 3.1 %collective-permute-start = (f32[776,128]{1,0:T(8,128)S(1)}, f32[776,128]{1,0:T(8,128)S(1)}, u32[]{:S(2)}, u32[]{:S(2)}) collective-permute-start(f32[776,128]{1,0:T(8,128)S(1)} %get-tuple-element.29), channel_id=1, source_target_pairs={{0,4},{4,8},{8,12},{12,0},{1,5},{5,9},{9,13},{13,1},{2,6},{6,10},{... | collective-permute-start | bytes 1191944 | tf_op jit(solution)/shard_map/ppermute | solution.py:599
  5.6 2.1 %collective-permute-start.1 = (f32[776,128]{1,0:T(8,128)S(1)}, f32[776,128]{1,0:T(8,128)S(1)}, u32[]{:S(2)}, u32[]{:S(2)}) collective-permute-start(f32[776,128]{1,0:T(8,128)S(1)} %get-tuple-element.30), channel_id=1, source_target_pairs={{0,12},{4,0},{8,4},{12,8},{1,13},{5,1},{9,5},{13,9},{2,14},{6,2},{... | collective-permute-start | bytes 1191944 | tf_op jit(solution)/shard_map/ppermute | solution.py:599
  7.7 1.7 %collective-permute-start.3 = (f32[4,4,8,128]{3,2,1,0:T(8,128)S(1)}, f32[4,4,8,128]{3,2,1,0:T(8,128)S(1)}, u32[]{:S(2)}, u32[]{:S(2)}) collective-permute-start(f32[4,4,8,128]{3,2,1,0:T(8,128)S(1)} %get-tuple-element.32), channel_id=1, source_target_pairs={{0,3},{1,0},{2,1},{3,2},{4,7},{5,4},{6,5},{7,6},{8,11},{9,8},{10,9... | collective-permute-start | bytes 196616 | tf_op jit(solution)/shard_map/ppermute | solution.py:599
  9.4 1.9 %collective-permute-done.2.low_y = f32[4,4,8,128]{3,2,1,0:T(8,128)S(1)} collective-permute-done((f32[4,4,8,128]{3,2,1,0:T(8,128)S(1)}, f32[4,4,8,128]{3,2,1,0:T(8,128)S(1)}, u32[]{:S(2)}, u32[]{:S(2)}) %collective-permute-start.2) | collective-permute-done | bytes 65568 | tf_op jit(solution)/shard_map/ppermute | solution.py:599
  11.4 1.1 %shard_map.113 = (f32[264,128]{1,0:T(8,128)S(1)}, f32[2,128,128]{2,1,0:T(8,128)S(1)}, f32[2,128,128]{2,1,0:T(8,128)S(1)}) custom-call(f32[3,4,128,128]{3,2,1,0:T(8,128)} %flow.7, f32[4,128,128]{2,1,0:T(8,128)} %thermal.7, s32[4,128,128]{2,1,0:T(8,128)} %flag.3, f32[4,4,8,128]{3,2,1,0:T(8,128)S(1)} %collective-permute-done.2.low_y, ...), custom_call_target="tpu_custom_call" | custom-call | tf_op jit(solution)/shard_map/pallas_call | solution.py:614
  12.5 1.5 %collective-permute-start.7 = (f32[2,128,128]{2,1,0:T(8,128)S(1)}, f32[2,128,128]{2,1,0:T(8,128)S(1)}, u32[]{:S(2)}, u32[]{:S(2)}) collective-permute-start(f32[2,128,128]{2,1,0:T(8,128)S(1)} %get-tuple-element.41), channel_id=1, source_target_pairs={{0,4},{4,8},{8,12},{12,0},{1,5},{5,9},{9,13},{13,1},{2,6},{6,10},{... | collective-permute-start | bytes 393224 | tf_op jit(solution)/shard_map/ppermute | solution.py:599
  14.4 2.4 %collective-permute-start.9 = (f32[2,128,128]{2,1,0:T(8,128)S(1)}, f32[2,128,128]{2,1,0:T(8,128)S(1)}, u32[]{:S(2)}, u32[]{:S(2)}) collective-permute-start(f32[2,128,128]{2,1,0:T(8,128)S(1)} %get-tuple-element.42), channel_id=1, source_target_pairs={{0,12},{4,0},{8,4},{12,8},{1,13},{5,1},{9,5},{13,9},{2,14},{6,2},{... | collective-permute-start | bytes 393224 | tf_op jit(solution)/shard_map/ppermute | solution.py:599
  16.9 12.4 %collective-permute-done.4.extra = f32[264,128]{1,0:T(8,128)S(1)} collective-permute-done((f32[264,128]{1,0:T(8,128)S(1)}, f32[264,128]{1,0:T(8,128)S(1)}, u32[]{:S(2)}, u32[]{:S(2)}) %collective-permute-start.4) | collective-permute-done | bytes 135200 | tf_op jit(solution)/shard_map/ppermute | solution.py:599
  29.3 1.5 %shard_map.115 = (f32[3,4,128,128]{3,2,1,0:T(8,128)S(1)}, f32[128,128]{1,0:T(8,128)S(1)}, f32[4,128]{1,0:T(4,128)S(1)}) custom-call(f32[3,4,128,128]{3,2,1,0:T(8,128)S(1)} %copy-done, f32[776,128]{1,0:T(8,128)S(1)} %collective-permute-done.low_x, f32[776,128]{1,0:T(8,128)S(1)} %collective-permute-done.1.high_x, f32[4,128,128]{2,1,0:T(8,128)S(1)} %copy-done.1, ...), custom_call_target="tpu_custom_call" | custom-call | flops 1048576 | bytes 1708032 | tf_op jit(solution)/shard_map/pallas_call | solution.py:30
  30.8 0.8 %shard_map.116 = (f32[4,128,128]{2,1,0:T(8,128)S(1)}, f32[256,128]{1,0:T(8,128)S(1)}) custom-call(f32[3,4,128,128]{3,2,1,0:T(8,128)S(1)} %get-tuple-element.35.star, f32[128,128]{1,0:T(8,128)S(1)} %get-tuple-element.36.side_x, f32[128,128]{1,0:T(8,128)S(1)} %copy-done.2, f32[128,128]{1,0:T(8,128)S(1)} %copy-done.2, ...), custom_call_target="tpu_custom_call" | custom-call | flops 1048576 | bytes 786432 | tf_op jit(solution)/shard_map/pallas_call | solution.py:30
  32.0 2.8 %collective-permute-done.6.before_y = f32[4,128]{1,0:T(4,128)S(1)} collective-permute-done((f32[4,128]{1,0:T(4,128)S(1)}, f32[4,128]{1,0:T(4,128)S(1)}, u32[]{:S(2)}, u32[]{:S(2)}) %collective-permute-start.6) | collective-permute-done | bytes 2080 | tf_op jit(solution)/shard_map/ppermute | solution.py:599
  35.5 2.0 %collective-permute-start.8 = (f32[56,128]{1,0:T(8,128)S(1)}, f32[56,128]{1,0:T(8,128)S(1)}, u32[]{:S(2)}, u32[]{:S(2)}) collective-permute-start(f32[56,128]{1,0:T(8,128)S(1)} %shard_map.117.faces), channel_id=1, source_target_pairs={{0,4},{1,5},{2,6},{3,7},{4,0},{5,1},{6,2},{7,3},{8,12},{9,13},{10,... | collective-permute-start | bytes 86024 | tf_op jit(solution)/shard_map/ppermute | solution.py:609
  37.5 1.9 %collective-permute-done.8.other_faces = f32[56,128]{1,0:T(8,128)S(1)} collective-permute-done((f32[56,128]{1,0:T(8,128)S(1)}, f32[56,128]{1,0:T(8,128)S(1)}, u32[]{:S(2)}, u32[]{:S(2)}) %collective-permute-start.8) | collective-permute-done | bytes 28704 | tf_op jit(solution)/shard_map/ppermute | solution.py:609
  39.6 1.6 %collective-permute-start.10 = (f32[296,128]{1,0:T(8,128)S(1)}, f32[296,128]{1,0:T(8,128)S(1)}, u32[]{:S(2)}, u32[]{:S(2)}) collective-permute-start(f32[296,128]{1,0:T(8,128)S(1)} %get-tuple-element.43.refs_1_), channel_id=1, source_target_pairs={{0,8},{1,9},{2,10},{3,11},{4,12},{5,13},{6,14},{7,15},{8,0},{9,1},... | collective-permute-start | bytes 454664 | tf_op jit(solution)/shard_map/ppermute | solution.py:609
  41.2 2.8 %collective-permute-start.12 = (f32[16,128]{1,0:T(8,128)S(1)}, f32[16,128]{1,0:T(8,128)S(1)}, u32[]{:S(2)}, u32[]{:S(2)}) collective-permute-start(f32[16,128]{1,0:T(8,128)S(1)} %get-tuple-element.45), channel_id=1, source_target_pairs={{0,9},{1,10},{2,11},{3,8},{4,13},{5,14},{6,15},{7,12},{8,1},{9,2},... | collective-permute-start | bytes 24584 | tf_op jit(solution)/shard_map/ppermute | solution.py:609
  44.0 1.5 %collective-permute-start.14 = (f32[16,128]{1,0:T(8,128)S(1)}, f32[16,128]{1,0:T(8,128)S(1)}, u32[]{:S(2)}, u32[]{:S(2)}) collective-permute-start(f32[16,128]{1,0:T(8,128)S(1)} %get-tuple-element.46), channel_id=1, source_target_pairs={{0,11},{1,8},{2,9},{3,10},{4,15},{5,12},{6,13},{7,14},{8,3},{9,0},... | collective-permute-start | bytes 24584 | tf_op jit(solution)/shard_map/ppermute | solution.py:609
  45.5 1.9 %shard_map.119.refs_11_ = f32[4,128,128]{2,1,0:T(8,128)} custom-call(s32[8]{0:T(128)S(1)} %copy-done.7, s32[8]{0:T(128)S(1)} %copy-done.8, f32[4,128,128]{2,1,0:T(8,128)S(1)} %copy-done.1, f32[2,128,128]{2,1,0:T(8,128)S(1)} %collective-permute-done.7.refs_0_.low_x, f32[2,128,128]{2,1,0:T(8,128)S(1)} %collective-permute-done.9._.high_x, ...), custom_call_target="tpu_custom_call" | custom-call | flops 1048576 | bytes 524288 | tf_op jit(solution)/shard_map/pallas_call | solution.py:30
  48.6 0.9 %copy-done.4 = f32[4,128,128]{2,1,0:T(8,128)S(1)} copy-done((f32[4,128,128]{2,1,0:T(8,128)S(1)}, f32[4,128,128]{2,1,0:T(8,128)}, u32[]{:S(2)}) %copy-start.4) | copy-done | bytes 262168
  49.6 1.0 %shard_map.120 = (f32[5,128,128]{2,1,0:T(8,128)S(1)}, f32[5,128,128]{2,1,0:T(8,128)S(1)}, f32[40,128]{1,0:T(8,128)S(1)}, f32[48,128]{1,0:T(8,128)S(1)}) custom-call(f32[4,128,128]{2,1,0:T(8,128)S(1)} %get-tuple-element.38.source.refs_0_, f32[296,128]{1,0:T(8,128)S(1)} %get-tuple-element.43.refs_1_, f32[296,128]{1,0:T(8,128)S(1)} %collective-permute-done.10.refs_2_, ...), custom_call_target="tpu_custom_call" | custom-call | flops 1048576 | bytes 1400832 | tf_op jit(solution)/shard_map/pallas_call | solution.py:30
  50.6 0.8 %collective-permute-start.15 = (f32[40,128]{1,0:T(8,128)S(1)}, f32[40,128]{1,0:T(8,128)S(1)}, u32[]{:S(2)}, u32[]{:S(2)}) collective-permute-start(f32[40,128]{1,0:T(8,128)S(1)} %get-tuple-element.52.refs_0_), channel_id=1, source_target_pairs={{0,1},{1,2},{2,3},{3,0},{4,5},{5,6},{6,7},{7,4},{8,9},{9,10},{10,1... | collective-permute-start | bytes 61448 | tf_op jit(solution)/shard_map/ppermute | solution.py:599
  52.1 0.9 %collective-permute-start.17 = (f32[40,128]{1,0:T(8,128)S(1)}, f32[40,128]{1,0:T(8,128)S(1)}, u32[]{:S(2)}, u32[]{:S(2)}) collective-permute-start(f32[40,128]{1,0:T(8,128)S(1)} %get-tuple-element.52.refs_0_), channel_id=1, source_target_pairs={{0,3},{1,0},{2,1},{3,2},{4,7},{5,4},{6,5},{7,6},{8,11},{9,8},{10,9... | collective-permute-start | bytes 61448 | tf_op jit(solution)/shard_map/ppermute | solution.py:599
  53.0 1.4 %shard_map.121 = (f32[5,128,128]{2,1,0:T(8,128)S(1)}, f32[5,128,128]{2,1,0:T(8,128)S(1)}) custom-call(f32[5,128,128]{2,1,0:T(8,128)S(1)} %get-tuple-element.47.precond, f32[5,128,128]{2,1,0:T(8,128)S(1)} %get-tuple-element.48.image, f32[128,128]{1,0:T(8,128)S(1)} %copy-done.2, f32[128,128]{1,0:T(8,128)S(1)} %copy-done.2), custom_call_target="tpu_custom_call" | custom-call | flops 1048576 | bytes 1310720 | tf_op jit(solution)/shard_map/pallas_call | solution.py:30
  55.2 1.2 %shard_map.122 = (f32[3,4,128,128]{3,2,1,0:T(8,128)}, f32[4,128,128]{2,1,0:T(8,128)}) custom-call(f32[3,4,128,128]{3,2,1,0:T(8,128)S(1)} %get-tuple-element.35.star, f32[5,128,128]{2,1,0:T(8,128)S(1)} %get-tuple-element.49.precond, f32[5,128,128]{2,1,0:T(8,128)S(1)} %get-tuple-element.50.image, f32[48,128]{1,0:T(8,128)S(1)} %get-tuple-element.51.faces, ...), custom_call_target="tpu_custom_call" | custom-call | flops 1048576 | bytes 2097152 | tf_op jit(solution)/shard_map/pallas_call | solution.py:30
  (42 shorter events, 4.4 us)
Async XLA Ops:
  0.6 13.4 %copy-start.6 = (f32[128,128]{1,0:T(8,128)S(1)}, f32[128,128]{1,0:T(8,128)}, u32[]{:S(2)}) copy-start(f32[128,128]{1,0:T(8,128)} %constant.10.clone.diagonal) | copy-start | bytes 196612
  0.6 28.6 %copy-start.1 = (f32[4,128,128]{2,1,0:T(8,128)S(1)}, f32[4,128,128]{2,1,0:T(8,128)}, u32[]{:S(2)}) copy-start(f32[4,128,128]{2,1,0:T(8,128)} %thermal.7) | copy-start | bytes 786436
  0.7 28.6 %copy-start = (f32[3,4,128,128]{3,2,1,0:T(8,128)S(1)}, f32[3,4,128,128]{3,2,1,0:T(8,128)}, u32[]{:S(2)}) copy-start(f32[3,4,128,128]{3,2,1,0:T(8,128)} %flow.7) | copy-start | bytes 2359300
  0.7 28.6 %copy-start.3 = (s32[4,128,128]{2,1,0:T(8,128)S(1)}, s32[4,128,128]{2,1,0:T(8,128)}, u32[]{:S(2)}) copy-start(s32[4,128,128]{2,1,0:T(8,128)} %flag.3) | copy-start | bytes 786436
  2.5 26.7 %collective-permute-start = (f32[776,128]{1,0:T(8,128)S(1)}, f32[776,128]{1,0:T(8,128)S(1)}, u32[]{:S(2)}, u32[]{:S(2)}) collective-permute-start(f32[776,128]{1,0:T(8,128)S(1)} %get-tuple-element.29), channel_id=1, source_target_pairs={{0,4},{4,8},{8,12},{12,0},{1,5},{5,9},{9,13},{13,1},{2,6},{6,10},{... | collective-permute-start | bytes 1191944 | tf_op jit(solution)/shard_map/ppermute | solution.py:599
  5.6 23.7 %collective-permute-start.1 = (f32[776,128]{1,0:T(8,128)S(1)}, f32[776,128]{1,0:T(8,128)S(1)}, u32[]{:S(2)}, u32[]{:S(2)}) collective-permute-start(f32[776,128]{1,0:T(8,128)S(1)} %get-tuple-element.30), channel_id=1, source_target_pairs={{0,12},{4,0},{8,4},{12,8},{1,13},{5,1},{9,5},{13,9},{2,14},{6,2},{... | collective-permute-start | bytes 1191944 | tf_op jit(solution)/shard_map/ppermute | solution.py:599
  7.7 3.7 %collective-permute-start.2 = (f32[4,4,8,128]{3,2,1,0:T(8,128)S(1)}, f32[4,4,8,128]{3,2,1,0:T(8,128)S(1)}, u32[]{:S(2)}, u32[]{:S(2)}) collective-permute-start(f32[4,4,8,128]{3,2,1,0:T(8,128)S(1)} %get-tuple-element.31), channel_id=1, source_target_pairs={{0,1},{1,2},{2,3},{3,0},{4,5},{5,6},{6,7},{7,4},{8,9},{9,10},{10,1... | collective-permute-start | bytes 196616 | tf_op jit(solution)/shard_map/ppermute | solution.py:599
  7.7 3.7 %collective-permute-start.3 = (f32[4,4,8,128]{3,2,1,0:T(8,128)S(1)}, f32[4,4,8,128]{3,2,1,0:T(8,128)S(1)}, u32[]{:S(2)}, u32[]{:S(2)}) collective-permute-start(f32[4,4,8,128]{3,2,1,0:T(8,128)S(1)} %get-tuple-element.32), channel_id=1, source_target_pairs={{0,3},{1,0},{2,1},{3,2},{4,7},{5,4},{6,5},{7,6},{8,11},{9,8},{10,9... | collective-permute-start | bytes 196616 | tf_op jit(solution)/shard_map/ppermute | solution.py:599
  12.5 16.8 %collective-permute-start.4 = (f32[264,128]{1,0:T(8,128)S(1)}, f32[264,128]{1,0:T(8,128)S(1)}, u32[]{:S(2)}, u32[]{:S(2)}) collective-permute-start(f32[264,128]{1,0:T(8,128)S(1)} %get-tuple-element.33), channel_id=1, source_target_pairs={{0,4},{4,8},{8,12},{12,0},{1,5},{5,9},{9,13},{13,1},{2,6},{6,10},{... | collective-permute-start | bytes 405512 | tf_op jit(solution)/shard_map/ppermute | solution.py:599
  12.5 19.4 %collective-permute-start.7 = (f32[2,128,128]{2,1,0:T(8,128)S(1)}, f32[2,128,128]{2,1,0:T(8,128)S(1)}, u32[]{:S(2)}, u32[]{:S(2)}) collective-permute-start(f32[2,128,128]{2,1,0:T(8,128)S(1)} %get-tuple-element.41), channel_id=1, source_target_pairs={{0,4},{4,8},{8,12},{12,0},{1,5},{5,9},{9,13},{13,1},{2,6},{6,10},{... | collective-permute-start | bytes 393224 | tf_op jit(solution)/shard_map/ppermute | solution.py:599
  14.4 23.1 %collective-permute-start.9 = (f32[2,128,128]{2,1,0:T(8,128)S(1)}, f32[2,128,128]{2,1,0:T(8,128)S(1)}, u32[]{:S(2)}, u32[]{:S(2)}) collective-permute-start(f32[2,128,128]{2,1,0:T(8,128)S(1)} %get-tuple-element.42), channel_id=1, source_target_pairs={{0,12},{4,0},{8,4},{12,8},{1,13},{5,1},{9,5},{13,9},{2,14},{6,2},{... | collective-permute-start | bytes 393224 | tf_op jit(solution)/shard_map/ppermute | solution.py:599
  31.7 7.8 %collective-permute-start.5 = (f32[256,128]{1,0:T(8,128)S(1)}, f32[256,128]{1,0:T(8,128)S(1)}, u32[]{:S(2)}, u32[]{:S(2)}) collective-permute-start(f32[256,128]{1,0:T(8,128)S(1)} %get-tuple-element.39.message), channel_id=1, source_target_pairs={{0,4},{1,5},{2,6},{3,7},{4,0},{5,1},{6,2},{7,3},{8,12},{9,13},{10,... | collective-permute-start | bytes 393224 | tf_op jit(solution)/shard_map/ppermute | solution.py:609
  31.8 3.1 %collective-permute-start.6 = (f32[4,128]{1,0:T(4,128)S(1)}, f32[4,128]{1,0:T(4,128)S(1)}, u32[]{:S(2)}, u32[]{:S(2)}) collective-permute-start(f32[4,128]{1,0:T(4,128)S(1)} %get-tuple-element.40), channel_id=1, source_target_pairs={{0,1},{1,2},{2,3},{3,0},{4,5},{5,6},{6,7},{7,4},{8,9},{9,10},{10,1... | collective-permute-start | bytes 6152 | tf_op jit(solution)/shard_map/ppermute | solution.py:599
  35.5 9.9 %copy-start.7 = (s32[8]{0:T(128)S(1)}, s32[8]{0:T(128)}, u32[]{:S(2)}) copy-start(s32[8]{0:T(128)} %spots_a.1) | copy-start | bytes 100
  35.5 9.9 %copy-start.8 = (s32[8]{0:T(128)S(1)}, s32[8]{0:T(128)}, u32[]{:S(2)}) copy-start(s32[8]{0:T(128)} %spots_b.1) | copy-start | bytes 100
  35.5 3.9 %collective-permute-start.8 = (f32[56,128]{1,0:T(8,128)S(1)}, f32[56,128]{1,0:T(8,128)S(1)}, u32[]{:S(2)}, u32[]{:S(2)}) collective-permute-start(f32[56,128]{1,0:T(8,128)S(1)} %shard_map.117.faces), channel_id=1, source_target_pairs={{0,4},{1,5},{2,6},{3,7},{4,0},{5,1},{6,2},{7,3},{8,12},{9,13},{10,... | collective-permute-start | bytes 86024 | tf_op jit(solution)/shard_map/ppermute | solution.py:609
  39.6 9.0 %collective-permute-start.10 = (f32[296,128]{1,0:T(8,128)S(1)}, f32[296,128]{1,0:T(8,128)S(1)}, u32[]{:S(2)}, u32[]{:S(2)}) collective-permute-start(f32[296,128]{1,0:T(8,128)S(1)} %get-tuple-element.43.refs_1_), channel_id=1, source_target_pairs={{0,8},{1,9},{2,10},{3,11},{4,12},{5,13},{6,14},{7,15},{8,0},{9,1},... | collective-permute-start | bytes 454664 | tf_op jit(solution)/shard_map/ppermute | solution.py:609
  41.2 6.1 %collective-permute-start.11 = (f32[16,128]{1,0:T(8,128)S(1)}, f32[16,128]{1,0:T(8,128)S(1)}, u32[]{:S(2)}, u32[]{:S(2)}) collective-permute-start(f32[16,128]{1,0:T(8,128)S(1)} %get-tuple-element.45), channel_id=1, source_target_pairs={{0,1},{1,2},{2,3},{3,0},{4,5},{5,6},{6,7},{7,4},{8,9},{9,10},{10,1... | collective-permute-start | bytes 24584 | tf_op jit(solution)/shard_map/ppermute | solution.py:609
  41.2 6.1 %collective-permute-start.12 = (f32[16,128]{1,0:T(8,128)S(1)}, f32[16,128]{1,0:T(8,128)S(1)}, u32[]{:S(2)}, u32[]{:S(2)}) collective-permute-start(f32[16,128]{1,0:T(8,128)S(1)} %get-tuple-element.45), channel_id=1, source_target_pairs={{0,9},{1,10},{2,11},{3,8},{4,13},{5,14},{6,15},{7,12},{8,1},{9,2},... | collective-permute-start | bytes 24584 | tf_op jit(solution)/shard_map/ppermute | solution.py:609
  44.0 3.4 %collective-permute-start.13 = (f32[16,128]{1,0:T(8,128)S(1)}, f32[16,128]{1,0:T(8,128)S(1)}, u32[]{:S(2)}, u32[]{:S(2)}) collective-permute-start(f32[16,128]{1,0:T(8,128)S(1)} %get-tuple-element.46), channel_id=1, source_target_pairs={{0,3},{1,0},{2,1},{3,2},{4,7},{5,4},{6,5},{7,6},{8,11},{9,8},{10,9... | collective-permute-start | bytes 24584 | tf_op jit(solution)/shard_map/ppermute | solution.py:609
  44.0 4.1 %collective-permute-start.14 = (f32[16,128]{1,0:T(8,128)S(1)}, f32[16,128]{1,0:T(8,128)S(1)}, u32[]{:S(2)}, u32[]{:S(2)}) collective-permute-start(f32[16,128]{1,0:T(8,128)S(1)} %get-tuple-element.46), channel_id=1, source_target_pairs={{0,11},{1,8},{2,9},{3,10},{4,15},{5,12},{6,13},{7,14},{8,3},{9,0},... | collective-permute-start | bytes 24584 | tf_op jit(solution)/shard_map/ppermute | solution.py:609
  50.6 3.9 %collective-permute-start.15 = (f32[40,128]{1,0:T(8,128)S(1)}, f32[40,128]{1,0:T(8,128)S(1)}, u32[]{:S(2)}, u32[]{:S(2)}) collective-permute-start(f32[40,128]{1,0:T(8,128)S(1)} %get-tuple-element.52.refs_0_), channel_id=1, source_target_pairs={{0,1},{1,2},{2,3},{3,0},{4,5},{5,6},{6,7},{7,4},{8,9},{9,10},{10,1... | collective-permute-start | bytes 61448 | tf_op jit(solution)/shard_map/ppermute | solution.py:599
  51.4 3.8 %collective-permute-start.16 = (f32[40,128]{1,0:T(8,128)S(1)}, f32[40,128]{1,0:T(8,128)S(1)}, u32[]{:S(2)}, u32[]{:S(2)}) collective-permute-start(f32[40,128]{1,0:T(8,128)S(1)} %get-tuple-element.52.refs_0_), channel_id=1, source_target_pairs={{0,2},{1,3},{2,0},{3,1},{4,6},{5,7},{6,4},{7,5},{8,10},{9,11},{10,... | collective-permute-start | bytes 61448 | tf_op jit(solution)/shard_map/ppermute | solution.py:599
  52.1 3.1 %collective-permute-start.17 = (f32[40,128]{1,0:T(8,128)S(1)}, f32[40,128]{1,0:T(8,128)S(1)}, u32[]{:S(2)}, u32[]{:S(2)}) collective-permute-start(f32[40,128]{1,0:T(8,128)S(1)} %get-tuple-element.52.refs_0_), channel_id=1, source_target_pairs={{0,3},{1,0},{2,1},{3,2},{4,7},{5,4},{6,5},{7,6},{8,11},{9,8},{10,9... | collective-permute-start | bytes 61448 | tf_op jit(solution)/shard_map/ppermute | solution.py:599
  (3 other events, 6.5 us)

commit v7 on v6

--- a/solution.py
+++ b/solution.py
@@ -151,9 +151,20 @@
     pad_rows(padded, 3, low_y[3, index, 6:], thermal[index], high_y[3, index, :2])
 
 
+def row_kernel(flow, low_x, high_x, thermal, flag, low_y, high_y, _, side_y, padded):
+    refs = (flow, low_x, high_x, thermal, flag)
+    _, layers, rows, depth = flow.shape
+    for index in range(layers):
+        for part, cells in ((1, flow.at[1, index]), (3, thermal.at[index])):
+            padded[part, pl.ds(rows - 8, 16), :] = cells[pl.ds(rows - 16, 16), :]
+            padded[part, pl.ds(8 + rows, 2), :] = high_y[part, index, :2]
+        (value,) = march_layer(refs, padded, index, [1], rows - 8, 8)
+        side_y[pl.ds(index, 1), :] = value[7:, :]
+
+
 def march_kernel(
-    flow, low_x, high_x, thermal, flag, low_y, high_y, extra, weight,
-    star, side_x, side_y, padded,
+    flow, low_x, high_x, thermal, flag, low_y, high_y, extra, _,
+    star, side_x, padded,
 ):
     refs = (flow, low_x, high_x, thermal, flag)
     _, layers, rows, depth = flow.shape
@@ -162,7 +173,6 @@
         value = march_layer(refs, padded, index, range(3), 0, rows)
         for part in range(3):
             star[part, index] = value[part]
-        side_y[pl.ds(index, 1), :] = value[1][rows - 1 :, :]
     plane = lambda index: low_x[pl.ds(index * rows, rows), pl.ds(0, depth)]
     beside = extra[pl.ds(2 * rows, 8), pl.ds(0, depth)]
     pad_rows(padded, 0, beside[2:4], plane(1), beside[4:6])
@@ -177,7 +187,7 @@
 
 
 def transform_kernel(
-    group, length, star, side_x, table_y, table_z, ratio, source, message, rows_
+    group, length, star, side_x, table_y, table_z, ratio, _, source, message, rows_
 ):
     _, layers, rows, depth = star.shape
     first = position(group) * layers
@@ -215,16 +225,15 @@
 def halo_kernel(flow, thermal, ahead, behind, last_rows, first_rows, tops, sems):
     parts, layers, rows, depth = flow.shape
     pairs = [(thermal.at[layers - 1], tops.at[0]), (thermal.at[0], tops.at[1])]
-    for part in range(parts + 1):
-        for layer in range(layers):
-            source = thermal.at[layer] if part == parts else flow.at[part, layer]
-            pairs.append((source.at[pl.ds(rows - 8, 8), :], last_rows.at[part, layer]))
-            pairs.append((source.at[pl.ds(0, 8), :], first_rows.at[part, layer]))
     for part in range(parts):
         for layer in range(2):
             span = pl.ds((2 * part + layer) * rows, rows)
             pairs.append((flow.at[part, layers - 2 + layer], ahead.at[span, :]))
             pairs.append((flow.at[part, layer], behind.at[span, :]))
+    for target, start in ((last_rows, rows - 8), (first_rows, 0)):
+        span = pl.ds(start, 8)
+        pairs.append((flow.at[:, :, span, :], target.at[pl.ds(0, parts)]))
+        pairs.append((thermal.at[:, span, :], target.at[parts]))
     copies = started(
         [pltpu.make_async_copy(*pair, sems.at[index]) for index, pair in enumerate(pairs)]
     )
@@ -236,10 +245,9 @@
         copy.wait()
 
 
-def extra_kernel(flow, thermal, flag, low_y, high_y, extra, last, first, flags, sems):
+def extra_kernel(flow, thermal, flag, low_y, high_y, extra, last, flags, sems):
     _, layers, rows, depth = flow.shape
     pairs = [(flag.at[layers - 1], flags), (thermal.at[pl.ds(layers - 2, 2)], last)]
-    pairs.append((thermal.at[pl.ds(0, 2)], first))
     pairs.append((flow.at[0, layers - 3], extra.at[pl.ds(0, rows), :]))
     copies = started(
         [pltpu.make_async_copy(*pair, sems.at[index]) for index, pair in enumerate(pairs)]
@@ -278,9 +286,11 @@
 
 
 def heat_kernel(
-    spots_a, spots_b, thermal, low_x, high_x, low_y, high_y, flow, warmed, padded
+    spots_a, spots_b, thermal, low_x, high_x, low_y, high_y, flow,
+    warmed, token, padded,
 ):
     layers, rows, depth = thermal.shape
+    token[...] = jnp.zeros(token.shape, F32)
     top = lax.broadcasted_iota(jnp.int32, (rows, depth), 1) == depth - 1
     for index in range(layers):
         pad_rows(padded, 0, low_y[3, index, 6:], thermal[index], high_y[3, index, :2])
@@ -344,10 +354,10 @@
 
 
 def faces_kernel(
-    group, length, source, before_y, table_z, ratio, weight, edge, *refs
+    group, length, source, before_y, table_z, ratio, weight, edge, thermal, _, faces, late, sweep
 ):
-    faces, sweep = refs[-2:]
     layers, rows, depth = source.shape
+    late[...] = thermal[:2]
     first = position(group) * layers
     zero = jnp.zeros((rows, depth), F32)
     extra = dot(before_y[...], table_z[...])
@@ -403,7 +413,7 @@
 
 
 def merge_kernel(
-    turn, group, length, message, other, faces, other_faces, sums, weight, _,
+    turn, group, length, message, other, faces, other_faces, sums, weight,
     new_message, new_sums, head, tail,
 ):
     rows, depth = weight.shape[1:]
@@ -648,19 +658,19 @@
         [],
         [outer_planes, outer_planes] + [(parts + 1, layers, 8, depth)] * 2,
         pltpu.VMEM((2,) + plane, F32),
-        2 + 2 * layers * (parts + 1) + 4 * parts,
+        6 + 4 * parts,
     )
     low_x = along(ahead, "gx", 1)
     high_x = along(behind, "gx", -1)
     low_y = along(last_rows, "gy", 1)
     high_y = along(first_rows, "gy", -1)
-    extra, last, first = pack(
+    extra, last = pack(
         extra_kernel,
         [melt_flow, thermal_state, powder_flag],
         [low_y, high_y],
-        [(2 * rows + 8, width), (2,) + plane, (2,) + plane],
+        [(2 * rows + 8, width), (2,) + plane],
         pltpu.VMEM(plane, jnp.int32),
-        4,
+        3,
     )
     extra = along(extra, "gx", 1)
     ratio, weight = call(
@@ -669,39 +679,45 @@
         [(length + 1,) + plane, (4 * rounds + 1,) + plane],
     )
     early_low = along(last, "gx", 1)
-    early_high = along(first, "gx", -1)
-    star, side_x, side_y = call(
+    marched = [melt_flow, low_x, high_x, thermal_state, powder_flag, low_y, high_y]
+    padded = pltpu.VMEM((4, rows + 16, depth), F32)
+    (side_y,) = call(row_kernel, marched + [weight], [(layers, depth)], [padded], loose=1)
+    before_y = along(side_y, "gy", 1)
+    star, side_x = call(
         march_kernel,
-        [
-            melt_flow, low_x, high_x, thermal_state, powder_flag, low_y, high_y, extra, weight,
-        ],
-        [(3, layers) + plane, plane, (layers, depth)],
-        [pltpu.VMEM((4, rows + 16, depth), F32)],
-    )
-    before_y = along(side_y, "gy", 1)
+        marched + [extra, side_y],
+        [(3, layers) + plane, plane],
+        [padded],
+        loose=1,
+        flops=3 << 29,
+    )
     source, message = call(
         functools.partial(transform_kernel, group, length),
-        [star, side_x, table_y, table_z, ratio],
+        [star, side_x, table_y, table_z, ratio, before_y],
         [(layers,) + plane, (2 * rows, depth)],
         [pltpu.VMEM((rows + 16, depth), F32)],
-    )
-    (faces,) = call(
+        loose=1,
+        flops=1 << 30,
+    )
+    faces, late = call(
         functools.partial(faces_kernel, group, length),
-        [source, before_y, table_z, ratio, weight, edge, early_low],
-        [(3 * length + 8, depth)],
+        [source, before_y, table_z, ratio, weight, edge, thermal_state, early_low],
+        [(3 * length + 8, depth), (2,) + plane],
         [pltpu.VMEM((max(length, layers + 1),) + plane, F32)],
         loose=1,
     )
+    early_high = along(late, "gx", -1)
     alone = blocks == 1
-    (warmed,) = call(
+    warmed, token = call(
         heat_kernel,
         [
             spot_lateral_a_cell, spot_lateral_b_cell, thermal_state, early_low, early_high,
             low_y, high_y, melt_flow,
         ],
-        [(layers,) + plane],
+        [(layers,) + plane, (8, depth)],
         [pltpu.VMEM((1, rows + 16, depth), F32)],
         scalars=2,
+        flops=1 << 28,
     )
     sums = jnp.zeros((2,) + plane, F32)
     for turn in range(rounds - 1):
@@ -709,10 +725,9 @@
             functools.partial(merge_kernel, turn, group, length),
             [
                 message, swapped(message, 1 << turn), faces, swapped(faces, 1 << turn),
-                sums, weight, early_high,
+                sums, weight,
             ],
             [(2 * rows + 2 * length + 8, depth), (2,) + plane, line, line],
-            loose=1,
         )
         if turn + 2 < rounds:
             rest = message[2 * rows + length :]
@@ -733,7 +748,7 @@
         )
         outer = [jnp.stack([along(ends[0], "gx", group), along(ends[1], "gx", -group)])]
     operands = [source, message, other, sums] + rim
-    operands += [weight, ratio, edge] + outer + [warmed]
+    operands += [weight, ratio, edge] + outer + [token]
 
     def coarse(*refs):
         coarse_kernel(rounds - 1, group, length, alone, *refs[:4], refs[4:8], *refs[8:])

time: 56.7 us -> 54.2 us (0.956)
  starting transfers between devices: 21.3 us -> 19.1 us
  local copies, waits for them, and re-layouts: 1.01 us -> 0.06 us
  waiting for transfers between devices: 21.3 us -> 22 us
    ppermute x7, starting transfers between devices: 7.89 us -> 6.78 us  [swapped(): return lax.ppermute(array, ('gx', 'gy'), pairs)]
    ppermute x11, starting transfers between devices: 13.4 us -> 12.3 us  [along(): lax.ppermute(array, axis, [(i, (i + by) % length) for i in range(length)])]
    unnamed x18 -> x16, local copies, waits for them, and re-layouts: 1 us -> 0.05 us
    ppermute x7, waiting for transfers between devices: 3.16 us -> 3.81 us  [swapped(): return lax.ppermute(array, ('gx', 'gy'), pairs)]
    pallas_call x9 -> x10, Pallas kernels: 9.18 us -> 9.61 us  [call(): pl.pallas_call(body, out_shape=out_shape, in_specs=[SMEM] * scalars + [VM...]
  transfers between devices with their start and end apart: 18 -> 18, of which waited for: 8 -> 8; matrix products, arithmetic and copies ran while one was open for 0% -> 0% of each run, Pallas kernels for 14% -> 16%
where the time goes in v7:
time: 54.2 us; the launch traced here: 54.1 us
  waiting for transfers between devices  22 us (41%)
  starting transfers between devices  19.1 us (35%)
  Pallas kernels  12.1 us (22%)
  between operations  0.81 us (1%)
    ppermute x11, waiting for transfers between devices, along(): lax.ppermute(array, axis, [(i, (i + by) % length) for i in range(length)])  18.2 us
    ppermute x11, starting transfers between devices, along(): lax.ppermute(array, axis, [(i, (i + by) % length) for i in range(length)])  12.3 us
    pallas_call x10, Pallas kernels, call(): pl.pallas_call(body, out_shape=out_shape, in_specs=[SMEM] * scalars + [VM...  9.61 us
    ppermute x7, starting transfers between devices, swapped(): return lax.ppermute(array, ('gx', 'gy'), pairs)  6.78 us
    ppermute x7, waiting for transfers between devices, swapped(): return lax.ppermute(array, ('gx', 'gy'), pairs)  3.81 us
    pallas_call x2, Pallas kernels, pack(): pl.pallas_call(body, out_shape=[jax.ShapeDtypeStruct(shape, F32) for shap...  2.52 us
  transfers between devices with their start and end apart: 18, of which 8 were waited for; matrix products, arithmetic and copies ran while one was open for 0% of the time, Pallas kernels for 16%

profile of v7, /device:TPU:0, one launch (start us, length us, event | category | flops | bytes accessed | tf_op | source)
XLA Modules:
  0.0 54.1 jit_solution(220704256981800920)
XLA Ops:
  0.7 1.5 %shard_map.112 = (f32[776,128]{1,0:T(8,128)S(1)}, f32[776,128]{1,0:T(8,128)S(1)}, f32[4,4,8,128]{3,2,1,0:T(8,128)S(1)}, f32[4,4,8,128]{3,2,1,0:T(8,128)S(1)}) custom-call(f32[3,4,128,128]{3,2,1,0:T(8,128)} %flow.9, f32[4,128,128]{2,1,0:T(8,128)} %thermal.11), custom_call_target="tpu_custom_call" | custom-call | tf_op jit(solution)/shard_map/pallas_call | solution.py:624
  2.1 3.1 %collective-permute-start = (f32[776,128]{1,0:T(8,128)S(1)}, f32[776,128]{1,0:T(8,128)S(1)}, u32[]{:S(2)}, u32[]{:S(2)}) collective-permute-start(f32[776,128]{1,0:T(8,128)S(1)} %get-tuple-element.31), channel_id=1, source_target_pairs={{0,4},{4,8},{8,12},{12,0},{1,5},{5,9},{9,13},{13,1},{2,6},{6,10},{... | collective-permute-start | bytes 1191944 | tf_op jit(solution)/shard_map/ppermute | solution.py:609
  5.2 2.1 %collective-permute-start.1 = (f32[776,128]{1,0:T(8,128)S(1)}, f32[776,128]{1,0:T(8,128)S(1)}, u32[]{:S(2)}, u32[]{:S(2)}) collective-permute-start(f32[776,128]{1,0:T(8,128)S(1)} %get-tuple-element.32), channel_id=1, source_target_pairs={{0,12},{4,0},{8,4},{12,8},{1,13},{5,1},{9,5},{13,9},{2,14},{6,2},{... | collective-permute-start | bytes 1191944 | tf_op jit(solution)/shard_map/ppermute | solution.py:609
  7.3 1.7 %collective-permute-start.3 = (f32[4,4,8,128]{3,2,1,0:T(8,128)S(1)}, f32[4,4,8,128]{3,2,1,0:T(8,128)S(1)}, u32[]{:S(2)}, u32[]{:S(2)}) collective-permute-start(f32[4,4,8,128]{3,2,1,0:T(8,128)S(1)} %get-tuple-element.34), channel_id=1, source_target_pairs={{0,3},{1,0},{2,1},{3,2},{4,7},{5,4},{6,5},{7,6},{8,11},{9,8},{10,9... | collective-permute-start | bytes 196616 | tf_op jit(solution)/shard_map/ppermute | solution.py:609
  9.1 1.9 %collective-permute-done.2.low_y = f32[4,4,8,128]{3,2,1,0:T(8,128)S(1)} collective-permute-done((f32[4,4,8,128]{3,2,1,0:T(8,128)S(1)}, f32[4,4,8,128]{3,2,1,0:T(8,128)S(1)}, u32[]{:S(2)}, u32[]{:S(2)}) %collective-permute-start.2) | collective-permute-done | bytes 65568 | tf_op jit(solution)/shard_map/ppermute | solution.py:609
  11.0 1.1 %shard_map.113 = (f32[264,128]{1,0:T(8,128)S(1)}, f32[2,128,128]{2,1,0:T(8,128)S(1)}) custom-call(f32[3,4,128,128]{3,2,1,0:T(8,128)} %flow.9, f32[4,128,128]{2,1,0:T(8,128)} %thermal.11, s32[4,128,128]{2,1,0:T(8,128)} %flag.5, f32[4,4,8,128]{3,2,1,0:T(8,128)S(1)} %collective-permute-done.2.low_y, f32[4,4,8,128]{3,2,1,0:T(8,128)S(1)} %collective-permute-done.3.high_y), custom_call_target="tpu_custom_call" | custom-call | tf_op jit(solution)/shard_map/pallas_call | solution.py:624
  12.6 1.5 %collective-permute-start.7 = (f32[2,128,128]{2,1,0:T(8,128)S(1)}, f32[2,128,128]{2,1,0:T(8,128)S(1)}, u32[]{:S(2)}, u32[]{:S(2)}) collective-permute-start(f32[2,128,128]{2,1,0:T(8,128)S(1)} %get-tuple-element.42), channel_id=1, source_target_pairs={{0,4},{4,8},{8,12},{12,0},{1,5},{5,9},{9,13},{13,1},{2,6},{6,10},{... | collective-permute-start | bytes 393224 | tf_op jit(solution)/shard_map/ppermute | solution.py:609
  14.1 3.2 %collective-permute-done.low_x = f32[776,128]{1,0:T(8,128)S(1)} collective-permute-done((f32[776,128]{1,0:T(8,128)S(1)}, f32[776,128]{1,0:T(8,128)S(1)}, u32[]{:S(2)}, u32[]{:S(2)}) %collective-permute-start) | collective-permute-done | bytes 397344 | tf_op jit(solution)/shard_map/ppermute | solution.py:609
  17.3 7.3 %collective-permute-done.1.high_x = f32[776,128]{1,0:T(8,128)S(1)} collective-permute-done((f32[776,128]{1,0:T(8,128)S(1)}, f32[776,128]{1,0:T(8,128)S(1)}, u32[]{:S(2)}, u32[]{:S(2)}) %collective-permute-start.1) | collective-permute-done | bytes 397344 | tf_op jit(solution)/shard_map/ppermute | solution.py:609
  24.8 3.9 %collective-permute-done.4.extra = f32[264,128]{1,0:T(8,128)S(1)} collective-permute-done((f32[264,128]{1,0:T(8,128)S(1)}, f32[264,128]{1,0:T(8,128)S(1)}, u32[]{:S(2)}, u32[]{:S(2)}) %collective-permute-start.4) | collective-permute-done | bytes 135200 | tf_op jit(solution)/shard_map/ppermute | solution.py:609
  28.7 1.8 %shard_map.116 = (f32[3,4,128,128]{3,2,1,0:T(8,128)S(1)}, f32[128,128]{1,0:T(8,128)S(1)}) custom-call(f32[3,4,128,128]{3,2,1,0:T(8,128)S(1)} %copy-done, f32[776,128]{1,0:T(8,128)S(1)} %collective-permute-done.low_x, f32[776,128]{1,0:T(8,128)S(1)} %collective-permute-done.1.high_x, f32[4,128,128]{2,1,0:T(8,128)S(1)} %copy-done.1, ...), custom_call_target="tpu_custom_call" | custom-call | flops 1610612736 | bytes 1703936 | tf_op jit(solution)/shard_map/pallas_call | solution.py:30
  30.6 0.8 %shard_map.117 = (f32[4,128,128]{2,1,0:T(8,128)S(1)}, f32[256,128]{1,0:T(8,128)S(1)}) custom-call(f32[3,4,128,128]{3,2,1,0:T(8,128)S(1)} %get-tuple-element.37.star, f32[128,128]{1,0:T(8,128)S(1)} %get-tuple-element.38.side_x, f32[128,128]{1,0:T(8,128)S(1)} %copy-done.2, f32[128,128]{1,0:T(8,128)S(1)} %copy-done.2, ...), custom_call_target="tpu_custom_call" | custom-call | flops 1073741824 | bytes 786432 | tf_op jit(solution)/shard_map/pallas_call | solution.py:30
  32.3 2.0 %collective-permute-start.8 = (f32[56,128]{1,0:T(8,128)S(1)}, f32[56,128]{1,0:T(8,128)S(1)}, u32[]{:S(2)}, u32[]{:S(2)}) collective-permute-start(f32[56,128]{1,0:T(8,128)S(1)} %get-tuple-element.43.faces), channel_id=1, source_target_pairs={{0,4},{1,5},{2,6},{3,7},{4,0},{5,1},{6,2},{7,3},{8,12},{9,13},{10,... | collective-permute-start | bytes 86024 | tf_op jit(solution)/shard_map/ppermute | solution.py:619
  34.3 1.3 %collective-permute-start.14 = (f32[2,128,128]{2,1,0:T(8,128)S(1)}, f32[2,128,128]{2,1,0:T(8,128)S(1)}, u32[]{:S(2)}, u32[]{:S(2)}) collective-permute-start(f32[2,128,128]{2,1,0:T(8,128)S(1)} %get-tuple-element.48), channel_id=1, source_target_pairs={{0,12},{4,0},{8,4},{12,8},{1,13},{5,1},{9,5},{13,9},{2,14},{6,2},{... | collective-permute-start | bytes 393224 | tf_op jit(solution)/shard_map/ppermute | solution.py:609
  35.5 2.3 %collective-permute-done.8.other_faces = f32[56,128]{1,0:T(8,128)S(1)} collective-permute-done((f32[56,128]{1,0:T(8,128)S(1)}, f32[56,128]{1,0:T(8,128)S(1)}, u32[]{:S(2)}, u32[]{:S(2)}) %collective-permute-start.8) | collective-permute-done | bytes 28704 | tf_op jit(solution)/shard_map/ppermute | solution.py:619
  38.5 3.5 %collective-permute-start.10 = (f32[16,128]{1,0:T(8,128)S(1)}, f32[16,128]{1,0:T(8,128)S(1)}, u32[]{:S(2)}, u32[]{:S(2)}) collective-permute-start(f32[16,128]{1,0:T(8,128)S(1)} %get-tuple-element.46), channel_id=1, source_target_pairs={{0,1},{1,2},{2,3},{3,0},{4,5},{5,6},{6,7},{7,4},{8,9},{9,10},{10,1... | collective-permute-start | bytes 24584 | tf_op jit(solution)/shard_map/ppermute | solution.py:619
  42.7 1.9 %shard_map.120 = (f32[4,128,128]{2,1,0:T(8,128)}, f32[8,128]{1,0:T(8,128)S(1)}) custom-call(s32[8]{0:T(128)S(1)} %copy-done.6, s32[8]{0:T(128)S(1)} %copy-done.7, f32[4,128,128]{2,1,0:T(8,128)S(1)} %copy-done.1, f32[2,128,128]{2,1,0:T(8,128)S(1)} %collective-permute-done.7._.low_x, f32[2,128,128]{2,1,0:T(8,128)S(1)} %collective-permute-done.14.high_x, ...), custom_call_target="tpu_custom_call" | custom-call | flops 268435456 | bytes 532480 | tf_op jit(solution)/shard_map/pallas_call | solution.py:30
  44.6 1.5 %collective-permute-done.13.refs_7_ = f32[16,128]{1,0:T(8,128)S(1)} collective-permute-done((f32[16,128]{1,0:T(8,128)S(1)}, f32[16,128]{1,0:T(8,128)S(1)}, u32[]{:S(2)}, u32[]{:S(2)}) %collective-permute-start.13) | collective-permute-done | bytes 8224 | tf_op jit(solution)/shard_map/ppermute | solution.py:619
  46.1 1.0 %shard_map.121 = (f32[5,128,128]{2,1,0:T(8,128)S(1)}, f32[5,128,128]{2,1,0:T(8,128)S(1)}, f32[40,128]{1,0:T(8,128)S(1)}, f32[48,128]{1,0:T(8,128)S(1)}) custom-call(f32[4,128,128]{2,1,0:T(8,128)S(1)} %get-tuple-element.40.source.refs_0_, f32[296,128]{1,0:T(8,128)S(1)} %get-tuple-element.44.refs_1_, f32[296,128]{1,0:T(8,128)S(1)} %collective-permute-done.9.refs_2_, ...), custom_call_target="tpu_custom_call" | custom-call | flops 1048576 | bytes 1400832 | tf_op jit(solution)/shard_map/pallas_call | solution.py:30
  47.2 1.3 %collective-permute-start.17 = (f32[40,128]{1,0:T(8,128)S(1)}, f32[40,128]{1,0:T(8,128)S(1)}, u32[]{:S(2)}, u32[]{:S(2)}) collective-permute-start(f32[40,128]{1,0:T(8,128)S(1)} %get-tuple-element.55.refs_0_), channel_id=1, source_target_pairs={{0,3},{1,0},{2,1},{3,2},{4,7},{5,4},{6,5},{7,6},{8,11},{9,8},{10,9... | collective-permute-start | bytes 61448 | tf_op jit(solution)/shard_map/ppermute | solution.py:609
  48.4 1.2 %collective-permute-start.16 = (f32[40,128]{1,0:T(8,128)S(1)}, f32[40,128]{1,0:T(8,128)S(1)}, u32[]{:S(2)}, u32[]{:S(2)}) collective-permute-start(f32[40,128]{1,0:T(8,128)S(1)} %get-tuple-element.55.refs_0_), channel_id=1, source_target_pairs={{0,2},{1,3},{2,0},{3,1},{4,6},{5,7},{6,4},{7,5},{8,10},{9,11},{10,... | collective-permute-start | bytes 61448 | tf_op jit(solution)/shard_map/ppermute | solution.py:609
  49.6 1.4 %shard_map.122 = (f32[5,128,128]{2,1,0:T(8,128)S(1)}, f32[5,128,128]{2,1,0:T(8,128)S(1)}) custom-call(f32[5,128,128]{2,1,0:T(8,128)S(1)} %get-tuple-element.50.precond, f32[5,128,128]{2,1,0:T(8,128)S(1)} %get-tuple-element.51.image, f32[128,128]{1,0:T(8,128)S(1)} %copy-done.2, f32[128,128]{1,0:T(8,128)S(1)} %copy-done.2), custom_call_target="tpu_custom_call" | custom-call | flops 1048576 | bytes 1310720 | tf_op jit(solution)/shard_map/pallas_call | solution.py:30
  51.1 1.1 %collective-permute-done.16.refs_2_ = f32[40,128]{1,0:T(8,128)S(1)} collective-permute-done((f32[40,128]{1,0:T(8,128)S(1)}, f32[40,128]{1,0:T(8,128)S(1)}, u32[]{:S(2)}, u32[]{:S(2)}) %collective-permute-start.16) | collective-permute-done | bytes 20512 | tf_op jit(solution)/shard_map/ppermute | solution.py:609
  52.8 1.2 %shard_map.123 = (f32[3,4,128,128]{3,2,1,0:T(8,128)}, f32[4,128,128]{2,1,0:T(8,128)}) custom-call(f32[3,4,128,128]{3,2,1,0:T(8,128)S(1)} %get-tuple-element.37.star, f32[5,128,128]{2,1,0:T(8,128)S(1)} %get-tuple-element.52.precond, f32[5,128,128]{2,1,0:T(8,128)S(1)} %get-tuple-element.53.image, f32[48,128]{1,0:T(8,128)S(1)} %get-tuple-element.54.faces, ...), custom_call_target="tpu_custom_call" | custom-call | flops 1048576 | bytes 2097152 | tf_op jit(solution)/shard_map/pallas_call | solution.py:30
  (41 shorter events, 3.6 us)
Async XLA Ops:
  0.6 11.5 %copy-start.5 = (f32[128,128]{1,0:T(8,128)S(1)}, f32[128,128]{1,0:T(8,128)}, u32[]{:S(2)}) copy-start(f32[128,128]{1,0:T(8,128)} %constant.10.clone.diagonal) | copy-start | bytes 196612
  0.6 24.0 %copy-start.1 = (f32[4,128,128]{2,1,0:T(8,128)S(1)}, f32[4,128,128]{2,1,0:T(8,128)}, u32[]{:S(2)}) copy-start(f32[4,128,128]{2,1,0:T(8,128)} %thermal.11) | copy-start | bytes 786436
  0.7 24.0 %copy-start = (f32[3,4,128,128]{3,2,1,0:T(8,128)S(1)}, f32[3,4,128,128]{3,2,1,0:T(8,128)}, u32[]{:S(2)}) copy-start(f32[3,4,128,128]{3,2,1,0:T(8,128)} %flow.9) | copy-start | bytes 2359300
  0.7 24.0 %copy-start.3 = (s32[4,128,128]{2,1,0:T(8,128)S(1)}, s32[4,128,128]{2,1,0:T(8,128)}, u32[]{:S(2)}) copy-start(s32[4,128,128]{2,1,0:T(8,128)} %flag.5) | copy-start | bytes 786436
  2.1 15.2 %collective-permute-start = (f32[776,128]{1,0:T(8,128)S(1)}, f32[776,128]{1,0:T(8,128)S(1)}, u32[]{:S(2)}, u32[]{:S(2)}) collective-permute-start(f32[776,128]{1,0:T(8,128)S(1)} %get-tuple-element.31), channel_id=1, source_target_pairs={{0,4},{4,8},{8,12},{12,0},{1,5},{5,9},{9,13},{13,1},{2,6},{6,10},{... | collective-permute-start | bytes 1191944 | tf_op jit(solution)/shard_map/ppermute | solution.py:609
  5.2 19.4 %collective-permute-start.1 = (f32[776,128]{1,0:T(8,128)S(1)}, f32[776,128]{1,0:T(8,128)S(1)}, u32[]{:S(2)}, u32[]{:S(2)}) collective-permute-start(f32[776,128]{1,0:T(8,128)S(1)} %get-tuple-element.32), channel_id=1, source_target_pairs={{0,12},{4,0},{8,4},{12,8},{1,13},{5,1},{9,5},{13,9},{2,14},{6,2},{... | collective-permute-start | bytes 1191944 | tf_op jit(solution)/shard_map/ppermute | solution.py:609
  7.3 3.7 %collective-permute-start.2 = (f32[4,4,8,128]{3,2,1,0:T(8,128)S(1)}, f32[4,4,8,128]{3,2,1,0:T(8,128)S(1)}, u32[]{:S(2)}, u32[]{:S(2)}) collective-permute-start(f32[4,4,8,128]{3,2,1,0:T(8,128)S(1)} %get-tuple-element.33), channel_id=1, source_target_pairs={{0,1},{1,2},{2,3},{3,0},{4,5},{5,6},{6,7},{7,4},{8,9},{9,10},{10,1... | collective-permute-start | bytes 196616 | tf_op jit(solution)/shard_map/ppermute | solution.py:609
  7.3 3.7 %collective-permute-start.3 = (f32[4,4,8,128]{3,2,1,0:T(8,128)S(1)}, f32[4,4,8,128]{3,2,1,0:T(8,128)S(1)}, u32[]{:S(2)}, u32[]{:S(2)}) collective-permute-start(f32[4,4,8,128]{3,2,1,0:T(8,128)S(1)} %get-tuple-element.34), channel_id=1, source_target_pairs={{0,3},{1,0},{2,1},{3,2},{4,7},{5,4},{6,5},{7,6},{8,11},{9,8},{10,9... | collective-permute-start | bytes 196616 | tf_op jit(solution)/shard_map/ppermute | solution.py:609
  12.1 16.6 %collective-permute-start.4 = (f32[264,128]{1,0:T(8,128)S(1)}, f32[264,128]{1,0:T(8,128)S(1)}, u32[]{:S(2)}, u32[]{:S(2)}) collective-permute-start(f32[264,128]{1,0:T(8,128)S(1)} %get-tuple-element.35), channel_id=1, source_target_pairs={{0,4},{4,8},{8,12},{12,0},{1,5},{5,9},{9,13},{13,1},{2,6},{6,10},{... | collective-permute-start | bytes 405512 | tf_op jit(solution)/shard_map/ppermute | solution.py:609
  12.6 19.0 %collective-permute-start.7 = (f32[2,128,128]{2,1,0:T(8,128)S(1)}, f32[2,128,128]{2,1,0:T(8,128)S(1)}, u32[]{:S(2)}, u32[]{:S(2)}) collective-permute-start(f32[2,128,128]{2,1,0:T(8,128)S(1)} %get-tuple-element.42), channel_id=1, source_target_pairs={{0,4},{4,8},{8,12},{12,0},{1,5},{5,9},{9,13},{13,1},{2,6},{6,10},{... | collective-permute-start | bytes 393224 | tf_op jit(solution)/shard_map/ppermute | solution.py:609
  24.7 5.8 %collective-permute-start.5 = (f32[4,128]{1,0:T(4,128)S(1)}, f32[4,128]{1,0:T(4,128)S(1)}, u32[]{:S(2)}, u32[]{:S(2)}) collective-permute-start(f32[4,128]{1,0:T(4,128)S(1)} %shard_map.115._), channel_id=1, source_target_pairs={{0,1},{1,2},{2,3},{3,0},{4,5},{5,6},{6,7},{7,4},{8,9},{9,10},{10,1... | collective-permute-start | bytes 6152 | tf_op jit(solution)/shard_map/ppermute | solution.py:609
  31.4 6.5 %collective-permute-start.6 = (f32[256,128]{1,0:T(8,128)S(1)}, f32[256,128]{1,0:T(8,128)S(1)}, u32[]{:S(2)}, u32[]{:S(2)}) collective-permute-start(f32[256,128]{1,0:T(8,128)S(1)} %get-tuple-element.41.message), channel_id=1, source_target_pairs={{0,4},{1,5},{2,6},{3,7},{4,0},{5,1},{6,2},{7,3},{8,12},{9,13},{10,... | collective-permute-start | bytes 393224 | tf_op jit(solution)/shard_map/ppermute | solution.py:619
  32.3 10.5 %copy-start.6 = (s32[8]{0:T(128)S(1)}, s32[8]{0:T(128)}, u32[]{:S(2)}) copy-start(s32[8]{0:T(128)} %spots_a.1) | copy-start | bytes 100
  32.3 10.5 %copy-start.7 = (s32[8]{0:T(128)S(1)}, s32[8]{0:T(128)}, u32[]{:S(2)}) copy-start(s32[8]{0:T(128)} %spots_b.1) | copy-start | bytes 100
  32.3 5.6 %collective-permute-start.8 = (f32[56,128]{1,0:T(8,128)S(1)}, f32[56,128]{1,0:T(8,128)S(1)}, u32[]{:S(2)}, u32[]{:S(2)}) collective-permute-start(f32[56,128]{1,0:T(8,128)S(1)} %get-tuple-element.43.faces), channel_id=1, source_target_pairs={{0,4},{1,5},{2,6},{3,7},{4,0},{5,1},{6,2},{7,3},{8,12},{9,13},{10,... | collective-permute-start | bytes 86024 | tf_op jit(solution)/shard_map/ppermute | solution.py:619
  34.3 7.9 %collective-permute-start.14 = (f32[2,128,128]{2,1,0:T(8,128)S(1)}, f32[2,128,128]{2,1,0:T(8,128)S(1)}, u32[]{:S(2)}, u32[]{:S(2)}) collective-permute-start(f32[2,128,128]{2,1,0:T(8,128)S(1)} %get-tuple-element.48), channel_id=1, source_target_pairs={{0,12},{4,0},{8,4},{12,8},{1,13},{5,1},{9,5},{13,9},{2,14},{6,2},{... | collective-permute-start | bytes 393224 | tf_op jit(solution)/shard_map/ppermute | solution.py:609
  38.0 8.1 %collective-permute-start.9 = (f32[296,128]{1,0:T(8,128)S(1)}, f32[296,128]{1,0:T(8,128)S(1)}, u32[]{:S(2)}, u32[]{:S(2)}) collective-permute-start(f32[296,128]{1,0:T(8,128)S(1)} %get-tuple-element.44.refs_1_), channel_id=1, source_target_pairs={{0,8},{1,9},{2,10},{3,11},{4,12},{5,13},{6,14},{7,15},{8,0},{9,1},... | collective-permute-start | bytes 454664 | tf_op jit(solution)/shard_map/ppermute | solution.py:619
  38.5 6.1 %collective-permute-start.11 = (f32[16,128]{1,0:T(8,128)S(1)}, f32[16,128]{1,0:T(8,128)S(1)}, u32[]{:S(2)}, u32[]{:S(2)}) collective-permute-start(f32[16,128]{1,0:T(8,128)S(1)} %get-tuple-element.46), channel_id=1, source_target_pairs={{0,9},{1,10},{2,11},{3,8},{4,13},{5,14},{6,15},{7,12},{8,1},{9,2},... | collective-permute-start | bytes 24584 | tf_op jit(solution)/shard_map/ppermute | solution.py:619
  38.5 6.1 %collective-permute-start.10 = (f32[16,128]{1,0:T(8,128)S(1)}, f32[16,128]{1,0:T(8,128)S(1)}, u32[]{:S(2)}, u32[]{:S(2)}) collective-permute-start(f32[16,128]{1,0:T(8,128)S(1)} %get-tuple-element.46), channel_id=1, source_target_pairs={{0,1},{1,2},{2,3},{3,0},{4,5},{5,6},{6,7},{7,4},{8,9},{9,10},{10,1... | collective-permute-start | bytes 24584 | tf_op jit(solution)/shard_map/ppermute | solution.py:619
  42.0 4.1 %collective-permute-start.13 = (f32[16,128]{1,0:T(8,128)S(1)}, f32[16,128]{1,0:T(8,128)S(1)}, u32[]{:S(2)}, u32[]{:S(2)}) collective-permute-start(f32[16,128]{1,0:T(8,128)S(1)} %get-tuple-element.47), channel_id=1, source_target_pairs={{0,11},{1,8},{2,9},{3,10},{4,15},{5,12},{6,13},{7,14},{8,3},{9,0},... | collective-permute-start | bytes 24584 | tf_op jit(solution)/shard_map/ppermute | solution.py:619
  42.2 4.0 %collective-permute-start.12 = (f32[16,128]{1,0:T(8,128)S(1)}, f32[16,128]{1,0:T(8,128)S(1)}, u32[]{:S(2)}, u32[]{:S(2)}) collective-permute-start(f32[16,128]{1,0:T(8,128)S(1)} %get-tuple-element.47), channel_id=1, source_target_pairs={{0,3},{1,0},{2,1},{3,2},{4,7},{5,4},{6,5},{7,6},{8,11},{9,8},{10,9... | collective-permute-start | bytes 24584 | tf_op jit(solution)/shard_map/ppermute | solution.py:619
  47.2 3.9 %collective-permute-start.17 = (f32[40,128]{1,0:T(8,128)S(1)}, f32[40,128]{1,0:T(8,128)S(1)}, u32[]{:S(2)}, u32[]{:S(2)}) collective-permute-start(f32[40,128]{1,0:T(8,128)S(1)} %get-tuple-element.55.refs_0_), channel_id=1, source_target_pairs={{0,3},{1,0},{2,1},{3,2},{4,7},{5,4},{6,5},{7,6},{8,11},{9,8},{10,9... | collective-permute-start | bytes 61448 | tf_op jit(solution)/shard_map/ppermute | solution.py:609
  48.4 3.8 %collective-permute-start.16 = (f32[40,128]{1,0:T(8,128)S(1)}, f32[40,128]{1,0:T(8,128)S(1)}, u32[]{:S(2)}, u32[]{:S(2)}) collective-permute-start(f32[40,128]{1,0:T(8,128)S(1)} %get-tuple-element.55.refs_0_), channel_id=1, source_target_pairs={{0,2},{1,3},{2,0},{3,1},{4,6},{5,7},{6,4},{7,5},{8,10},{9,11},{10,... | collective-permute-start | bytes 61448 | tf_op jit(solution)/shard_map/ppermute | solution.py:609
  49.6 3.2 %collective-permute-start.15 = (f32[40,128]{1,0:T(8,128)S(1)}, f32[40,128]{1,0:T(8,128)S(1)}, u32[]{:S(2)}, u32[]{:S(2)}) collective-permute-start(f32[40,128]{1,0:T(8,128)S(1)} %get-tuple-element.55.refs_0_), channel_id=1, source_target_pairs={{0,1},{1,2},{2,3},{3,0},{4,5},{5,6},{6,7},{7,4},{8,9},{9,10},{10,1... | collective-permute-start | bytes 61448 | tf_op jit(solution)/shard_map/ppermute | solution.py:609
  (2 other events, 6.8 us)

commit v8 on v7

--- a/solution.py
+++ b/solution.py
@@ -22,19 +22,21 @@
 SMEM = pl.BlockSpec(memory_space=pltpu.SMEM)
 
 
-def call(body, operands, shapes, scratch=(), scalars=0, loose=0, flops=1 << 20):
+def call(body, operands, shapes, scratch=(), scalars=0, loose=0, semaphores=0, flops=1 << 20):
     out_shape = [jax.ShapeDtypeStruct(shape, F32) for shape in shapes]
     moved = 4 * sum(math.prod(shape) for shape in shapes)
     held = moved + 4 * sum(operand.size for operand in operands)
     held += 4 * sum(math.prod(space.shape) for space in scratch)
+    where = pl.BlockSpec(memory_space=pl.ANY) if semaphores else VMEM
+    waits = [pltpu.SemaphoreType.DMA((semaphores,))] if semaphores else []
     return pl.pallas_call(
         body,
         out_shape=out_shape,
         in_specs=[SMEM] * scalars
         + [VMEM] * (len(operands) - scalars - loose)
         + [pl.BlockSpec(memory_space=pl.ANY)] * loose,
-        out_specs=[VMEM] * len(shapes),
-        scratch_shapes=list(scratch),
+        out_specs=[where] * len(shapes),
+        scratch_shapes=list(scratch) + waits,
         compiler_params=pltpu.CompilerParams(vmem_limit_bytes=held + (4 << 20)),
         cost_estimate=pl.CostEstimate(flops=flops, bytes_accessed=2 * moved, transcendentals=0),
     )(*operands)
@@ -42,6 +44,41 @@
 
 def dot(left, right):
     return jnp.dot(left, right, precision=lax.Precision.HIGHEST, preferred_element_type=F32)
+
+
+def split(cells):
+    high = cells.astype(jnp.bfloat16)
+    return high, (cells - high.astype(F32)).astype(jnp.bfloat16)
+
+
+def folded(product):
+    half = product.shape[1] // 2
+    return product[:, :half] + product[:, half:]
+
+
+def packed_tables(left, right):
+    left_high, left_low = split(np.asarray(left, np.float32))
+    right_high, right_low = split(np.asarray(right, np.float32))
+    zero = np.zeros_like(right_low)
+    return (
+        jnp.asarray(np.concatenate([left_high, left_low], 1)),
+        jnp.asarray(np.block([[right_high, right_low], [right_high, zero]])),
+    )
+
+
+def transformed(planes, left, right):
+    rows = planes[0].shape[0]
+    high, low = split(jnp.concatenate(planes, 0))
+    cells = jnp.concatenate([high, low], 1)
+    cells = folded(jnp.dot(cells, right[...], preferred_element_type=F32))
+    out = []
+    for index in range(len(planes)):
+        high, low = split(cells[index * rows : (index + 1) * rows])
+        upper = jnp.concatenate([high, low], 1)
+        lower = jnp.concatenate([high, jnp.zeros_like(low)], 1)
+        cells_ = jnp.concatenate([upper, lower], 0)
+        out.append(folded(jnp.dot(left[...], cells_, preferred_element_type=F32)))
+    return out
 
 
 def total(cells):
@@ -83,23 +120,38 @@
     return jnp.sum(jnp.where(same, row, 0.0), axis=1, keepdims=True)
 
 
-def advance(layers, padded, index, speed, start=0):
+def coefficients(speed, scale):
+    factors = [0.5 * TIME_INCREMENT * jnp.abs(each) for each in speed]
+    if scale is not None:
+        factors = [each * scale for each in factors]
+    centre = (1.0 if scale is None else scale) - 3.0 * (factors[0] + factors[1] + factors[2])
+    near, far = 4.0 * factors[2], -factors[2]
+    ahead = speed[2] >= 0.0
+    lane = lax.broadcasted_iota(jnp.int32, near.shape, 1)
+    width = near.shape[1]
+    depth = (
+        jnp.where(ahead & (lane >= 1), near, 0.0),
+        jnp.where(ahead & (lane >= 2), far, 0.0),
+        jnp.where(ahead | (lane >= width - 1), 0.0, near),
+        jnp.where(ahead | (lane >= width - 2), 0.0, far),
+    )
+    return centre, speed[0] >= 0.0, factors[0], speed[1] >= 0.0, factors[1], depth
+
+
+def advance(layers, padded, index, weights, start=0):
     middle = layers[2]
-    rows = middle.shape[0]
-    speed_x, speed_y, speed_z = speed
-    ahead = speed_x >= 0.0
-    near = jnp.where(ahead, layers[1], layers[3])
-    far = jnp.where(ahead, layers[0], layers[4])
-    rate = jnp.abs(speed_x) * (1.5 * middle - 2.0 * near + 0.5 * far)
-    ahead = speed_y >= 0.0
-    near = jnp.where(ahead, padded[index, pl.ds(7 + start, rows), :], padded[index, pl.ds(9 + start, rows), :])
-    far = jnp.where(ahead, padded[index, pl.ds(6 + start, rows), :], padded[index, pl.ds(10 + start, rows), :])
-    rate = rate + jnp.abs(speed_y) * (1.5 * middle - 2.0 * near + 0.5 * far)
-    ahead = speed_z >= 0.0
-    near = jnp.where(ahead, lane_shift(middle, -1), lane_shift(middle, 1))
-    far = jnp.where(ahead, lane_shift(middle, -2), lane_shift(middle, 2))
-    rate = rate + jnp.abs(speed_z) * (1.5 * middle - 2.0 * near + 0.5 * far)
-    return middle - TIME_INCREMENT * rate
+    rows, width = middle.shape
+    centre, ahead_x, factor_x, ahead_y, factor_y, depth = weights
+    near = jnp.where(ahead_x, layers[1], layers[3])
+    far = jnp.where(ahead_x, layers[0], layers[4])
+    moved = centre * middle + factor_x * (4.0 * near - far)
+    beside = lambda offset: padded[index, pl.ds(8 + offset + start, rows), :]
+    near = jnp.where(ahead_y, beside(-1), beside(1))
+    far = jnp.where(ahead_y, beside(-2), beside(2))
+    moved = moved + factor_y * (4.0 * near - far)
+    for factor, offset in zip(depth, (1, 2, width - 1, width - 2)):
+        moved = moved + factor * pltpu.roll(middle, offset, 1)
+    return moved
 
 
 def pad_rows(padded, index, before, middle, after):
@@ -116,7 +168,8 @@
     speed = [flow[part, index, span, :] for part in range(3)]
     drag = 1.0 / (1.0 + TIME_INCREMENT * DRAG_RATE * flag[index, span, :].astype(F32))
     top = lax.broadcasted_iota(jnp.int32, (count, depth), 1) == depth - 1
-    pull = -MARANGONI * 0.5 * TIME_INCREMENT
+    pull = jnp.where(top, (-MARANGONI * 0.5 * TIME_INCREMENT) * drag, 0.0)
+    weights = coefficients(speed, drag)
     out = []
     for part in parts:
         around = []
@@ -129,16 +182,16 @@
                 around.append(high_x[pl.ds(first, count), :])
             else:
                 around.append(flow[part, other, span, :])
-        moved = advance(around, padded, part, speed, start)
+        moved = advance(around, padded, part, weights, start)
         if part == 0:
             edge = lambda halo: column(halo[pl.ds(halo.shape[0] - 8, 1), pl.ds(0, rows)])
             behind = thermal[index - 1] if index > 0 else edge(low_x)
             before = thermal[index + 1] if index + 1 < layers else edge(high_x)
-            moved = moved + jnp.where(top, pull * (before - behind), 0.0)
+            moved = moved + pull * (before - behind)
         if part == 1:
             slope = padded[3, pl.ds(9 + start, count), :] - padded[3, pl.ds(7 + start, count), :]
-            moved = moved + jnp.where(top, pull * slope, 0.0)
-        out.append(moved * drag)
+            moved = moved + pull * slope
+        out.append(moved)
     return out
 
 
@@ -177,28 +230,30 @@
     beside = extra[pl.ds(2 * rows, 8), pl.ds(0, depth)]
     pad_rows(padded, 0, beside[2:4], plane(1), beside[4:6])
     around = [extra[pl.ds(0, rows), pl.ds(0, depth)], plane(0), plane(1), flow[0, 0], flow[0, 1]]
-    moved = advance(around, padded, 0, [plane(1), plane(3), plane(5)])
     top = lax.broadcasted_iota(jnp.int32, (rows, depth), 1) == depth - 1
-    pull = -MARANGONI * 0.5 * TIME_INCREMENT
+    drag = 1.0 / (1.0 + TIME_INCREMENT * DRAG_RATE * extra[pl.ds(rows, rows), pl.ds(0, depth)])
+    pull = jnp.where(top, (-MARANGONI * 0.5 * TIME_INCREMENT) * drag, 0.0)
     behind = column(extra[pl.ds(2 * rows, 1), pl.ds(0, rows)])
-    moved = moved + jnp.where(top, pull * (thermal[0] - behind), 0.0)
-    drag = 1.0 + TIME_INCREMENT * DRAG_RATE * extra[pl.ds(rows, rows), pl.ds(0, depth)]
-    side_x[...] = moved / drag
+    weights = coefficients([plane(1), plane(3), plane(5)], drag)
+    side_x[...] = advance(around, padded, 0, weights) + pull * (thermal[0] - behind)
 
 
 def transform_kernel(
-    group, length, star, side_x, table_y, table_z, ratio, _, source, message, rows_
+    group, length, star, side_x, left, right, ratio, _, source, message, rows_
 ):
     _, layers, rows, depth = star.shape
     first = position(group) * layers
     rows_[pl.ds(0, 8), :] = jnp.zeros((8, depth), F32)
+    planes = []
     for index in range(layers):
         rows_[pl.ds(8, rows), :] = star[1, index]
         behind = star[0, index - 1] if index > 0 else side_x[...]
         sink = star[0, index] - behind
         sink = sink + (star[1, index] - rows_[pl.ds(7, rows), :])
         sink = sink + (star[2, index] - lane_shift(star[2, index], -1))
-        source[index] = dot(dot(table_y[...], -sink), table_z[...])
+        planes.append(-sink)
+    for index, plane in enumerate(transformed(planes, left, right)):
+        source[index] = plane
     forward = source[0]
     for index in range(1, layers):
         forward = source[index] + ratio[first + index] * forward
@@ -304,7 +359,8 @@
                 around.append(thermal[other])
         speed = [flow[part, index] for part in range(3)]
         gain = TIME_INCREMENT * column(laser_row(index, layers, rows, spots_a, spots_b))
-        warmed[index] = advance(around, padded, 0, speed) + jnp.where(top, gain, 0.0)
+        moved = advance(around, padded, 0, coefficients(speed, None))
+        warmed[index] = moved + jnp.where(top, gain, 0.0)
 
 
 def tables_kernel(group, layers, diagonal, ratio, weight):
@@ -346,10 +402,20 @@
     weight[4 * rounds] = inner * green(first + layers)
 
 
-def face_rows(plane, edge):
+def grouped(plane):
+    return plane.reshape(plane.shape[0] // 8, 8, plane.shape[1])
+
+
+def signs(depth):
+    row = lax.broadcasted_iota(jnp.int32, (8, depth), 0)
+    return jnp.where(row % 2 == 0, 1.0, -1.0)
+
+
+def face_rows(plane, lead):
+    sums = jnp.sum(plane * lead, axis=0)
     return (
-        jnp.sum(plane * edge[0], axis=0, keepdims=True),
-        jnp.sum(plane * edge[1], axis=0, keepdims=True),
+        jnp.sum(sums, axis=0, keepdims=True),
+        jnp.sum(sums * signs(sums.shape[1]), axis=0, keepdims=True),
     )
 
 
@@ -375,19 +441,23 @@
         energy = energy + source[index] * value
     faces[pl.ds(3 * length, 8), :] = jnp.broadcast_to(total(energy), (8, depth))
 
+    lead = grouped(edge[...])
+    zero = grouped(zero)
+
     def down(index, previous):
         inside = (index >= first) & (index < first + layers)
         own = jnp.where(inside, source[jnp.clip(index - first, 0, layers - 1)], 0.0)
-        current = own + edge[0] * faces[pl.ds(2 * length + index, 1), :] + ratio[index] * previous
-        sweep[index] = current
+        row = faces[pl.ds(2 * length + index, 1), :]
+        current = grouped(own) + lead * row + grouped(ratio[index]) * previous
+        sweep[index] = current.reshape(rows, depth)
         return current
 
     loop(0, length, down, zero)
 
     def up(back, following):
         index = length - 1 - back
-        value = ratio[index + 1] * (sweep[index] + following)
-        low, high = face_rows(value, edge)
+        value = grouped(ratio[index + 1]) * (grouped(sweep[index]) + following)
+        low, high = face_rows(value, lead)
         faces[pl.ds(index, 1), :] = low
         faces[pl.ds(length + index, 1), :] = high
         return value
@@ -433,27 +503,28 @@
 
 
 def late_solve(length, message, other, ratio, edge, late, sweep):
-    rows, depth = edge.shape[1:]
+    rows, depth = edge.shape
+    lead = grouped(edge[...])
     own = pl.ds(2 * rows + length, length)
     late[pl.ds(0, length), :] = message[own, :] + other[own, :]
 
     def down(index, previous):
-        current = edge[0] * late[pl.ds(index, 1), :] + ratio[index] * previous
-        sweep[index] = current
+        current = lead * late[pl.ds(index, 1), :] + grouped(ratio[index]) * previous
+        sweep[index] = current.reshape(rows, depth)
         return current
 
-    zero = jnp.zeros((rows, depth), F32)
+    zero = jnp.zeros(lead.shape, F32)
     loop(0, length, down, zero)
 
     def up(back, following):
         index = length - 1 - back
-        value = ratio[index + 1] * (sweep[index] + following)
-        sweep[index] = value
-        late[pl.ds(length + index, 1), :] = jnp.sum(value * edge[0], axis=0, keepdims=True)
+        value = grouped(ratio[index + 1]) * (grouped(sweep[index]) + following)
+        sweep[index] = value.reshape(rows, depth)
+        late[pl.ds(length + index, 1), :] = face_rows(value, lead)[0]
         return value
 
     loop(0, length, up, zero)
-    sweep[length] = zero
+    sweep[length] = jnp.zeros((rows, depth), F32)
 
 
 def close_kernel(
@@ -497,7 +568,8 @@
     for index in range(layers - 1, -1, -1):
         value = ratio[first + index + 1] * (precond[index] + value)
         precond[index] = value + sweep[first + index]
-    lead, trail = edge[0], edge[1]
+    lead = grouped(edge[...])
+    sign = signs(depth)
 
     def pull(index):
         below = faces[pl.ds(length + index, 1), :]
@@ -506,28 +578,28 @@
 
     def down(index, previous):
         below, above = pull(index)
-        current = lead * below + trail * above + ratio[index] * previous
+        current = lead * (below + sign * above) + grouped(ratio[index]) * previous
         if isinstance(index, int):
             if index == 0:
-                current = current + beyond[0]
+                current = current + grouped(beyond[0])
             if index == length - 1:
-                current = current + beyond[1]
+                current = current + grouped(beyond[1])
         else:
-            current = current + jnp.where(index == 0, beyond[0], 0.0)
-            current = current + jnp.where(index == length - 1, beyond[1], 0.0)
-        sweep[index] = current
+            current = current + jnp.where(index == 0, grouped(beyond[0]), 0.0)
+            current = current + jnp.where(index == length - 1, grouped(beyond[1]), 0.0)
+        sweep[index] = current.reshape(rows, depth)
         return current
 
-    zero = jnp.zeros((rows, depth), F32)
+    zero = jnp.zeros(lead.shape, F32)
     loop(0, length, down, zero)
     line = jnp.zeros((1, depth), F32)
 
     def up(back, carry):
         following, linked, squared = carry
         index = length - 1 - back
-        value = ratio[index + 1] * (sweep[index] + following)
-        sweep[index] = value
-        low, high = face_rows(value, edge)
+        value = grouped(ratio[index + 1]) * (grouped(sweep[index]) + following)
+        sweep[index] = value.reshape(rows, depth)
+        low, high = face_rows(value, lead)
         report[pl.ds(index, 1), :] = low
         report[pl.ds(length + index, 1), :] = high
         below, above = pull(index)
@@ -551,27 +623,31 @@
     report[pl.ds(where + 4, 4), :] = jnp.zeros((4, depth), F32)
 
 
-def physical_kernel(precond, image, table_y, table_z, precond_out, image_out):
-    for index in range(precond.shape[0]):
-        precond_out[index] = dot(dot(table_y[...], precond[index]), table_z[...])
-        image_out[index] = dot(dot(table_y[...], image[index]), table_z[...])
+def physical_kernel(precond, image, left, right, precond_out, image_out):
+    count = precond.shape[0]
+    planes = [precond[index] for index in range(count)] + [image[index] for index in range(count)]
+    planes = transformed(planes, left, right)
+    for index in range(count):
+        precond_out[index] = planes[index]
+        image_out[index] = planes[count + index]
 
 
 def project_kernel(
     group, length, paired, star, precond, image, faces, table_z, *refs
 ):
-    reports, (flow, pressure, field, rows_) = refs[:-4], refs[-4:]
+    given, (flow, pressure, flows, field, rows_, sems) = refs[:-6], refs[-6:]
     _, layers, rows, depth = star.shape
     first = position(group) * layers
     where = 2 * length
-    sums = reports[0][pl.ds(where, 8), :]
+    reports = ring([each[...] for each in given])
+    sums = reports[0][where:]
     for other in reports[1:]:
-        sums = sums + other[pl.ds(where, 8), :]
+        sums = sums + other[where:]
     pairs = jnp.zeros((1, depth), F32)
     for index in range(len(reports)):
         upper, lower = reports[index], reports[(index + 1) % len(reports)]
         pairs = pairs + jnp.sum(
-            upper[pl.ds(0, length), :] * lower[pl.ds(length, length), :], axis=0, keepdims=True
+            upper[:length] * lower[length:where], axis=0, keepdims=True
         )
     energy, linked, squared, crossing = (sums[k : k + 1, 0:1] for k in range(4))
     if not paired:
@@ -591,17 +667,34 @@
     gamma = second_step * step
     for index in range(layers + 1):
         field[index] = alpha * precond[index] + gamma * image[index]
-    own = pl.ds(2 * length + first, layers)
-    following = alpha * faces[own, :] + gamma * reports[-1][pl.ds(first, layers), :]
-    following = dot(following, table_z[...])
+    after = rows_.at[pl.ds(rows + 8, length), :]
+    after[...] = alpha * faces[pl.ds(2 * length, length), :] + gamma * reports[-1][:length]
+    following = dot(after[pl.ds(first, layers), :], table_z[...])
+    copies = []
     for index in range(layers):
         value = field[index]
-        pressure[index] = value
         rows_[pl.ds(0, rows), :] = value
         rows_[pl.ds(rows, 1), :] = following[index : index + 1]
-        flow[0, index] = star[0, index] - (field[index + 1] - value)
-        flow[1, index] = star[1, index] - (rows_[pl.ds(1, rows), :] - value)
-        flow[2, index] = star[2, index] - (lane_shift(value, 1) - value)
+        flows[0, index] = star[0, index] - (field[index + 1] - value)
+        flows[1, index] = star[1, index] - (rows_[pl.ds(1, rows), :] - value)
+        flows[2, index] = star[2, index] - (lane_shift(value, 1) - value)
+        pairs = ((flows.at[:, index], flow.at[:, index]), (field.at[index], pressure.at[index]))
+        copies += started(
+            [
+                pltpu.make_async_copy(*pair, sems.at[2 * index + side])
+                for side, pair in enumerate(pairs)
+            ]
+        )
+    for copy in copies:
+        copy.wait()
+
+
+def ring(reports):
+    if len(reports) != 4:
+        return reports
+    own, near, across, far = reports
+    even = lax.rem(lax.axis_index("gy"), 2) == 0
+    return [own, jnp.where(even, far, near), across, jnp.where(even, near, far)]
 
 
 def along(array, axis, by):
@@ -638,15 +731,13 @@
     blocks = count_x // group
     length = group * layers
     rounds = group.bit_length() - 1
+    plane = (rows, depth)
     sine_y, values_y = sines(rows)
     sine_z, values_z = sines(depth)
-    table_y = jnp.asarray(sine_y, F32)
+    left, right = packed_tables(sine_y, sine_z)
     table_z = jnp.asarray(sine_z, F32)
-    edge = jnp.asarray(
-        np.broadcast_to(sine_y[[0, rows - 1]][:, :, None], (2, rows, depth)), F32
-    )
+    edge = jnp.asarray(np.broadcast_to(sine_y[0][:, None], plane), F32)
     diagonal = jnp.asarray(2.0 + values_y[:, None] + values_z[None, :], F32)
-    plane = (rows, depth)
     line = (length, depth)
 
     parts = melt_flow.shape[0]
@@ -693,7 +784,7 @@
     )
     source, message = call(
         functools.partial(transform_kernel, group, length),
-        [star, side_x, table_y, table_z, ratio, before_y],
+        [star, side_x, left, right, ratio, before_y],
         [(layers,) + plane, (2 * rows, depth)],
         [pltpu.VMEM((rows + 16, depth), F32)],
         loose=1,
@@ -773,17 +864,25 @@
         numbers = report[2 * length :].at[3].set(2.0 * crossing)
         numbers = lax.psum(jnp.where(at_end, numbers, 0.0), "gx")
         report = report.at[2 * length :].set(numbers)
-    reports = [report] + [along(report, "gy", by) for by in range(1, count_y)]
+    reports = [report]
+    for by in range(1, count_y):
+        pairs = [(i, i ^ by if count_y == 4 else (i + by) % count_y) for i in range(count_y)]
+        reports.append(lax.ppermute(report, "gy", pairs))
     precond, image = call(
         physical_kernel,
-        [precond, image, table_y, table_z],
+        [precond, image, left, right],
         [(layers + 1,) + plane, (layers + 1,) + plane],
     )
     flow, pressure = call(
         functools.partial(project_kernel, group, length, blocks > 1),
         [star, precond, image, faces, table_z] + reports,
         [(3, layers) + plane, (layers,) + plane],
-        [pltpu.VMEM((layers + 1,) + plane, F32), pltpu.VMEM((rows + 16, depth), F32)],
+        [
+            pltpu.VMEM((3, layers) + plane, F32),
+            pltpu.VMEM((layers + 1,) + plane, F32),
+            pltpu.VMEM((rows + 8 + length, depth), F32),
+        ],
+        semaphores=2 * layers,
     )
     return (flow, warmed, pressure)
 

time: 54.2 us -> 53.3 us (0.983)
  Pallas kernels: 12.1 us -> 11 us
    ppermute x11 -> x8, starting transfers between devices: 12.3 us -> 9.83 us  [along(): lax.ppermute(array, axis, [(i, (i + by) % length) for i in range(length)])]
    ppermute x0 -> x3, starting transfers between devices: none -> 2.33 us  [per_device(): reports.append(lax.ppermute(report, 'gy', pairs))]
    ppermute x0 -> x3, waiting for transfers between devices: none -> 1.82 us  [per_device(): reports.append(lax.ppermute(report, 'gy', pairs))]
    ppermute x11 -> x8, waiting for transfers between devices: 18.2 us -> 16.4 us  [along(): lax.ppermute(array, axis, [(i, (i + by) % length) for i in range(length)])]
    pallas_call x10, Pallas kernels: 9.61 us -> 8.5 us  [call(): pl.pallas_call(body, out_shape=out_shape, in_specs=[SMEM] * scalars + [VM...]
  transfers between devices with their start and end apart: 18 -> 18, of which waited for: 8 -> 8; matrix products, arithmetic and copies ran while one was open for 0% -> 0% of each run, Pallas kernels for 16% -> 14%
where the time goes in v8:
time: 53.3 us; the launch traced here: 53.1 us
  waiting for transfers between devices  22.2 us (42%)
  starting transfers between devices  18.7 us (35%)
  Pallas kernels  11 us (21%)
  between operations  0.82 us (2%)
    ppermute x8, waiting for transfers between devices, along(): lax.ppermute(array, axis, [(i, (i + by) % length) for i in range(length)])  16.4 us
    ppermute x8, starting transfers between devices, along(): lax.ppermute(array, axis, [(i, (i + by) % length) for i in range(length)])  9.83 us
    pallas_call x10, Pallas kernels, call(): pl.pallas_call(body, out_shape=out_shape, in_specs=[SMEM] * scalars + [VM...  8.5 us
    ppermute x7, starting transfers between devices, swapped(): return lax.ppermute(array, ('gx', 'gy'), pairs)  6.58 us
    ppermute x7, waiting for transfers between devices, swapped(): return lax.ppermute(array, ('gx', 'gy'), pairs)  3.99 us
    pallas_call x2, Pallas kernels, pack(): pl.pallas_call(body, out_shape=[jax.ShapeDtypeStruct(shape, F32) for shap...  2.52 us
    ppermute x3, starting transfers between devices, per_device(): reports.append(lax.ppermute(report, 'gy', pairs))  2.33 us
    ppermute x3, waiting for transfers between devices, per_device(): reports.append(lax.ppermute(report, 'gy', pairs))  1.82 us
  transfers between devices with their start and end apart: 18, of which 8 were waited for; matrix products, arithmetic and copies ran while one was open for 0% of the time, Pallas kernels for 14%

profile of v8, /device:TPU:0, one launch (start us, length us, event | category | flops | bytes accessed | tf_op | source)
XLA Modules:
  0.0 53.1 jit_solution(383886934961080930)
XLA Ops:
  0.7 1.5 %shard_map.121 = (f32[776,128]{1,0:T(8,128)S(1)}, f32[776,128]{1,0:T(8,128)S(1)}, f32[4,4,8,128]{3,2,1,0:T(8,128)S(1)}, f32[4,4,8,128]{3,2,1,0:T(8,128)S(1)}) custom-call(f32[3,4,128,128]{3,2,1,0:T(8,128)} %flow.9, f32[4,128,128]{2,1,0:T(8,128)} %thermal.11), custom_call_target="tpu_custom_call" | custom-call | tf_op jit(solution)/shard_map/pallas_call | solution.py:717
  2.1 3.1 %collective-permute-start = (f32[776,128]{1,0:T(8,128)S(1)}, f32[776,128]{1,0:T(8,128)S(1)}, u32[]{:S(2)}, u32[]{:S(2)}) collective-permute-start(f32[776,128]{1,0:T(8,128)S(1)} %get-tuple-element.31), channel_id=1, source_target_pairs={{0,4},{4,8},{8,12},{12,0},{1,5},{5,9},{9,13},{13,1},{2,6},{6,10},{... | collective-permute-start | bytes 1191944 | tf_op jit(solution)/shard_map/ppermute | solution.py:702
  5.2 2.1 %collective-permute-start.1 = (f32[776,128]{1,0:T(8,128)S(1)}, f32[776,128]{1,0:T(8,128)S(1)}, u32[]{:S(2)}, u32[]{:S(2)}) collective-permute-start(f32[776,128]{1,0:T(8,128)S(1)} %get-tuple-element.32), channel_id=1, source_target_pairs={{0,12},{4,0},{8,4},{12,8},{1,13},{5,1},{9,5},{13,9},{2,14},{6,2},{... | collective-permute-start | bytes 1191944 | tf_op jit(solution)/shard_map/ppermute | solution.py:702
  7.3 1.7 %collective-permute-start.3 = (f32[4,4,8,128]{3,2,1,0:T(8,128)S(1)}, f32[4,4,8,128]{3,2,1,0:T(8,128)S(1)}, u32[]{:S(2)}, u32[]{:S(2)}) collective-permute-start(f32[4,4,8,128]{3,2,1,0:T(8,128)S(1)} %get-tuple-element.34), channel_id=1, source_target_pairs={{0,3},{1,0},{2,1},{3,2},{4,7},{5,4},{6,5},{7,6},{8,11},{9,8},{10,9... | collective-permute-start | bytes 196616 | tf_op jit(solution)/shard_map/ppermute | solution.py:702
  9.1 1.9 %collective-permute-done.2.low_y = f32[4,4,8,128]{3,2,1,0:T(8,128)S(1)} collective-permute-done((f32[4,4,8,128]{3,2,1,0:T(8,128)S(1)}, f32[4,4,8,128]{3,2,1,0:T(8,128)S(1)}, u32[]{:S(2)}, u32[]{:S(2)}) %collective-permute-start.2) | collective-permute-done | bytes 65568 | tf_op jit(solution)/shard_map/ppermute | solution.py:702
  11.0 1.1 %shard_map.122 = (f32[264,128]{1,0:T(8,128)S(1)}, f32[2,128,128]{2,1,0:T(8,128)S(1)}) custom-call(f32[3,4,128,128]{3,2,1,0:T(8,128)} %flow.9, f32[4,128,128]{2,1,0:T(8,128)} %thermal.11, s32[4,128,128]{2,1,0:T(8,128)} %flag.5, f32[4,4,8,128]{3,2,1,0:T(8,128)S(1)} %collective-permute-done.2.low_y, f32[4,4,8,128]{3,2,1,0:T(8,128)S(1)} %collective-permute-done.3.high_y), custom_call_target="tpu_custom_call" | custom-call | tf_op jit(solution)/shard_map/pallas_call | solution.py:717
  12.6 1.5 %collective-permute-start.7 = (f32[2,128,128]{2,1,0:T(8,128)S(1)}, f32[2,128,128]{2,1,0:T(8,128)S(1)}, u32[]{:S(2)}, u32[]{:S(2)}) collective-permute-start(f32[2,128,128]{2,1,0:T(8,128)S(1)} %get-tuple-element.42), channel_id=1, source_target_pairs={{0,4},{4,8},{8,12},{12,0},{1,5},{5,9},{9,13},{13,1},{2,6},{6,10},{... | collective-permute-start | bytes 393224 | tf_op jit(solution)/shard_map/ppermute | solution.py:702
  14.1 3.2 %collective-permute-done.low_x = f32[776,128]{1,0:T(8,128)S(1)} collective-permute-done((f32[776,128]{1,0:T(8,128)S(1)}, f32[776,128]{1,0:T(8,128)S(1)}, u32[]{:S(2)}, u32[]{:S(2)}) %collective-permute-start) | collective-permute-done | bytes 397344 | tf_op jit(solution)/shard_map/ppermute | solution.py:702
  17.3 7.3 %collective-permute-done.1.high_x = f32[776,128]{1,0:T(8,128)S(1)} collective-permute-done((f32[776,128]{1,0:T(8,128)S(1)}, f32[776,128]{1,0:T(8,128)S(1)}, u32[]{:S(2)}, u32[]{:S(2)}) %collective-permute-start.1) | collective-permute-done | bytes 397344 | tf_op jit(solution)/shard_map/ppermute | solution.py:702
  24.8 3.9 %collective-permute-done.4.extra = f32[264,128]{1,0:T(8,128)S(1)} collective-permute-done((f32[264,128]{1,0:T(8,128)S(1)}, f32[264,128]{1,0:T(8,128)S(1)}, u32[]{:S(2)}, u32[]{:S(2)}) %collective-permute-start.4) | collective-permute-done | bytes 135200 | tf_op jit(solution)/shard_map/ppermute | solution.py:702
  28.7 1.7 %shard_map.125 = (f32[3,4,128,128]{3,2,1,0:T(8,128)S(1)}, f32[128,128]{1,0:T(8,128)S(1)}) custom-call(f32[3,4,128,128]{3,2,1,0:T(8,128)S(1)} %copy-done, f32[776,128]{1,0:T(8,128)S(1)} %collective-permute-done.low_x, f32[776,128]{1,0:T(8,128)S(1)} %collective-permute-done.1.high_x, f32[4,128,128]{2,1,0:T(8,128)S(1)} %copy-done.1, ...), custom_call_target="tpu_custom_call" | custom-call | flops 1610612736 | bytes 1703936 | tf_op jit(solution)/shard_map/pallas_call | solution.py:32
  31.3 0.7 %shard_map.127 = (f32[56,128]{1,0:T(8,128)S(1)}, f32[2,128,128]{2,1,0:T(8,128)S(1)}) custom-call(f32[4,128,128]{2,1,0:T(8,128)S(1)} %get-tuple-element.40.source.refs_0_, f32[4,128]{1,0:T(4,128)S(1)} %collective-permute-done.5._.before_y, f32[128,128]{1,0:T(8,128)S(1)} %copy-done.3, f32[17,128,128]{2,1,0:T(8,128)S(1)} %get-tuple-element.39.ratio.refs_9_, ...), custom_call_target="tpu_custom_call" | custom-call | flops 1048576 | bytes 319488 | tf_op jit(solution)/shard_map/pallas_call | solution.py:32
  32.0 1.8 %collective-permute-start.8 = (f32[56,128]{1,0:T(8,128)S(1)}, f32[56,128]{1,0:T(8,128)S(1)}, u32[]{:S(2)}, u32[]{:S(2)}) collective-permute-start(f32[56,128]{1,0:T(8,128)S(1)} %get-tuple-element.43.faces), channel_id=1, source_target_pairs={{0,4},{1,5},{2,6},{3,7},{4,0},{5,1},{6,2},{7,3},{8,12},{9,13},{10,... | collective-permute-start | bytes 86024 | tf_op jit(solution)/shard_map/ppermute | solution.py:712
  33.8 1.3 %collective-permute-start.14 = (f32[2,128,128]{2,1,0:T(8,128)S(1)}, f32[2,128,128]{2,1,0:T(8,128)S(1)}, u32[]{:S(2)}, u32[]{:S(2)}) collective-permute-start(f32[2,128,128]{2,1,0:T(8,128)S(1)} %get-tuple-element.48), channel_id=1, source_target_pairs={{0,12},{4,0},{8,4},{12,8},{1,13},{5,1},{9,5},{13,9},{2,14},{6,2},{... | collective-permute-start | bytes 393224 | tf_op jit(solution)/shard_map/ppermute | solution.py:702
  35.1 2.3 %collective-permute-done.8.other_faces = f32[56,128]{1,0:T(8,128)S(1)} collective-permute-done((f32[56,128]{1,0:T(8,128)S(1)}, f32[56,128]{1,0:T(8,128)S(1)}, u32[]{:S(2)}, u32[]{:S(2)}) %collective-permute-start.8) | collective-permute-done | bytes 28704 | tf_op jit(solution)/shard_map/ppermute | solution.py:712
  38.1 3.5 %collective-permute-start.10 = (f32[16,128]{1,0:T(8,128)S(1)}, f32[16,128]{1,0:T(8,128)S(1)}, u32[]{:S(2)}, u32[]{:S(2)}) collective-permute-start(f32[16,128]{1,0:T(8,128)S(1)} %get-tuple-element.46), channel_id=1, source_target_pairs={{0,1},{1,2},{2,3},{3,0},{4,5},{5,6},{6,7},{7,4},{8,9},{9,10},{10,1... | collective-permute-start | bytes 24584 | tf_op jit(solution)/shard_map/ppermute | solution.py:712
  42.3 2.0 %shard_map.129 = (f32[4,128,128]{2,1,0:T(8,128)}, f32[8,128]{1,0:T(8,128)S(1)}) custom-call(s32[8]{0:T(128)S(1)} %copy-done.8, s32[8]{0:T(128)S(1)} %copy-done.9, f32[4,128,128]{2,1,0:T(8,128)S(1)} %copy-done.1, f32[2,128,128]{2,1,0:T(8,128)S(1)} %collective-permute-done.7._.low_x, f32[2,128,128]{2,1,0:T(8,128)S(1)} %collective-permute-done.14.high_x, ...), custom_call_target="tpu_custom_call" | custom-call | flops 268435456 | bytes 532480 | tf_op jit(solution)/shard_map/pallas_call | solution.py:32
  44.3 1.7 %collective-permute-done.13.refs_7_ = f32[16,128]{1,0:T(8,128)S(1)} collective-permute-done((f32[16,128]{1,0:T(8,128)S(1)}, f32[16,128]{1,0:T(8,128)S(1)}, u32[]{:S(2)}, u32[]{:S(2)}) %collective-permute-start.13) | collective-permute-done | bytes 8224 | tf_op jit(solution)/shard_map/ppermute | solution.py:712
  45.9 1.0 %shard_map.130 = (f32[5,128,128]{2,1,0:T(8,128)S(1)}, f32[5,128,128]{2,1,0:T(8,128)S(1)}, f32[40,128]{1,0:T(8,128)S(1)}, f32[48,128]{1,0:T(8,128)S(1)}) custom-call(f32[4,128,128]{2,1,0:T(8,128)S(1)} %get-tuple-element.40.source.refs_0_, f32[296,128]{1,0:T(8,128)S(1)} %get-tuple-element.44.refs_1_, f32[296,128]{1,0:T(8,128)S(1)} %collective-permute-done.9.refs_2_, ...), custom_call_target="tpu_custom_call" | custom-call | flops 1048576 | bytes 1400832 | tf_op jit(solution)/shard_map/pallas_call | solution.py:32
  46.9 1.0 %collective-permute-start.17 = (f32[40,128]{1,0:T(8,128)S(1)}, f32[40,128]{1,0:T(8,128)S(1)}, u32[]{:S(2)}, u32[]{:S(2)}) collective-permute-start(f32[40,128]{1,0:T(8,128)S(1)} %get-tuple-element.55.refs_0_), channel_id=1, source_target_pairs={{0,3},{1,2},{2,1},{3,0},{4,7},{5,6},{6,5},{7,4},{8,11},{9,10},{10,... | collective-permute-start | bytes 61448 | tf_op jit(solution)/shard_map/ppermute | solution.py:870
  47.9 1.3 %collective-permute-start.16 = (f32[40,128]{1,0:T(8,128)S(1)}, f32[40,128]{1,0:T(8,128)S(1)}, u32[]{:S(2)}, u32[]{:S(2)}) collective-permute-start(f32[40,128]{1,0:T(8,128)S(1)} %get-tuple-element.55.refs_0_), channel_id=1, source_target_pairs={{0,2},{1,3},{2,0},{3,1},{4,6},{5,7},{6,4},{7,5},{8,10},{9,11},{10,... | collective-permute-start | bytes 61448 | tf_op jit(solution)/shard_map/ppermute | solution.py:870
  49.2 0.7 %shard_map.131 = (f32[5,128,128]{2,1,0:T(8,128)S(1)}, f32[5,128,128]{2,1,0:T(8,128)S(1)}) custom-call(f32[5,128,128]{2,1,0:T(8,128)S(1)} %get-tuple-element.50.precond, f32[5,128,128]{2,1,0:T(8,128)S(1)} %get-tuple-element.51.image, bf16[128,256]{1,0:T(8,128)(2,1)S(1)} %copy-done.7, bf16[256,256]{1,0:T(8,128)(2,1)S(1)} %copy-done.5), custom_call_target="tpu_custom_call" | custom-call | flops 1048576 | bytes 1310720 | tf_op jit(solution)/shard_map/pallas_call | solution.py:32
  50.1 1.5 %collective-permute-done.16.refs_2_ = f32[40,128]{1,0:T(8,128)S(1)} collective-permute-done((f32[40,128]{1,0:T(8,128)S(1)}, f32[40,128]{1,0:T(8,128)S(1)}, u32[]{:S(2)}, u32[]{:S(2)}) %collective-permute-start.16) | collective-permute-done | bytes 20512 | tf_op jit(solution)/shard_map/ppermute | solution.py:870
  51.7 1.4 %shard_map.132 = (f32[3,4,128,128]{3,2,1,0:T(8,128)}, f32[4,128,128]{2,1,0:T(8,128)}) custom-call(f32[3,4,128,128]{3,2,1,0:T(8,128)S(1)} %get-tuple-element.37.star, f32[5,128,128]{2,1,0:T(8,128)S(1)} %get-tuple-element.52.precond, f32[5,128,128]{2,1,0:T(8,128)S(1)} %get-tuple-element.53.image, f32[48,128]{1,0:T(8,128)S(1)} %get-tuple-element.54.faces, ...), custom_call_target="tpu_custom_call" | custom-call | flops 1048576 | bytes 2097152 | tf_op jit(solution)/shard_map/pallas_call | solution.py:32
  (45 shorter events, 3.1 us)
Async XLA Ops:
  0.6 11.5 %copy-start.6 = (f32[128,128]{1,0:T(8,128)S(1)}, f32[128,128]{1,0:T(8,128)}, u32[]{:S(2)}) copy-start(f32[128,128]{1,0:T(8,128)} %constant.16.clone.diagonal) | copy-start | bytes 196612
  0.6 24.0 %copy-start.1 = (f32[4,128,128]{2,1,0:T(8,128)S(1)}, f32[4,128,128]{2,1,0:T(8,128)}, u32[]{:S(2)}) copy-start(f32[4,128,128]{2,1,0:T(8,128)} %thermal.11) | copy-start | bytes 786436
  0.7 24.0 %copy-start = (f32[3,4,128,128]{3,2,1,0:T(8,128)S(1)}, f32[3,4,128,128]{3,2,1,0:T(8,128)}, u32[]{:S(2)}) copy-start(f32[3,4,128,128]{3,2,1,0:T(8,128)} %flow.9) | copy-start | bytes 2359300
  0.7 24.0 %copy-start.2 = (s32[4,128,128]{2,1,0:T(8,128)S(1)}, s32[4,128,128]{2,1,0:T(8,128)}, u32[]{:S(2)}) copy-start(s32[4,128,128]{2,1,0:T(8,128)} %flag.5) | copy-start | bytes 786436
  2.1 15.2 %collective-permute-start = (f32[776,128]{1,0:T(8,128)S(1)}, f32[776,128]{1,0:T(8,128)S(1)}, u32[]{:S(2)}, u32[]{:S(2)}) collective-permute-start(f32[776,128]{1,0:T(8,128)S(1)} %get-tuple-element.31), channel_id=1, source_target_pairs={{0,4},{4,8},{8,12},{12,0},{1,5},{5,9},{9,13},{13,1},{2,6},{6,10},{... | collective-permute-start | bytes 1191944 | tf_op jit(solution)/shard_map/ppermute | solution.py:702
  5.2 19.4 %collective-permute-start.1 = (f32[776,128]{1,0:T(8,128)S(1)}, f32[776,128]{1,0:T(8,128)S(1)}, u32[]{:S(2)}, u32[]{:S(2)}) collective-permute-start(f32[776,128]{1,0:T(8,128)S(1)} %get-tuple-element.32), channel_id=1, source_target_pairs={{0,12},{4,0},{8,4},{12,8},{1,13},{5,1},{9,5},{13,9},{2,14},{6,2},{... | collective-permute-start | bytes 1191944 | tf_op jit(solution)/shard_map/ppermute | solution.py:702
  7.3 3.7 %collective-permute-start.2 = (f32[4,4,8,128]{3,2,1,0:T(8,128)S(1)}, f32[4,4,8,128]{3,2,1,0:T(8,128)S(1)}, u32[]{:S(2)}, u32[]{:S(2)}) collective-permute-start(f32[4,4,8,128]{3,2,1,0:T(8,128)S(1)} %get-tuple-element.33), channel_id=1, source_target_pairs={{0,1},{1,2},{2,3},{3,0},{4,5},{5,6},{6,7},{7,4},{8,9},{9,10},{10,1... | collective-permute-start | bytes 196616 | tf_op jit(solution)/shard_map/ppermute | solution.py:702
  7.3 3.7 %collective-permute-start.3 = (f32[4,4,8,128]{3,2,1,0:T(8,128)S(1)}, f32[4,4,8,128]{3,2,1,0:T(8,128)S(1)}, u32[]{:S(2)}, u32[]{:S(2)}) collective-permute-start(f32[4,4,8,128]{3,2,1,0:T(8,128)S(1)} %get-tuple-element.34), channel_id=1, source_target_pairs={{0,3},{1,0},{2,1},{3,2},{4,7},{5,4},{6,5},{7,6},{8,11},{9,8},{10,9... | collective-permute-start | bytes 196616 | tf_op jit(solution)/shard_map/ppermute | solution.py:702
  12.1 16.6 %collective-permute-start.4 = (f32[264,128]{1,0:T(8,128)S(1)}, f32[264,128]{1,0:T(8,128)S(1)}, u32[]{:S(2)}, u32[]{:S(2)}) collective-permute-start(f32[264,128]{1,0:T(8,128)S(1)} %get-tuple-element.35), channel_id=1, source_target_pairs={{0,4},{4,8},{8,12},{12,0},{1,5},{5,9},{9,13},{13,1},{2,6},{6,10},{... | collective-permute-start | bytes 405512 | tf_op jit(solution)/shard_map/ppermute | solution.py:702
  12.6 18.5 %collective-permute-start.7 = (f32[2,128,128]{2,1,0:T(8,128)S(1)}, f32[2,128,128]{2,1,0:T(8,128)S(1)}, u32[]{:S(2)}, u32[]{:S(2)}) collective-permute-start(f32[2,128,128]{2,1,0:T(8,128)S(1)} %get-tuple-element.42), channel_id=1, source_target_pairs={{0,4},{4,8},{8,12},{12,0},{1,5},{5,9},{9,13},{13,1},{2,6},{6,10},{... | collective-permute-start | bytes 393224 | tf_op jit(solution)/shard_map/ppermute | solution.py:702
  24.7 5.6 %collective-permute-start.5 = (f32[4,128]{1,0:T(4,128)S(1)}, f32[4,128]{1,0:T(4,128)S(1)}, u32[]{:S(2)}, u32[]{:S(2)}) collective-permute-start(f32[4,128]{1,0:T(4,128)S(1)} %shard_map.124._), channel_id=1, source_target_pairs={{0,1},{1,2},{2,3},{3,0},{4,5},{5,6},{6,7},{7,4},{8,9},{9,10},{10,1... | collective-permute-start | bytes 6152 | tf_op jit(solution)/shard_map/ppermute | solution.py:702
  31.0 6.4 %collective-permute-start.6 = (f32[256,128]{1,0:T(8,128)S(1)}, f32[256,128]{1,0:T(8,128)S(1)}, u32[]{:S(2)}, u32[]{:S(2)}) collective-permute-start(f32[256,128]{1,0:T(8,128)S(1)} %get-tuple-element.41.message), channel_id=1, source_target_pairs={{0,4},{1,5},{2,6},{3,7},{4,0},{5,1},{6,2},{7,3},{8,12},{9,13},{10,... | collective-permute-start | bytes 393224 | tf_op jit(solution)/shard_map/ppermute | solution.py:712
  32.0 10.3 %copy-start.8 = (s32[8]{0:T(128)S(1)}, s32[8]{0:T(128)}, u32[]{:S(2)}) copy-start(s32[8]{0:T(128)} %spots_a.1) | copy-start | bytes 100
  32.0 10.3 %copy-start.9 = (s32[8]{0:T(128)S(1)}, s32[8]{0:T(128)}, u32[]{:S(2)}) copy-start(s32[8]{0:T(128)} %spots_b.1) | copy-start | bytes 100
  32.0 5.4 %collective-permute-start.8 = (f32[56,128]{1,0:T(8,128)S(1)}, f32[56,128]{1,0:T(8,128)S(1)}, u32[]{:S(2)}, u32[]{:S(2)}) collective-permute-start(f32[56,128]{1,0:T(8,128)S(1)} %get-tuple-element.43.faces), channel_id=1, source_target_pairs={{0,4},{1,5},{2,6},{3,7},{4,0},{5,1},{6,2},{7,3},{8,12},{9,13},{10,... | collective-permute-start | bytes 86024 | tf_op jit(solution)/shard_map/ppermute | solution.py:712
  33.8 7.9 %collective-permute-start.14 = (f32[2,128,128]{2,1,0:T(8,128)S(1)}, f32[2,128,128]{2,1,0:T(8,128)S(1)}, u32[]{:S(2)}, u32[]{:S(2)}) collective-permute-start(f32[2,128,128]{2,1,0:T(8,128)S(1)} %get-tuple-element.48), channel_id=1, source_target_pairs={{0,12},{4,0},{8,4},{12,8},{1,13},{5,1},{9,5},{13,9},{2,14},{6,2},{... | collective-permute-start | bytes 393224 | tf_op jit(solution)/shard_map/ppermute | solution.py:702
  37.6 8.3 %collective-permute-start.9 = (f32[296,128]{1,0:T(8,128)S(1)}, f32[296,128]{1,0:T(8,128)S(1)}, u32[]{:S(2)}, u32[]{:S(2)}) collective-permute-start(f32[296,128]{1,0:T(8,128)S(1)} %get-tuple-element.44.refs_1_), channel_id=1, source_target_pairs={{0,8},{1,9},{2,10},{3,11},{4,12},{5,13},{6,14},{7,15},{8,0},{9,1},... | collective-permute-start | bytes 454664 | tf_op jit(solution)/shard_map/ppermute | solution.py:712
  38.1 6.2 %collective-permute-start.11 = (f32[16,128]{1,0:T(8,128)S(1)}, f32[16,128]{1,0:T(8,128)S(1)}, u32[]{:S(2)}, u32[]{:S(2)}) collective-permute-start(f32[16,128]{1,0:T(8,128)S(1)} %get-tuple-element.46), channel_id=1, source_target_pairs={{0,9},{1,10},{2,11},{3,8},{4,13},{5,14},{6,15},{7,12},{8,1},{9,2},... | collective-permute-start | bytes 24584 | tf_op jit(solution)/shard_map/ppermute | solution.py:712
  38.1 6.2 %collective-permute-start.10 = (f32[16,128]{1,0:T(8,128)S(1)}, f32[16,128]{1,0:T(8,128)S(1)}, u32[]{:S(2)}, u32[]{:S(2)}) collective-permute-start(f32[16,128]{1,0:T(8,128)S(1)} %get-tuple-element.46), channel_id=1, source_target_pairs={{0,1},{1,2},{2,3},{3,0},{4,5},{5,6},{6,7},{7,4},{8,9},{9,10},{10,1... | collective-permute-start | bytes 24584 | tf_op jit(solution)/shard_map/ppermute | solution.py:712
  41.6 4.3 %collective-permute-start.13 = (f32[16,128]{1,0:T(8,128)S(1)}, f32[16,128]{1,0:T(8,128)S(1)}, u32[]{:S(2)}, u32[]{:S(2)}) collective-permute-start(f32[16,128]{1,0:T(8,128)S(1)} %get-tuple-element.47), channel_id=1, source_target_pairs={{0,11},{1,8},{2,9},{3,10},{4,15},{5,12},{6,13},{7,14},{8,3},{9,0},... | collective-permute-start | bytes 24584 | tf_op jit(solution)/shard_map/ppermute | solution.py:712
  41.7 4.2 %collective-permute-start.12 = (f32[16,128]{1,0:T(8,128)S(1)}, f32[16,128]{1,0:T(8,128)S(1)}, u32[]{:S(2)}, u32[]{:S(2)}) collective-permute-start(f32[16,128]{1,0:T(8,128)S(1)} %get-tuple-element.47), channel_id=1, source_target_pairs={{0,3},{1,0},{2,1},{3,2},{4,7},{5,4},{6,5},{7,6},{8,11},{9,8},{10,9... | collective-permute-start | bytes 24584 | tf_op jit(solution)/shard_map/ppermute | solution.py:712
  46.9 3.3 %collective-permute-start.17 = (f32[40,128]{1,0:T(8,128)S(1)}, f32[40,128]{1,0:T(8,128)S(1)}, u32[]{:S(2)}, u32[]{:S(2)}) collective-permute-start(f32[40,128]{1,0:T(8,128)S(1)} %get-tuple-element.55.refs_0_), channel_id=1, source_target_pairs={{0,3},{1,2},{2,1},{3,0},{4,7},{5,6},{6,5},{7,4},{8,11},{9,10},{10,... | collective-permute-start | bytes 61448 | tf_op jit(solution)/shard_map/ppermute | solution.py:870
  47.9 3.8 %collective-permute-start.16 = (f32[40,128]{1,0:T(8,128)S(1)}, f32[40,128]{1,0:T(8,128)S(1)}, u32[]{:S(2)}, u32[]{:S(2)}) collective-permute-start(f32[40,128]{1,0:T(8,128)S(1)} %get-tuple-element.55.refs_0_), channel_id=1, source_target_pairs={{0,2},{1,3},{2,0},{3,1},{4,6},{5,7},{6,4},{7,5},{8,10},{9,11},{10,... | collective-permute-start | bytes 61448 | tf_op jit(solution)/shard_map/ppermute | solution.py:870
  49.2 2.5 %collective-permute-start.15 = (f32[40,128]{1,0:T(8,128)S(1)}, f32[40,128]{1,0:T(8,128)S(1)}, u32[]{:S(2)}, u32[]{:S(2)}) collective-permute-start(f32[40,128]{1,0:T(8,128)S(1)} %get-tuple-element.55.refs_0_), channel_id=1, source_target_pairs={{0,1},{1,0},{2,3},{3,2},{4,5},{5,4},{6,7},{7,6},{8,9},{9,8},{10,11... | collective-permute-start | bytes 61448 | tf_op jit(solution)/shard_map/ppermute | solution.py:870
  (4 other events, 13.1 us)

commit v9 on v8

--- a/solution.py
+++ b/solution.py
@@ -22,21 +22,19 @@
 SMEM = pl.BlockSpec(memory_space=pltpu.SMEM)
 
 
-def call(body, operands, shapes, scratch=(), scalars=0, loose=0, semaphores=0, flops=1 << 20):
+def call(body, operands, shapes, scratch=(), scalars=0, loose=0, flops=1 << 20):
     out_shape = [jax.ShapeDtypeStruct(shape, F32) for shape in shapes]
     moved = 4 * sum(math.prod(shape) for shape in shapes)
     held = moved + 4 * sum(operand.size for operand in operands)
     held += 4 * sum(math.prod(space.shape) for space in scratch)
-    where = pl.BlockSpec(memory_space=pl.ANY) if semaphores else VMEM
-    waits = [pltpu.SemaphoreType.DMA((semaphores,))] if semaphores else []
     return pl.pallas_call(
         body,
         out_shape=out_shape,
         in_specs=[SMEM] * scalars
         + [VMEM] * (len(operands) - scalars - loose)
         + [pl.BlockSpec(memory_space=pl.ANY)] * loose,
-        out_specs=[where] * len(shapes),
-        scratch_shapes=list(scratch) + waits,
+        out_specs=[VMEM] * len(shapes),
+        scratch_shapes=list(scratch),
         compiler_params=pltpu.CompilerParams(vmem_limit_bytes=held + (4 << 20)),
         cost_estimate=pl.CostEstimate(flops=flops, bytes_accessed=2 * moved, transcendentals=0),
     )(*operands)
@@ -161,7 +159,7 @@
     padded[index, pl.ds(8 + rows, 2), :] = after
 
 
-def march_layer(refs, padded, index, parts, start, count):
+def march_layer(refs, padded, index, parts, start, count, edges=None):
     flow, low_x, high_x, thermal, flag = refs
     _, layers, rows, depth = flow.shape
     span = pl.ds(start, count)
@@ -184,9 +182,10 @@
                 around.append(flow[part, other, span, :])
         moved = advance(around, padded, part, weights, start)
         if part == 0:
-            edge = lambda halo: column(halo[pl.ds(halo.shape[0] - 8, 1), pl.ds(0, rows)])
-            behind = thermal[index - 1] if index > 0 else edge(low_x)
-            before = thermal[index + 1] if index + 1 < layers else edge(high_x)
+            behind = edges[0][start : start + count]
+            before = edges[1][start : start + count]
+            behind = thermal[index - 1, span, :] if index > 0 else behind
+            before = thermal[index + 1, span, :] if index + 1 < layers else before
             moved = moved + pull * (before - behind)
         if part == 1:
             slope = padded[3, pl.ds(9 + start, count), :] - padded[3, pl.ds(7 + start, count), :]
@@ -216,16 +215,22 @@
 
 
 def march_kernel(
-    flow, low_x, high_x, thermal, flag, low_y, high_y, extra, _,
-    star, side_x, padded,
+    flow, low_x, high_x, thermal, flag, low_y, high_y, _, star, padded
 ):
     refs = (flow, low_x, high_x, thermal, flag)
     _, layers, rows, depth = flow.shape
+    edges = [column(halo[pl.ds(halo.shape[0] - 8, 1), pl.ds(0, rows)]) for halo in (low_x, high_x)]
+    count = math.gcd(rows, 16)
     for index in range(layers):
         pad_layer(refs, low_y, high_y, padded, index)
-        value = march_layer(refs, padded, index, range(3), 0, rows)
-        for part in range(3):
-            star[part, index] = value[part]
+        for start in range(0, rows, count):
+            value = march_layer(refs, padded, index, range(3), start, count, edges)
+            for part in range(3):
+                star[part, index, pl.ds(start, count), :] = value[part]
+
+
+def side_plane(flow, low_x, thermal, extra, padded):
+    rows, depth = flow.shape[2:]
     plane = lambda index: low_x[pl.ds(index * rows, rows), pl.ds(0, depth)]
     beside = extra[pl.ds(2 * rows, 8), pl.ds(0, depth)]
     pad_rows(padded, 0, beside[2:4], plane(1), beside[4:6])
@@ -235,33 +240,43 @@
     pull = jnp.where(top, (-MARANGONI * 0.5 * TIME_INCREMENT) * drag, 0.0)
     behind = column(extra[pl.ds(2 * rows, 1), pl.ds(0, rows)])
     weights = coefficients([plane(1), plane(3), plane(5)], drag)
-    side_x[...] = advance(around, padded, 0, weights) + pull * (thermal[0] - behind)
-
-
-def transform_kernel(
-    group, length, star, side_x, left, right, ratio, _, source, message, rows_
-):
+    return advance(around, padded, 0, weights) + pull * (thermal[0] - behind)
+
+
+def transform_kernel(star, left, right, partial, rows_):
     _, layers, rows, depth = star.shape
-    first = position(group) * layers
     rows_[pl.ds(0, 8), :] = jnp.zeros((8, depth), F32)
     planes = []
     for index in range(layers):
         rows_[pl.ds(8, rows), :] = star[1, index]
-        behind = star[0, index - 1] if index > 0 else side_x[...]
-        sink = star[0, index] - behind
+        sink = star[0, index]
+        if index > 0:
+            sink = sink - star[0, index - 1]
         sink = sink + (star[1, index] - rows_[pl.ds(7, rows), :])
         sink = sink + (star[2, index] - lane_shift(star[2, index], -1))
         planes.append(-sink)
     for index, plane in enumerate(transformed(planes, left, right)):
-        source[index] = plane
+        partial[index] = plane
+
+
+def source_kernel(
+    group, length, flow, low_x, thermal, extra, partial, left, right, ratio, _,
+    source, message, padded,
+):
+    layers, rows, depth = partial.shape
+    first = position(group) * layers
+    (onward,) = transformed([side_plane(flow, low_x, thermal, extra, padded)], left, right)
+    source[0] = partial[0] + onward
+    for index in range(1, layers):
+        source[index] = partial[index]
+    backward = partial[layers - 1]
+    for index in range(layers - 2, 0, -1):
+        backward = partial[index] + ratio[length - 1 - first - index] * backward
     forward = source[0]
+    message[pl.ds(rows, rows), :] = forward + ratio[length - 1 - first] * backward
     for index in range(1, layers):
-        forward = source[index] + ratio[first + index] * forward
+        forward = partial[index] + ratio[first + index] * forward
     message[pl.ds(0, rows), :] = forward
-    backward = source[layers - 1]
-    for index in range(layers - 2, -1, -1):
-        backward = source[index] + ratio[length - 1 - first - index] * backward
-    message[pl.ds(rows, rows), :] = backward
 
 
 def started(copies):
@@ -300,9 +315,9 @@
         copy.wait()
 
 
-def extra_kernel(flow, thermal, flag, low_y, high_y, extra, last, flags, sems):
+def extra_kernel(flow, thermal, flag, low_y, high_y, extra, flags, top, sems):
     _, layers, rows, depth = flow.shape
-    pairs = [(flag.at[layers - 1], flags), (thermal.at[pl.ds(layers - 2, 2)], last)]
+    pairs = [(flag.at[layers - 1], flags), (thermal.at[layers - 2], top)]
     pairs.append((flow.at[0, layers - 3], extra.at[pl.ds(0, rows), :]))
     copies = started(
         [pltpu.make_async_copy(*pair, sems.at[index]) for index, pair in enumerate(pairs)]
@@ -314,7 +329,7 @@
     for copy in copies[:2]:
         copy.wait()
     extra[pl.ds(rows, rows), :] = flags[...].astype(F32)
-    extra[pl.ds(base, 1), pl.ds(0, rows)] = surface(last[0])
+    extra[pl.ds(base, 1), pl.ds(0, rows)] = surface(top[...])
     for copy in copies[2:]:
         copy.wait()
 
@@ -341,26 +356,35 @@
 
 
 def heat_kernel(
-    spots_a, spots_b, thermal, low_x, high_x, low_y, high_y, flow,
-    warmed, token, padded,
+    spots_a, spots_b, thermal, halo, low_y, high_y, flow, warmed, token, padded
 ):
     layers, rows, depth = thermal.shape
     token[...] = jnp.zeros(token.shape, F32)
     top = lax.broadcasted_iota(jnp.int32, (rows, depth), 1) == depth - 1
+    none = jnp.zeros((rows, depth), F32)
     for index in range(layers):
         pad_rows(padded, 0, low_y[3, index, 6:], thermal[index], high_y[3, index, :2])
         around = []
         for other in range(index - 2, index + 3):
             if other < 0:
-                around.append(low_x[other + 2])
+                around.append(halo[other + 2])
             elif other >= layers:
-                around.append(high_x[other - layers])
+                around.append(none)
             else:
                 around.append(thermal[other])
         speed = [flow[part, index] for part in range(3)]
         gain = TIME_INCREMENT * column(laser_row(index, layers, rows, spots_a, spots_b))
         moved = advance(around, padded, 0, coefficients(speed, None))
         warmed[index] = moved + jnp.where(top, gain, 0.0)
+
+
+def heat_last_kernel(flow, halo, warm, warmed):
+    layers = warm.shape[0]
+    warmed[: layers - 2] = warm[: layers - 2]
+    for index, added in ((layers - 2, -halo[0]), (layers - 1, 4.0 * halo[0] - halo[1])):
+        speed = flow[0, index]
+        factor = jnp.where(speed >= 0.0, 0.0, 0.5 * TIME_INCREMENT * jnp.abs(speed))
+        warmed[index] = warm[index] + factor * added
 
 
 def tables_kernel(group, layers, diagonal, ratio, weight):
@@ -420,10 +444,10 @@
 
 
 def faces_kernel(
-    group, length, source, before_y, table_z, ratio, weight, edge, thermal, _, faces, late, sweep
+    group, length, source, before_y, table_z, ratio, weight, edge, thermal, faces, late, sweep
 ):
     layers, rows, depth = source.shape
-    late[...] = thermal[:2]
+    late[...] = thermal[layers - 2 :]
     first = position(group) * layers
     zero = jnp.zeros((rows, depth), F32)
     extra = dot(before_y[...], table_z[...])
@@ -537,10 +561,12 @@
 
 
 def coarse_kernel(
-    turn, group, length, alone, source, message, other, sums, faces_in, weight, ratio, edge, *refs
+    turn, group, length, alone, source, message, other, sums, faces_in, weight, ratio, edge,
+    thermal, *refs
 ):
-    precond, image, report, faces, late, sweep, ends = refs[-7:]
+    precond, image, report, faces, onward, late, sweep, ends = refs[-8:]
     layers, rows, depth = source.shape
+    onward[...] = thermal[:2]
     first = position(group) * layers
     below, below_far, above, above_far = faces_in
     forward, backward, before, after, energy = joined(turn, group, message, other, sums, weight)
@@ -635,7 +661,7 @@
 def project_kernel(
     group, length, paired, star, precond, image, faces, table_z, *refs
 ):
-    given, (flow, pressure, flows, field, rows_, sems) = refs[:-6], refs[-6:]
+    given, (flow, pressure, field, rows_) = refs[:-4], refs[-4:]
     _, layers, rows, depth = star.shape
     first = position(group) * layers
     where = 2 * length
@@ -670,23 +696,14 @@
     after = rows_.at[pl.ds(rows + 8, length), :]
     after[...] = alpha * faces[pl.ds(2 * length, length), :] + gamma * reports[-1][:length]
     following = dot(after[pl.ds(first, layers), :], table_z[...])
-    copies = []
     for index in range(layers):
         value = field[index]
+        pressure[index] = value
         rows_[pl.ds(0, rows), :] = value
         rows_[pl.ds(rows, 1), :] = following[index : index + 1]
-        flows[0, index] = star[0, index] - (field[index + 1] - value)
-        flows[1, index] = star[1, index] - (rows_[pl.ds(1, rows), :] - value)
-        flows[2, index] = star[2, index] - (lane_shift(value, 1) - value)
-        pairs = ((flows.at[:, index], flow.at[:, index]), (field.at[index], pressure.at[index]))
-        copies += started(
-            [
-                pltpu.make_async_copy(*pair, sems.at[2 * index + side])
-                for side, pair in enumerate(pairs)
-            ]
-        )
-    for copy in copies:
-        copy.wait()
+        flow[0, index] = star[0, index] - (field[index + 1] - value)
+        flow[1, index] = star[1, index] - (rows_[pl.ds(1, rows), :] - value)
+        flow[2, index] = star[2, index] - (lane_shift(value, 1) - value)
 
 
 def ring(reports):
@@ -719,7 +736,7 @@
         out_shape=[jax.ShapeDtypeStruct(shape, F32) for shape in shapes],
         in_specs=[pl.BlockSpec(memory_space=pltpu.HBM)] * len(inputs) + [VMEM] * len(received),
         out_specs=[VMEM] * len(shapes),
-        scratch_shapes=[scratch, pltpu.SemaphoreType.DMA((count,))],
+        scratch_shapes=scratch + [pltpu.SemaphoreType.DMA((count,))],
         compiler_params=pltpu.CompilerParams(vmem_limit_bytes=4 << 20),
     )(*inputs, *received)
 
@@ -748,19 +765,19 @@
         [melt_flow, thermal_state],
         [],
         [outer_planes, outer_planes] + [(parts + 1, layers, 8, depth)] * 2,
-        pltpu.VMEM((2,) + plane, F32),
+        [pltpu.VMEM((2,) + plane, F32)],
         6 + 4 * parts,
     )
     low_x = along(ahead, "gx", 1)
     high_x = along(behind, "gx", -1)
     low_y = along(last_rows, "gy", 1)
     high_y = along(first_rows, "gy", -1)
-    extra, last = pack(
+    (extra,) = pack(
         extra_kernel,
         [melt_flow, thermal_state, powder_flag],
         [low_y, high_y],
-        [(2 * rows + 8, width), (2,) + plane],
-        pltpu.VMEM(plane, jnp.int32),
+        [(2 * rows + 8, width)],
+        [pltpu.VMEM(plane, jnp.int32), pltpu.VMEM(plane, F32)],
         3,
     )
     extra = along(extra, "gx", 1)
@@ -769,44 +786,43 @@
         [diagonal],
         [(length + 1,) + plane, (4 * rounds + 1,) + plane],
     )
-    early_low = along(last, "gx", 1)
     marched = [melt_flow, low_x, high_x, thermal_state, powder_flag, low_y, high_y]
     padded = pltpu.VMEM((4, rows + 16, depth), F32)
+    one_padded = pltpu.VMEM((1, rows + 16, depth), F32)
     (side_y,) = call(row_kernel, marched + [weight], [(layers, depth)], [padded], loose=1)
     before_y = along(side_y, "gy", 1)
-    star, side_x = call(
-        march_kernel,
-        marched + [extra, side_y],
-        [(3, layers) + plane, plane],
-        [padded],
+    (star,) = call(
+        march_kernel, marched + [side_y], [(3, layers) + plane], [padded], loose=1, flops=3 << 29
+    )
+    (partial,) = call(
+        transform_kernel,
+        [star, left, right],
+        [(layers,) + plane],
+        [pltpu.VMEM((rows + 16, depth), F32)],
+        flops=1 << 29,
+    )
+    source, message = call(
+        functools.partial(source_kernel, group, length),
+        [melt_flow, low_x, thermal_state, extra, partial, left, right, ratio, before_y],
+        [(layers,) + plane, (2 * rows, depth)],
+        [one_padded],
         loose=1,
-        flops=3 << 29,
-    )
-    source, message = call(
-        functools.partial(transform_kernel, group, length),
-        [star, side_x, left, right, ratio, before_y],
-        [(layers,) + plane, (2 * rows, depth)],
-        [pltpu.VMEM((rows + 16, depth), F32)],
-        loose=1,
-        flops=1 << 30,
     )
     faces, late = call(
         functools.partial(faces_kernel, group, length),
-        [source, before_y, table_z, ratio, weight, edge, thermal_state, early_low],
+        [source, before_y, table_z, ratio, weight, edge, thermal_state],
         [(3 * length + 8, depth), (2,) + plane],
         [pltpu.VMEM((max(length, layers + 1),) + plane, F32)],
-        loose=1,
-    )
-    early_high = along(late, "gx", -1)
+    )
     alone = blocks == 1
-    warmed, token = call(
+    warm, token = call(
         heat_kernel,
         [
-            spot_lateral_a_cell, spot_lateral_b_cell, thermal_state, early_low, early_high,
+            spot_lateral_a_cell, spot_lateral_b_cell, thermal_state, along(late, "gx", 1),
             low_y, high_y, melt_flow,
         ],
         [(layers,) + plane, (8, depth)],
-        [pltpu.VMEM((1, rows + 16, depth), F32)],
+        [one_padded],
         scalars=2,
         flops=1 << 28,
     )
@@ -839,17 +855,17 @@
         )
         outer = [jnp.stack([along(ends[0], "gx", group), along(ends[1], "gx", -group)])]
     operands = [source, message, other, sums] + rim
-    operands += [weight, ratio, edge] + outer + [token]
+    operands += [weight, ratio, edge, thermal_state] + outer + [token]
 
     def coarse(*refs):
         coarse_kernel(rounds - 1, group, length, alone, *refs[:4], refs[4:8], *refs[8:])
 
-    precond, image, report, faces = call(
+    precond, image, report, faces, late = call(
         coarse,
         operands,
         [
             (layers + 1,) + plane, (layers + 1,) + plane, (2 * length + 8, depth),
-            (3 * length, depth),
+            (3 * length, depth), (2,) + plane,
         ],
         scratch + [pltpu.VMEM((2,) + plane, F32)],
         loose=1,
@@ -873,16 +889,16 @@
         [precond, image, left, right],
         [(layers + 1,) + plane, (layers + 1,) + plane],
     )
+    late = along(late, "gx", -1)
+    (warmed,) = call(heat_last_kernel, [melt_flow, late, warm], [(layers,) + plane])
     flow, pressure = call(
         functools.partial(project_kernel, group, length, blocks > 1),
         [star, precond, image, faces, table_z] + reports,
         [(3, layers) + plane, (layers,) + plane],
         [
-            pltpu.VMEM((3, layers) + plane, F32),
             pltpu.VMEM((layers + 1,) + plane, F32),
             pltpu.VMEM((rows + 8 + length, depth), F32),
         ],
-        semaphores=2 * layers,
     )
     return (flow, warmed, pressure)
 

time: 53.3 us -> 55.7 us (1.045)
  starting transfers between devices: 18.7 us -> 20.8 us
  local copies, waits for them, and re-layouts: 0.28 us -> 0.9 us
    ppermute x7, starting transfers between devices: 6.58 us -> 8.54 us  [swapped(): return lax.ppermute(array, ('gx', 'gy'), pairs)]
    ppermute x8, waiting for transfers between devices: 16.4 us -> 14.7 us  [along(): lax.ppermute(array, axis, [(i, (i + by) % length) for i in range(length)])]
    ppermute x7, waiting for transfers between devices: 3.99 us -> 5.49 us  [swapped(): return lax.ppermute(array, ('gx', 'gy'), pairs)]
    unnamed x20, local copies, waits for them, and re-layouts: 0.27 us -> 0.89 us
    pallas_call x10 -> x12, Pallas kernels: 8.5 us -> 8.28 us  [call(): pl.pallas_call(body, out_shape=out_shape, in_specs=[SMEM] * scalars + [VM...]
  transfers between devices with their start and end apart: 18 -> 18, of which waited for: 8 -> 8; matrix products, arithmetic and copies ran while one was open for 0% -> 0% of each run, Pallas kernels for 14% -> 13%
where the time goes in v9:
time: 55.7 us; the launch traced here: 55.5 us
  waiting for transfers between devices  22.3 us (40%)
  starting transfers between devices  20.8 us (37%)
  Pallas kernels  10.7 us (19%)
  local copies, waits for them, and re-layouts  0.9 us (2%)
  between operations  0.81 us (1%)
    ppermute x8, waiting for transfers between devices, along(): lax.ppermute(array, axis, [(i, (i + by) % length) for i in range(length)])  14.7 us
    ppermute x8, starting transfers between devices, along(): lax.ppermute(array, axis, [(i, (i + by) % length) for i in range(length)])  10.4 us
    ppermute x7, starting transfers between devices, swapped(): return lax.ppermute(array, ('gx', 'gy'), pairs)  8.54 us
    pallas_call x12, Pallas kernels, call(): pl.pallas_call(body, out_shape=out_shape, in_specs=[SMEM] * scalars + [VM...  8.28 us
    ppermute x7, waiting for transfers between devices, swapped(): return lax.ppermute(array, ('gx', 'gy'), pairs)  5.49 us
    pallas_call x2, Pallas kernels, pack(): pl.pallas_call(body, out_shape=[jax.ShapeDtypeStruct(shape, F32) for shap...  2.45 us
    ppermute x3, waiting for transfers between devices, per_device(): reports.append(lax.ppermute(report, 'gy', pairs))  2.05 us
    ppermute x3, starting transfers between devices, per_device(): reports.append(lax.ppermute(report, 'gy', pairs))  1.86 us
  transfers between devices with their start and end apart: 18, of which 8 were waited for; matrix products, arithmetic and copies ran while one was open for 0% of the time, Pallas kernels for 13%

profile of v9, /device:TPU:0, one launch (start us, length us, event | category | flops | bytes accessed | tf_op | source)
XLA Modules:
  0.0 55.5 jit_solution(1626728908674471095)
XLA Ops:
  0.7 1.5 %shard_map.121 = (f32[776,128]{1,0:T(8,128)S(1)}, f32[776,128]{1,0:T(8,128)S(1)}, f32[4,4,8,128]{3,2,1,0:T(8,128)S(1)}, f32[4,4,8,128]{3,2,1,0:T(8,128)S(1)}) custom-call(f32[3,4,128,128]{3,2,1,0:T(8,128)} %flow.13, f32[4,128,128]{2,1,0:T(8,128)} %refs_11_.1), custom_call_target="tpu_custom_call" | custom-call | tf_op jit(solution)/shard_map/pallas_call | solution.py:734
  2.1 3.1 %collective-permute-start = (f32[776,128]{1,0:T(8,128)S(1)}, f32[776,128]{1,0:T(8,128)S(1)}, u32[]{:S(2)}, u32[]{:S(2)}) collective-permute-start(f32[776,128]{1,0:T(8,128)S(1)} %get-tuple-element.28), channel_id=1, source_target_pairs={{0,4},{4,8},{8,12},{12,0},{1,5},{5,9},{9,13},{13,1},{2,6},{6,10},{... | collective-permute-start | bytes 1191944 | tf_op jit(solution)/shard_map/ppermute | solution.py:719
  5.2 2.1 %collective-permute-start.1 = (f32[776,128]{1,0:T(8,128)S(1)}, f32[776,128]{1,0:T(8,128)S(1)}, u32[]{:S(2)}, u32[]{:S(2)}) collective-permute-start(f32[776,128]{1,0:T(8,128)S(1)} %get-tuple-element.29), channel_id=1, source_target_pairs={{0,12},{4,0},{8,4},{12,8},{1,13},{5,1},{9,5},{13,9},{2,14},{6,2},{... | collective-permute-start | bytes 1191944 | tf_op jit(solution)/shard_map/ppermute | solution.py:719
  7.3 1.7 %collective-permute-start.3 = (f32[4,4,8,128]{3,2,1,0:T(8,128)S(1)}, f32[4,4,8,128]{3,2,1,0:T(8,128)S(1)}, u32[]{:S(2)}, u32[]{:S(2)}) collective-permute-start(f32[4,4,8,128]{3,2,1,0:T(8,128)S(1)} %get-tuple-element.31), channel_id=1, source_target_pairs={{0,3},{1,0},{2,1},{3,2},{4,7},{5,4},{6,5},{7,6},{8,11},{9,8},{10,9... | collective-permute-start | bytes 196616 | tf_op jit(solution)/shard_map/ppermute | solution.py:719
  9.0 0.8 %copy-done.7 = f32[128,128]{1,0:T(8,128)S(1)} copy-done((f32[128,128]{1,0:T(8,128)S(1)}, f32[128,128]{1,0:T(8,128)}, u32[]{:S(2)}) %copy-start.7) | copy-done | bytes 65560
  11.0 1.0 %shard_map.125 = f32[264,128]{1,0:T(8,128)S(1)} custom-call(f32[3,4,128,128]{3,2,1,0:T(8,128)} %flow.13, f32[4,128,128]{2,1,0:T(8,128)} %refs_11_.1, s32[4,128,128]{2,1,0:T(8,128)} %flag.5, f32[4,4,8,128]{3,2,1,0:T(8,128)S(1)} %collective-permute-done.2.low_y, f32[4,4,8,128]{3,2,1,0:T(8,128)S(1)} %collective-permute-done.3.high_y), custom_call_target="tpu_custom_call" | custom-call | tf_op jit(solution)/shard_map/pallas_call | solution.py:734
  12.1 5.2 %collective-permute-done.low_x = f32[776,128]{1,0:T(8,128)S(1)} collective-permute-done((f32[776,128]{1,0:T(8,128)S(1)}, f32[776,128]{1,0:T(8,128)S(1)}, u32[]{:S(2)}, u32[]{:S(2)}) %collective-permute-start) | collective-permute-done | bytes 397344 | tf_op jit(solution)/shard_map/ppermute | solution.py:719
  17.3 7.3 %collective-permute-done.1.high_x = f32[776,128]{1,0:T(8,128)S(1)} collective-permute-done((f32[776,128]{1,0:T(8,128)S(1)}, f32[776,128]{1,0:T(8,128)S(1)}, u32[]{:S(2)}, u32[]{:S(2)}) %collective-permute-start.1) | collective-permute-done | bytes 397344 | tf_op jit(solution)/shard_map/ppermute | solution.py:719
  24.8 1.1 %shard_map.124.star = f32[3,4,128,128]{3,2,1,0:T(8,128)S(1)} custom-call(f32[3,4,128,128]{3,2,1,0:T(8,128)S(1)} %copy-done, f32[776,128]{1,0:T(8,128)S(1)} %collective-permute-done.low_x, f32[776,128]{1,0:T(8,128)S(1)} %collective-permute-done.1.high_x, f32[4,128,128]{2,1,0:T(8,128)S(1)} %copy-done.1, s32[4,128,128]{2,1,0:T(8,128)S(1)} %copy-done.2, ...), custom_call_target="tpu_custom_call" | custom-call | flops 1610612736 | bytes 1572864 | tf_op jit(solution)/shard_map/pallas_call | solution.py:30
  26.4 1.5 %collective-permute-done.4.extra = f32[264,128]{1,0:T(8,128)S(1)} collective-permute-done((f32[264,128]{1,0:T(8,128)S(1)}, f32[264,128]{1,0:T(8,128)S(1)}, u32[]{:S(2)}, u32[]{:S(2)}) %collective-permute-start.4) | collective-permute-done | bytes 135200 | tf_op jit(solution)/shard_map/ppermute | solution.py:719
  28.5 1.7 %collective-permute-start.6 = (f32[256,128]{1,0:T(8,128)S(1)}, f32[256,128]{1,0:T(8,128)S(1)}, u32[]{:S(2)}, u32[]{:S(2)}) collective-permute-start(f32[256,128]{1,0:T(8,128)S(1)} %get-tuple-element.35.message), channel_id=1, source_target_pairs={{0,4},{1,5},{2,6},{3,7},{4,0},{5,1},{6,2},{7,3},{8,12},{9,13},{10,... | collective-permute-start | bytes 393224 | tf_op jit(solution)/shard_map/ppermute | solution.py:729
  31.3 1.6 %collective-permute-start.13 = (f32[2,128,128]{2,1,0:T(8,128)S(1)}, f32[2,128,128]{2,1,0:T(8,128)S(1)}, u32[]{:S(2)}, u32[]{:S(2)}) collective-permute-start(f32[2,128,128]{2,1,0:T(8,128)S(1)} %get-tuple-element.41), channel_id=1, source_target_pairs={{0,4},{4,8},{8,12},{12,0},{1,5},{5,9},{9,13},{13,1},{2,6},{6,10},{... | collective-permute-start | bytes 393224 | tf_op jit(solution)/shard_map/ppermute | solution.py:719
  32.9 2.1 %collective-permute-done.7.other_faces = f32[56,128]{1,0:T(8,128)S(1)} collective-permute-done((f32[56,128]{1,0:T(8,128)S(1)}, f32[56,128]{1,0:T(8,128)S(1)}, u32[]{:S(2)}, u32[]{:S(2)}) %collective-permute-start.7) | collective-permute-done | bytes 28704 | tf_op jit(solution)/shard_map/ppermute | solution.py:729
  35.2 2.2 %collective-permute-start.8 = (f32[296,128]{1,0:T(8,128)S(1)}, f32[296,128]{1,0:T(8,128)S(1)}, u32[]{:S(2)}, u32[]{:S(2)}) collective-permute-start(f32[296,128]{1,0:T(8,128)S(1)} %get-tuple-element.37.refs_1_), channel_id=1, source_target_pairs={{0,8},{1,9},{2,10},{3,11},{4,12},{5,13},{6,14},{7,15},{8,0},{9,1},... | collective-permute-start | bytes 454664 | tf_op jit(solution)/shard_map/ppermute | solution.py:729
  37.4 2.1 %collective-permute-start.9 = (f32[16,128]{1,0:T(8,128)S(1)}, f32[16,128]{1,0:T(8,128)S(1)}, u32[]{:S(2)}, u32[]{:S(2)}) collective-permute-start(f32[16,128]{1,0:T(8,128)S(1)} %get-tuple-element.39), channel_id=1, source_target_pairs={{0,1},{1,2},{2,3},{3,0},{4,5},{5,6},{6,7},{7,4},{8,9},{9,10},{10,1... | collective-permute-start | bytes 24584 | tf_op jit(solution)/shard_map/ppermute | solution.py:729
  39.5 1.5 %collective-permute-start.12 = (f32[16,128]{1,0:T(8,128)S(1)}, f32[16,128]{1,0:T(8,128)S(1)}, u32[]{:S(2)}, u32[]{:S(2)}) collective-permute-start(f32[16,128]{1,0:T(8,128)S(1)} %get-tuple-element.40), channel_id=1, source_target_pairs={{0,11},{1,8},{2,9},{3,10},{4,15},{5,12},{6,13},{7,14},{8,3},{9,0},... | collective-permute-start | bytes 24584 | tf_op jit(solution)/shard_map/ppermute | solution.py:729
  41.6 1.2 %shard_map.130 = (f32[4,128,128]{2,1,0:T(8,128)S(1)}, f32[8,128]{1,0:T(8,128)S(1)}) custom-call(s32[8]{0:T(128)S(1)} %copy-done.8, s32[8]{0:T(128)S(1)} %copy-done.9, f32[4,128,128]{2,1,0:T(8,128)S(1)} %copy-done.1, f32[2,128,128]{2,1,0:T(8,128)S(1)} %collective-permute-done.13.halo, f32[4,4,8,128]{3,2,1,0:T(8,128)S(1)} %collective-permute-done.2.low_y, ...), custom_call_target="tpu_custom_call" | custom-call | flops 268435456 | bytes 532480 | tf_op jit(solution)/shard_map/pallas_call | solution.py:30
  42.8 3.4 %collective-permute-done.10.refs_5_ = f32[16,128]{1,0:T(8,128)S(1)} collective-permute-done((f32[16,128]{1,0:T(8,128)S(1)}, f32[16,128]{1,0:T(8,128)S(1)}, u32[]{:S(2)}, u32[]{:S(2)}) %collective-permute-start.10) | collective-permute-done | bytes 8224 | tf_op jit(solution)/shard_map/ppermute | solution.py:729
  46.2 0.9 %shard_map.131 = (f32[5,128,128]{2,1,0:T(8,128)S(1)}, f32[5,128,128]{2,1,0:T(8,128)S(1)}, f32[40,128]{1,0:T(8,128)S(1)}, f32[48,128]{1,0:T(8,128)S(1)}, f32[2,128,128]{2,1,0:T(8,128)S(1)}) custom-call(f32[4,128,128]{2,1,0:T(8,128)S(1)} %get-tuple-element.34.source.refs_0_, f32[296,128]{1,0:T(8,128)S(1)} %get-tuple-element.37.refs_1_, ...), custom_call_target="tpu_custom_call" | custom-call | flops 1048576 | bytes 1662976 | tf_op jit(solution)/shard_map/pallas_call | solution.py:30
  47.1 1.7 %collective-permute-start.17 = (f32[2,128,128]{2,1,0:T(8,128)S(1)}, f32[2,128,128]{2,1,0:T(8,128)S(1)}, u32[]{:S(2)}, u32[]{:S(2)}) collective-permute-start(f32[2,128,128]{2,1,0:T(8,128)S(1)} %get-tuple-element.50), channel_id=1, source_target_pairs={{0,12},{4,0},{8,4},{12,8},{1,13},{5,1},{9,5},{13,9},{2,14},{6,2},{... | collective-permute-start | bytes 393224 | tf_op jit(solution)/shard_map/ppermute | solution.py:719
  48.9 0.8 %collective-permute-start.16 = (f32[40,128]{1,0:T(8,128)S(1)}, f32[40,128]{1,0:T(8,128)S(1)}, u32[]{:S(2)}, u32[]{:S(2)}) collective-permute-start(f32[40,128]{1,0:T(8,128)S(1)} %get-tuple-element.48.refs_0_), channel_id=1, source_target_pairs={{0,3},{1,2},{2,1},{3,0},{4,7},{5,6},{6,5},{7,4},{8,11},{9,10},{10,... | collective-permute-start | bytes 61448 | tf_op jit(solution)/shard_map/ppermute | solution.py:886
  51.4 0.9 %collective-permute-done.16.refs_3_ = f32[40,128]{1,0:T(8,128)S(1)} collective-permute-done((f32[40,128]{1,0:T(8,128)S(1)}, f32[40,128]{1,0:T(8,128)S(1)}, u32[]{:S(2)}, u32[]{:S(2)}) %collective-permute-start.16) | collective-permute-done | bytes 20512 | tf_op jit(solution)/shard_map/ppermute | solution.py:886
  52.3 1.2 %collective-permute-done.15.refs_2_ = f32[40,128]{1,0:T(8,128)S(1)} collective-permute-done((f32[40,128]{1,0:T(8,128)S(1)}, f32[40,128]{1,0:T(8,128)S(1)}, u32[]{:S(2)}, u32[]{:S(2)}) %collective-permute-start.15) | collective-permute-done | bytes 20512 | tf_op jit(solution)/shard_map/ppermute | solution.py:886
  53.5 1.2 %shard_map.133 = (f32[3,4,128,128]{3,2,1,0:T(8,128)}, f32[4,128,128]{2,1,0:T(8,128)}) custom-call(f32[3,4,128,128]{3,2,1,0:T(8,128)S(1)} %shard_map.124.star, f32[5,128,128]{2,1,0:T(8,128)S(1)} %get-tuple-element.45.precond, f32[5,128,128]{2,1,0:T(8,128)S(1)} %get-tuple-element.46.image, f32[48,128]{1,0:T(8,128)S(1)} %get-tuple-element.47.faces, ...), custom_call_target="tpu_custom_call" | custom-call | flops 1048576 | bytes 2097152 | tf_op jit(solution)/shard_map/pallas_call | solution.py:30
  (47 shorter events, 7.0 us)
Async XLA Ops:
  0.6 24.0 %copy-start.1 = (f32[4,128,128]{2,1,0:T(8,128)S(1)}, f32[4,128,128]{2,1,0:T(8,128)}, u32[]{:S(2)}) copy-start(f32[4,128,128]{2,1,0:T(8,128)} %refs_11_.1) | copy-start | bytes 786436
  0.6 24.0 %copy-start = (f32[3,4,128,128]{3,2,1,0:T(8,128)S(1)}, f32[3,4,128,128]{3,2,1,0:T(8,128)}, u32[]{:S(2)}) copy-start(f32[3,4,128,128]{3,2,1,0:T(8,128)} %flow.13) | copy-start | bytes 2359300
  0.7 24.0 %copy-start.2 = (s32[4,128,128]{2,1,0:T(8,128)S(1)}, s32[4,128,128]{2,1,0:T(8,128)}, u32[]{:S(2)}) copy-start(s32[4,128,128]{2,1,0:T(8,128)} %flag.5) | copy-start | bytes 786436
  2.1 15.2 %collective-permute-start = (f32[776,128]{1,0:T(8,128)S(1)}, f32[776,128]{1,0:T(8,128)S(1)}, u32[]{:S(2)}, u32[]{:S(2)}) collective-permute-start(f32[776,128]{1,0:T(8,128)S(1)} %get-tuple-element.28), channel_id=1, source_target_pairs={{0,4},{4,8},{8,12},{12,0},{1,5},{5,9},{9,13},{13,1},{2,6},{6,10},{... | collective-permute-start | bytes 1191944 | tf_op jit(solution)/shard_map/ppermute | solution.py:719
  5.2 19.4 %collective-permute-start.1 = (f32[776,128]{1,0:T(8,128)S(1)}, f32[776,128]{1,0:T(8,128)S(1)}, u32[]{:S(2)}, u32[]{:S(2)}) collective-permute-start(f32[776,128]{1,0:T(8,128)S(1)} %get-tuple-element.29), channel_id=1, source_target_pairs={{0,12},{4,0},{8,4},{12,8},{1,13},{5,1},{9,5},{13,9},{2,14},{6,2},{... | collective-permute-start | bytes 1191944 | tf_op jit(solution)/shard_map/ppermute | solution.py:719
  7.3 3.7 %collective-permute-start.2 = (f32[4,4,8,128]{3,2,1,0:T(8,128)S(1)}, f32[4,4,8,128]{3,2,1,0:T(8,128)S(1)}, u32[]{:S(2)}, u32[]{:S(2)}) collective-permute-start(f32[4,4,8,128]{3,2,1,0:T(8,128)S(1)} %get-tuple-element.30), channel_id=1, source_target_pairs={{0,1},{1,2},{2,3},{3,0},{4,5},{5,6},{6,7},{7,4},{8,9},{9,10},{10,1... | collective-permute-start | bytes 196616 | tf_op jit(solution)/shard_map/ppermute | solution.py:719
  7.3 3.7 %collective-permute-start.3 = (f32[4,4,8,128]{3,2,1,0:T(8,128)S(1)}, f32[4,4,8,128]{3,2,1,0:T(8,128)S(1)}, u32[]{:S(2)}, u32[]{:S(2)}) collective-permute-start(f32[4,4,8,128]{3,2,1,0:T(8,128)S(1)} %get-tuple-element.31), channel_id=1, source_target_pairs={{0,3},{1,0},{2,1},{3,2},{4,7},{5,4},{6,5},{7,6},{8,11},{9,8},{10,9... | collective-permute-start | bytes 196616 | tf_op jit(solution)/shard_map/ppermute | solution.py:719
  12.0 15.9 %collective-permute-start.4 = (f32[264,128]{1,0:T(8,128)S(1)}, f32[264,128]{1,0:T(8,128)S(1)}, u32[]{:S(2)}, u32[]{:S(2)}) collective-permute-start(f32[264,128]{1,0:T(8,128)S(1)} %shard_map.125), channel_id=1, source_target_pairs={{0,4},{4,8},{8,12},{12,0},{1,5},{5,9},{9,13},{13,1},{2,6},{6,10},{... | collective-permute-start | bytes 405512 | tf_op jit(solution)/shard_map/ppermute | solution.py:719
  24.7 3.2 %collective-permute-start.5 = (f32[4,128]{1,0:T(4,128)S(1)}, f32[4,128]{1,0:T(4,128)S(1)}, u32[]{:S(2)}, u32[]{:S(2)}) collective-permute-start(f32[4,128]{1,0:T(4,128)S(1)} %shard_map.123._), channel_id=1, source_target_pairs={{0,1},{1,2},{2,3},{3,0},{4,5},{5,6},{6,7},{7,4},{8,9},{9,10},{10,1... | collective-permute-start | bytes 6152 | tf_op jit(solution)/shard_map/ppermute | solution.py:719
  27.9 2.3 %copy-start.5 = (f32[128,128]{1,0:T(8,128)S(1)}, f32[128,128]{1,0:T(8,128)}, u32[]{:S(2)}) copy-start(f32[128,128]{1,0:T(8,128)} %constant.15.clone.edge.refs_10_) | copy-start | bytes 196612
  28.5 6.5 %collective-permute-start.6 = (f32[256,128]{1,0:T(8,128)S(1)}, f32[256,128]{1,0:T(8,128)S(1)}, u32[]{:S(2)}, u32[]{:S(2)}) collective-permute-start(f32[256,128]{1,0:T(8,128)S(1)} %get-tuple-element.35.message), channel_id=1, source_target_pairs={{0,4},{1,5},{2,6},{3,7},{4,0},{5,1},{6,2},{7,3},{8,12},{9,13},{10,... | collective-permute-start | bytes 393224 | tf_op jit(solution)/shard_map/ppermute | solution.py:729
  30.9 10.7 %copy-start.8 = (s32[8]{0:T(128)S(1)}, s32[8]{0:T(128)}, u32[]{:S(2)}) copy-start(s32[8]{0:T(128)} %spots_a.1) | copy-start | bytes 100
  30.9 10.7 %copy-start.9 = (s32[8]{0:T(128)S(1)}, s32[8]{0:T(128)}, u32[]{:S(2)}) copy-start(s32[8]{0:T(128)} %spots_b.1) | copy-start | bytes 100
  30.9 4.1 %collective-permute-start.7 = (f32[56,128]{1,0:T(8,128)S(1)}, f32[56,128]{1,0:T(8,128)S(1)}, u32[]{:S(2)}, u32[]{:S(2)}) collective-permute-start(f32[56,128]{1,0:T(8,128)S(1)} %get-tuple-element.36.faces), channel_id=1, source_target_pairs={{0,4},{1,5},{2,6},{3,7},{4,0},{5,1},{6,2},{7,3},{8,12},{9,13},{10,... | collective-permute-start | bytes 86024 | tf_op jit(solution)/shard_map/ppermute | solution.py:729
  31.3 9.6 %collective-permute-start.13 = (f32[2,128,128]{2,1,0:T(8,128)S(1)}, f32[2,128,128]{2,1,0:T(8,128)S(1)}, u32[]{:S(2)}, u32[]{:S(2)}) collective-permute-start(f32[2,128,128]{2,1,0:T(8,128)S(1)} %get-tuple-element.41), channel_id=1, source_target_pairs={{0,4},{4,8},{8,12},{12,0},{1,5},{5,9},{9,13},{13,1},{2,6},{6,10},{... | collective-permute-start | bytes 393224 | tf_op jit(solution)/shard_map/ppermute | solution.py:719
  35.2 11.0 %collective-permute-start.8 = (f32[296,128]{1,0:T(8,128)S(1)}, f32[296,128]{1,0:T(8,128)S(1)}, u32[]{:S(2)}, u32[]{:S(2)}) collective-permute-start(f32[296,128]{1,0:T(8,128)S(1)} %get-tuple-element.37.refs_1_), channel_id=1, source_target_pairs={{0,8},{1,9},{2,10},{3,11},{4,12},{5,13},{6,14},{7,15},{8,0},{9,1},... | collective-permute-start | bytes 454664 | tf_op jit(solution)/shard_map/ppermute | solution.py:729
  37.4 8.8 %collective-permute-start.10 = (f32[16,128]{1,0:T(8,128)S(1)}, f32[16,128]{1,0:T(8,128)S(1)}, u32[]{:S(2)}, u32[]{:S(2)}) collective-permute-start(f32[16,128]{1,0:T(8,128)S(1)} %get-tuple-element.39), channel_id=1, source_target_pairs={{0,9},{1,10},{2,11},{3,8},{4,13},{5,14},{6,15},{7,12},{8,1},{9,2},... | collective-permute-start | bytes 24584 | tf_op jit(solution)/shard_map/ppermute | solution.py:729
  37.4 8.8 %collective-permute-start.9 = (f32[16,128]{1,0:T(8,128)S(1)}, f32[16,128]{1,0:T(8,128)S(1)}, u32[]{:S(2)}, u32[]{:S(2)}) collective-permute-start(f32[16,128]{1,0:T(8,128)S(1)} %get-tuple-element.39), channel_id=1, source_target_pairs={{0,1},{1,2},{2,3},{3,0},{4,5},{5,6},{6,7},{7,4},{8,9},{9,10},{10,1... | collective-permute-start | bytes 24584 | tf_op jit(solution)/shard_map/ppermute | solution.py:729
  39.5 6.8 %collective-permute-start.12 = (f32[16,128]{1,0:T(8,128)S(1)}, f32[16,128]{1,0:T(8,128)S(1)}, u32[]{:S(2)}, u32[]{:S(2)}) collective-permute-start(f32[16,128]{1,0:T(8,128)S(1)} %get-tuple-element.40), channel_id=1, source_target_pairs={{0,11},{1,8},{2,9},{3,10},{4,15},{5,12},{6,13},{7,14},{8,3},{9,0},... | collective-permute-start | bytes 24584 | tf_op jit(solution)/shard_map/ppermute | solution.py:729
  40.9 5.3 %collective-permute-start.11 = (f32[16,128]{1,0:T(8,128)S(1)}, f32[16,128]{1,0:T(8,128)S(1)}, u32[]{:S(2)}, u32[]{:S(2)}) collective-permute-start(f32[16,128]{1,0:T(8,128)S(1)} %get-tuple-element.40), channel_id=1, source_target_pairs={{0,3},{1,0},{2,1},{3,2},{4,7},{5,4},{6,5},{7,6},{8,11},{9,8},{10,9... | collective-permute-start | bytes 24584 | tf_op jit(solution)/shard_map/ppermute | solution.py:729
  47.1 7.6 %collective-permute-start.17 = (f32[2,128,128]{2,1,0:T(8,128)S(1)}, f32[2,128,128]{2,1,0:T(8,128)S(1)}, u32[]{:S(2)}, u32[]{:S(2)}) collective-permute-start(f32[2,128,128]{2,1,0:T(8,128)S(1)} %get-tuple-element.50), channel_id=1, source_target_pairs={{0,12},{4,0},{8,4},{12,8},{1,13},{5,1},{9,5},{13,9},{2,14},{6,2},{... | collective-permute-start | bytes 393224 | tf_op jit(solution)/shard_map/ppermute | solution.py:719
  48.9 3.4 %collective-permute-start.16 = (f32[40,128]{1,0:T(8,128)S(1)}, f32[40,128]{1,0:T(8,128)S(1)}, u32[]{:S(2)}, u32[]{:S(2)}) collective-permute-start(f32[40,128]{1,0:T(8,128)S(1)} %get-tuple-element.48.refs_0_), channel_id=1, source_target_pairs={{0,3},{1,2},{2,1},{3,0},{4,7},{5,6},{6,5},{7,4},{8,11},{9,10},{10,... | collective-permute-start | bytes 61448 | tf_op jit(solution)/shard_map/ppermute | solution.py:886
  49.7 3.8 %collective-permute-start.15 = (f32[40,128]{1,0:T(8,128)S(1)}, f32[40,128]{1,0:T(8,128)S(1)}, u32[]{:S(2)}, u32[]{:S(2)}) collective-permute-start(f32[40,128]{1,0:T(8,128)S(1)} %get-tuple-element.48.refs_0_), channel_id=1, source_target_pairs={{0,2},{1,3},{2,0},{3,1},{4,6},{5,7},{6,4},{7,5},{8,10},{9,11},{10,... | collective-permute-start | bytes 61448 | tf_op jit(solution)/shard_map/ppermute | solution.py:886
  50.4 3.1 %collective-permute-start.14 = (f32[40,128]{1,0:T(8,128)S(1)}, f32[40,128]{1,0:T(8,128)S(1)}, u32[]{:S(2)}, u32[]{:S(2)}) collective-permute-start(f32[40,128]{1,0:T(8,128)S(1)} %get-tuple-element.48.refs_0_), channel_id=1, source_target_pairs={{0,1},{1,0},{2,3},{3,2},{4,5},{5,4},{6,7},{7,6},{8,9},{9,8},{10,11... | collective-permute-start | bytes 61448 | tf_op jit(solution)/shard_map/ppermute | solution.py:886
  (4 other events, 5.5 us)

commit v10 on v9

--- a/solution.py
+++ b/solution.py
@@ -315,9 +315,9 @@
         copy.wait()
 
 
-def extra_kernel(flow, thermal, flag, low_y, high_y, extra, flags, top, sems):
+def extra_kernel(flow, thermal, flag, low_y, high_y, extra, last, flags, sems):
     _, layers, rows, depth = flow.shape
-    pairs = [(flag.at[layers - 1], flags), (thermal.at[layers - 2], top)]
+    pairs = [(flag.at[layers - 1], flags), (thermal.at[pl.ds(layers - 2, 2)], last)]
     pairs.append((flow.at[0, layers - 3], extra.at[pl.ds(0, rows), :]))
     copies = started(
         [pltpu.make_async_copy(*pair, sems.at[index]) for index, pair in enumerate(pairs)]
@@ -329,7 +329,7 @@
     for copy in copies[:2]:
         copy.wait()
     extra[pl.ds(rows, rows), :] = flags[...].astype(F32)
-    extra[pl.ds(base, 1), pl.ds(0, rows)] = surface(top[...])
+    extra[pl.ds(base, 1), pl.ds(0, rows)] = surface(last[0])
     for copy in copies[2:]:
         copy.wait()
 
@@ -356,35 +356,25 @@
 
 
 def heat_kernel(
-    spots_a, spots_b, thermal, halo, low_y, high_y, flow, warmed, token, padded
+    spots_a, spots_b, thermal, low_x, high_x, low_y, high_y, flow, warmed, token, padded
 ):
     layers, rows, depth = thermal.shape
     token[...] = jnp.zeros(token.shape, F32)
     top = lax.broadcasted_iota(jnp.int32, (rows, depth), 1) == depth - 1
-    none = jnp.zeros((rows, depth), F32)
     for index in range(layers):
         pad_rows(padded, 0, low_y[3, index, 6:], thermal[index], high_y[3, index, :2])
         around = []
         for other in range(index - 2, index + 3):
             if other < 0:
-                around.append(halo[other + 2])
+                around.append(low_x[other + 2])
             elif other >= layers:
-                around.append(none)
+                around.append(high_x[other - layers])
             else:
                 around.append(thermal[other])
         speed = [flow[part, index] for part in range(3)]
         gain = TIME_INCREMENT * column(laser_row(index, layers, rows, spots_a, spots_b))
         moved = advance(around, padded, 0, coefficients(speed, None))
         warmed[index] = moved + jnp.where(top, gain, 0.0)
-
-
-def heat_last_kernel(flow, halo, warm, warmed):
-    layers = warm.shape[0]
-    warmed[: layers - 2] = warm[: layers - 2]
-    for index, added in ((layers - 2, -halo[0]), (layers - 1, 4.0 * halo[0] - halo[1])):
-        speed = flow[0, index]
-        factor = jnp.where(speed >= 0.0, 0.0, 0.5 * TIME_INCREMENT * jnp.abs(speed))
-        warmed[index] = warm[index] + factor * added
 
 
 def tables_kernel(group, layers, diagonal, ratio, weight):
@@ -444,10 +434,10 @@
 
 
 def faces_kernel(
-    group, length, source, before_y, table_z, ratio, weight, edge, thermal, faces, late, sweep
+    group, length, source, before_y, table_z, ratio, weight, edge, thermal, _, faces, late, sweep
 ):
     layers, rows, depth = source.shape
-    late[...] = thermal[layers - 2 :]
+    late[...] = thermal[:2]
     first = position(group) * layers
     zero = jnp.zeros((rows, depth), F32)
     extra = dot(before_y[...], table_z[...])
@@ -561,12 +551,10 @@
 
 
 def coarse_kernel(
-    turn, group, length, alone, source, message, other, sums, faces_in, weight, ratio, edge,
-    thermal, *refs
+    turn, group, length, alone, source, message, other, sums, faces_in, weight, ratio, edge, *refs
 ):
-    precond, image, report, faces, onward, late, sweep, ends = refs[-8:]
+    precond, image, report, faces, late, sweep, ends = refs[-7:]
     layers, rows, depth = source.shape
-    onward[...] = thermal[:2]
     first = position(group) * layers
     below, below_far, above, above_far = faces_in
     forward, backward, before, after, energy = joined(turn, group, message, other, sums, weight)
@@ -772,15 +760,16 @@
     high_x = along(behind, "gx", -1)
     low_y = along(last_rows, "gy", 1)
     high_y = along(first_rows, "gy", -1)
-    (extra,) = pack(
+    extra, last = pack(
         extra_kernel,
         [melt_flow, thermal_state, powder_flag],
         [low_y, high_y],
-        [(2 * rows + 8, width)],
-        [pltpu.VMEM(plane, jnp.int32), pltpu.VMEM(plane, F32)],
+        [(2 * rows + 8, width), (2,) + plane],
+        [pltpu.VMEM(plane, jnp.int32)],
         3,
     )
     extra = along(extra, "gx", 1)
+    early_low = along(last, "gx", 1)
     ratio, weight = call(
         functools.partial(tables_kernel, group, layers),
         [diagonal],
@@ -792,14 +781,14 @@
     (side_y,) = call(row_kernel, marched + [weight], [(layers, depth)], [padded], loose=1)
     before_y = along(side_y, "gy", 1)
     (star,) = call(
-        march_kernel, marched + [side_y], [(3, layers) + plane], [padded], loose=1, flops=3 << 29
+        march_kernel, marched + [side_y], [(3, layers) + plane], [padded], loose=1, flops=3 << 27
     )
     (partial,) = call(
         transform_kernel,
         [star, left, right],
         [(layers,) + plane],
         [pltpu.VMEM((rows + 16, depth), F32)],
-        flops=1 << 29,
+        flops=1 << 27,
     )
     source, message = call(
         functools.partial(source_kernel, group, length),
@@ -810,15 +799,17 @@
     )
     faces, late = call(
         functools.partial(faces_kernel, group, length),
-        [source, before_y, table_z, ratio, weight, edge, thermal_state],
+        [source, before_y, table_z, ratio, weight, edge, thermal_state, early_low],
         [(3 * length + 8, depth), (2,) + plane],
         [pltpu.VMEM((max(length, layers + 1),) + plane, F32)],
+        loose=1,
     )
     alone = blocks == 1
-    warm, token = call(
+    early_high = along(late, "gx", -1)
+    warmed, token = call(
         heat_kernel,
         [
-            spot_lateral_a_cell, spot_lateral_b_cell, thermal_state, along(late, "gx", 1),
+            spot_lateral_a_cell, spot_lateral_b_cell, thermal_state, early_low, early_high,
             low_y, high_y, melt_flow,
         ],
         [(layers,) + plane, (8, depth)],
@@ -855,17 +846,17 @@
         )
         outer = [jnp.stack([along(ends[0], "gx", group), along(ends[1], "gx", -group)])]
     operands = [source, message, other, sums] + rim
-    operands += [weight, ratio, edge, thermal_state] + outer + [token]
+    operands += [weight, ratio, edge] + outer + [token]
 
     def coarse(*refs):
         coarse_kernel(rounds - 1, group, length, alone, *refs[:4], refs[4:8], *refs[8:])
 
-    precond, image, report, faces, late = call(
+    precond, image, report, faces = call(
         coarse,
         operands,
         [
             (layers + 1,) + plane, (layers + 1,) + plane, (2 * length + 8, depth),
-            (3 * length, depth), (2,) + plane,
+            (3 * length, depth),
         ],
         scratch + [pltpu.VMEM((2,) + plane, F32)],
         loose=1,
@@ -889,8 +880,6 @@
         [precond, image, left, right],
         [(layers + 1,) + plane, (layers + 1,) + plane],
     )
-    late = along(late, "gx", -1)
-    (warmed,) = call(heat_last_kernel, [melt_flow, late, warm], [(layers,) + plane])
     flow, pressure = call(
         functools.partial(project_kernel, group, length, blocks > 1),
         [star, precond, image, faces, table_z] + reports,

time: 55.7 us -> 52.3 us (0.939)
  waiting for transfers between devices: 22.3 us -> 20.2 us
  local copies, waits for them, and re-layouts: 0.9 us -> 0.06 us
    ppermute x7, waiting for transfers between devices: 5.49 us -> 3.02 us  [swapped(): return lax.ppermute(array, ('gx', 'gy'), pairs)]
    ppermute x7, starting transfers between devices: 8.54 us -> 7.27 us  [swapped(): return lax.ppermute(array, ('gx', 'gy'), pairs)]
    unnamed x20, local copies, waits for them, and re-layouts: 0.89 us -> 0.05 us
    ppermute x3, starting transfers between devices: 1.86 us -> 2.43 us  [per_device(): reports.append(lax.ppermute(report, 'gy', pairs))]
    ppermute x8, waiting for transfers between devices: 14.7 us -> 15.3 us  [along(): lax.ppermute(array, axis, [(i, (i + by) % length) for i in range(length)])]
    pallas_call x12 -> x11, Pallas kernels: 8.28 us -> 8.2 us  [call(): pl.pallas_call(body, out_shape=out_shape, in_specs=[SMEM] * scalars + [VM...]
  transfers between devices with their start and end apart: 18 -> 18, of which waited for: 8 -> 11; matrix products, arithmetic and copies ran while one was open for 0% -> 0% of each run, Pallas kernels for 13% -> 14%
where the time goes in v10:
time: 52.3 us; the launch traced here: 52.1 us
  starting transfers between devices  20.4 us (39%)
  waiting for transfers between devices  20.2 us (39%)
  Pallas kernels  10.7 us (20%)
  between operations  0.81 us (2%)
    ppermute x8, waiting for transfers between devices, along(): lax.ppermute(array, axis, [(i, (i + by) % length) for i in range(length)])  15.3 us
    ppermute x8, starting transfers between devices, along(): lax.ppermute(array, axis, [(i, (i + by) % length) for i in range(length)])  10.7 us
    pallas_call x11, Pallas kernels, call(): pl.pallas_call(body, out_shape=out_shape, in_specs=[SMEM] * scalars + [VM...  8.2 us
    ppermute x7, starting transfers between devices, swapped(): return lax.ppermute(array, ('gx', 'gy'), pairs)  7.27 us
    ppermute x7, waiting for transfers between devices, swapped(): return lax.ppermute(array, ('gx', 'gy'), pairs)  3.02 us
    pallas_call x2, Pallas kernels, pack(): pl.pallas_call(body, out_shape=[jax.ShapeDtypeStruct(shape, F32) for shap...  2.52 us
    ppermute x3, starting transfers between devices, per_device(): reports.append(lax.ppermute(report, 'gy', pairs))  2.43 us
    ppermute x3, waiting for transfers between devices, per_device(): reports.append(lax.ppermute(report, 'gy', pairs))  1.83 us
  transfers between devices with their start and end apart: 18, of which 11 were waited for; matrix products, arithmetic and copies ran while one was open for 0% of the time, Pallas kernels for 14%

profile of v10, /device:TPU:0, one launch (start us, length us, event | category | flops | bytes accessed | tf_op | source)
XLA Modules:
  0.0 52.1 jit_solution(9398111398276673589)
XLA Ops:
  0.7 1.5 %shard_map.121 = (f32[776,128]{1,0:T(8,128)S(1)}, f32[776,128]{1,0:T(8,128)S(1)}, f32[4,4,8,128]{3,2,1,0:T(8,128)S(1)}, f32[4,4,8,128]{3,2,1,0:T(8,128)S(1)}) custom-call(f32[3,4,128,128]{3,2,1,0:T(8,128)} %flow.11, f32[4,128,128]{2,1,0:T(8,128)} %thermal.13), custom_call_target="tpu_custom_call" | custom-call | tf_op jit(solution)/shard_map/pallas_call | solution.py:722
  2.1 3.1 %collective-permute-start = (f32[776,128]{1,0:T(8,128)S(1)}, f32[776,128]{1,0:T(8,128)S(1)}, u32[]{:S(2)}, u32[]{:S(2)}) collective-permute-start(f32[776,128]{1,0:T(8,128)S(1)} %get-tuple-element.29), channel_id=1, source_target_pairs={{0,4},{4,8},{8,12},{12,0},{1,5},{5,9},{9,13},{13,1},{2,6},{6,10},{... | collective-permute-start | bytes 1191944 | tf_op jit(solution)/shard_map/ppermute | solution.py:707
  5.2 2.1 %collective-permute-start.1 = (f32[776,128]{1,0:T(8,128)S(1)}, f32[776,128]{1,0:T(8,128)S(1)}, u32[]{:S(2)}, u32[]{:S(2)}) collective-permute-start(f32[776,128]{1,0:T(8,128)S(1)} %get-tuple-element.30), channel_id=1, source_target_pairs={{0,12},{4,0},{8,4},{12,8},{1,13},{5,1},{9,5},{13,9},{2,14},{6,2},{... | collective-permute-start | bytes 1191944 | tf_op jit(solution)/shard_map/ppermute | solution.py:707
  7.3 1.7 %collective-permute-start.3 = (f32[4,4,8,128]{3,2,1,0:T(8,128)S(1)}, f32[4,4,8,128]{3,2,1,0:T(8,128)S(1)}, u32[]{:S(2)}, u32[]{:S(2)}) collective-permute-start(f32[4,4,8,128]{3,2,1,0:T(8,128)S(1)} %get-tuple-element.32), channel_id=1, source_target_pairs={{0,3},{1,0},{2,1},{3,2},{4,7},{5,4},{6,5},{7,6},{8,11},{9,8},{10,9... | collective-permute-start | bytes 196616 | tf_op jit(solution)/shard_map/ppermute | solution.py:707
  9.1 1.9 %collective-permute-done.2.low_y = f32[4,4,8,128]{3,2,1,0:T(8,128)S(1)} collective-permute-done((f32[4,4,8,128]{3,2,1,0:T(8,128)S(1)}, f32[4,4,8,128]{3,2,1,0:T(8,128)S(1)}, u32[]{:S(2)}, u32[]{:S(2)}) %collective-permute-start.2) | collective-permute-done | bytes 65568 | tf_op jit(solution)/shard_map/ppermute | solution.py:707
  11.0 1.1 %shard_map.125 = (f32[264,128]{1,0:T(8,128)S(1)}, f32[2,128,128]{2,1,0:T(8,128)S(1)}) custom-call(f32[3,4,128,128]{3,2,1,0:T(8,128)} %flow.11, f32[4,128,128]{2,1,0:T(8,128)} %thermal.13, s32[4,128,128]{2,1,0:T(8,128)} %flag.5, f32[4,4,8,128]{3,2,1,0:T(8,128)S(1)} %collective-permute-done.2.low_y, f32[4,4,8,128]{3,2,1,0:T(8,128)S(1)} %collective-permute-done.3.high_y), custom_call_target="tpu_custom_call" | custom-call | tf_op jit(solution)/shard_map/pallas_call | solution.py:722
  12.6 1.5 %collective-permute-start.7 = (f32[2,128,128]{2,1,0:T(8,128)S(1)}, f32[2,128,128]{2,1,0:T(8,128)S(1)}, u32[]{:S(2)}, u32[]{:S(2)}) collective-permute-start(f32[2,128,128]{2,1,0:T(8,128)S(1)} %get-tuple-element.38), channel_id=1, source_target_pairs={{0,4},{4,8},{8,12},{12,0},{1,5},{5,9},{9,13},{13,1},{2,6},{6,10},{... | collective-permute-start | bytes 393224 | tf_op jit(solution)/shard_map/ppermute | solution.py:707
  14.1 3.2 %collective-permute-done.low_x = f32[776,128]{1,0:T(8,128)S(1)} collective-permute-done((f32[776,128]{1,0:T(8,128)S(1)}, f32[776,128]{1,0:T(8,128)S(1)}, u32[]{:S(2)}, u32[]{:S(2)}) %collective-permute-start) | collective-permute-done | bytes 397344 | tf_op jit(solution)/shard_map/ppermute | solution.py:707
  17.3 7.3 %collective-permute-done.1.high_x = f32[776,128]{1,0:T(8,128)S(1)} collective-permute-done((f32[776,128]{1,0:T(8,128)S(1)}, f32[776,128]{1,0:T(8,128)S(1)}, u32[]{:S(2)}, u32[]{:S(2)}) %collective-permute-start.1) | collective-permute-done | bytes 397344 | tf_op jit(solution)/shard_map/ppermute | solution.py:707
  24.8 1.1 %shard_map.124.star = f32[3,4,128,128]{3,2,1,0:T(8,128)S(1)} custom-call(f32[3,4,128,128]{3,2,1,0:T(8,128)S(1)} %copy-done, f32[776,128]{1,0:T(8,128)S(1)} %collective-permute-done.low_x, f32[776,128]{1,0:T(8,128)S(1)} %collective-permute-done.1.high_x, f32[4,128,128]{2,1,0:T(8,128)S(1)} %copy-done.1, s32[4,128,128]{2,1,0:T(8,128)S(1)} %copy-done.2, ...), custom_call_target="tpu_custom_call" | custom-call | flops 402653184 | bytes 1572864 | tf_op jit(solution)/shard_map/pallas_call | solution.py:30
  26.4 2.3 %collective-permute-done.4.extra = f32[264,128]{1,0:T(8,128)S(1)} collective-permute-done((f32[264,128]{1,0:T(8,128)S(1)}, f32[264,128]{1,0:T(8,128)S(1)}, u32[]{:S(2)}, u32[]{:S(2)}) %collective-permute-start.4) | collective-permute-done | bytes 135200 | tf_op jit(solution)/shard_map/ppermute | solution.py:707
  29.4 0.8 %collective-permute-start.6 = (f32[256,128]{1,0:T(8,128)S(1)}, f32[256,128]{1,0:T(8,128)S(1)}, u32[]{:S(2)}, u32[]{:S(2)}) collective-permute-start(f32[256,128]{1,0:T(8,128)S(1)} %get-tuple-element.37.message), channel_id=1, source_target_pairs={{0,4},{1,5},{2,6},{3,7},{4,0},{5,1},{6,2},{7,3},{8,12},{9,13},{10,... | collective-permute-start | bytes 393224 | tf_op jit(solution)/shard_map/ppermute | solution.py:717
  31.4 0.8 %collective-permute-start.8 = (f32[56,128]{1,0:T(8,128)S(1)}, f32[56,128]{1,0:T(8,128)S(1)}, u32[]{:S(2)}, u32[]{:S(2)}) collective-permute-start(f32[56,128]{1,0:T(8,128)S(1)} %get-tuple-element.39.faces), channel_id=1, source_target_pairs={{0,4},{1,5},{2,6},{3,7},{4,0},{5,1},{6,2},{7,3},{8,12},{9,13},{10,... | collective-permute-start | bytes 86024 | tf_op jit(solution)/shard_map/ppermute | solution.py:717
  32.2 2.1 %collective-permute-start.14 = (f32[2,128,128]{2,1,0:T(8,128)S(1)}, f32[2,128,128]{2,1,0:T(8,128)S(1)}, u32[]{:S(2)}, u32[]{:S(2)}) collective-permute-start(f32[2,128,128]{2,1,0:T(8,128)S(1)} %get-tuple-element.44), channel_id=1, source_target_pairs={{0,12},{4,0},{8,4},{12,8},{1,13},{5,1},{9,5},{13,9},{2,14},{6,2},{... | collective-permute-start | bytes 393224 | tf_op jit(solution)/shard_map/ppermute | solution.py:707
  34.3 1.5 %collective-permute-done.8.other_faces = f32[56,128]{1,0:T(8,128)S(1)} collective-permute-done((f32[56,128]{1,0:T(8,128)S(1)}, f32[56,128]{1,0:T(8,128)S(1)}, u32[]{:S(2)}, u32[]{:S(2)}) %collective-permute-start.8) | collective-permute-done | bytes 28704 | tf_op jit(solution)/shard_map/ppermute | solution.py:717
  35.9 1.4 %collective-permute-start.9 = (f32[296,128]{1,0:T(8,128)S(1)}, f32[296,128]{1,0:T(8,128)S(1)}, u32[]{:S(2)}, u32[]{:S(2)}) collective-permute-start(f32[296,128]{1,0:T(8,128)S(1)} %get-tuple-element.40.refs_1_), channel_id=1, source_target_pairs={{0,8},{1,9},{2,10},{3,11},{4,12},{5,13},{6,14},{7,15},{8,0},{9,1},... | collective-permute-start | bytes 454664 | tf_op jit(solution)/shard_map/ppermute | solution.py:717
  37.4 3.2 %collective-permute-start.10 = (f32[16,128]{1,0:T(8,128)S(1)}, f32[16,128]{1,0:T(8,128)S(1)}, u32[]{:S(2)}, u32[]{:S(2)}) collective-permute-start(f32[16,128]{1,0:T(8,128)S(1)} %get-tuple-element.42), channel_id=1, source_target_pairs={{0,1},{1,2},{2,3},{3,0},{4,5},{5,6},{6,7},{7,4},{8,9},{9,10},{10,1... | collective-permute-start | bytes 24584 | tf_op jit(solution)/shard_map/ppermute | solution.py:717
  41.6 1.9 %shard_map.130 = (f32[4,128,128]{2,1,0:T(8,128)}, f32[8,128]{1,0:T(8,128)S(1)}) custom-call(s32[8]{0:T(128)S(1)} %copy-done.8, s32[8]{0:T(128)S(1)} %copy-done.9, f32[4,128,128]{2,1,0:T(8,128)S(1)} %copy-done.1, f32[2,128,128]{2,1,0:T(8,128)S(1)} %collective-permute-done.7._.low_x, f32[2,128,128]{2,1,0:T(8,128)S(1)} %collective-permute-done.14.high_x, ...), custom_call_target="tpu_custom_call" | custom-call | flops 268435456 | bytes 532480 | tf_op jit(solution)/shard_map/pallas_call | solution.py:30
  43.5 0.9 %collective-permute-done.11.refs_5_ = f32[16,128]{1,0:T(8,128)S(1)} collective-permute-done((f32[16,128]{1,0:T(8,128)S(1)}, f32[16,128]{1,0:T(8,128)S(1)}, u32[]{:S(2)}, u32[]{:S(2)}) %collective-permute-start.11) | collective-permute-done | bytes 8224 | tf_op jit(solution)/shard_map/ppermute | solution.py:717
  45.1 0.9 %shard_map.131 = (f32[5,128,128]{2,1,0:T(8,128)S(1)}, f32[5,128,128]{2,1,0:T(8,128)S(1)}, f32[40,128]{1,0:T(8,128)S(1)}, f32[48,128]{1,0:T(8,128)S(1)}) custom-call(f32[4,128,128]{2,1,0:T(8,128)S(1)} %get-tuple-element.36.source.refs_0_, f32[296,128]{1,0:T(8,128)S(1)} %get-tuple-element.40.refs_1_, f32[296,128]{1,0:T(8,128)S(1)} %collective-permute-done.9.refs_2_, ...), custom_call_target="tpu_custom_call" | custom-call | flops 1048576 | bytes 1400832 | tf_op jit(solution)/shard_map/pallas_call | solution.py:30
  46.0 1.1 %collective-permute-start.17 = (f32[40,128]{1,0:T(8,128)S(1)}, f32[40,128]{1,0:T(8,128)S(1)}, u32[]{:S(2)}, u32[]{:S(2)}) collective-permute-start(f32[40,128]{1,0:T(8,128)S(1)} %get-tuple-element.51.refs_0_), channel_id=1, source_target_pairs={{0,3},{1,2},{2,1},{3,0},{4,7},{5,6},{6,5},{7,4},{8,11},{9,10},{10,... | collective-permute-start | bytes 61448 | tf_op jit(solution)/shard_map/ppermute | solution.py:877
  47.1 1.3 %collective-permute-start.16 = (f32[40,128]{1,0:T(8,128)S(1)}, f32[40,128]{1,0:T(8,128)S(1)}, u32[]{:S(2)}, u32[]{:S(2)}) collective-permute-start(f32[40,128]{1,0:T(8,128)S(1)} %get-tuple-element.51.refs_0_), channel_id=1, source_target_pairs={{0,2},{1,3},{2,0},{3,1},{4,6},{5,7},{6,4},{7,5},{8,10},{9,11},{10,... | collective-permute-start | bytes 61448 | tf_op jit(solution)/shard_map/ppermute | solution.py:877
  49.2 1.6 %collective-permute-done.16.refs_2_ = f32[40,128]{1,0:T(8,128)S(1)} collective-permute-done((f32[40,128]{1,0:T(8,128)S(1)}, f32[40,128]{1,0:T(8,128)S(1)}, u32[]{:S(2)}, u32[]{:S(2)}) %collective-permute-start.16) | collective-permute-done | bytes 20512 | tf_op jit(solution)/shard_map/ppermute | solution.py:877
  50.9 1.2 %shard_map.133 = (f32[3,4,128,128]{3,2,1,0:T(8,128)}, f32[4,128,128]{2,1,0:T(8,128)}) custom-call(f32[3,4,128,128]{3,2,1,0:T(8,128)S(1)} %shard_map.124.star, f32[5,128,128]{2,1,0:T(8,128)S(1)} %get-tuple-element.48.precond, f32[5,128,128]{2,1,0:T(8,128)S(1)} %get-tuple-element.49.image, f32[48,128]{1,0:T(8,128)S(1)} %get-tuple-element.50.faces, ...), custom_call_target="tpu_custom_call" | custom-call | flops 1048576 | bytes 2097152 | tf_op jit(solution)/shard_map/pallas_call | solution.py:30
  (46 shorter events, 5.6 us)
Async XLA Ops:
  0.6 11.5 %copy-start.7 = (f32[128,128]{1,0:T(8,128)S(1)}, f32[128,128]{1,0:T(8,128)}, u32[]{:S(2)}) copy-start(f32[128,128]{1,0:T(8,128)} %constant.16.clone.diagonal) | copy-start | bytes 196612
  0.6 24.0 %copy-start.1 = (f32[4,128,128]{2,1,0:T(8,128)S(1)}, f32[4,128,128]{2,1,0:T(8,128)}, u32[]{:S(2)}) copy-start(f32[4,128,128]{2,1,0:T(8,128)} %thermal.13) | copy-start | bytes 786436
  0.7 24.0 %copy-start = (f32[3,4,128,128]{3,2,1,0:T(8,128)S(1)}, f32[3,4,128,128]{3,2,1,0:T(8,128)}, u32[]{:S(2)}) copy-start(f32[3,4,128,128]{3,2,1,0:T(8,128)} %flow.11) | copy-start | bytes 2359300
  0.7 24.0 %copy-start.2 = (s32[4,128,128]{2,1,0:T(8,128)S(1)}, s32[4,128,128]{2,1,0:T(8,128)}, u32[]{:S(2)}) copy-start(s32[4,128,128]{2,1,0:T(8,128)} %flag.5) | copy-start | bytes 786436
  2.1 15.2 %collective-permute-start = (f32[776,128]{1,0:T(8,128)S(1)}, f32[776,128]{1,0:T(8,128)S(1)}, u32[]{:S(2)}, u32[]{:S(2)}) collective-permute-start(f32[776,128]{1,0:T(8,128)S(1)} %get-tuple-element.29), channel_id=1, source_target_pairs={{0,4},{4,8},{8,12},{12,0},{1,5},{5,9},{9,13},{13,1},{2,6},{6,10},{... | collective-permute-start | bytes 1191944 | tf_op jit(solution)/shard_map/ppermute | solution.py:707
  5.2 19.4 %collective-permute-start.1 = (f32[776,128]{1,0:T(8,128)S(1)}, f32[776,128]{1,0:T(8,128)S(1)}, u32[]{:S(2)}, u32[]{:S(2)}) collective-permute-start(f32[776,128]{1,0:T(8,128)S(1)} %get-tuple-element.30), channel_id=1, source_target_pairs={{0,12},{4,0},{8,4},{12,8},{1,13},{5,1},{9,5},{13,9},{2,14},{6,2},{... | collective-permute-start | bytes 1191944 | tf_op jit(solution)/shard_map/ppermute | solution.py:707
  7.3 3.7 %collective-permute-start.2 = (f32[4,4,8,128]{3,2,1,0:T(8,128)S(1)}, f32[4,4,8,128]{3,2,1,0:T(8,128)S(1)}, u32[]{:S(2)}, u32[]{:S(2)}) collective-permute-start(f32[4,4,8,128]{3,2,1,0:T(8,128)S(1)} %get-tuple-element.31), channel_id=1, source_target_pairs={{0,1},{1,2},{2,3},{3,0},{4,5},{5,6},{6,7},{7,4},{8,9},{9,10},{10,1... | collective-permute-start | bytes 196616 | tf_op jit(solution)/shard_map/ppermute | solution.py:707
  7.3 3.7 %collective-permute-start.3 = (f32[4,4,8,128]{3,2,1,0:T(8,128)S(1)}, f32[4,4,8,128]{3,2,1,0:T(8,128)S(1)}, u32[]{:S(2)}, u32[]{:S(2)}) collective-permute-start(f32[4,4,8,128]{3,2,1,0:T(8,128)S(1)} %get-tuple-element.32), channel_id=1, source_target_pairs={{0,3},{1,0},{2,1},{3,2},{4,7},{5,4},{6,5},{7,6},{8,11},{9,8},{10,9... | collective-permute-start | bytes 196616 | tf_op jit(solution)/shard_map/ppermute | solution.py:707
  12.1 16.6 %collective-permute-start.4 = (f32[264,128]{1,0:T(8,128)S(1)}, f32[264,128]{1,0:T(8,128)S(1)}, u32[]{:S(2)}, u32[]{:S(2)}) collective-permute-start(f32[264,128]{1,0:T(8,128)S(1)} %get-tuple-element.34), channel_id=1, source_target_pairs={{0,4},{4,8},{8,12},{12,0},{1,5},{5,9},{9,13},{13,1},{2,6},{6,10},{... | collective-permute-start | bytes 405512 | tf_op jit(solution)/shard_map/ppermute | solution.py:707
  12.6 18.1 %collective-permute-start.7 = (f32[2,128,128]{2,1,0:T(8,128)S(1)}, f32[2,128,128]{2,1,0:T(8,128)S(1)}, u32[]{:S(2)}, u32[]{:S(2)}) collective-permute-start(f32[2,128,128]{2,1,0:T(8,128)S(1)} %get-tuple-element.38), channel_id=1, source_target_pairs={{0,4},{4,8},{8,12},{12,0},{1,5},{5,9},{9,13},{13,1},{2,6},{6,10},{... | collective-permute-start | bytes 393224 | tf_op jit(solution)/shard_map/ppermute | solution.py:707
  24.7 4.0 %collective-permute-start.5 = (f32[4,128]{1,0:T(4,128)S(1)}, f32[4,128]{1,0:T(4,128)S(1)}, u32[]{:S(2)}, u32[]{:S(2)}) collective-permute-start(f32[4,128]{1,0:T(4,128)S(1)} %shard_map.123._), channel_id=1, source_target_pairs={{0,1},{1,2},{2,3},{3,0},{4,5},{5,6},{6,7},{7,4},{8,9},{9,10},{10,1... | collective-permute-start | bytes 6152 | tf_op jit(solution)/shard_map/ppermute | solution.py:707
  29.4 6.4 %collective-permute-start.6 = (f32[256,128]{1,0:T(8,128)S(1)}, f32[256,128]{1,0:T(8,128)S(1)}, u32[]{:S(2)}, u32[]{:S(2)}) collective-permute-start(f32[256,128]{1,0:T(8,128)S(1)} %get-tuple-element.37.message), channel_id=1, source_target_pairs={{0,4},{1,5},{2,6},{3,7},{4,0},{5,1},{6,2},{7,3},{8,12},{9,13},{10,... | collective-permute-start | bytes 393224 | tf_op jit(solution)/shard_map/ppermute | solution.py:717
  31.4 10.2 %copy-start.8 = (s32[8]{0:T(128)S(1)}, s32[8]{0:T(128)}, u32[]{:S(2)}) copy-start(s32[8]{0:T(128)} %spots_a.1) | copy-start | bytes 100
  31.4 10.2 %copy-start.9 = (s32[8]{0:T(128)S(1)}, s32[8]{0:T(128)}, u32[]{:S(2)}) copy-start(s32[8]{0:T(128)} %spots_b.1) | copy-start | bytes 100
  31.4 4.4 %collective-permute-start.8 = (f32[56,128]{1,0:T(8,128)S(1)}, f32[56,128]{1,0:T(8,128)S(1)}, u32[]{:S(2)}, u32[]{:S(2)}) collective-permute-start(f32[56,128]{1,0:T(8,128)S(1)} %get-tuple-element.39.faces), channel_id=1, source_target_pairs={{0,4},{1,5},{2,6},{3,7},{4,0},{5,1},{6,2},{7,3},{8,12},{9,13},{10,... | collective-permute-start | bytes 86024 | tf_op jit(solution)/shard_map/ppermute | solution.py:717
  32.2 8.8 %collective-permute-start.14 = (f32[2,128,128]{2,1,0:T(8,128)S(1)}, f32[2,128,128]{2,1,0:T(8,128)S(1)}, u32[]{:S(2)}, u32[]{:S(2)}) collective-permute-start(f32[2,128,128]{2,1,0:T(8,128)S(1)} %get-tuple-element.44), channel_id=1, source_target_pairs={{0,12},{4,0},{8,4},{12,8},{1,13},{5,1},{9,5},{13,9},{2,14},{6,2},{... | collective-permute-start | bytes 393224 | tf_op jit(solution)/shard_map/ppermute | solution.py:707
  35.9 9.1 %collective-permute-start.9 = (f32[296,128]{1,0:T(8,128)S(1)}, f32[296,128]{1,0:T(8,128)S(1)}, u32[]{:S(2)}, u32[]{:S(2)}) collective-permute-start(f32[296,128]{1,0:T(8,128)S(1)} %get-tuple-element.40.refs_1_), channel_id=1, source_target_pairs={{0,8},{1,9},{2,10},{3,11},{4,12},{5,13},{6,14},{7,15},{8,0},{9,1},... | collective-permute-start | bytes 454664 | tf_op jit(solution)/shard_map/ppermute | solution.py:717
  37.4 7.1 %collective-permute-start.11 = (f32[16,128]{1,0:T(8,128)S(1)}, f32[16,128]{1,0:T(8,128)S(1)}, u32[]{:S(2)}, u32[]{:S(2)}) collective-permute-start(f32[16,128]{1,0:T(8,128)S(1)} %get-tuple-element.42), channel_id=1, source_target_pairs={{0,9},{1,10},{2,11},{3,8},{4,13},{5,14},{6,15},{7,12},{8,1},{9,2},... | collective-permute-start | bytes 24584 | tf_op jit(solution)/shard_map/ppermute | solution.py:717
  37.4 7.1 %collective-permute-start.10 = (f32[16,128]{1,0:T(8,128)S(1)}, f32[16,128]{1,0:T(8,128)S(1)}, u32[]{:S(2)}, u32[]{:S(2)}) collective-permute-start(f32[16,128]{1,0:T(8,128)S(1)} %get-tuple-element.42), channel_id=1, source_target_pairs={{0,1},{1,2},{2,3},{3,0},{4,5},{5,6},{6,7},{7,4},{8,9},{9,10},{10,1... | collective-permute-start | bytes 24584 | tf_op jit(solution)/shard_map/ppermute | solution.py:717
  40.6 4.1 %collective-permute-start.13 = (f32[16,128]{1,0:T(8,128)S(1)}, f32[16,128]{1,0:T(8,128)S(1)}, u32[]{:S(2)}, u32[]{:S(2)}) collective-permute-start(f32[16,128]{1,0:T(8,128)S(1)} %get-tuple-element.43), channel_id=1, source_target_pairs={{0,11},{1,8},{2,9},{3,10},{4,15},{5,12},{6,13},{7,14},{8,3},{9,0},... | collective-permute-start | bytes 24584 | tf_op jit(solution)/shard_map/ppermute | solution.py:717
  40.9 3.8 %collective-permute-start.12 = (f32[16,128]{1,0:T(8,128)S(1)}, f32[16,128]{1,0:T(8,128)S(1)}, u32[]{:S(2)}, u32[]{:S(2)}) collective-permute-start(f32[16,128]{1,0:T(8,128)S(1)} %get-tuple-element.43), channel_id=1, source_target_pairs={{0,3},{1,0},{2,1},{3,2},{4,7},{5,4},{6,5},{7,6},{8,11},{9,8},{10,9... | collective-permute-start | bytes 24584 | tf_op jit(solution)/shard_map/ppermute | solution.py:717
  46.0 3.3 %collective-permute-start.17 = (f32[40,128]{1,0:T(8,128)S(1)}, f32[40,128]{1,0:T(8,128)S(1)}, u32[]{:S(2)}, u32[]{:S(2)}) collective-permute-start(f32[40,128]{1,0:T(8,128)S(1)} %get-tuple-element.51.refs_0_), channel_id=1, source_target_pairs={{0,3},{1,2},{2,1},{3,0},{4,7},{5,6},{6,5},{7,4},{8,11},{9,10},{10,... | collective-permute-start | bytes 61448 | tf_op jit(solution)/shard_map/ppermute | solution.py:877
  47.1 3.8 %collective-permute-start.16 = (f32[40,128]{1,0:T(8,128)S(1)}, f32[40,128]{1,0:T(8,128)S(1)}, u32[]{:S(2)}, u32[]{:S(2)}) collective-permute-start(f32[40,128]{1,0:T(8,128)S(1)} %get-tuple-element.51.refs_0_), channel_id=1, source_target_pairs={{0,2},{1,3},{2,0},{3,1},{4,6},{5,7},{6,4},{7,5},{8,10},{9,11},{10,... | collective-permute-start | bytes 61448 | tf_op jit(solution)/shard_map/ppermute | solution.py:877
  48.4 2.5 %collective-permute-start.15 = (f32[40,128]{1,0:T(8,128)S(1)}, f32[40,128]{1,0:T(8,128)S(1)}, u32[]{:S(2)}, u32[]{:S(2)}) collective-permute-start(f32[40,128]{1,0:T(8,128)S(1)} %get-tuple-element.51.refs_0_), channel_id=1, source_target_pairs={{0,1},{1,0},{2,3},{3,2},{4,5},{5,4},{6,7},{7,6},{8,9},{9,8},{10,11... | collective-permute-start | bytes 61448 | tf_op jit(solution)/shard_map/ppermute | solution.py:877
  (4 other events, 6.3 us)

commit v11 on v10

--- a/solution.py
+++ b/solution.py
@@ -232,15 +232,18 @@
 def side_plane(flow, low_x, thermal, extra, padded):
     rows, depth = flow.shape[2:]
     plane = lambda index: low_x[pl.ds(index * rows, rows), pl.ds(0, depth)]
-    beside = extra[pl.ds(2 * rows, 8), pl.ds(0, depth)]
+    beside = extra[pl.ds(rows, 8), pl.ds(0, depth)]
+    given = extra[pl.ds(0, rows), pl.ds(0, depth)]
     pad_rows(padded, 0, beside[2:4], plane(1), beside[4:6])
-    around = [extra[pl.ds(0, rows), pl.ds(0, depth)], plane(0), plane(1), flow[0, 0], flow[0, 1]]
+    none = jnp.zeros((rows, depth), F32)
+    around = [none, plane(0), plane(1), flow[0, 0], flow[0, 1]]
+    moved = advance(around, padded, 0, coefficients([plane(1), plane(3), plane(5)], given))
+    moved = jnp.where(plane(1) >= 0.0, given, moved)
     top = lax.broadcasted_iota(jnp.int32, (rows, depth), 1) == depth - 1
-    drag = 1.0 / (1.0 + TIME_INCREMENT * DRAG_RATE * extra[pl.ds(rows, rows), pl.ds(0, depth)])
-    pull = jnp.where(top, (-MARANGONI * 0.5 * TIME_INCREMENT) * drag, 0.0)
-    behind = column(extra[pl.ds(2 * rows, 1), pl.ds(0, rows)])
-    weights = coefficients([plane(1), plane(3), plane(5)], drag)
-    return advance(around, padded, 0, weights) + pull * (thermal[0] - behind)
+    behind = column(extra[pl.ds(rows, 1), pl.ds(0, rows)])
+    drag = column(extra[pl.ds(rows + 6, 1), pl.ds(0, rows)])
+    pull = (-MARANGONI * 0.5 * TIME_INCREMENT) * drag
+    return moved + jnp.where(top, pull * (thermal[0] - behind), 0.0)
 
 
 def transform_kernel(star, left, right, partial, rows_):
@@ -315,23 +318,31 @@
         copy.wait()
 
 
-def extra_kernel(flow, thermal, flag, low_y, high_y, extra, last, flags, sems):
+def extra_kernel(
+    flow, thermal, flag, low_y, high_y, extra, last, planes, flags, padded, sems
+):
     _, layers, rows, depth = flow.shape
     pairs = [(flag.at[layers - 1], flags), (thermal.at[pl.ds(layers - 2, 2)], last)]
-    pairs.append((flow.at[0, layers - 3], extra.at[pl.ds(0, rows), :]))
+    sources = [(0, layers - 3), (0, layers - 2), (0, layers - 1), (1, layers - 1), (2, layers - 1)]
+    for index, (part, layer) in enumerate(sources):
+        pairs.append((flow.at[part, layer], planes.at[index]))
     copies = started(
         [pltpu.make_async_copy(*pair, sems.at[index]) for index, pair in enumerate(pairs)]
     )
-    base = 2 * rows
-    extra[pl.ds(base, 8), :] = jnp.zeros((8, extra.shape[1]), F32)
-    extra[pl.ds(base + 2, 2), pl.ds(0, depth)] = low_y[0, layers - 1, 6:, :]
-    extra[pl.ds(base + 4, 2), pl.ds(0, depth)] = high_y[0, layers - 1, :2, :]
-    for copy in copies[:2]:
+    extra[pl.ds(rows, 8), :] = jnp.zeros((8, extra.shape[1]), F32)
+    extra[pl.ds(rows + 2, 2), pl.ds(0, depth)] = low_y[0, layers - 1, 6:, :]
+    extra[pl.ds(rows + 4, 2), pl.ds(0, depth)] = high_y[0, layers - 1, :2, :]
+    for copy in copies:
         copy.wait()
-    extra[pl.ds(rows, rows), :] = flags[...].astype(F32)
-    extra[pl.ds(base, 1), pl.ds(0, rows)] = surface(last[0])
-    for copy in copies[2:]:
-        copy.wait()
+    speed = [planes[index] for index in (2, 3, 4)]
+    drag = 1.0 / (1.0 + TIME_INCREMENT * DRAG_RATE * flags[...].astype(F32))
+    pad_rows(padded, 0, low_y[0, layers - 1, 6:], speed[0], high_y[0, layers - 1, :2])
+    none = jnp.zeros((rows, depth), F32)
+    around = [planes[0], planes[1], speed[0], none, none]
+    moved = advance(around, padded, 0, coefficients(speed, drag))
+    extra[pl.ds(0, rows), pl.ds(0, depth)] = jnp.where(speed[0] >= 0.0, moved, drag)
+    extra[pl.ds(rows, 1), pl.ds(0, rows)] = surface(last[0])
+    extra[pl.ds(rows + 6, 1), pl.ds(0, rows)] = surface(drag)
 
 
 def wrapped(distance, span):
@@ -764,9 +775,13 @@
         extra_kernel,
         [melt_flow, thermal_state, powder_flag],
         [low_y, high_y],
-        [(2 * rows + 8, width), (2,) + plane],
-        [pltpu.VMEM(plane, jnp.int32)],
-        3,
+        [(rows + 8, width), (2,) + plane],
+        [
+            pltpu.VMEM((5,) + plane, F32),
+            pltpu.VMEM(plane, jnp.int32),
+            pltpu.VMEM((1, rows + 16, depth), F32),
+        ],
+        7,
     )
     extra = along(extra, "gx", 1)
     early_low = along(last, "gx", 1)

time: 52.3 us -> 52.6 us (level)
  starting transfers between devices: 20.4 us -> 21.6 us
  waiting for transfers between devices: 20.2 us -> 19 us
    ppermute x8, waiting for transfers between devices: 15.3 us -> 13.6 us  [along(): lax.ppermute(array, axis, [(i, (i + by) % length) for i in range(length)])]
    ppermute x8, starting transfers between devices: 10.7 us -> 11.6 us  [along(): lax.ppermute(array, axis, [(i, (i + by) % length) for i in range(length)])]
    ppermute x7, starting transfers between devices: 7.27 us -> 8.1 us  [swapped(): return lax.ppermute(array, ('gx', 'gy'), pairs)]
  transfers between devices with their start and end apart: 18 -> 18, of which waited for: 11 -> 10; matrix products, arithmetic and copies ran while one was open for 0% -> 0% of each run, Pallas kernels for 14% -> 14%
where the time goes in v11:
time: 52.6 us; the launch traced here: 52.5 us
  starting transfers between devices  21.6 us (41%)
  waiting for transfers between devices  19 us (36%)
  Pallas kernels  11 us (21%)
  between operations  0.81 us (2%)
    ppermute x8, waiting for transfers between devices, along(): lax.ppermute(array, axis, [(i, (i + by) % length) for i in range(length)])  13.6 us
    ppermute x8, starting transfers between devices, along(): lax.ppermute(array, axis, [(i, (i + by) % length) for i in range(length)])  11.6 us
    pallas_call x11, Pallas kernels, call(): pl.pallas_call(body, out_shape=out_shape, in_specs=[SMEM] * scalars + [VM...  8.23 us
    ppermute x7, starting transfers between devices, swapped(): return lax.ppermute(array, ('gx', 'gy'), pairs)  8.1 us
    ppermute x7, waiting for transfers between devices, swapped(): return lax.ppermute(array, ('gx', 'gy'), pairs)  3 us
    pallas_call x2, Pallas kernels, pack(): pl.pallas_call(body, out_shape=[jax.ShapeDtypeStruct(shape, F32) for shap...  2.77 us
    ppermute x3, waiting for transfers between devices, per_device(): reports.append(lax.ppermute(report, 'gy', pairs))  2.33 us
    ppermute x3, starting transfers between devices, per_device(): reports.append(lax.ppermute(report, 'gy', pairs))  1.93 us
  transfers between devices with their start and end apart: 18, of which 10 were waited for; matrix products, arithmetic and copies ran while one was open for 0% of the time, Pallas kernels for 14%

profile of v11, /device:TPU:0, one launch (start us, length us, event | category | flops | bytes accessed | tf_op | source)
XLA Modules:
  0.0 52.5 jit_solution(15876492941511429827)
XLA Ops:
  0.7 1.5 %shard_map.121 = (f32[776,128]{1,0:T(8,128)S(1)}, f32[776,128]{1,0:T(8,128)S(1)}, f32[4,4,8,128]{3,2,1,0:T(8,128)S(1)}, f32[4,4,8,128]{3,2,1,0:T(8,128)S(1)}) custom-call(f32[3,4,128,128]{3,2,1,0:T(8,128)} %flow.11, f32[4,128,128]{2,1,0:T(8,128)} %thermal.13), custom_call_target="tpu_custom_call" | custom-call | tf_op jit(solution)/shard_map/pallas_call | solution.py:733
  2.1 3.1 %collective-permute-start = (f32[776,128]{1,0:T(8,128)S(1)}, f32[776,128]{1,0:T(8,128)S(1)}, u32[]{:S(2)}, u32[]{:S(2)}) collective-permute-start(f32[776,128]{1,0:T(8,128)S(1)} %get-tuple-element.29), channel_id=1, source_target_pairs={{0,4},{4,8},{8,12},{12,0},{1,5},{5,9},{9,13},{13,1},{2,6},{6,10},{... | collective-permute-start | bytes 1191944 | tf_op jit(solution)/shard_map/ppermute | solution.py:718
  5.2 2.1 %collective-permute-start.1 = (f32[776,128]{1,0:T(8,128)S(1)}, f32[776,128]{1,0:T(8,128)S(1)}, u32[]{:S(2)}, u32[]{:S(2)}) collective-permute-start(f32[776,128]{1,0:T(8,128)S(1)} %get-tuple-element.30), channel_id=1, source_target_pairs={{0,12},{4,0},{8,4},{12,8},{1,13},{5,1},{9,5},{13,9},{2,14},{6,2},{... | collective-permute-start | bytes 1191944 | tf_op jit(solution)/shard_map/ppermute | solution.py:718
  7.3 1.7 %collective-permute-start.3 = (f32[4,4,8,128]{3,2,1,0:T(8,128)S(1)}, f32[4,4,8,128]{3,2,1,0:T(8,128)S(1)}, u32[]{:S(2)}, u32[]{:S(2)}) collective-permute-start(f32[4,4,8,128]{3,2,1,0:T(8,128)S(1)} %get-tuple-element.32), channel_id=1, source_target_pairs={{0,3},{1,0},{2,1},{3,2},{4,7},{5,4},{6,5},{7,6},{8,11},{9,8},{10,9... | collective-permute-start | bytes 196616 | tf_op jit(solution)/shard_map/ppermute | solution.py:718
  9.1 1.9 %collective-permute-done.2.low_y = f32[4,4,8,128]{3,2,1,0:T(8,128)S(1)} collective-permute-done((f32[4,4,8,128]{3,2,1,0:T(8,128)S(1)}, f32[4,4,8,128]{3,2,1,0:T(8,128)S(1)}, u32[]{:S(2)}, u32[]{:S(2)}) %collective-permute-start.2) | collective-permute-done | bytes 65568 | tf_op jit(solution)/shard_map/ppermute | solution.py:718
  11.0 1.3 %shard_map.125 = (f32[136,128]{1,0:T(8,128)S(1)}, f32[2,128,128]{2,1,0:T(8,128)S(1)}) custom-call(f32[3,4,128,128]{3,2,1,0:T(8,128)} %flow.11, f32[4,128,128]{2,1,0:T(8,128)} %thermal.13, s32[4,128,128]{2,1,0:T(8,128)} %flag.5, f32[4,4,8,128]{3,2,1,0:T(8,128)S(1)} %collective-permute-done.2.low_y, f32[4,4,8,128]{3,2,1,0:T(8,128)S(1)} %collective-permute-done.3.high_y), custom_call_target="tpu_custom_call" | custom-call | tf_op jit(solution)/shard_map/pallas_call | solution.py:733
  12.8 1.5 %collective-permute-start.7 = (f32[2,128,128]{2,1,0:T(8,128)S(1)}, f32[2,128,128]{2,1,0:T(8,128)S(1)}, u32[]{:S(2)}, u32[]{:S(2)}) collective-permute-start(f32[2,128,128]{2,1,0:T(8,128)S(1)} %get-tuple-element.38), channel_id=1, source_target_pairs={{0,4},{4,8},{8,12},{12,0},{1,5},{5,9},{9,13},{13,1},{2,6},{6,10},{... | collective-permute-start | bytes 393224 | tf_op jit(solution)/shard_map/ppermute | solution.py:718
  14.3 3.0 %collective-permute-done.low_x = f32[776,128]{1,0:T(8,128)S(1)} collective-permute-done((f32[776,128]{1,0:T(8,128)S(1)}, f32[776,128]{1,0:T(8,128)S(1)}, u32[]{:S(2)}, u32[]{:S(2)}) %collective-permute-start) | collective-permute-done | bytes 397344 | tf_op jit(solution)/shard_map/ppermute | solution.py:718
  17.3 7.3 %collective-permute-done.1.high_x = f32[776,128]{1,0:T(8,128)S(1)} collective-permute-done((f32[776,128]{1,0:T(8,128)S(1)}, f32[776,128]{1,0:T(8,128)S(1)}, u32[]{:S(2)}, u32[]{:S(2)}) %collective-permute-start.1) | collective-permute-done | bytes 397344 | tf_op jit(solution)/shard_map/ppermute | solution.py:718
  24.8 1.1 %shard_map.124.star = f32[3,4,128,128]{3,2,1,0:T(8,128)S(1)} custom-call(f32[3,4,128,128]{3,2,1,0:T(8,128)S(1)} %copy-done, f32[776,128]{1,0:T(8,128)S(1)} %collective-permute-done.low_x, f32[776,128]{1,0:T(8,128)S(1)} %collective-permute-done.1.high_x, f32[4,128,128]{2,1,0:T(8,128)S(1)} %copy-done.1, s32[4,128,128]{2,1,0:T(8,128)S(1)} %copy-done.2, ...), custom_call_target="tpu_custom_call" | custom-call | flops 402653184 | bytes 1572864 | tf_op jit(solution)/shard_map/pallas_call | solution.py:30
  26.4 0.9 %collective-permute-done.4.extra = f32[136,128]{1,0:T(8,128)S(1)} collective-permute-done((f32[136,128]{1,0:T(8,128)S(1)}, f32[136,128]{1,0:T(8,128)S(1)}, u32[]{:S(2)}, u32[]{:S(2)}) %collective-permute-start.4) | collective-permute-done | bytes 69664 | tf_op jit(solution)/shard_map/ppermute | solution.py:718
  28.5 1.8 %collective-permute-start.6 = (f32[256,128]{1,0:T(8,128)S(1)}, f32[256,128]{1,0:T(8,128)S(1)}, u32[]{:S(2)}, u32[]{:S(2)}) collective-permute-start(f32[256,128]{1,0:T(8,128)S(1)} %get-tuple-element.37.message), channel_id=1, source_target_pairs={{0,4},{1,5},{2,6},{3,7},{4,0},{5,1},{6,2},{7,3},{8,12},{9,13},{10,... | collective-permute-start | bytes 393224 | tf_op jit(solution)/shard_map/ppermute | solution.py:728
  31.3 3.1 %collective-permute-start.14 = (f32[2,128,128]{2,1,0:T(8,128)S(1)}, f32[2,128,128]{2,1,0:T(8,128)S(1)}, u32[]{:S(2)}, u32[]{:S(2)}) collective-permute-start(f32[2,128,128]{2,1,0:T(8,128)S(1)} %get-tuple-element.44), channel_id=1, source_target_pairs={{0,12},{4,0},{8,4},{12,8},{1,13},{5,1},{9,5},{13,9},{2,14},{6,2},{... | collective-permute-start | bytes 393224 | tf_op jit(solution)/shard_map/ppermute | solution.py:718
  34.3 1.1 %collective-permute-done.8.other_faces = f32[56,128]{1,0:T(8,128)S(1)} collective-permute-done((f32[56,128]{1,0:T(8,128)S(1)}, f32[56,128]{1,0:T(8,128)S(1)}, u32[]{:S(2)}, u32[]{:S(2)}) %collective-permute-start.8) | collective-permute-done | bytes 28704 | tf_op jit(solution)/shard_map/ppermute | solution.py:728
  35.6 1.8 %collective-permute-start.9 = (f32[296,128]{1,0:T(8,128)S(1)}, f32[296,128]{1,0:T(8,128)S(1)}, u32[]{:S(2)}, u32[]{:S(2)}) collective-permute-start(f32[296,128]{1,0:T(8,128)S(1)} %get-tuple-element.40.refs_1_), channel_id=1, source_target_pairs={{0,8},{1,9},{2,10},{3,11},{4,12},{5,13},{6,14},{7,15},{8,0},{9,1},... | collective-permute-start | bytes 454664 | tf_op jit(solution)/shard_map/ppermute | solution.py:728
  37.4 2.3 %collective-permute-start.10 = (f32[16,128]{1,0:T(8,128)S(1)}, f32[16,128]{1,0:T(8,128)S(1)}, u32[]{:S(2)}, u32[]{:S(2)}) collective-permute-start(f32[16,128]{1,0:T(8,128)S(1)} %get-tuple-element.42), channel_id=1, source_target_pairs={{0,1},{1,2},{2,3},{3,0},{4,5},{5,6},{6,7},{7,4},{8,9},{9,10},{10,1... | collective-permute-start | bytes 24584 | tf_op jit(solution)/shard_map/ppermute | solution.py:728
  39.7 1.2 %collective-permute-start.13 = (f32[16,128]{1,0:T(8,128)S(1)}, f32[16,128]{1,0:T(8,128)S(1)}, u32[]{:S(2)}, u32[]{:S(2)}) collective-permute-start(f32[16,128]{1,0:T(8,128)S(1)} %get-tuple-element.43), channel_id=1, source_target_pairs={{0,11},{1,8},{2,9},{3,10},{4,15},{5,12},{6,13},{7,14},{8,3},{9,0},... | collective-permute-start | bytes 24584 | tf_op jit(solution)/shard_map/ppermute | solution.py:728
  41.6 1.9 %shard_map.130 = (f32[4,128,128]{2,1,0:T(8,128)}, f32[8,128]{1,0:T(8,128)S(1)}) custom-call(s32[8]{0:T(128)S(1)} %copy-done.8, s32[8]{0:T(128)S(1)} %copy-done.9, f32[4,128,128]{2,1,0:T(8,128)S(1)} %copy-done.1, f32[2,128,128]{2,1,0:T(8,128)S(1)} %collective-permute-done.7._.low_x, f32[2,128,128]{2,1,0:T(8,128)S(1)} %collective-permute-done.14.high_x, ...), custom_call_target="tpu_custom_call" | custom-call | flops 268435456 | bytes 532480 | tf_op jit(solution)/shard_map/pallas_call | solution.py:30
  43.6 1.1 %collective-permute-done.11.refs_5_ = f32[16,128]{1,0:T(8,128)S(1)} collective-permute-done((f32[16,128]{1,0:T(8,128)S(1)}, f32[16,128]{1,0:T(8,128)S(1)}, u32[]{:S(2)}, u32[]{:S(2)}) %collective-permute-start.11) | collective-permute-done | bytes 8224 | tf_op jit(solution)/shard_map/ppermute | solution.py:728
  44.6 0.8 %collective-permute-done.9.refs_2_ = f32[296,128]{1,0:T(8,128)S(1)} collective-permute-done((f32[296,128]{1,0:T(8,128)S(1)}, f32[296,128]{1,0:T(8,128)S(1)}, u32[]{:S(2)}, u32[]{:S(2)}) %collective-permute-start.9) | collective-permute-done | bytes 151584 | tf_op jit(solution)/shard_map/ppermute | solution.py:728
  45.4 0.9 %shard_map.131 = (f32[5,128,128]{2,1,0:T(8,128)S(1)}, f32[5,128,128]{2,1,0:T(8,128)S(1)}, f32[40,128]{1,0:T(8,128)S(1)}, f32[48,128]{1,0:T(8,128)S(1)}) custom-call(f32[4,128,128]{2,1,0:T(8,128)S(1)} %get-tuple-element.36.source.refs_0_, f32[296,128]{1,0:T(8,128)S(1)} %get-tuple-element.40.refs_1_, f32[296,128]{1,0:T(8,128)S(1)} %collective-permute-done.9.refs_2_, ...), custom_call_target="tpu_custom_call" | custom-call | flops 1048576 | bytes 1400832 | tf_op jit(solution)/shard_map/pallas_call | solution.py:30
  46.3 1.1 %collective-permute-start.17 = (f32[40,128]{1,0:T(8,128)S(1)}, f32[40,128]{1,0:T(8,128)S(1)}, u32[]{:S(2)}, u32[]{:S(2)}) collective-permute-start(f32[40,128]{1,0:T(8,128)S(1)} %get-tuple-element.51.refs_0_), channel_id=1, source_target_pairs={{0,3},{1,2},{2,1},{3,0},{4,7},{5,6},{6,5},{7,4},{8,11},{9,10},{10,... | collective-permute-start | bytes 61448 | tf_op jit(solution)/shard_map/ppermute | solution.py:892
  49.6 1.6 %collective-permute-done.16.refs_2_ = f32[40,128]{1,0:T(8,128)S(1)} collective-permute-done((f32[40,128]{1,0:T(8,128)S(1)}, f32[40,128]{1,0:T(8,128)S(1)}, u32[]{:S(2)}, u32[]{:S(2)}) %collective-permute-start.16) | collective-permute-done | bytes 20512 | tf_op jit(solution)/shard_map/ppermute | solution.py:892
  51.2 1.2 %shard_map.133 = (f32[3,4,128,128]{3,2,1,0:T(8,128)}, f32[4,128,128]{2,1,0:T(8,128)}) custom-call(f32[3,4,128,128]{3,2,1,0:T(8,128)S(1)} %shard_map.124.star, f32[5,128,128]{2,1,0:T(8,128)S(1)} %get-tuple-element.48.precond, f32[5,128,128]{2,1,0:T(8,128)S(1)} %get-tuple-element.49.image, f32[48,128]{1,0:T(8,128)S(1)} %get-tuple-element.50.faces, ...), custom_call_target="tpu_custom_call" | custom-call | flops 1048576 | bytes 2097152 | tf_op jit(solution)/shard_map/pallas_call | solution.py:30
  (46 shorter events, 6.3 us)
Async XLA Ops:
  0.6 11.8 %copy-start.7 = (f32[128,128]{1,0:T(8,128)S(1)}, f32[128,128]{1,0:T(8,128)}, u32[]{:S(2)}) copy-start(f32[128,128]{1,0:T(8,128)} %constant.16.clone.diagonal) | copy-start | bytes 196612
  0.6 24.0 %copy-start.1 = (f32[4,128,128]{2,1,0:T(8,128)S(1)}, f32[4,128,128]{2,1,0:T(8,128)}, u32[]{:S(2)}) copy-start(f32[4,128,128]{2,1,0:T(8,128)} %thermal.13) | copy-start | bytes 786436
  0.7 24.0 %copy-start = (f32[3,4,128,128]{3,2,1,0:T(8,128)S(1)}, f32[3,4,128,128]{3,2,1,0:T(8,128)}, u32[]{:S(2)}) copy-start(f32[3,4,128,128]{3,2,1,0:T(8,128)} %flow.11) | copy-start | bytes 2359300
  0.7 24.0 %copy-start.2 = (s32[4,128,128]{2,1,0:T(8,128)S(1)}, s32[4,128,128]{2,1,0:T(8,128)}, u32[]{:S(2)}) copy-start(s32[4,128,128]{2,1,0:T(8,128)} %flag.5) | copy-start | bytes 786436
  2.1 15.2 %collective-permute-start = (f32[776,128]{1,0:T(8,128)S(1)}, f32[776,128]{1,0:T(8,128)S(1)}, u32[]{:S(2)}, u32[]{:S(2)}) collective-permute-start(f32[776,128]{1,0:T(8,128)S(1)} %get-tuple-element.29), channel_id=1, source_target_pairs={{0,4},{4,8},{8,12},{12,0},{1,5},{5,9},{9,13},{13,1},{2,6},{6,10},{... | collective-permute-start | bytes 1191944 | tf_op jit(solution)/shard_map/ppermute | solution.py:718
  5.2 19.4 %collective-permute-start.1 = (f32[776,128]{1,0:T(8,128)S(1)}, f32[776,128]{1,0:T(8,128)S(1)}, u32[]{:S(2)}, u32[]{:S(2)}) collective-permute-start(f32[776,128]{1,0:T(8,128)S(1)} %get-tuple-element.30), channel_id=1, source_target_pairs={{0,12},{4,0},{8,4},{12,8},{1,13},{5,1},{9,5},{13,9},{2,14},{6,2},{... | collective-permute-start | bytes 1191944 | tf_op jit(solution)/shard_map/ppermute | solution.py:718
  7.3 3.7 %collective-permute-start.2 = (f32[4,4,8,128]{3,2,1,0:T(8,128)S(1)}, f32[4,4,8,128]{3,2,1,0:T(8,128)S(1)}, u32[]{:S(2)}, u32[]{:S(2)}) collective-permute-start(f32[4,4,8,128]{3,2,1,0:T(8,128)S(1)} %get-tuple-element.31), channel_id=1, source_target_pairs={{0,1},{1,2},{2,3},{3,0},{4,5},{5,6},{6,7},{7,4},{8,9},{9,10},{10,1... | collective-permute-start | bytes 196616 | tf_op jit(solution)/shard_map/ppermute | solution.py:718
  7.3 3.7 %collective-permute-start.3 = (f32[4,4,8,128]{3,2,1,0:T(8,128)S(1)}, f32[4,4,8,128]{3,2,1,0:T(8,128)S(1)}, u32[]{:S(2)}, u32[]{:S(2)}) collective-permute-start(f32[4,4,8,128]{3,2,1,0:T(8,128)S(1)} %get-tuple-element.32), channel_id=1, source_target_pairs={{0,3},{1,0},{2,1},{3,2},{4,7},{5,4},{6,5},{7,6},{8,11},{9,8},{10,9... | collective-permute-start | bytes 196616 | tf_op jit(solution)/shard_map/ppermute | solution.py:718
  12.3 15.0 %collective-permute-start.4 = (f32[136,128]{1,0:T(8,128)S(1)}, f32[136,128]{1,0:T(8,128)S(1)}, u32[]{:S(2)}, u32[]{:S(2)}) collective-permute-start(f32[136,128]{1,0:T(8,128)S(1)} %get-tuple-element.34), channel_id=1, source_target_pairs={{0,4},{4,8},{8,12},{12,0},{1,5},{5,9},{9,13},{13,1},{2,6},{6,10},{... | collective-permute-start | bytes 208904 | tf_op jit(solution)/shard_map/ppermute | solution.py:718
  12.8 17.4 %collective-permute-start.7 = (f32[2,128,128]{2,1,0:T(8,128)S(1)}, f32[2,128,128]{2,1,0:T(8,128)S(1)}, u32[]{:S(2)}, u32[]{:S(2)}) collective-permute-start(f32[2,128,128]{2,1,0:T(8,128)S(1)} %get-tuple-element.38), channel_id=1, source_target_pairs={{0,4},{4,8},{8,12},{12,0},{1,5},{5,9},{9,13},{13,1},{2,6},{6,10},{... | collective-permute-start | bytes 393224 | tf_op jit(solution)/shard_map/ppermute | solution.py:718
  24.7 3.1 %collective-permute-start.5 = (f32[4,128]{1,0:T(4,128)S(1)}, f32[4,128]{1,0:T(4,128)S(1)}, u32[]{:S(2)}, u32[]{:S(2)}) collective-permute-start(f32[4,128]{1,0:T(4,128)S(1)} %shard_map.123._), channel_id=1, source_target_pairs={{0,1},{1,2},{2,3},{3,0},{4,5},{5,6},{6,7},{7,4},{8,9},{9,10},{10,1... | collective-permute-start | bytes 6152 | tf_op jit(solution)/shard_map/ppermute | solution.py:718
  28.5 7.0 %collective-permute-start.6 = (f32[256,128]{1,0:T(8,128)S(1)}, f32[256,128]{1,0:T(8,128)S(1)}, u32[]{:S(2)}, u32[]{:S(2)}) collective-permute-start(f32[256,128]{1,0:T(8,128)S(1)} %get-tuple-element.37.message), channel_id=1, source_target_pairs={{0,4},{1,5},{2,6},{3,7},{4,0},{5,1},{6,2},{7,3},{8,12},{9,13},{10,... | collective-permute-start | bytes 393224 | tf_op jit(solution)/shard_map/ppermute | solution.py:728
  30.9 10.7 %copy-start.8 = (s32[8]{0:T(128)S(1)}, s32[8]{0:T(128)}, u32[]{:S(2)}) copy-start(s32[8]{0:T(128)} %spots_a.1) | copy-start | bytes 100
  30.9 10.7 %copy-start.9 = (s32[8]{0:T(128)S(1)}, s32[8]{0:T(128)}, u32[]{:S(2)}) copy-start(s32[8]{0:T(128)} %spots_b.1) | copy-start | bytes 100
  30.9 4.5 %collective-permute-start.8 = (f32[56,128]{1,0:T(8,128)S(1)}, f32[56,128]{1,0:T(8,128)S(1)}, u32[]{:S(2)}, u32[]{:S(2)}) collective-permute-start(f32[56,128]{1,0:T(8,128)S(1)} %get-tuple-element.39.faces), channel_id=1, source_target_pairs={{0,4},{1,5},{2,6},{3,7},{4,0},{5,1},{6,2},{7,3},{8,12},{9,13},{10,... | collective-permute-start | bytes 86024 | tf_op jit(solution)/shard_map/ppermute | solution.py:728
  31.3 9.7 %collective-permute-start.14 = (f32[2,128,128]{2,1,0:T(8,128)S(1)}, f32[2,128,128]{2,1,0:T(8,128)S(1)}, u32[]{:S(2)}, u32[]{:S(2)}) collective-permute-start(f32[2,128,128]{2,1,0:T(8,128)S(1)} %get-tuple-element.44), channel_id=1, source_target_pairs={{0,12},{4,0},{8,4},{12,8},{1,13},{5,1},{9,5},{13,9},{2,14},{6,2},{... | collective-permute-start | bytes 393224 | tf_op jit(solution)/shard_map/ppermute | solution.py:718
  35.6 9.8 %collective-permute-start.9 = (f32[296,128]{1,0:T(8,128)S(1)}, f32[296,128]{1,0:T(8,128)S(1)}, u32[]{:S(2)}, u32[]{:S(2)}) collective-permute-start(f32[296,128]{1,0:T(8,128)S(1)} %get-tuple-element.40.refs_1_), channel_id=1, source_target_pairs={{0,8},{1,9},{2,10},{3,11},{4,12},{5,13},{6,14},{7,15},{8,0},{9,1},... | collective-permute-start | bytes 454664 | tf_op jit(solution)/shard_map/ppermute | solution.py:728
  37.4 7.2 %collective-permute-start.11 = (f32[16,128]{1,0:T(8,128)S(1)}, f32[16,128]{1,0:T(8,128)S(1)}, u32[]{:S(2)}, u32[]{:S(2)}) collective-permute-start(f32[16,128]{1,0:T(8,128)S(1)} %get-tuple-element.42), channel_id=1, source_target_pairs={{0,9},{1,10},{2,11},{3,8},{4,13},{5,14},{6,15},{7,12},{8,1},{9,2},... | collective-permute-start | bytes 24584 | tf_op jit(solution)/shard_map/ppermute | solution.py:728
  37.4 7.2 %collective-permute-start.10 = (f32[16,128]{1,0:T(8,128)S(1)}, f32[16,128]{1,0:T(8,128)S(1)}, u32[]{:S(2)}, u32[]{:S(2)}) collective-permute-start(f32[16,128]{1,0:T(8,128)S(1)} %get-tuple-element.42), channel_id=1, source_target_pairs={{0,1},{1,2},{2,3},{3,0},{4,5},{5,6},{6,7},{7,4},{8,9},{9,10},{10,1... | collective-permute-start | bytes 24584 | tf_op jit(solution)/shard_map/ppermute | solution.py:728
  39.7 4.9 %collective-permute-start.13 = (f32[16,128]{1,0:T(8,128)S(1)}, f32[16,128]{1,0:T(8,128)S(1)}, u32[]{:S(2)}, u32[]{:S(2)}) collective-permute-start(f32[16,128]{1,0:T(8,128)S(1)} %get-tuple-element.43), channel_id=1, source_target_pairs={{0,11},{1,8},{2,9},{3,10},{4,15},{5,12},{6,13},{7,14},{8,3},{9,0},... | collective-permute-start | bytes 24584 | tf_op jit(solution)/shard_map/ppermute | solution.py:728
  41.0 3.7 %collective-permute-start.12 = (f32[16,128]{1,0:T(8,128)S(1)}, f32[16,128]{1,0:T(8,128)S(1)}, u32[]{:S(2)}, u32[]{:S(2)}) collective-permute-start(f32[16,128]{1,0:T(8,128)S(1)} %get-tuple-element.43), channel_id=1, source_target_pairs={{0,3},{1,0},{2,1},{3,2},{4,7},{5,4},{6,5},{7,6},{8,11},{9,8},{10,9... | collective-permute-start | bytes 24584 | tf_op jit(solution)/shard_map/ppermute | solution.py:728
  46.3 3.3 %collective-permute-start.17 = (f32[40,128]{1,0:T(8,128)S(1)}, f32[40,128]{1,0:T(8,128)S(1)}, u32[]{:S(2)}, u32[]{:S(2)}) collective-permute-start(f32[40,128]{1,0:T(8,128)S(1)} %get-tuple-element.51.refs_0_), channel_id=1, source_target_pairs={{0,3},{1,2},{2,1},{3,0},{4,7},{5,6},{6,5},{7,4},{8,11},{9,10},{10,... | collective-permute-start | bytes 61448 | tf_op jit(solution)/shard_map/ppermute | solution.py:892
  47.5 3.8 %collective-permute-start.16 = (f32[40,128]{1,0:T(8,128)S(1)}, f32[40,128]{1,0:T(8,128)S(1)}, u32[]{:S(2)}, u32[]{:S(2)}) collective-permute-start(f32[40,128]{1,0:T(8,128)S(1)} %get-tuple-element.51.refs_0_), channel_id=1, source_target_pairs={{0,2},{1,3},{2,0},{3,1},{4,6},{5,7},{6,4},{7,5},{8,10},{9,11},{10,... | collective-permute-start | bytes 61448 | tf_op jit(solution)/shard_map/ppermute | solution.py:892
  48.2 3.1 %collective-permute-start.15 = (f32[40,128]{1,0:T(8,128)S(1)}, f32[40,128]{1,0:T(8,128)S(1)}, u32[]{:S(2)}, u32[]{:S(2)}) collective-permute-start(f32[40,128]{1,0:T(8,128)S(1)} %get-tuple-element.51.refs_0_), channel_id=1, source_target_pairs={{0,1},{1,0},{2,3},{3,2},{4,5},{5,4},{6,7},{7,6},{8,9},{9,8},{10,11... | collective-permute-start | bytes 61448 | tf_op jit(solution)/shard_map/ppermute | solution.py:892
  (4 other events, 7.2 us)

commit v12 on v11

--- a/solution.py
+++ b/solution.py
@@ -203,17 +203,6 @@
     pad_rows(padded, 3, low_y[3, index, 6:], thermal[index], high_y[3, index, :2])
 
 
-def row_kernel(flow, low_x, high_x, thermal, flag, low_y, high_y, _, side_y, padded):
-    refs = (flow, low_x, high_x, thermal, flag)
-    _, layers, rows, depth = flow.shape
-    for index in range(layers):
-        for part, cells in ((1, flow.at[1, index]), (3, thermal.at[index])):
-            padded[part, pl.ds(rows - 8, 16), :] = cells[pl.ds(rows - 16, 16), :]
-            padded[part, pl.ds(8 + rows, 2), :] = high_y[part, index, :2]
-        (value,) = march_layer(refs, padded, index, [1], rows - 8, 8)
-        side_y[pl.ds(index, 1), :] = value[7:, :]
-
-
 def march_kernel(
     flow, low_x, high_x, thermal, flag, low_y, high_y, _, star, padded
 ):
@@ -262,23 +251,54 @@
         partial[index] = plane
 
 
+def side_rows(flow, thermal, low_y, extra, back, padded):
+    _, layers, rows, depth = flow.shape
+    row = lambda ref, index: jnp.broadcast_to(ref[pl.ds(index, 1), pl.ds(0, depth)], (8, depth))
+    top = lax.broadcasted_iota(jnp.int32, (8, depth), 1) == depth - 1
+    padded[0, pl.ds(0, 8), :] = jnp.zeros((8, depth), F32)
+    out = []
+    for index in range(layers):
+        around = []
+        for other in range(index - 2, index + 3):
+            if other < 0:
+                around.append(row(extra, rows + 1 if other == -2 else rows + 7))
+            elif other >= layers:
+                around.append(row(back, other - layers))
+            else:
+                around.append(low_y[1, other])
+        drag = 1.0 / (1.0 + TIME_INCREMENT * DRAG_RATE * low_y[4, index])
+        pull = jnp.where(top, (-MARANGONI * 0.5 * TIME_INCREMENT) * drag, 0.0)
+        padded[0, pl.ds(8, 8), :] = low_y[3, index]
+        padded[0, pl.ds(16, 8), :] = thermal[index, :8, :]
+        slope = padded[0, pl.ds(9, 8), :] - padded[0, pl.ds(7, 8), :]
+        padded[0, pl.ds(8, 8), :] = low_y[1, index]
+        padded[0, pl.ds(16, 8), :] = flow[1, index, :8, :]
+        weights = coefficients([low_y[part, index] for part in range(3)], drag)
+        moved = advance(around, padded, 0, weights) + pull * slope
+        out.append(moved[7:])
+    return out
+
+
 def source_kernel(
-    group, length, flow, low_x, thermal, extra, partial, left, right, ratio, _,
-    source, message, padded,
+    group, length, flow, low_x, thermal, extra, back, low_y, partial, left, right, table_z, edge,
+    ratio, source, message, padded, rows_,
 ):
     layers, rows, depth = partial.shape
     first = position(group) * layers
+    for index, row in enumerate(side_rows(flow, thermal, low_y, extra, back, padded)):
+        rows_[pl.ds(index, 1), :] = row
+    beside = dot(rows_[...], table_z[...])
     (onward,) = transformed([side_plane(flow, low_x, thermal, extra, padded)], left, right)
-    source[0] = partial[0] + onward
+    for index in range(layers):
+        value = partial[index] + edge[...] * beside[index : index + 1]
+        source[index] = value + onward if index == 0 else value
+    backward = source[layers - 1]
+    for index in range(layers - 2, -1, -1):
+        backward = source[index] + ratio[length - 1 - first - index] * backward
+    message[pl.ds(rows, rows), :] = backward
+    forward = source[0]
     for index in range(1, layers):
-        source[index] = partial[index]
-    backward = partial[layers - 1]
-    for index in range(layers - 2, 0, -1):
-        backward = partial[index] + ratio[length - 1 - first - index] * backward
-    forward = source[0]
-    message[pl.ds(rows, rows), :] = forward + ratio[length - 1 - first] * backward
-    for index in range(1, layers):
-        forward = partial[index] + ratio[first + index] * forward
+        forward = source[index] + ratio[first + index] * forward
     message[pl.ds(0, rows), :] = forward
 
 
@@ -295,7 +315,9 @@
     return jnp.sum(jnp.where(same, plane[:, depth - 1 :], 0.0), axis=0, keepdims=True)
 
 
-def halo_kernel(flow, thermal, ahead, behind, last_rows, first_rows, tops, sems):
+def halo_kernel(
+    flow, thermal, flag, ahead, behind, last_rows, first_rows, tops, flags, sems
+):
     parts, layers, rows, depth = flow.shape
     pairs = [(thermal.at[layers - 1], tops.at[0]), (thermal.at[0], tops.at[1])]
     for part in range(parts):
@@ -307,6 +329,7 @@
         span = pl.ds(start, 8)
         pairs.append((flow.at[:, :, span, :], target.at[pl.ds(0, parts)]))
         pairs.append((thermal.at[:, span, :], target.at[parts]))
+    pairs.append((flag.at[:, pl.ds(rows - 8, 8), :], flags))
     copies = started(
         [pltpu.make_async_copy(*pair, sems.at[index]) for index, pair in enumerate(pairs)]
     )
@@ -316,10 +339,11 @@
         message[pl.ds(2 * parts * rows, 8), pl.ds(0, rows)] = row
     for copy in copies[2:]:
         copy.wait()
+    last_rows[parts + 1] = flags[...].astype(F32)
 
 
 def extra_kernel(
-    flow, thermal, flag, low_y, high_y, extra, last, planes, flags, padded, sems
+    flow, thermal, flag, low_y, high_y, extra, back, last, planes, flags, padded, sems
 ):
     _, layers, rows, depth = flow.shape
     pairs = [(flag.at[layers - 1], flags), (thermal.at[pl.ds(layers - 2, 2)], last)]
@@ -332,6 +356,11 @@
     extra[pl.ds(rows, 8), :] = jnp.zeros((8, extra.shape[1]), F32)
     extra[pl.ds(rows + 2, 2), pl.ds(0, depth)] = low_y[0, layers - 1, 6:, :]
     extra[pl.ds(rows + 4, 2), pl.ds(0, depth)] = high_y[0, layers - 1, :2, :]
+    extra[pl.ds(rows + 1, 1), pl.ds(0, depth)] = low_y[1, layers - 2, 7:, :]
+    extra[pl.ds(rows + 7, 1), pl.ds(0, depth)] = low_y[1, layers - 1, 7:, :]
+    back[...] = jnp.zeros(back.shape, F32)
+    for index in range(2):
+        back[pl.ds(index, 1), :] = low_y[1, index, 7:, :]
     for copy in copies:
         copy.wait()
     speed = [planes[index] for index in (2, 3, 4)]
@@ -445,16 +474,12 @@
 
 
 def faces_kernel(
-    group, length, source, before_y, table_z, ratio, weight, edge, thermal, _, faces, late, sweep
+    group, length, source, ratio, weight, edge, thermal, _, faces, late, sweep
 ):
     layers, rows, depth = source.shape
     late[...] = thermal[:2]
     first = position(group) * layers
     zero = jnp.zeros((rows, depth), F32)
-    extra = dot(before_y[...], table_z[...])
-    faces[...] = jnp.zeros(faces.shape, F32)
-    for index in range(layers):
-        faces[pl.ds(2 * length + first + index, 1), :] = extra[index : index + 1]
     forward = zero
     for index in range(layers):
         forward = source[index] + ratio[first + index] * forward
@@ -464,7 +489,7 @@
     for index in range(layers - 1, -1, -1):
         value = ratio[first + index + 1] * (sweep[index] + value)
         energy = energy + source[index] * value
-    faces[pl.ds(3 * length, 8), :] = jnp.broadcast_to(total(energy), (8, depth))
+    faces[pl.ds(2 * length, 8), :] = jnp.broadcast_to(total(energy), (8, depth))
 
     lead = grouped(edge[...])
     zero = grouped(zero)
@@ -472,8 +497,7 @@
     def down(index, previous):
         inside = (index >= first) & (index < first + layers)
         own = jnp.where(inside, source[jnp.clip(index - first, 0, layers - 1)], 0.0)
-        row = faces[pl.ds(2 * length + index, 1), :]
-        current = grouped(own) + lead * row + grouped(ratio[index]) * previous
+        current = grouped(own) + grouped(ratio[index]) * previous
         sweep[index] = current.reshape(rows, depth)
         return current
 
@@ -518,81 +542,47 @@
     new_message[pl.ds(0, rows), :] = forward
     new_message[pl.ds(rows, rows), :] = backward
     low, high = pl.ds(0, length), pl.ds(length, length)
-    late, number = pl.ds(2 * length, length), pl.ds(3 * length, 8)
+    number = pl.ds(2 * length, 8)
     head[...] = faces[low, :] + other_faces[low, :]
     tail[...] = faces[high, :] + other_faces[high, :]
     new_message[pl.ds(2 * rows, length), :] = head[...]
-    new_message[pl.ds(2 * rows + length, length), :] = faces[late, :] + other_faces[late, :]
     energy = faces[number, :] + other_faces[number, :] + energy
-    new_message[pl.ds(2 * rows + 2 * length, 8), :] = energy
-
-
-def late_solve(length, message, other, ratio, edge, late, sweep):
-    rows, depth = edge.shape
-    lead = grouped(edge[...])
-    own = pl.ds(2 * rows + length, length)
-    late[pl.ds(0, length), :] = message[own, :] + other[own, :]
-
-    def down(index, previous):
-        current = lead * late[pl.ds(index, 1), :] + grouped(ratio[index]) * previous
-        sweep[index] = current.reshape(rows, depth)
-        return current
-
-    zero = jnp.zeros(lead.shape, F32)
-    loop(0, length, down, zero)
-
-    def up(back, following):
-        index = length - 1 - back
-        value = grouped(ratio[index + 1]) * (grouped(sweep[index]) + following)
-        sweep[index] = value.reshape(rows, depth)
-        late[pl.ds(length + index, 1), :] = face_rows(value, lead)[0]
-        return value
-
-    loop(0, length, up, zero)
-    sweep[length] = jnp.zeros((rows, depth), F32)
-
-
-def close_kernel(
-    turn, group, length, message, other, sums, weight, ratio, edge, ends, late, sweep
-):
+    new_message[pl.ds(2 * rows + length, 8), :] = energy
+
+
+def close_kernel(turn, group, length, message, other, sums, weight, ratio, ends):
     forward, backward, _, _, _ = joined(turn, group, message, other, sums, weight)
-    late_solve(length, message, other, ratio, edge, late, sweep)
-    ends[0] = ratio[length] * forward + sweep[length - 1]
-    ends[1] = ratio[length] * backward + sweep[0]
+    ends[0] = ratio[length] * forward
+    ends[1] = ratio[length] * backward
 
 
 def coarse_kernel(
     turn, group, length, alone, source, message, other, sums, faces_in, weight, ratio, edge, *refs
 ):
-    precond, image, report, faces, late, sweep, ends = refs[-7:]
+    precond, image, report, faces, sweep, ends = refs[-6:]
     layers, rows, depth = source.shape
     first = position(group) * layers
     below, below_far, above, above_far = faces_in
     forward, backward, before, after, energy = joined(turn, group, message, other, sums, weight)
-    late_solve(length, message, other, ratio, edge, late, sweep)
-    ends[0] = ratio[length] * forward + sweep[length - 1]
-    ends[1] = ratio[length] * backward + sweep[0]
+    ends[0] = ratio[length] * forward
+    ends[1] = ratio[length] * backward
     beyond = ends if alone else refs[0]
     own = pl.ds(2 * rows, length)
     faces[pl.ds(0, length), :] = message[own, :] + other[own, :]
     faces[pl.ds(length, length), :] = below[...] + below_far[...]
     faces[pl.ds(2 * length, length), :] = above[...] + above_far[...]
-    number = pl.ds(2 * rows + 2 * length, 8)
+    number = pl.ds(2 * rows + length, 8)
     energy = message[number, :] + other[number, :] + energy
-    late_rows = late[pl.ds(0, length), :]
-    energy = energy + total(
-        late_rows * (2.0 * faces[pl.ds(0, length), :] - late[pl.ds(length, length), :])
-    )
     forward = before
     for index in range(layers):
         forward = source[index] + ratio[first + index] * forward
         precond[index] = forward
     value = weight[weight.shape[0] - 1] * (after + ratio[first + layers] * forward)
     is_last = first + layers == length
-    precond[layers] = jnp.where(is_last, beyond[1], value + sweep[first + layers])
+    precond[layers] = jnp.where(is_last, beyond[1], value)
     for index in range(layers - 1, -1, -1):
         value = ratio[first + index + 1] * (precond[index] + value)
-        precond[index] = value + sweep[first + index]
+        precond[index] = value
     lead = grouped(edge[...])
     sign = signs(depth)
 
@@ -761,21 +751,21 @@
     outer_planes = (2 * parts * rows + 8, width)
     ahead, behind, last_rows, first_rows = pack(
         halo_kernel,
-        [melt_flow, thermal_state],
+        [melt_flow, thermal_state, powder_flag],
         [],
-        [outer_planes, outer_planes] + [(parts + 1, layers, 8, depth)] * 2,
-        [pltpu.VMEM((2,) + plane, F32)],
-        6 + 4 * parts,
+        [outer_planes] * 2 + [(parts + extra, layers, 8, depth) for extra in (2, 1)],
+        [pltpu.VMEM((2,) + plane, F32), pltpu.VMEM((layers, 8, depth), jnp.int32)],
+        7 + 4 * parts,
     )
     low_x = along(ahead, "gx", 1)
     high_x = along(behind, "gx", -1)
     low_y = along(last_rows, "gy", 1)
     high_y = along(first_rows, "gy", -1)
-    extra, last = pack(
+    extra, back, last = pack(
         extra_kernel,
         [melt_flow, thermal_state, powder_flag],
         [low_y, high_y],
-        [(rows + 8, width), (2,) + plane],
+        [(rows + 8, width), (8, depth), (2,) + plane],
         [
             pltpu.VMEM((5,) + plane, F32),
             pltpu.VMEM(plane, jnp.int32),
@@ -784,6 +774,7 @@
         7,
     )
     extra = along(extra, "gx", 1)
+    back = along(back, "gx", -1)
     early_low = along(last, "gx", 1)
     ratio, weight = call(
         functools.partial(tables_kernel, group, layers),
@@ -793,10 +784,8 @@
     marched = [melt_flow, low_x, high_x, thermal_state, powder_flag, low_y, high_y]
     padded = pltpu.VMEM((4, rows + 16, depth), F32)
     one_padded = pltpu.VMEM((1, rows + 16, depth), F32)
-    (side_y,) = call(row_kernel, marched + [weight], [(layers, depth)], [padded], loose=1)
-    before_y = along(side_y, "gy", 1)
     (star,) = call(
-        march_kernel, marched + [side_y], [(3, layers) + plane], [padded], loose=1, flops=3 << 27
+        march_kernel, marched + [weight], [(3, layers) + plane], [padded], loose=1, flops=3 << 27
     )
     (partial,) = call(
         transform_kernel,
@@ -807,15 +796,17 @@
     )
     source, message = call(
         functools.partial(source_kernel, group, length),
-        [melt_flow, low_x, thermal_state, extra, partial, left, right, ratio, before_y],
+        [
+            melt_flow, low_x, thermal_state, extra, back, low_y, partial, left, right, table_z,
+            edge, ratio,
+        ],
         [(layers,) + plane, (2 * rows, depth)],
-        [one_padded],
-        loose=1,
+        [one_padded, pltpu.VMEM((layers, depth), F32)],
     )
     faces, late = call(
         functools.partial(faces_kernel, group, length),
-        [source, before_y, table_z, ratio, weight, edge, thermal_state, early_low],
-        [(3 * length + 8, depth), (2,) + plane],
+        [source, ratio, weight, edge, thermal_state, early_low],
+        [(2 * length + 8, depth), (2,) + plane],
         [pltpu.VMEM((max(length, layers + 1),) + plane, F32)],
         loose=1,
     )
@@ -840,7 +831,7 @@
                 message, swapped(message, 1 << turn), faces, swapped(faces, 1 << turn),
                 sums, weight,
             ],
-            [(2 * rows + 2 * length + 8, depth), (2,) + plane, line, line],
+            [(2 * rows + length + 8, depth), (2,) + plane, line, line],
         )
         if turn + 2 < rounds:
             rest = message[2 * rows + length :]
@@ -851,13 +842,12 @@
         swapped(tail, 0, 1), swapped(tail, bit, 1), swapped(head, 0, -1), swapped(head, bit, -1)
     ]
     outer = []
-    scratch = [pltpu.VMEM((2 * length, depth), F32), pltpu.VMEM((length + 1,) + plane, F32)]
+    scratch = [pltpu.VMEM((length + 1,) + plane, F32)]
     if not alone:
         (ends,) = call(
             functools.partial(close_kernel, rounds - 1, group, length),
-            [message, other, sums, weight, ratio, edge],
+            [message, other, sums, weight, ratio],
             [(2,) + plane],
-            scratch,
         )
         outer = [jnp.stack([along(ends[0], "gx", group), along(ends[1], "gx", -group)])]
     operands = [source, message, other, sums] + rim

time: 52.6 us -> 50.2 us (0.954)
  waiting for transfers between devices: 19 us -> 15.5 us
  starting transfers between devices: 21.6 us -> 23 us
    ppermute x8, waiting for transfers between devices: 13.6 us -> 11.1 us  [along(): lax.ppermute(array, axis, [(i, (i + by) % length) for i in range(length)])]
    ppermute x8, starting transfers between devices: 11.6 us -> 13.3 us  [along(): lax.ppermute(array, axis, [(i, (i + by) % length) for i in range(length)])]
    ppermute x7, starting transfers between devices: 8.1 us -> 7.14 us  [swapped(): return lax.ppermute(array, ('gx', 'gy'), pairs)]
    ppermute x3, starting transfers between devices: 1.93 us -> 2.65 us  [per_device(): reports.append(lax.ppermute(report, 'gy', pairs))]
    ppermute x3, waiting for transfers between devices: 2.33 us -> 1.8 us  [per_device(): reports.append(lax.ppermute(report, 'gy', pairs))]
    pallas_call x11 -> x10, Pallas kernels: 8.23 us -> 7.78 us  [call(): pl.pallas_call(body, out_shape=out_shape, in_specs=[SMEM] * scalars + [VM...]
  transfers between devices with their start and end apart: 18 -> 18, of which waited for: 10 -> 9; matrix products, arithmetic and copies ran while one was open for 0% -> 0% of each run, Pallas kernels for 14% -> 15%
where the time goes in v12:
time: 50.2 us; the launch traced here: 50 us
  starting transfers between devices  23 us (46%)
  waiting for transfers between devices  15.5 us (31%)
  Pallas kernels  10.6 us (21%)
  between operations  0.84 us (2%)
    ppermute x8, starting transfers between devices, along(): lax.ppermute(array, axis, [(i, (i + by) % length) for i in range(length)])  13.3 us
    ppermute x8, waiting for transfers between devices, along(): lax.ppermute(array, axis, [(i, (i + by) % length) for i in range(length)])  11.1 us
    pallas_call x10, Pallas kernels, call(): pl.pallas_call(body, out_shape=out_shape, in_specs=[SMEM] * scalars + [VM...  7.78 us
    ppermute x7, starting transfers between devices, swapped(): return lax.ppermute(array, ('gx', 'gy'), pairs)  7.14 us
    pallas_call x2, Pallas kernels, pack(): pl.pallas_call(body, out_shape=[jax.ShapeDtypeStruct(shape, F32) for shap...  2.78 us
    ppermute x3, starting transfers between devices, per_device(): reports.append(lax.ppermute(report, 'gy', pairs))  2.65 us
    ppermute x7, waiting for transfers between devices, swapped(): return lax.ppermute(array, ('gx', 'gy'), pairs)  2.6 us
    ppermute x3, waiting for transfers between devices, per_device(): reports.append(lax.ppermute(report, 'gy', pairs))  1.8 us
  transfers between devices with their start and end apart: 18, of which 9 were waited for; matrix products, arithmetic and copies ran while one was open for 0% of the time, Pallas kernels for 15%

profile of v12, /device:TPU:0, one launch (start us, length us, event | category | flops | bytes accessed | tf_op | source)
XLA Modules:
  0.0 50.0 jit_solution(5658627834642184489)
XLA Ops:
  0.7 1.5 %shard_map.121 = (f32[776,128]{1,0:T(8,128)S(1)}, f32[776,128]{1,0:T(8,128)S(1)}, f32[5,4,8,128]{3,2,1,0:T(8,128)S(1)}, f32[4,4,8,128]{3,2,1,0:T(8,128)S(1)}) custom-call(f32[3,4,128,128]{3,2,1,0:T(8,128)} %flow.9, f32[4,128,128]{2,1,0:T(8,128)} %thermal.11, s32[4,128,128]{2,1,0:T(8,128)} %flag.5), custom_call_target="tpu_custom_call" | custom-call | tf_op jit(solution)/shard_map/pallas_call | solution.py:723
  2.2 3.1 %collective-permute-start = (f32[776,128]{1,0:T(8,128)S(1)}, f32[776,128]{1,0:T(8,128)S(1)}, u32[]{:S(2)}, u32[]{:S(2)}) collective-permute-start(f32[776,128]{1,0:T(8,128)S(1)} %get-tuple-element.30), channel_id=1, source_target_pairs={{0,4},{4,8},{8,12},{12,0},{1,5},{5,9},{9,13},{13,1},{2,6},{6,10},{... | collective-permute-start | bytes 1191944 | tf_op jit(solution)/shard_map/ppermute | solution.py:708
  5.2 2.1 %collective-permute-start.1 = (f32[776,128]{1,0:T(8,128)S(1)}, f32[776,128]{1,0:T(8,128)S(1)}, u32[]{:S(2)}, u32[]{:S(2)}) collective-permute-start(f32[776,128]{1,0:T(8,128)S(1)} %get-tuple-element.31), channel_id=1, source_target_pairs={{0,12},{4,0},{8,4},{12,8},{1,13},{5,1},{9,5},{13,9},{2,14},{6,2},{... | collective-permute-start | bytes 1191944 | tf_op jit(solution)/shard_map/ppermute | solution.py:708
  7.3 1.7 %collective-permute-start.3 = (f32[4,4,8,128]{3,2,1,0:T(8,128)S(1)}, f32[4,4,8,128]{3,2,1,0:T(8,128)S(1)}, u32[]{:S(2)}, u32[]{:S(2)}) collective-permute-start(f32[4,4,8,128]{3,2,1,0:T(8,128)S(1)} %get-tuple-element.33), channel_id=1, source_target_pairs={{0,3},{1,0},{2,1},{3,2},{4,7},{5,4},{6,5},{7,6},{8,11},{9,8},{10,9... | collective-permute-start | bytes 196616 | tf_op jit(solution)/shard_map/ppermute | solution.py:708
  9.1 2.0 %collective-permute-done.3.high_y = f32[4,4,8,128]{3,2,1,0:T(8,128)S(1)} collective-permute-done((f32[4,4,8,128]{3,2,1,0:T(8,128)S(1)}, f32[4,4,8,128]{3,2,1,0:T(8,128)S(1)}, u32[]{:S(2)}, u32[]{:S(2)}) %collective-permute-start.3) | collective-permute-done | bytes 65568 | tf_op jit(solution)/shard_map/ppermute | solution.py:708
  11.2 1.3 %shard_map.124 = (f32[136,128]{1,0:T(8,128)S(1)}, f32[8,128]{1,0:T(8,128)S(1)}, f32[2,128,128]{2,1,0:T(8,128)S(1)}) custom-call(f32[3,4,128,128]{3,2,1,0:T(8,128)} %flow.9, f32[4,128,128]{2,1,0:T(8,128)} %thermal.11, s32[4,128,128]{2,1,0:T(8,128)} %flag.5, f32[5,4,8,128]{3,2,1,0:T(8,128)S(1)} %collective-permute-done.2.low_y, ...), custom_call_target="tpu_custom_call" | custom-call | tf_op jit(solution)/shard_map/pallas_call | solution.py:723
  13.0 3.9 %collective-permute-start.5 = (f32[8,128]{1,0:T(8,128)S(1)}, f32[8,128]{1,0:T(8,128)S(1)}, u32[]{:S(2)}, u32[]{:S(2)}) collective-permute-start(f32[8,128]{1,0:T(8,128)S(1)} %get-tuple-element.36), channel_id=1, source_target_pairs={{0,12},{4,0},{8,4},{12,8},{1,13},{5,1},{9,5},{13,9},{2,14},{6,2},{... | collective-permute-start | bytes 12296 | tf_op jit(solution)/shard_map/ppermute | solution.py:708
  17.3 7.4 %collective-permute-done.1.high_x = f32[776,128]{1,0:T(8,128)S(1)} collective-permute-done((f32[776,128]{1,0:T(8,128)S(1)}, f32[776,128]{1,0:T(8,128)S(1)}, u32[]{:S(2)}, u32[]{:S(2)}) %collective-permute-start.1) | collective-permute-done | bytes 397344 | tf_op jit(solution)/shard_map/ppermute | solution.py:708
  24.8 1.1 %shard_map.123.star = f32[3,4,128,128]{3,2,1,0:T(8,128)S(1)} custom-call(f32[3,4,128,128]{3,2,1,0:T(8,128)S(1)} %copy-done, f32[776,128]{1,0:T(8,128)S(1)} %collective-permute-done.low_x, f32[776,128]{1,0:T(8,128)S(1)} %collective-permute-done.1.high_x, f32[4,128,128]{2,1,0:T(8,128)S(1)} %copy-done.1, s32[4,128,128]{2,1,0:T(8,128)S(1)} %copy-done.2, ...), custom_call_target="tpu_custom_call" | custom-call | flops 402653184 | bytes 1572864 | tf_op jit(solution)/shard_map/pallas_call | solution.py:30
  26.5 0.9 %collective-permute-done.4.extra = f32[136,128]{1,0:T(8,128)S(1)} collective-permute-done((f32[136,128]{1,0:T(8,128)S(1)}, f32[136,128]{1,0:T(8,128)S(1)}, u32[]{:S(2)}, u32[]{:S(2)}) %collective-permute-start.4) | collective-permute-done | bytes 69664 | tf_op jit(solution)/shard_map/ppermute | solution.py:708
  27.3 0.7 %shard_map.126 = (f32[4,128,128]{2,1,0:T(8,128)S(1)}, f32[256,128]{1,0:T(8,128)S(1)}) custom-call(f32[3,4,128,128]{3,2,1,0:T(8,128)S(1)} %copy-done, f32[776,128]{1,0:T(8,128)S(1)} %collective-permute-done.low_x, f32[4,128,128]{2,1,0:T(8,128)S(1)} %copy-done.1, f32[136,128]{1,0:T(8,128)S(1)} %collective-permute-done.4.extra, ...), custom_call_target="tpu_custom_call" | custom-call | flops 1048576 | bytes 786432 | tf_op jit(solution)/shard_map/pallas_call | solution.py:30
  28.0 1.1 %collective-permute-start.6 = (f32[256,128]{1,0:T(8,128)S(1)}, f32[256,128]{1,0:T(8,128)S(1)}, u32[]{:S(2)}, u32[]{:S(2)}) collective-permute-start(f32[256,128]{1,0:T(8,128)S(1)} %get-tuple-element.39.message), channel_id=1, source_target_pairs={{0,4},{1,5},{2,6},{3,7},{4,0},{5,1},{6,2},{7,3},{8,12},{9,13},{10,... | collective-permute-start | bytes 393224 | tf_op jit(solution)/shard_map/ppermute | solution.py:718
  29.9 0.8 %collective-permute-start.8 = (f32[40,128]{1,0:T(8,128)S(1)}, f32[40,128]{1,0:T(8,128)S(1)}, u32[]{:S(2)}, u32[]{:S(2)}) collective-permute-start(f32[40,128]{1,0:T(8,128)S(1)} %get-tuple-element.41.faces), channel_id=1, source_target_pairs={{0,4},{1,5},{2,6},{3,7},{4,0},{5,1},{6,2},{7,3},{8,12},{9,13},{10,... | collective-permute-start | bytes 61448 | tf_op jit(solution)/shard_map/ppermute | solution.py:718
  30.7 2.4 %collective-permute-start.14 = (f32[2,128,128]{2,1,0:T(8,128)S(1)}, f32[2,128,128]{2,1,0:T(8,128)S(1)}, u32[]{:S(2)}, u32[]{:S(2)}) collective-permute-start(f32[2,128,128]{2,1,0:T(8,128)S(1)} %get-tuple-element.46), channel_id=1, source_target_pairs={{0,12},{4,0},{8,4},{12,8},{1,13},{5,1},{9,5},{13,9},{2,14},{6,2},{... | collective-permute-start | bytes 393224 | tf_op jit(solution)/shard_map/ppermute | solution.py:708
  33.1 1.5 %collective-permute-done.8.other_faces = f32[40,128]{1,0:T(8,128)S(1)} collective-permute-done((f32[40,128]{1,0:T(8,128)S(1)}, f32[40,128]{1,0:T(8,128)S(1)}, u32[]{:S(2)}, u32[]{:S(2)}) %collective-permute-start.8) | collective-permute-done | bytes 20512 | tf_op jit(solution)/shard_map/ppermute | solution.py:718
  34.8 1.0 %collective-permute-start.9 = (f32[280,128]{1,0:T(8,128)S(1)}, f32[280,128]{1,0:T(8,128)S(1)}, u32[]{:S(2)}, u32[]{:S(2)}) collective-permute-start(f32[280,128]{1,0:T(8,128)S(1)} %get-tuple-element.42.refs_1_), channel_id=1, source_target_pairs={{0,8},{1,9},{2,10},{3,11},{4,12},{5,13},{6,14},{7,15},{8,0},{9,1},... | collective-permute-start | bytes 430088 | tf_op jit(solution)/shard_map/ppermute | solution.py:718
  35.8 3.3 %collective-permute-start.10 = (f32[16,128]{1,0:T(8,128)S(1)}, f32[16,128]{1,0:T(8,128)S(1)}, u32[]{:S(2)}, u32[]{:S(2)}) collective-permute-start(f32[16,128]{1,0:T(8,128)S(1)} %get-tuple-element.44), channel_id=1, source_target_pairs={{0,1},{1,2},{2,3},{3,0},{4,5},{5,6},{6,7},{7,4},{8,9},{9,10},{10,1... | collective-permute-start | bytes 24584 | tf_op jit(solution)/shard_map/ppermute | solution.py:718
  39.3 0.7 %collective-permute-start.12 = (f32[16,128]{1,0:T(8,128)S(1)}, f32[16,128]{1,0:T(8,128)S(1)}, u32[]{:S(2)}, u32[]{:S(2)}) collective-permute-start(f32[16,128]{1,0:T(8,128)S(1)} %get-tuple-element.45), channel_id=1, source_target_pairs={{0,3},{1,0},{2,1},{3,2},{4,7},{5,4},{6,5},{7,6},{8,11},{9,8},{10,9... | collective-permute-start | bytes 24584 | tf_op jit(solution)/shard_map/ppermute | solution.py:718
  40.0 2.0 %shard_map.129 = (f32[4,128,128]{2,1,0:T(8,128)}, f32[8,128]{1,0:T(8,128)S(1)}) custom-call(s32[8]{0:T(128)S(1)} %copy-done.8, s32[8]{0:T(128)S(1)} %copy-done.9, f32[4,128,128]{2,1,0:T(8,128)S(1)} %copy-done.1, f32[2,128,128]{2,1,0:T(8,128)S(1)} %collective-permute-done.7._.low_x, f32[2,128,128]{2,1,0:T(8,128)S(1)} %collective-permute-done.14.high_x, ...), custom_call_target="tpu_custom_call" | custom-call | flops 268435456 | bytes 532480 | tf_op jit(solution)/shard_map/pallas_call | solution.py:30
  42.0 1.1 %collective-permute-done.13.refs_7_ = f32[16,128]{1,0:T(8,128)S(1)} collective-permute-done((f32[16,128]{1,0:T(8,128)S(1)}, f32[16,128]{1,0:T(8,128)S(1)}, u32[]{:S(2)}, u32[]{:S(2)}) %collective-permute-start.13) | collective-permute-done | bytes 8224 | tf_op jit(solution)/shard_map/ppermute | solution.py:718
  43.6 1.3 %collective-permute-start.17 = (f32[40,128]{1,0:T(8,128)S(1)}, f32[40,128]{1,0:T(8,128)S(1)}, u32[]{:S(2)}, u32[]{:S(2)}) collective-permute-start(f32[40,128]{1,0:T(8,128)S(1)} %get-tuple-element.53.refs_0_), channel_id=1, source_target_pairs={{0,3},{1,2},{2,1},{3,0},{4,7},{5,6},{6,5},{7,4},{8,11},{9,10},{10,... | collective-permute-start | bytes 61448 | tf_op jit(solution)/shard_map/ppermute | solution.py:882
  45.0 1.3 %collective-permute-start.16 = (f32[40,128]{1,0:T(8,128)S(1)}, f32[40,128]{1,0:T(8,128)S(1)}, u32[]{:S(2)}, u32[]{:S(2)}) collective-permute-start(f32[40,128]{1,0:T(8,128)S(1)} %get-tuple-element.53.refs_0_), channel_id=1, source_target_pairs={{0,2},{1,3},{2,0},{3,1},{4,6},{5,7},{6,4},{7,5},{8,10},{9,11},{10,... | collective-permute-start | bytes 61448 | tf_op jit(solution)/shard_map/ppermute | solution.py:882
  47.0 1.8 %collective-permute-done.16.refs_2_ = f32[40,128]{1,0:T(8,128)S(1)} collective-permute-done((f32[40,128]{1,0:T(8,128)S(1)}, f32[40,128]{1,0:T(8,128)S(1)}, u32[]{:S(2)}, u32[]{:S(2)}) %collective-permute-start.16) | collective-permute-done | bytes 20512 | tf_op jit(solution)/shard_map/ppermute | solution.py:882
  48.8 1.3 %shard_map.132 = (f32[3,4,128,128]{3,2,1,0:T(8,128)}, f32[4,128,128]{2,1,0:T(8,128)}) custom-call(f32[3,4,128,128]{3,2,1,0:T(8,128)S(1)} %shard_map.123.star, f32[5,128,128]{2,1,0:T(8,128)S(1)} %get-tuple-element.50.precond, f32[5,128,128]{2,1,0:T(8,128)S(1)} %get-tuple-element.51.image, f32[48,128]{1,0:T(8,128)S(1)} %get-tuple-element.52.faces, ...), custom_call_target="tpu_custom_call" | custom-call | flops 1048576 | bytes 2097152 | tf_op jit(solution)/shard_map/pallas_call | solution.py:30
  (45 shorter events, 4.0 us)
Async XLA Ops:
  0.6 11.9 %copy-start.7 = (f32[128,128]{1,0:T(8,128)S(1)}, f32[128,128]{1,0:T(8,128)}, u32[]{:S(2)}) copy-start(f32[128,128]{1,0:T(8,128)} %constant.16.clone.diagonal) | copy-start | bytes 196612
  0.6 24.1 %copy-start.1 = (f32[4,128,128]{2,1,0:T(8,128)S(1)}, f32[4,128,128]{2,1,0:T(8,128)}, u32[]{:S(2)}) copy-start(f32[4,128,128]{2,1,0:T(8,128)} %thermal.11) | copy-start | bytes 786436
  0.7 24.1 %copy-start = (f32[3,4,128,128]{3,2,1,0:T(8,128)S(1)}, f32[3,4,128,128]{3,2,1,0:T(8,128)}, u32[]{:S(2)}) copy-start(f32[3,4,128,128]{3,2,1,0:T(8,128)} %flow.9) | copy-start | bytes 2359300
  0.7 24.1 %copy-start.2 = (s32[4,128,128]{2,1,0:T(8,128)S(1)}, s32[4,128,128]{2,1,0:T(8,128)}, u32[]{:S(2)}) copy-start(s32[4,128,128]{2,1,0:T(8,128)} %flag.5) | copy-start | bytes 786436
  2.2 15.2 %collective-permute-start = (f32[776,128]{1,0:T(8,128)S(1)}, f32[776,128]{1,0:T(8,128)S(1)}, u32[]{:S(2)}, u32[]{:S(2)}) collective-permute-start(f32[776,128]{1,0:T(8,128)S(1)} %get-tuple-element.30), channel_id=1, source_target_pairs={{0,4},{4,8},{8,12},{12,0},{1,5},{5,9},{9,13},{13,1},{2,6},{6,10},{... | collective-permute-start | bytes 1191944 | tf_op jit(solution)/shard_map/ppermute | solution.py:708
  5.2 19.5 %collective-permute-start.1 = (f32[776,128]{1,0:T(8,128)S(1)}, f32[776,128]{1,0:T(8,128)S(1)}, u32[]{:S(2)}, u32[]{:S(2)}) collective-permute-start(f32[776,128]{1,0:T(8,128)S(1)} %get-tuple-element.31), channel_id=1, source_target_pairs={{0,12},{4,0},{8,4},{12,8},{1,13},{5,1},{9,5},{13,9},{2,14},{6,2},{... | collective-permute-start | bytes 1191944 | tf_op jit(solution)/shard_map/ppermute | solution.py:708
  7.3 3.9 %collective-permute-start.2 = (f32[5,4,8,128]{3,2,1,0:T(8,128)S(1)}, f32[5,4,8,128]{3,2,1,0:T(8,128)S(1)}, u32[]{:S(2)}, u32[]{:S(2)}) collective-permute-start(f32[5,4,8,128]{3,2,1,0:T(8,128)S(1)} %get-tuple-element.32), channel_id=1, source_target_pairs={{0,1},{1,2},{2,3},{3,0},{4,5},{5,6},{6,7},{7,4},{8,9},{9,10},{10,1... | collective-permute-start | bytes 245768 | tf_op jit(solution)/shard_map/ppermute | solution.py:708
  7.3 3.7 %collective-permute-start.3 = (f32[4,4,8,128]{3,2,1,0:T(8,128)S(1)}, f32[4,4,8,128]{3,2,1,0:T(8,128)S(1)}, u32[]{:S(2)}, u32[]{:S(2)}) collective-permute-start(f32[4,4,8,128]{3,2,1,0:T(8,128)S(1)} %get-tuple-element.33), channel_id=1, source_target_pairs={{0,3},{1,0},{2,1},{3,2},{4,7},{5,4},{6,5},{7,6},{8,11},{9,8},{10,9... | collective-permute-start | bytes 196616 | tf_op jit(solution)/shard_map/ppermute | solution.py:708
  12.5 14.8 %collective-permute-start.4 = (f32[136,128]{1,0:T(8,128)S(1)}, f32[136,128]{1,0:T(8,128)S(1)}, u32[]{:S(2)}, u32[]{:S(2)}) collective-permute-start(f32[136,128]{1,0:T(8,128)S(1)} %get-tuple-element.35), channel_id=1, source_target_pairs={{0,4},{4,8},{8,12},{12,0},{1,5},{5,9},{9,13},{13,1},{2,6},{6,10},{... | collective-permute-start | bytes 208904 | tf_op jit(solution)/shard_map/ppermute | solution.py:708
  13.0 13.5 %collective-permute-start.5 = (f32[8,128]{1,0:T(8,128)S(1)}, f32[8,128]{1,0:T(8,128)S(1)}, u32[]{:S(2)}, u32[]{:S(2)}) collective-permute-start(f32[8,128]{1,0:T(8,128)S(1)} %get-tuple-element.36), channel_id=1, source_target_pairs={{0,12},{4,0},{8,4},{12,8},{1,13},{5,1},{9,5},{13,9},{2,14},{6,2},{... | collective-permute-start | bytes 12296 | tf_op jit(solution)/shard_map/ppermute | solution.py:708
  16.8 12.6 %collective-permute-start.7 = (f32[2,128,128]{2,1,0:T(8,128)S(1)}, f32[2,128,128]{2,1,0:T(8,128)S(1)}, u32[]{:S(2)}, u32[]{:S(2)}) collective-permute-start(f32[2,128,128]{2,1,0:T(8,128)S(1)} %get-tuple-element.40), channel_id=1, source_target_pairs={{0,4},{4,8},{8,12},{12,0},{1,5},{5,9},{9,13},{13,1},{2,6},{6,10},{... | collective-permute-start | bytes 393224 | tf_op jit(solution)/shard_map/ppermute | solution.py:708
  28.0 6.6 %collective-permute-start.6 = (f32[256,128]{1,0:T(8,128)S(1)}, f32[256,128]{1,0:T(8,128)S(1)}, u32[]{:S(2)}, u32[]{:S(2)}) collective-permute-start(f32[256,128]{1,0:T(8,128)S(1)} %get-tuple-element.39.message), channel_id=1, source_target_pairs={{0,4},{1,5},{2,6},{3,7},{4,0},{5,1},{6,2},{7,3},{8,12},{9,13},{10,... | collective-permute-start | bytes 393224 | tf_op jit(solution)/shard_map/ppermute | solution.py:718
  29.9 10.2 %copy-start.8 = (s32[8]{0:T(128)S(1)}, s32[8]{0:T(128)}, u32[]{:S(2)}) copy-start(s32[8]{0:T(128)} %spots_a.1) | copy-start | bytes 100
  29.9 10.2 %copy-start.9 = (s32[8]{0:T(128)S(1)}, s32[8]{0:T(128)}, u32[]{:S(2)}) copy-start(s32[8]{0:T(128)} %spots_b.1) | copy-start | bytes 100
  29.9 4.7 %collective-permute-start.8 = (f32[40,128]{1,0:T(8,128)S(1)}, f32[40,128]{1,0:T(8,128)S(1)}, u32[]{:S(2)}, u32[]{:S(2)}) collective-permute-start(f32[40,128]{1,0:T(8,128)S(1)} %get-tuple-element.41.faces), channel_id=1, source_target_pairs={{0,4},{1,5},{2,6},{3,7},{4,0},{5,1},{6,2},{7,3},{8,12},{9,13},{10,... | collective-permute-start | bytes 61448 | tf_op jit(solution)/shard_map/ppermute | solution.py:718
  30.7 8.7 %collective-permute-start.14 = (f32[2,128,128]{2,1,0:T(8,128)S(1)}, f32[2,128,128]{2,1,0:T(8,128)S(1)}, u32[]{:S(2)}, u32[]{:S(2)}) collective-permute-start(f32[2,128,128]{2,1,0:T(8,128)S(1)} %get-tuple-element.46), channel_id=1, source_target_pairs={{0,12},{4,0},{8,4},{12,8},{1,13},{5,1},{9,5},{13,9},{2,14},{6,2},{... | collective-permute-start | bytes 393224 | tf_op jit(solution)/shard_map/ppermute | solution.py:708
  34.8 8.3 %collective-permute-start.9 = (f32[280,128]{1,0:T(8,128)S(1)}, f32[280,128]{1,0:T(8,128)S(1)}, u32[]{:S(2)}, u32[]{:S(2)}) collective-permute-start(f32[280,128]{1,0:T(8,128)S(1)} %get-tuple-element.42.refs_1_), channel_id=1, source_target_pairs={{0,8},{1,9},{2,10},{3,11},{4,12},{5,13},{6,14},{7,15},{8,0},{9,1},... | collective-permute-start | bytes 430088 | tf_op jit(solution)/shard_map/ppermute | solution.py:718
  35.8 6.2 %collective-permute-start.11 = (f32[16,128]{1,0:T(8,128)S(1)}, f32[16,128]{1,0:T(8,128)S(1)}, u32[]{:S(2)}, u32[]{:S(2)}) collective-permute-start(f32[16,128]{1,0:T(8,128)S(1)} %get-tuple-element.44), channel_id=1, source_target_pairs={{0,9},{1,10},{2,11},{3,8},{4,13},{5,14},{6,15},{7,12},{8,1},{9,2},... | collective-permute-start | bytes 24584 | tf_op jit(solution)/shard_map/ppermute | solution.py:718
  35.8 6.2 %collective-permute-start.10 = (f32[16,128]{1,0:T(8,128)S(1)}, f32[16,128]{1,0:T(8,128)S(1)}, u32[]{:S(2)}, u32[]{:S(2)}) collective-permute-start(f32[16,128]{1,0:T(8,128)S(1)} %get-tuple-element.44), channel_id=1, source_target_pairs={{0,1},{1,2},{2,3},{3,0},{4,5},{5,6},{6,7},{7,4},{8,9},{9,10},{10,1... | collective-permute-start | bytes 24584 | tf_op jit(solution)/shard_map/ppermute | solution.py:718
  39.1 4.0 %collective-permute-start.13 = (f32[16,128]{1,0:T(8,128)S(1)}, f32[16,128]{1,0:T(8,128)S(1)}, u32[]{:S(2)}, u32[]{:S(2)}) collective-permute-start(f32[16,128]{1,0:T(8,128)S(1)} %get-tuple-element.45), channel_id=1, source_target_pairs={{0,11},{1,8},{2,9},{3,10},{4,15},{5,12},{6,13},{7,14},{8,3},{9,0},... | collective-permute-start | bytes 24584 | tf_op jit(solution)/shard_map/ppermute | solution.py:718
  39.3 3.7 %collective-permute-start.12 = (f32[16,128]{1,0:T(8,128)S(1)}, f32[16,128]{1,0:T(8,128)S(1)}, u32[]{:S(2)}, u32[]{:S(2)}) collective-permute-start(f32[16,128]{1,0:T(8,128)S(1)} %get-tuple-element.45), channel_id=1, source_target_pairs={{0,3},{1,0},{2,1},{3,2},{4,7},{5,4},{6,5},{7,6},{8,11},{9,8},{10,9... | collective-permute-start | bytes 24584 | tf_op jit(solution)/shard_map/ppermute | solution.py:718
  43.6 3.3 %collective-permute-start.17 = (f32[40,128]{1,0:T(8,128)S(1)}, f32[40,128]{1,0:T(8,128)S(1)}, u32[]{:S(2)}, u32[]{:S(2)}) collective-permute-start(f32[40,128]{1,0:T(8,128)S(1)} %get-tuple-element.53.refs_0_), channel_id=1, source_target_pairs={{0,3},{1,2},{2,1},{3,0},{4,7},{5,6},{6,5},{7,4},{8,11},{9,10},{10,... | collective-permute-start | bytes 61448 | tf_op jit(solution)/shard_map/ppermute | solution.py:882
  45.0 3.8 %collective-permute-start.16 = (f32[40,128]{1,0:T(8,128)S(1)}, f32[40,128]{1,0:T(8,128)S(1)}, u32[]{:S(2)}, u32[]{:S(2)}) collective-permute-start(f32[40,128]{1,0:T(8,128)S(1)} %get-tuple-element.53.refs_0_), channel_id=1, source_target_pairs={{0,2},{1,3},{2,0},{3,1},{4,6},{5,7},{6,4},{7,5},{8,10},{9,11},{10,... | collective-permute-start | bytes 61448 | tf_op jit(solution)/shard_map/ppermute | solution.py:882
  46.3 2.5 %collective-permute-start.15 = (f32[40,128]{1,0:T(8,128)S(1)}, f32[40,128]{1,0:T(8,128)S(1)}, u32[]{:S(2)}, u32[]{:S(2)}) collective-permute-start(f32[40,128]{1,0:T(8,128)S(1)} %get-tuple-element.53.refs_0_), channel_id=1, source_target_pairs={{0,1},{1,0},{2,3},{3,2},{4,5},{5,4},{6,7},{7,6},{8,9},{9,8},{10,11... | collective-permute-start | bytes 61448 | tf_op jit(solution)/shard_map/ppermute | solution.py:882
  (4 other events, 5.2 us)

commit v13 on v12

--- a/solution.py
+++ b/solution.py
@@ -315,16 +315,36 @@
     return jnp.sum(jnp.where(same, plane[:, depth - 1 :], 0.0), axis=0, keepdims=True)
 
 
-def halo_kernel(
-    flow, thermal, flag, ahead, behind, last_rows, first_rows, tops, flags, sems
-):
+def outer_copies(flow, thermal, message, top, first):
     parts, layers, rows, depth = flow.shape
-    pairs = [(thermal.at[layers - 1], tops.at[0]), (thermal.at[0], tops.at[1])]
+    pairs = [(thermal.at[0 if first == 0 else layers - 1], top)]
     for part in range(parts):
         for layer in range(2):
             span = pl.ds((2 * part + layer) * rows, rows)
-            pairs.append((flow.at[part, layers - 2 + layer], ahead.at[span, :]))
-            pairs.append((flow.at[part, layer], behind.at[span, :]))
+            pairs.append((flow.at[part, first + layer], message.at[span, :]))
+    return pairs
+
+
+def finish(copies, message, top):
+    rows = top.shape[0]
+    copies[0].wait()
+    row = jnp.broadcast_to(surface(top[...]), (8, rows))
+    message[pl.ds(message.shape[0] - 8, 8), pl.ds(0, rows)] = row
+    for copy in copies[1:]:
+        copy.wait()
+
+
+def ahead_kernel(flow, thermal, message, top, sems):
+    pairs = outer_copies(flow, thermal, message, top, flow.shape[1] - 2)
+    copies = started(
+        [pltpu.make_async_copy(*pair, sems.at[index]) for index, pair in enumerate(pairs)]
+    )
+    finish(copies, message, top)
+
+
+def behind_kernel(flow, thermal, flag, message, last_rows, first_rows, top, flags, sems):
+    parts, layers, rows, depth = flow.shape
+    pairs = outer_copies(flow, thermal, message, top, 0)
     for target, start in ((last_rows, rows - 8), (first_rows, 0)):
         span = pl.ds(start, 8)
         pairs.append((flow.at[:, :, span, :], target.at[pl.ds(0, parts)]))
@@ -333,12 +353,7 @@
     copies = started(
         [pltpu.make_async_copy(*pair, sems.at[index]) for index, pair in enumerate(pairs)]
     )
-    for side, message in enumerate((ahead, behind)):
-        copies[side].wait()
-        row = jnp.broadcast_to(surface(tops[side]), (8, rows))
-        message[pl.ds(2 * parts * rows, 8), pl.ds(0, rows)] = row
-    for copy in copies[2:]:
-        copy.wait()
+    finish(copies, message, top)
     last_rows[parts + 1] = flags[...].astype(F32)
 
 
@@ -749,13 +764,21 @@
     parts = melt_flow.shape[0]
     width = max(rows, depth)
     outer_planes = (2 * parts * rows + 8, width)
-    ahead, behind, last_rows, first_rows = pack(
-        halo_kernel,
+    (ahead,) = pack(
+        ahead_kernel,
+        [melt_flow, thermal_state],
+        [],
+        [outer_planes],
+        [pltpu.VMEM(plane, F32)],
+        1 + 2 * parts,
+    )
+    behind, last_rows, first_rows = pack(
+        behind_kernel,
         [melt_flow, thermal_state, powder_flag],
         [],
-        [outer_planes] * 2 + [(parts + extra, layers, 8, depth) for extra in (2, 1)],
-        [pltpu.VMEM((2,) + plane, F32), pltpu.VMEM((layers, 8, depth), jnp.int32)],
-        7 + 4 * parts,
+        [outer_planes] + [(parts + extra, layers, 8, depth) for extra in (2, 1)],
+        [pltpu.VMEM(plane, F32), pltpu.VMEM((layers, 8, depth), jnp.int32)],
+        6 + 2 * parts,
     )
     low_x = along(ahead, "gx", 1)
     high_x = along(behind, "gx", -1)

time: 50.2 us -> 50.7 us (level)
  starting transfers between devices: 23 us -> 21.7 us
  Pallas kernels: 10.6 us -> 11.3 us
  waiting for transfers between devices: 15.5 us -> 16.1 us
    ppermute x7, waiting for transfers between devices: 2.6 us -> 4.29 us  [swapped(): return lax.ppermute(array, ('gx', 'gy'), pairs)]
    ppermute x8, waiting for transfers between devices: 11.1 us -> 10 us  [along(): lax.ppermute(array, axis, [(i, (i + by) % length) for i in range(length)])]
    ppermute x7, starting transfers between devices: 7.14 us -> 6.31 us  [swapped(): return lax.ppermute(array, ('gx', 'gy'), pairs)]
    pallas_call x2 -> x3, Pallas kernels: 2.78 us -> 3.56 us  [pack(): pl.pallas_call(body, out_shape=[jax.ShapeDtypeStruct(shape, F32) for shap...]
  transfers between devices with their start and end apart: 18 -> 18, of which waited for: 9 -> 9; matrix products, arithmetic and copies ran while one was open for 0% -> 0% of each run, Pallas kernels for 15% -> 17%
where the time goes in v13:
time: 50.7 us; the launch traced here: 50.4 us
  starting transfers between devices  21.7 us (43%)
  waiting for transfers between devices  16.1 us (32%)
  Pallas kernels  11.3 us (22%)
  between operations  0.85 us (2%)
    ppermute x8, starting transfers between devices, along(): lax.ppermute(array, axis, [(i, (i + by) % length) for i in range(length)])  12.9 us
    ppermute x8, waiting for transfers between devices, along(): lax.ppermute(array, axis, [(i, (i + by) % length) for i in range(length)])  10 us
    pallas_call x10, Pallas kernels, call(): pl.pallas_call(body, out_shape=out_shape, in_specs=[SMEM] * scalars + [VM...  7.77 us
    ppermute x7, starting transfers between devices, swapped(): return lax.ppermute(array, ('gx', 'gy'), pairs)  6.31 us
    ppermute x7, waiting for transfers between devices, swapped(): return lax.ppermute(array, ('gx', 'gy'), pairs)  4.29 us
    pallas_call x3, Pallas kernels, pack(): pl.pallas_call(body, out_shape=[jax.ShapeDtypeStruct(shape, F32) for shap...  3.56 us
    ppermute x3, starting transfers between devices, per_device(): reports.append(lax.ppermute(report, 'gy', pairs))  2.51 us
    ppermute x3, waiting for transfers between devices, per_device(): reports.append(lax.ppermute(report, 'gy', pairs))  1.81 us
  transfers between devices with their start and end apart: 18, of which 9 were waited for; matrix products, arithmetic and copies ran while one was open for 0% of the time, Pallas kernels for 17%

profile of v13, /device:TPU:0, one launch (start us, length us, event | category | flops | bytes accessed | tf_op | source)
XLA Modules:
  0.0 50.4 jit_solution(14632967839522469989)
XLA Ops:
  0.6 1.1 %shard_map.121 = f32[776,128]{1,0:T(8,128)S(1)} custom-call(f32[3,4,128,128]{3,2,1,0:T(8,128)} %flow.11, f32[4,128,128]{2,1,0:T(8,128)} %thermal.13), custom_call_target="tpu_custom_call" | custom-call | tf_op jit(solution)/shard_map/pallas_call | solution.py:738
  1.8 3.1 %collective-permute-start = (f32[776,128]{1,0:T(8,128)S(1)}, f32[776,128]{1,0:T(8,128)S(1)}, u32[]{:S(2)}, u32[]{:S(2)}) collective-permute-start(f32[776,128]{1,0:T(8,128)S(1)} %shard_map.121), channel_id=1, source_target_pairs={{0,4},{4,8},{8,12},{12,0},{1,5},{5,9},{9,13},{13,1},{2,6},{6,10},{... | collective-permute-start | bytes 1191944 | tf_op jit(solution)/shard_map/ppermute | solution.py:723
  4.9 1.2 %shard_map.122 = (f32[776,128]{1,0:T(8,128)S(1)}, f32[5,4,8,128]{3,2,1,0:T(8,128)S(1)}, f32[4,4,8,128]{3,2,1,0:T(8,128)S(1)}) custom-call(f32[3,4,128,128]{3,2,1,0:T(8,128)} %flow.11, f32[4,128,128]{2,1,0:T(8,128)} %thermal.13, s32[4,128,128]{2,1,0:T(8,128)} %flag.5), custom_call_target="tpu_custom_call" | custom-call | tf_op jit(solution)/shard_map/pallas_call | solution.py:738
  6.0 2.2 %collective-permute-start.1 = (f32[776,128]{1,0:T(8,128)S(1)}, f32[776,128]{1,0:T(8,128)S(1)}, u32[]{:S(2)}, u32[]{:S(2)}) collective-permute-start(f32[776,128]{1,0:T(8,128)S(1)} %get-tuple-element.29), channel_id=1, source_target_pairs={{0,12},{4,0},{8,4},{12,8},{1,13},{5,1},{9,5},{13,9},{2,14},{6,2},{... | collective-permute-start | bytes 1191944 | tf_op jit(solution)/shard_map/ppermute | solution.py:723
  8.2 1.8 %collective-permute-start.3 = (f32[4,4,8,128]{3,2,1,0:T(8,128)S(1)}, f32[4,4,8,128]{3,2,1,0:T(8,128)S(1)}, u32[]{:S(2)}, u32[]{:S(2)}) collective-permute-start(f32[4,4,8,128]{3,2,1,0:T(8,128)S(1)} %get-tuple-element.31), channel_id=1, source_target_pairs={{0,3},{1,0},{2,1},{3,2},{4,7},{5,4},{6,5},{7,6},{8,11},{9,8},{10,9... | collective-permute-start | bytes 196616 | tf_op jit(solution)/shard_map/ppermute | solution.py:723
  10.0 2.0 %collective-permute-done.3.high_y = f32[4,4,8,128]{3,2,1,0:T(8,128)S(1)} collective-permute-done((f32[4,4,8,128]{3,2,1,0:T(8,128)S(1)}, f32[4,4,8,128]{3,2,1,0:T(8,128)S(1)}, u32[]{:S(2)}, u32[]{:S(2)}) %collective-permute-start.3) | collective-permute-done | bytes 65568 | tf_op jit(solution)/shard_map/ppermute | solution.py:723
  12.1 1.3 %shard_map.125 = (f32[136,128]{1,0:T(8,128)S(1)}, f32[8,128]{1,0:T(8,128)S(1)}, f32[2,128,128]{2,1,0:T(8,128)S(1)}) custom-call(f32[3,4,128,128]{3,2,1,0:T(8,128)} %flow.11, f32[4,128,128]{2,1,0:T(8,128)} %thermal.13, s32[4,128,128]{2,1,0:T(8,128)} %flag.5, f32[5,4,8,128]{3,2,1,0:T(8,128)S(1)} %collective-permute-done.2.low_y, ...), custom_call_target="tpu_custom_call" | custom-call | tf_op jit(solution)/shard_map/pallas_call | solution.py:738
  13.9 3.9 %collective-permute-start.5 = (f32[8,128]{1,0:T(8,128)S(1)}, f32[8,128]{1,0:T(8,128)S(1)}, u32[]{:S(2)}, u32[]{:S(2)}) collective-permute-start(f32[8,128]{1,0:T(8,128)S(1)} %get-tuple-element.34), channel_id=1, source_target_pairs={{0,12},{4,0},{8,4},{12,8},{1,13},{5,1},{9,5},{13,9},{2,14},{6,2},{... | collective-permute-start | bytes 12296 | tf_op jit(solution)/shard_map/ppermute | solution.py:723
  17.7 7.7 %collective-permute-done.1.high_x = f32[776,128]{1,0:T(8,128)S(1)} collective-permute-done((f32[776,128]{1,0:T(8,128)S(1)}, f32[776,128]{1,0:T(8,128)S(1)}, u32[]{:S(2)}, u32[]{:S(2)}) %collective-permute-start.1) | collective-permute-done | bytes 397344 | tf_op jit(solution)/shard_map/ppermute | solution.py:723
  25.4 1.1 %shard_map.124.star = f32[3,4,128,128]{3,2,1,0:T(8,128)S(1)} custom-call(f32[3,4,128,128]{3,2,1,0:T(8,128)S(1)} %copy-done, f32[776,128]{1,0:T(8,128)S(1)} %collective-permute-done.low_x, f32[776,128]{1,0:T(8,128)S(1)} %collective-permute-done.1.high_x, f32[4,128,128]{2,1,0:T(8,128)S(1)} %copy-done.1, s32[4,128,128]{2,1,0:T(8,128)S(1)} %copy-done.2, ...), custom_call_target="tpu_custom_call" | custom-call | flops 402653184 | bytes 1572864 | tf_op jit(solution)/shard_map/pallas_call | solution.py:30
  27.5 0.7 %shard_map.127 = (f32[4,128,128]{2,1,0:T(8,128)S(1)}, f32[256,128]{1,0:T(8,128)S(1)}) custom-call(f32[3,4,128,128]{3,2,1,0:T(8,128)S(1)} %copy-done, f32[776,128]{1,0:T(8,128)S(1)} %collective-permute-done.low_x, f32[4,128,128]{2,1,0:T(8,128)S(1)} %copy-done.1, f32[136,128]{1,0:T(8,128)S(1)} %collective-permute-done.4.extra, ...), custom_call_target="tpu_custom_call" | custom-call | flops 1048576 | bytes 786432 | tf_op jit(solution)/shard_map/pallas_call | solution.py:30
  28.2 0.6 %collective-permute-start.6 = (f32[256,128]{1,0:T(8,128)S(1)}, f32[256,128]{1,0:T(8,128)S(1)}, u32[]{:S(2)}, u32[]{:S(2)}) collective-permute-start(f32[256,128]{1,0:T(8,128)S(1)} %get-tuple-element.37.message), channel_id=1, source_target_pairs={{0,4},{1,5},{2,6},{3,7},{4,0},{5,1},{6,2},{7,3},{8,12},{9,13},{10,... | collective-permute-start | bytes 393224 | tf_op jit(solution)/shard_map/ppermute | solution.py:733
  29.5 1.3 %collective-permute-start.8 = (f32[40,128]{1,0:T(8,128)S(1)}, f32[40,128]{1,0:T(8,128)S(1)}, u32[]{:S(2)}, u32[]{:S(2)}) collective-permute-start(f32[40,128]{1,0:T(8,128)S(1)} %get-tuple-element.39.faces), channel_id=1, source_target_pairs={{0,4},{1,5},{2,6},{3,7},{4,0},{5,1},{6,2},{7,3},{8,12},{9,13},{10,... | collective-permute-start | bytes 61448 | tf_op jit(solution)/shard_map/ppermute | solution.py:733
  30.8 1.9 %collective-permute-start.14 = (f32[2,128,128]{2,1,0:T(8,128)S(1)}, f32[2,128,128]{2,1,0:T(8,128)S(1)}, u32[]{:S(2)}, u32[]{:S(2)}) collective-permute-start(f32[2,128,128]{2,1,0:T(8,128)S(1)} %get-tuple-element.44), channel_id=1, source_target_pairs={{0,12},{4,0},{8,4},{12,8},{1,13},{5,1},{9,5},{13,9},{2,14},{6,2},{... | collective-permute-start | bytes 393224 | tf_op jit(solution)/shard_map/ppermute | solution.py:723
  32.7 2.3 %collective-permute-done.8.other_faces = f32[40,128]{1,0:T(8,128)S(1)} collective-permute-done((f32[40,128]{1,0:T(8,128)S(1)}, f32[40,128]{1,0:T(8,128)S(1)}, u32[]{:S(2)}, u32[]{:S(2)}) %collective-permute-start.8) | collective-permute-done | bytes 20512 | tf_op jit(solution)/shard_map/ppermute | solution.py:733
  35.5 4.0 %collective-permute-start.10 = (f32[16,128]{1,0:T(8,128)S(1)}, f32[16,128]{1,0:T(8,128)S(1)}, u32[]{:S(2)}, u32[]{:S(2)}) collective-permute-start(f32[16,128]{1,0:T(8,128)S(1)} %get-tuple-element.42), channel_id=1, source_target_pairs={{0,1},{1,2},{2,3},{3,0},{4,5},{5,6},{6,7},{7,4},{8,9},{9,10},{10,1... | collective-permute-start | bytes 24584 | tf_op jit(solution)/shard_map/ppermute | solution.py:733
  39.6 2.0 %shard_map.130 = (f32[4,128,128]{2,1,0:T(8,128)}, f32[8,128]{1,0:T(8,128)S(1)}) custom-call(s32[8]{0:T(128)S(1)} %copy-done.8, s32[8]{0:T(128)S(1)} %copy-done.9, f32[4,128,128]{2,1,0:T(8,128)S(1)} %copy-done.1, f32[2,128,128]{2,1,0:T(8,128)S(1)} %collective-permute-done.7._.low_x, f32[2,128,128]{2,1,0:T(8,128)S(1)} %collective-permute-done.14.high_x, ...), custom_call_target="tpu_custom_call" | custom-call | flops 268435456 | bytes 532480 | tf_op jit(solution)/shard_map/pallas_call | solution.py:30
  41.6 1.5 %collective-permute-done.11.refs_5_ = f32[16,128]{1,0:T(8,128)S(1)} collective-permute-done((f32[16,128]{1,0:T(8,128)S(1)}, f32[16,128]{1,0:T(8,128)S(1)}, u32[]{:S(2)}, u32[]{:S(2)}) %collective-permute-start.11) | collective-permute-done | bytes 8224 | tf_op jit(solution)/shard_map/ppermute | solution.py:733
  43.6 0.5 %shard_map.131 = (f32[5,128,128]{2,1,0:T(8,128)S(1)}, f32[5,128,128]{2,1,0:T(8,128)S(1)}, f32[40,128]{1,0:T(8,128)S(1)}, f32[48,128]{1,0:T(8,128)S(1)}) custom-call(f32[4,128,128]{2,1,0:T(8,128)S(1)} %get-tuple-element.36.source.refs_0_, f32[280,128]{1,0:T(8,128)S(1)} %get-tuple-element.40.refs_1_, f32[280,128]{1,0:T(8,128)S(1)} %collective-permute-done.9.refs_2_, ...), custom_call_target="tpu_custom_call" | custom-call | flops 1048576 | bytes 1400832 | tf_op jit(solution)/shard_map/pallas_call | solution.py:30
  44.1 1.2 %collective-permute-start.17 = (f32[40,128]{1,0:T(8,128)S(1)}, f32[40,128]{1,0:T(8,128)S(1)}, u32[]{:S(2)}, u32[]{:S(2)}) collective-permute-start(f32[40,128]{1,0:T(8,128)S(1)} %get-tuple-element.51.refs_0_), channel_id=1, source_target_pairs={{0,3},{1,2},{2,1},{3,0},{4,7},{5,6},{6,5},{7,4},{8,11},{9,10},{10,... | collective-permute-start | bytes 61448 | tf_op jit(solution)/shard_map/ppermute | solution.py:905
  45.3 1.3 %collective-permute-start.16 = (f32[40,128]{1,0:T(8,128)S(1)}, f32[40,128]{1,0:T(8,128)S(1)}, u32[]{:S(2)}, u32[]{:S(2)}) collective-permute-start(f32[40,128]{1,0:T(8,128)S(1)} %get-tuple-element.51.refs_0_), channel_id=1, source_target_pairs={{0,2},{1,3},{2,0},{3,1},{4,6},{5,7},{6,4},{7,5},{8,10},{9,11},{10,... | collective-permute-start | bytes 61448 | tf_op jit(solution)/shard_map/ppermute | solution.py:905
  46.6 0.7 %shard_map.132 = (f32[5,128,128]{2,1,0:T(8,128)S(1)}, f32[5,128,128]{2,1,0:T(8,128)S(1)}) custom-call(f32[5,128,128]{2,1,0:T(8,128)S(1)} %get-tuple-element.46.precond, f32[5,128,128]{2,1,0:T(8,128)S(1)} %get-tuple-element.47.image, bf16[128,256]{1,0:T(8,128)(2,1)S(1)} %copy-done.5, bf16[256,256]{1,0:T(8,128)(2,1)S(1)} %copy-done.3), custom_call_target="tpu_custom_call" | custom-call | flops 1048576 | bytes 1310720 | tf_op jit(solution)/shard_map/pallas_call | solution.py:30
  47.4 1.7 %collective-permute-done.16.refs_2_ = f32[40,128]{1,0:T(8,128)S(1)} collective-permute-done((f32[40,128]{1,0:T(8,128)S(1)}, f32[40,128]{1,0:T(8,128)S(1)}, u32[]{:S(2)}, u32[]{:S(2)}) %collective-permute-start.16) | collective-permute-done | bytes 20512 | tf_op jit(solution)/shard_map/ppermute | solution.py:905
  49.1 1.3 %shard_map.133 = (f32[3,4,128,128]{3,2,1,0:T(8,128)}, f32[4,128,128]{2,1,0:T(8,128)}) custom-call(f32[3,4,128,128]{3,2,1,0:T(8,128)S(1)} %shard_map.124.star, f32[5,128,128]{2,1,0:T(8,128)S(1)} %get-tuple-element.48.precond, f32[5,128,128]{2,1,0:T(8,128)S(1)} %get-tuple-element.49.image, f32[48,128]{1,0:T(8,128)S(1)} %get-tuple-element.50.faces, ...), custom_call_target="tpu_custom_call" | custom-call | flops 1048576 | bytes 2097152 | tf_op jit(solution)/shard_map/pallas_call | solution.py:30
  (46 shorter events, 3.3 us)
Async XLA Ops:
  1.7 11.7 %copy-start.7 = (f32[128,128]{1,0:T(8,128)S(1)}, f32[128,128]{1,0:T(8,128)}, u32[]{:S(2)}) copy-start(f32[128,128]{1,0:T(8,128)} %constant.16.clone.diagonal) | copy-start | bytes 196612
  1.7 23.6 %copy-start = (f32[3,4,128,128]{3,2,1,0:T(8,128)S(1)}, f32[3,4,128,128]{3,2,1,0:T(8,128)}, u32[]{:S(2)}) copy-start(f32[3,4,128,128]{3,2,1,0:T(8,128)} %flow.11) | copy-start | bytes 2359300
  1.8 23.6 %copy-start.1 = (f32[4,128,128]{2,1,0:T(8,128)S(1)}, f32[4,128,128]{2,1,0:T(8,128)}, u32[]{:S(2)}) copy-start(f32[4,128,128]{2,1,0:T(8,128)} %thermal.13) | copy-start | bytes 786436
  1.8 23.6 %copy-start.2 = (s32[4,128,128]{2,1,0:T(8,128)S(1)}, s32[4,128,128]{2,1,0:T(8,128)}, u32[]{:S(2)}) copy-start(s32[4,128,128]{2,1,0:T(8,128)} %flag.5) | copy-start | bytes 786436
  1.8 16.0 %collective-permute-start = (f32[776,128]{1,0:T(8,128)S(1)}, f32[776,128]{1,0:T(8,128)S(1)}, u32[]{:S(2)}, u32[]{:S(2)}) collective-permute-start(f32[776,128]{1,0:T(8,128)S(1)} %shard_map.121), channel_id=1, source_target_pairs={{0,4},{4,8},{8,12},{12,0},{1,5},{5,9},{9,13},{13,1},{2,6},{6,10},{... | collective-permute-start | bytes 1191944 | tf_op jit(solution)/shard_map/ppermute | solution.py:723
  6.0 19.4 %collective-permute-start.1 = (f32[776,128]{1,0:T(8,128)S(1)}, f32[776,128]{1,0:T(8,128)S(1)}, u32[]{:S(2)}, u32[]{:S(2)}) collective-permute-start(f32[776,128]{1,0:T(8,128)S(1)} %get-tuple-element.29), channel_id=1, source_target_pairs={{0,12},{4,0},{8,4},{12,8},{1,13},{5,1},{9,5},{13,9},{2,14},{6,2},{... | collective-permute-start | bytes 1191944 | tf_op jit(solution)/shard_map/ppermute | solution.py:723
  8.2 3.9 %collective-permute-start.2 = (f32[5,4,8,128]{3,2,1,0:T(8,128)S(1)}, f32[5,4,8,128]{3,2,1,0:T(8,128)S(1)}, u32[]{:S(2)}, u32[]{:S(2)}) collective-permute-start(f32[5,4,8,128]{3,2,1,0:T(8,128)S(1)} %get-tuple-element.30), channel_id=1, source_target_pairs={{0,1},{1,2},{2,3},{3,0},{4,5},{5,6},{6,7},{7,4},{8,9},{9,10},{10,1... | collective-permute-start | bytes 245768 | tf_op jit(solution)/shard_map/ppermute | solution.py:723
  8.2 3.8 %collective-permute-start.3 = (f32[4,4,8,128]{3,2,1,0:T(8,128)S(1)}, f32[4,4,8,128]{3,2,1,0:T(8,128)S(1)}, u32[]{:S(2)}, u32[]{:S(2)}) collective-permute-start(f32[4,4,8,128]{3,2,1,0:T(8,128)S(1)} %get-tuple-element.31), channel_id=1, source_target_pairs={{0,3},{1,0},{2,1},{3,2},{4,7},{5,4},{6,5},{7,6},{8,11},{9,8},{10,9... | collective-permute-start | bytes 196616 | tf_op jit(solution)/shard_map/ppermute | solution.py:723
  13.4 13.8 %collective-permute-start.4 = (f32[136,128]{1,0:T(8,128)S(1)}, f32[136,128]{1,0:T(8,128)S(1)}, u32[]{:S(2)}, u32[]{:S(2)}) collective-permute-start(f32[136,128]{1,0:T(8,128)S(1)} %get-tuple-element.33), channel_id=1, source_target_pairs={{0,4},{4,8},{8,12},{12,0},{1,5},{5,9},{9,13},{13,1},{2,6},{6,10},{... | collective-permute-start | bytes 208904 | tf_op jit(solution)/shard_map/ppermute | solution.py:723
  13.9 13.3 %collective-permute-start.5 = (f32[8,128]{1,0:T(8,128)S(1)}, f32[8,128]{1,0:T(8,128)S(1)}, u32[]{:S(2)}, u32[]{:S(2)}) collective-permute-start(f32[8,128]{1,0:T(8,128)S(1)} %get-tuple-element.34), channel_id=1, source_target_pairs={{0,12},{4,0},{8,4},{12,8},{1,13},{5,1},{9,5},{13,9},{2,14},{6,2},{... | collective-permute-start | bytes 12296 | tf_op jit(solution)/shard_map/ppermute | solution.py:723
  17.7 11.3 %collective-permute-start.7 = (f32[2,128,128]{2,1,0:T(8,128)S(1)}, f32[2,128,128]{2,1,0:T(8,128)S(1)}, u32[]{:S(2)}, u32[]{:S(2)}) collective-permute-start(f32[2,128,128]{2,1,0:T(8,128)S(1)} %get-tuple-element.38), channel_id=1, source_target_pairs={{0,4},{4,8},{8,12},{12,0},{1,5},{5,9},{9,13},{13,1},{2,6},{6,10},{... | collective-permute-start | bytes 393224 | tf_op jit(solution)/shard_map/ppermute | solution.py:723
  28.2 6.9 %collective-permute-start.6 = (f32[256,128]{1,0:T(8,128)S(1)}, f32[256,128]{1,0:T(8,128)S(1)}, u32[]{:S(2)}, u32[]{:S(2)}) collective-permute-start(f32[256,128]{1,0:T(8,128)S(1)} %get-tuple-element.37.message), channel_id=1, source_target_pairs={{0,4},{1,5},{2,6},{3,7},{4,0},{5,1},{6,2},{7,3},{8,12},{9,13},{10,... | collective-permute-start | bytes 393224 | tf_op jit(solution)/shard_map/ppermute | solution.py:733
  29.5 10.1 %copy-start.8 = (s32[8]{0:T(128)S(1)}, s32[8]{0:T(128)}, u32[]{:S(2)}) copy-start(s32[8]{0:T(128)} %spots_a.1) | copy-start | bytes 100
  29.5 10.1 %copy-start.9 = (s32[8]{0:T(128)S(1)}, s32[8]{0:T(128)}, u32[]{:S(2)}) copy-start(s32[8]{0:T(128)} %spots_b.1) | copy-start | bytes 100
  29.5 5.5 %collective-permute-start.8 = (f32[40,128]{1,0:T(8,128)S(1)}, f32[40,128]{1,0:T(8,128)S(1)}, u32[]{:S(2)}, u32[]{:S(2)}) collective-permute-start(f32[40,128]{1,0:T(8,128)S(1)} %get-tuple-element.39.faces), channel_id=1, source_target_pairs={{0,4},{1,5},{2,6},{3,7},{4,0},{5,1},{6,2},{7,3},{8,12},{9,13},{10,... | collective-permute-start | bytes 61448 | tf_op jit(solution)/shard_map/ppermute | solution.py:733
  30.8 8.6 %collective-permute-start.14 = (f32[2,128,128]{2,1,0:T(8,128)S(1)}, f32[2,128,128]{2,1,0:T(8,128)S(1)}, u32[]{:S(2)}, u32[]{:S(2)}) collective-permute-start(f32[2,128,128]{2,1,0:T(8,128)S(1)} %get-tuple-element.44), channel_id=1, source_target_pairs={{0,12},{4,0},{8,4},{12,8},{1,13},{5,1},{9,5},{13,9},{2,14},{6,2},{... | collective-permute-start | bytes 393224 | tf_op jit(solution)/shard_map/ppermute | solution.py:723
  35.2 8.3 %collective-permute-start.9 = (f32[280,128]{1,0:T(8,128)S(1)}, f32[280,128]{1,0:T(8,128)S(1)}, u32[]{:S(2)}, u32[]{:S(2)}) collective-permute-start(f32[280,128]{1,0:T(8,128)S(1)} %get-tuple-element.40.refs_1_), channel_id=1, source_target_pairs={{0,8},{1,9},{2,10},{3,11},{4,12},{5,13},{6,14},{7,15},{8,0},{9,1},... | collective-permute-start | bytes 430088 | tf_op jit(solution)/shard_map/ppermute | solution.py:733
  35.4 7.7 %collective-permute-start.11 = (f32[16,128]{1,0:T(8,128)S(1)}, f32[16,128]{1,0:T(8,128)S(1)}, u32[]{:S(2)}, u32[]{:S(2)}) collective-permute-start(f32[16,128]{1,0:T(8,128)S(1)} %get-tuple-element.42), channel_id=1, source_target_pairs={{0,9},{1,10},{2,11},{3,8},{4,13},{5,14},{6,15},{7,12},{8,1},{9,2},... | collective-permute-start | bytes 24584 | tf_op jit(solution)/shard_map/ppermute | solution.py:733
  35.5 7.6 %collective-permute-start.10 = (f32[16,128]{1,0:T(8,128)S(1)}, f32[16,128]{1,0:T(8,128)S(1)}, u32[]{:S(2)}, u32[]{:S(2)}) collective-permute-start(f32[16,128]{1,0:T(8,128)S(1)} %get-tuple-element.42), channel_id=1, source_target_pairs={{0,1},{1,2},{2,3},{3,0},{4,5},{5,6},{6,7},{7,4},{8,9},{9,10},{10,1... | collective-permute-start | bytes 24584 | tf_op jit(solution)/shard_map/ppermute | solution.py:733
  39.4 4.1 %collective-permute-start.13 = (f32[16,128]{1,0:T(8,128)S(1)}, f32[16,128]{1,0:T(8,128)S(1)}, u32[]{:S(2)}, u32[]{:S(2)}) collective-permute-start(f32[16,128]{1,0:T(8,128)S(1)} %get-tuple-element.43), channel_id=1, source_target_pairs={{0,11},{1,8},{2,9},{3,10},{4,15},{5,12},{6,13},{7,14},{8,3},{9,0},... | collective-permute-start | bytes 24584 | tf_op jit(solution)/shard_map/ppermute | solution.py:733
  39.4 4.1 %collective-permute-start.12 = (f32[16,128]{1,0:T(8,128)S(1)}, f32[16,128]{1,0:T(8,128)S(1)}, u32[]{:S(2)}, u32[]{:S(2)}) collective-permute-start(f32[16,128]{1,0:T(8,128)S(1)} %get-tuple-element.43), channel_id=1, source_target_pairs={{0,3},{1,0},{2,1},{3,2},{4,7},{5,4},{6,5},{7,6},{8,11},{9,8},{10,9... | collective-permute-start | bytes 24584 | tf_op jit(solution)/shard_map/ppermute | solution.py:733
  44.1 3.3 %collective-permute-start.17 = (f32[40,128]{1,0:T(8,128)S(1)}, f32[40,128]{1,0:T(8,128)S(1)}, u32[]{:S(2)}, u32[]{:S(2)}) collective-permute-start(f32[40,128]{1,0:T(8,128)S(1)} %get-tuple-element.51.refs_0_), channel_id=1, source_target_pairs={{0,3},{1,2},{2,1},{3,0},{4,7},{5,6},{6,5},{7,4},{8,11},{9,10},{10,... | collective-permute-start | bytes 61448 | tf_op jit(solution)/shard_map/ppermute | solution.py:905
  45.3 3.8 %collective-permute-start.16 = (f32[40,128]{1,0:T(8,128)S(1)}, f32[40,128]{1,0:T(8,128)S(1)}, u32[]{:S(2)}, u32[]{:S(2)}) collective-permute-start(f32[40,128]{1,0:T(8,128)S(1)} %get-tuple-element.51.refs_0_), channel_id=1, source_target_pairs={{0,2},{1,3},{2,0},{3,1},{4,6},{5,7},{6,4},{7,5},{8,10},{9,11},{10,... | collective-permute-start | bytes 61448 | tf_op jit(solution)/shard_map/ppermute | solution.py:905
  46.6 2.5 %collective-permute-start.15 = (f32[40,128]{1,0:T(8,128)S(1)}, f32[40,128]{1,0:T(8,128)S(1)}, u32[]{:S(2)}, u32[]{:S(2)}) collective-permute-start(f32[40,128]{1,0:T(8,128)S(1)} %get-tuple-element.51.refs_0_), channel_id=1, source_target_pairs={{0,1},{1,0},{2,3},{3,2},{4,5},{5,4},{6,7},{7,6},{8,9},{9,8},{10,11... | collective-permute-start | bytes 61448 | tf_op jit(solution)/shard_map/ppermute | solution.py:905
  (4 other events, 4.1 us)

commit v14 on v12

--- a/solution.py
+++ b/solution.py
@@ -876,10 +876,11 @@
         numbers = report[2 * length :].at[3].set(2.0 * crossing)
         numbers = lax.psum(jnp.where(at_end, numbers, 0.0), "gx")
         report = report.at[2 * length :].set(numbers)
-    reports = [report]
-    for by in range(1, count_y):
+    reports = {0: report}
+    for by in sorted(range(1, count_y), key=lambda by: (by == 2, by)):
         pairs = [(i, i ^ by if count_y == 4 else (i + by) % count_y) for i in range(count_y)]
-        reports.append(lax.ppermute(report, "gy", pairs))
+        reports[by] = lax.ppermute(report, "gy", pairs)
+    reports = [reports[by] for by in range(count_y)]
     precond, image = call(
         physical_kernel,
         [precond, image, left, right],

time: 50.2 us -> 50.2 us (level)
  no operation moved by 1% of the time
where the time goes in v14:
time: 50.2 us; the launch traced here: 50 us
  starting transfers between devices  23 us (46%)
  waiting for transfers between devices  15.5 us (31%)
  Pallas kernels  10.6 us (21%)
  between operations  0.84 us (2%)
    ppermute x8, starting transfers between devices, along(): lax.ppermute(array, axis, [(i, (i + by) % length) for i in range(length)])  13.3 us
    ppermute x8, waiting for transfers between devices, along(): lax.ppermute(array, axis, [(i, (i + by) % length) for i in range(length)])  11.1 us
    pallas_call x10, Pallas kernels, call(): pl.pallas_call(body, out_shape=out_shape, in_specs=[SMEM] * scalars + [VM...  7.78 us
    ppermute x7, starting transfers between devices, swapped(): return lax.ppermute(array, ('gx', 'gy'), pairs)  7.14 us
    pallas_call x2, Pallas kernels, pack(): pl.pallas_call(body, out_shape=[jax.ShapeDtypeStruct(shape, F32) for shap...  2.78 us
    ppermute x3, starting transfers between devices, per_device(): reports[by] = lax.ppermute(report, 'gy', pairs)  2.65 us
    ppermute x7, waiting for transfers between devices, swapped(): return lax.ppermute(array, ('gx', 'gy'), pairs)  2.6 us
    ppermute x3, waiting for transfers between devices, per_device(): reports[by] = lax.ppermute(report, 'gy', pairs)  1.8 us
  transfers between devices with their start and end apart: 18, of which 9 were waited for; matrix products, arithmetic and copies ran while one was open for 0% of the time, Pallas kernels for 15%

profile of v14, /device:TPU:0, one launch (start us, length us, event | category | flops | bytes accessed | tf_op | source)
XLA Modules:
  0.0 50.0 jit_solution(5658627834642184489)
XLA Ops:
  0.7 1.5 %shard_map.121 = (f32[776,128]{1,0:T(8,128)S(1)}, f32[776,128]{1,0:T(8,128)S(1)}, f32[5,4,8,128]{3,2,1,0:T(8,128)S(1)}, f32[4,4,8,128]{3,2,1,0:T(8,128)S(1)}) custom-call(f32[3,4,128,128]{3,2,1,0:T(8,128)} %flow.9, f32[4,128,128]{2,1,0:T(8,128)} %thermal.11, s32[4,128,128]{2,1,0:T(8,128)} %flag.5), custom_call_target="tpu_custom_call" | custom-call | tf_op jit(solution)/shard_map/pallas_call | solution.py:723
  2.2 3.1 %collective-permute-start = (f32[776,128]{1,0:T(8,128)S(1)}, f32[776,128]{1,0:T(8,128)S(1)}, u32[]{:S(2)}, u32[]{:S(2)}) collective-permute-start(f32[776,128]{1,0:T(8,128)S(1)} %get-tuple-element.30), channel_id=1, source_target_pairs={{0,4},{4,8},{8,12},{12,0},{1,5},{5,9},{9,13},{13,1},{2,6},{6,10},{... | collective-permute-start | bytes 1191944 | tf_op jit(solution)/shard_map/ppermute | solution.py:708
  5.2 2.1 %collective-permute-start.1 = (f32[776,128]{1,0:T(8,128)S(1)}, f32[776,128]{1,0:T(8,128)S(1)}, u32[]{:S(2)}, u32[]{:S(2)}) collective-permute-start(f32[776,128]{1,0:T(8,128)S(1)} %get-tuple-element.31), channel_id=1, source_target_pairs={{0,12},{4,0},{8,4},{12,8},{1,13},{5,1},{9,5},{13,9},{2,14},{6,2},{... | collective-permute-start | bytes 1191944 | tf_op jit(solution)/shard_map/ppermute | solution.py:708
  7.3 1.7 %collective-permute-start.3 = (f32[4,4,8,128]{3,2,1,0:T(8,128)S(1)}, f32[4,4,8,128]{3,2,1,0:T(8,128)S(1)}, u32[]{:S(2)}, u32[]{:S(2)}) collective-permute-start(f32[4,4,8,128]{3,2,1,0:T(8,128)S(1)} %get-tuple-element.33), channel_id=1, source_target_pairs={{0,3},{1,0},{2,1},{3,2},{4,7},{5,4},{6,5},{7,6},{8,11},{9,8},{10,9... | collective-permute-start | bytes 196616 | tf_op jit(solution)/shard_map/ppermute | solution.py:708
  9.1 2.0 %collective-permute-done.3.high_y = f32[4,4,8,128]{3,2,1,0:T(8,128)S(1)} collective-permute-done((f32[4,4,8,128]{3,2,1,0:T(8,128)S(1)}, f32[4,4,8,128]{3,2,1,0:T(8,128)S(1)}, u32[]{:S(2)}, u32[]{:S(2)}) %collective-permute-start.3) | collective-permute-done | bytes 65568 | tf_op jit(solution)/shard_map/ppermute | solution.py:708
  11.2 1.3 %shard_map.124 = (f32[136,128]{1,0:T(8,128)S(1)}, f32[8,128]{1,0:T(8,128)S(1)}, f32[2,128,128]{2,1,0:T(8,128)S(1)}) custom-call(f32[3,4,128,128]{3,2,1,0:T(8,128)} %flow.9, f32[4,128,128]{2,1,0:T(8,128)} %thermal.11, s32[4,128,128]{2,1,0:T(8,128)} %flag.5, f32[5,4,8,128]{3,2,1,0:T(8,128)S(1)} %collective-permute-done.2.low_y, ...), custom_call_target="tpu_custom_call" | custom-call | tf_op jit(solution)/shard_map/pallas_call | solution.py:723
  13.0 3.9 %collective-permute-start.5 = (f32[8,128]{1,0:T(8,128)S(1)}, f32[8,128]{1,0:T(8,128)S(1)}, u32[]{:S(2)}, u32[]{:S(2)}) collective-permute-start(f32[8,128]{1,0:T(8,128)S(1)} %get-tuple-element.36), channel_id=1, source_target_pairs={{0,12},{4,0},{8,4},{12,8},{1,13},{5,1},{9,5},{13,9},{2,14},{6,2},{... | collective-permute-start | bytes 12296 | tf_op jit(solution)/shard_map/ppermute | solution.py:708
  17.3 7.4 %collective-permute-done.1.high_x = f32[776,128]{1,0:T(8,128)S(1)} collective-permute-done((f32[776,128]{1,0:T(8,128)S(1)}, f32[776,128]{1,0:T(8,128)S(1)}, u32[]{:S(2)}, u32[]{:S(2)}) %collective-permute-start.1) | collective-permute-done | bytes 397344 | tf_op jit(solution)/shard_map/ppermute | solution.py:708
  24.8 1.1 %shard_map.123.star = f32[3,4,128,128]{3,2,1,0:T(8,128)S(1)} custom-call(f32[3,4,128,128]{3,2,1,0:T(8,128)S(1)} %copy-done, f32[776,128]{1,0:T(8,128)S(1)} %collective-permute-done.low_x, f32[776,128]{1,0:T(8,128)S(1)} %collective-permute-done.1.high_x, f32[4,128,128]{2,1,0:T(8,128)S(1)} %copy-done.1, s32[4,128,128]{2,1,0:T(8,128)S(1)} %copy-done.2, ...), custom_call_target="tpu_custom_call" | custom-call | flops 402653184 | bytes 1572864 | tf_op jit(solution)/shard_map/pallas_call | solution.py:30
  26.5 0.9 %collective-permute-done.4.extra = f32[136,128]{1,0:T(8,128)S(1)} collective-permute-done((f32[136,128]{1,0:T(8,128)S(1)}, f32[136,128]{1,0:T(8,128)S(1)}, u32[]{:S(2)}, u32[]{:S(2)}) %collective-permute-start.4) | collective-permute-done | bytes 69664 | tf_op jit(solution)/shard_map/ppermute | solution.py:708
  27.3 0.7 %shard_map.126 = (f32[4,128,128]{2,1,0:T(8,128)S(1)}, f32[256,128]{1,0:T(8,128)S(1)}) custom-call(f32[3,4,128,128]{3,2,1,0:T(8,128)S(1)} %copy-done, f32[776,128]{1,0:T(8,128)S(1)} %collective-permute-done.low_x, f32[4,128,128]{2,1,0:T(8,128)S(1)} %copy-done.1, f32[136,128]{1,0:T(8,128)S(1)} %collective-permute-done.4.extra, ...), custom_call_target="tpu_custom_call" | custom-call | flops 1048576 | bytes 786432 | tf_op jit(solution)/shard_map/pallas_call | solution.py:30
  28.0 1.1 %collective-permute-start.6 = (f32[256,128]{1,0:T(8,128)S(1)}, f32[256,128]{1,0:T(8,128)S(1)}, u32[]{:S(2)}, u32[]{:S(2)}) collective-permute-start(f32[256,128]{1,0:T(8,128)S(1)} %get-tuple-element.39.message), channel_id=1, source_target_pairs={{0,4},{1,5},{2,6},{3,7},{4,0},{5,1},{6,2},{7,3},{8,12},{9,13},{10,... | collective-permute-start | bytes 393224 | tf_op jit(solution)/shard_map/ppermute | solution.py:718
  29.9 0.8 %collective-permute-start.8 = (f32[40,128]{1,0:T(8,128)S(1)}, f32[40,128]{1,0:T(8,128)S(1)}, u32[]{:S(2)}, u32[]{:S(2)}) collective-permute-start(f32[40,128]{1,0:T(8,128)S(1)} %get-tuple-element.41.faces), channel_id=1, source_target_pairs={{0,4},{1,5},{2,6},{3,7},{4,0},{5,1},{6,2},{7,3},{8,12},{9,13},{10,... | collective-permute-start | bytes 61448 | tf_op jit(solution)/shard_map/ppermute | solution.py:718
  30.7 2.4 %collective-permute-start.14 = (f32[2,128,128]{2,1,0:T(8,128)S(1)}, f32[2,128,128]{2,1,0:T(8,128)S(1)}, u32[]{:S(2)}, u32[]{:S(2)}) collective-permute-start(f32[2,128,128]{2,1,0:T(8,128)S(1)} %get-tuple-element.46), channel_id=1, source_target_pairs={{0,12},{4,0},{8,4},{12,8},{1,13},{5,1},{9,5},{13,9},{2,14},{6,2},{... | collective-permute-start | bytes 393224 | tf_op jit(solution)/shard_map/ppermute | solution.py:708
  33.1 1.5 %collective-permute-done.8.other_faces = f32[40,128]{1,0:T(8,128)S(1)} collective-permute-done((f32[40,128]{1,0:T(8,128)S(1)}, f32[40,128]{1,0:T(8,128)S(1)}, u32[]{:S(2)}, u32[]{:S(2)}) %collective-permute-start.8) | collective-permute-done | bytes 20512 | tf_op jit(solution)/shard_map/ppermute | solution.py:718
  34.8 1.0 %collective-permute-start.9 = (f32[280,128]{1,0:T(8,128)S(1)}, f32[280,128]{1,0:T(8,128)S(1)}, u32[]{:S(2)}, u32[]{:S(2)}) collective-permute-start(f32[280,128]{1,0:T(8,128)S(1)} %get-tuple-element.42.refs_1_), channel_id=1, source_target_pairs={{0,8},{1,9},{2,10},{3,11},{4,12},{5,13},{6,14},{7,15},{8,0},{9,1},... | collective-permute-start | bytes 430088 | tf_op jit(solution)/shard_map/ppermute | solution.py:718
  35.8 3.3 %collective-permute-start.10 = (f32[16,128]{1,0:T(8,128)S(1)}, f32[16,128]{1,0:T(8,128)S(1)}, u32[]{:S(2)}, u32[]{:S(2)}) collective-permute-start(f32[16,128]{1,0:T(8,128)S(1)} %get-tuple-element.44), channel_id=1, source_target_pairs={{0,1},{1,2},{2,3},{3,0},{4,5},{5,6},{6,7},{7,4},{8,9},{9,10},{10,1... | collective-permute-start | bytes 24584 | tf_op jit(solution)/shard_map/ppermute | solution.py:718
  39.3 0.7 %collective-permute-start.12 = (f32[16,128]{1,0:T(8,128)S(1)}, f32[16,128]{1,0:T(8,128)S(1)}, u32[]{:S(2)}, u32[]{:S(2)}) collective-permute-start(f32[16,128]{1,0:T(8,128)S(1)} %get-tuple-element.45), channel_id=1, source_target_pairs={{0,3},{1,0},{2,1},{3,2},{4,7},{5,4},{6,5},{7,6},{8,11},{9,8},{10,9... | collective-permute-start | bytes 24584 | tf_op jit(solution)/shard_map/ppermute | solution.py:718
  40.0 2.0 %shard_map.129 = (f32[4,128,128]{2,1,0:T(8,128)}, f32[8,128]{1,0:T(8,128)S(1)}) custom-call(s32[8]{0:T(128)S(1)} %copy-done.8, s32[8]{0:T(128)S(1)} %copy-done.9, f32[4,128,128]{2,1,0:T(8,128)S(1)} %copy-done.1, f32[2,128,128]{2,1,0:T(8,128)S(1)} %collective-permute-done.7._.low_x, f32[2,128,128]{2,1,0:T(8,128)S(1)} %collective-permute-done.14.high_x, ...), custom_call_target="tpu_custom_call" | custom-call | flops 268435456 | bytes 532480 | tf_op jit(solution)/shard_map/pallas_call | solution.py:30
  42.0 1.1 %collective-permute-done.13.refs_7_ = f32[16,128]{1,0:T(8,128)S(1)} collective-permute-done((f32[16,128]{1,0:T(8,128)S(1)}, f32[16,128]{1,0:T(8,128)S(1)}, u32[]{:S(2)}, u32[]{:S(2)}) %collective-permute-start.13) | collective-permute-done | bytes 8224 | tf_op jit(solution)/shard_map/ppermute | solution.py:718
  43.6 1.3 %collective-permute-start.17 = (f32[40,128]{1,0:T(8,128)S(1)}, f32[40,128]{1,0:T(8,128)S(1)}, u32[]{:S(2)}, u32[]{:S(2)}) collective-permute-start(f32[40,128]{1,0:T(8,128)S(1)} %get-tuple-element.53.refs_0_), channel_id=1, source_target_pairs={{0,3},{1,2},{2,1},{3,0},{4,7},{5,6},{6,5},{7,4},{8,11},{9,10},{10,... | collective-permute-start | bytes 61448 | tf_op jit(solution)/shard_map/ppermute | solution.py:882
  45.0 1.3 %collective-permute-start.16 = (f32[40,128]{1,0:T(8,128)S(1)}, f32[40,128]{1,0:T(8,128)S(1)}, u32[]{:S(2)}, u32[]{:S(2)}) collective-permute-start(f32[40,128]{1,0:T(8,128)S(1)} %get-tuple-element.53.refs_0_), channel_id=1, source_target_pairs={{0,2},{1,3},{2,0},{3,1},{4,6},{5,7},{6,4},{7,5},{8,10},{9,11},{10,... | collective-permute-start | bytes 61448 | tf_op jit(solution)/shard_map/ppermute | solution.py:882
  47.0 1.8 %collective-permute-done.16.refs_2_ = f32[40,128]{1,0:T(8,128)S(1)} collective-permute-done((f32[40,128]{1,0:T(8,128)S(1)}, f32[40,128]{1,0:T(8,128)S(1)}, u32[]{:S(2)}, u32[]{:S(2)}) %collective-permute-start.16) | collective-permute-done | bytes 20512 | tf_op jit(solution)/shard_map/ppermute | solution.py:882
  48.8 1.3 %shard_map.132 = (f32[3,4,128,128]{3,2,1,0:T(8,128)}, f32[4,128,128]{2,1,0:T(8,128)}) custom-call(f32[3,4,128,128]{3,2,1,0:T(8,128)S(1)} %shard_map.123.star, f32[5,128,128]{2,1,0:T(8,128)S(1)} %get-tuple-element.50.precond, f32[5,128,128]{2,1,0:T(8,128)S(1)} %get-tuple-element.51.image, f32[48,128]{1,0:T(8,128)S(1)} %get-tuple-element.52.faces, ...), custom_call_target="tpu_custom_call" | custom-call | flops 1048576 | bytes 2097152 | tf_op jit(solution)/shard_map/pallas_call | solution.py:30
  (45 shorter events, 4.0 us)
Async XLA Ops:
  0.6 11.9 %copy-start.7 = (f32[128,128]{1,0:T(8,128)S(1)}, f32[128,128]{1,0:T(8,128)}, u32[]{:S(2)}) copy-start(f32[128,128]{1,0:T(8,128)} %constant.16.clone.diagonal) | copy-start | bytes 196612
  0.6 24.1 %copy-start.1 = (f32[4,128,128]{2,1,0:T(8,128)S(1)}, f32[4,128,128]{2,1,0:T(8,128)}, u32[]{:S(2)}) copy-start(f32[4,128,128]{2,1,0:T(8,128)} %thermal.11) | copy-start | bytes 786436
  0.7 24.1 %copy-start = (f32[3,4,128,128]{3,2,1,0:T(8,128)S(1)}, f32[3,4,128,128]{3,2,1,0:T(8,128)}, u32[]{:S(2)}) copy-start(f32[3,4,128,128]{3,2,1,0:T(8,128)} %flow.9) | copy-start | bytes 2359300
  0.7 24.1 %copy-start.2 = (s32[4,128,128]{2,1,0:T(8,128)S(1)}, s32[4,128,128]{2,1,0:T(8,128)}, u32[]{:S(2)}) copy-start(s32[4,128,128]{2,1,0:T(8,128)} %flag.5) | copy-start | bytes 786436
  2.2 15.2 %collective-permute-start = (f32[776,128]{1,0:T(8,128)S(1)}, f32[776,128]{1,0:T(8,128)S(1)}, u32[]{:S(2)}, u32[]{:S(2)}) collective-permute-start(f32[776,128]{1,0:T(8,128)S(1)} %get-tuple-element.30), channel_id=1, source_target_pairs={{0,4},{4,8},{8,12},{12,0},{1,5},{5,9},{9,13},{13,1},{2,6},{6,10},{... | collective-permute-start | bytes 1191944 | tf_op jit(solution)/shard_map/ppermute | solution.py:708
  5.2 19.5 %collective-permute-start.1 = (f32[776,128]{1,0:T(8,128)S(1)}, f32[776,128]{1,0:T(8,128)S(1)}, u32[]{:S(2)}, u32[]{:S(2)}) collective-permute-start(f32[776,128]{1,0:T(8,128)S(1)} %get-tuple-element.31), channel_id=1, source_target_pairs={{0,12},{4,0},{8,4},{12,8},{1,13},{5,1},{9,5},{13,9},{2,14},{6,2},{... | collective-permute-start | bytes 1191944 | tf_op jit(solution)/shard_map/ppermute | solution.py:708
  7.3 3.9 %collective-permute-start.2 = (f32[5,4,8,128]{3,2,1,0:T(8,128)S(1)}, f32[5,4,8,128]{3,2,1,0:T(8,128)S(1)}, u32[]{:S(2)}, u32[]{:S(2)}) collective-permute-start(f32[5,4,8,128]{3,2,1,0:T(8,128)S(1)} %get-tuple-element.32), channel_id=1, source_target_pairs={{0,1},{1,2},{2,3},{3,0},{4,5},{5,6},{6,7},{7,4},{8,9},{9,10},{10,1... | collective-permute-start | bytes 245768 | tf_op jit(solution)/shard_map/ppermute | solution.py:708
  7.3 3.7 %collective-permute-start.3 = (f32[4,4,8,128]{3,2,1,0:T(8,128)S(1)}, f32[4,4,8,128]{3,2,1,0:T(8,128)S(1)}, u32[]{:S(2)}, u32[]{:S(2)}) collective-permute-start(f32[4,4,8,128]{3,2,1,0:T(8,128)S(1)} %get-tuple-element.33), channel_id=1, source_target_pairs={{0,3},{1,0},{2,1},{3,2},{4,7},{5,4},{6,5},{7,6},{8,11},{9,8},{10,9... | collective-permute-start | bytes 196616 | tf_op jit(solution)/shard_map/ppermute | solution.py:708
  12.5 14.8 %collective-permute-start.4 = (f32[136,128]{1,0:T(8,128)S(1)}, f32[136,128]{1,0:T(8,128)S(1)}, u32[]{:S(2)}, u32[]{:S(2)}) collective-permute-start(f32[136,128]{1,0:T(8,128)S(1)} %get-tuple-element.35), channel_id=1, source_target_pairs={{0,4},{4,8},{8,12},{12,0},{1,5},{5,9},{9,13},{13,1},{2,6},{6,10},{... | collective-permute-start | bytes 208904 | tf_op jit(solution)/shard_map/ppermute | solution.py:708
  13.0 13.5 %collective-permute-start.5 = (f32[8,128]{1,0:T(8,128)S(1)}, f32[8,128]{1,0:T(8,128)S(1)}, u32[]{:S(2)}, u32[]{:S(2)}) collective-permute-start(f32[8,128]{1,0:T(8,128)S(1)} %get-tuple-element.36), channel_id=1, source_target_pairs={{0,12},{4,0},{8,4},{12,8},{1,13},{5,1},{9,5},{13,9},{2,14},{6,2},{... | collective-permute-start | bytes 12296 | tf_op jit(solution)/shard_map/ppermute | solution.py:708
  16.8 12.6 %collective-permute-start.7 = (f32[2,128,128]{2,1,0:T(8,128)S(1)}, f32[2,128,128]{2,1,0:T(8,128)S(1)}, u32[]{:S(2)}, u32[]{:S(2)}) collective-permute-start(f32[2,128,128]{2,1,0:T(8,128)S(1)} %get-tuple-element.40), channel_id=1, source_target_pairs={{0,4},{4,8},{8,12},{12,0},{1,5},{5,9},{9,13},{13,1},{2,6},{6,10},{... | collective-permute-start | bytes 393224 | tf_op jit(solution)/shard_map/ppermute | solution.py:708
  28.0 6.6 %collective-permute-start.6 = (f32[256,128]{1,0:T(8,128)S(1)}, f32[256,128]{1,0:T(8,128)S(1)}, u32[]{:S(2)}, u32[]{:S(2)}) collective-permute-start(f32[256,128]{1,0:T(8,128)S(1)} %get-tuple-element.39.message), channel_id=1, source_target_pairs={{0,4},{1,5},{2,6},{3,7},{4,0},{5,1},{6,2},{7,3},{8,12},{9,13},{10,... | collective-permute-start | bytes 393224 | tf_op jit(solution)/shard_map/ppermute | solution.py:718
  29.9 10.2 %copy-start.8 = (s32[8]{0:T(128)S(1)}, s32[8]{0:T(128)}, u32[]{:S(2)}) copy-start(s32[8]{0:T(128)} %spots_a.1) | copy-start | bytes 100
  29.9 10.2 %copy-start.9 = (s32[8]{0:T(128)S(1)}, s32[8]{0:T(128)}, u32[]{:S(2)}) copy-start(s32[8]{0:T(128)} %spots_b.1) | copy-start | bytes 100
  29.9 4.7 %collective-permute-start.8 = (f32[40,128]{1,0:T(8,128)S(1)}, f32[40,128]{1,0:T(8,128)S(1)}, u32[]{:S(2)}, u32[]{:S(2)}) collective-permute-start(f32[40,128]{1,0:T(8,128)S(1)} %get-tuple-element.41.faces), channel_id=1, source_target_pairs={{0,4},{1,5},{2,6},{3,7},{4,0},{5,1},{6,2},{7,3},{8,12},{9,13},{10,... | collective-permute-start | bytes 61448 | tf_op jit(solution)/shard_map/ppermute | solution.py:718
  30.7 8.7 %collective-permute-start.14 = (f32[2,128,128]{2,1,0:T(8,128)S(1)}, f32[2,128,128]{2,1,0:T(8,128)S(1)}, u32[]{:S(2)}, u32[]{:S(2)}) collective-permute-start(f32[2,128,128]{2,1,0:T(8,128)S(1)} %get-tuple-element.46), channel_id=1, source_target_pairs={{0,12},{4,0},{8,4},{12,8},{1,13},{5,1},{9,5},{13,9},{2,14},{6,2},{... | collective-permute-start | bytes 393224 | tf_op jit(solution)/shard_map/ppermute | solution.py:708
  34.8 8.3 %collective-permute-start.9 = (f32[280,128]{1,0:T(8,128)S(1)}, f32[280,128]{1,0:T(8,128)S(1)}, u32[]{:S(2)}, u32[]{:S(2)}) collective-permute-start(f32[280,128]{1,0:T(8,128)S(1)} %get-tuple-element.42.refs_1_), channel_id=1, source_target_pairs={{0,8},{1,9},{2,10},{3,11},{4,12},{5,13},{6,14},{7,15},{8,0},{9,1},... | collective-permute-start | bytes 430088 | tf_op jit(solution)/shard_map/ppermute | solution.py:718
  35.8 6.2 %collective-permute-start.11 = (f32[16,128]{1,0:T(8,128)S(1)}, f32[16,128]{1,0:T(8,128)S(1)}, u32[]{:S(2)}, u32[]{:S(2)}) collective-permute-start(f32[16,128]{1,0:T(8,128)S(1)} %get-tuple-element.44), channel_id=1, source_target_pairs={{0,9},{1,10},{2,11},{3,8},{4,13},{5,14},{6,15},{7,12},{8,1},{9,2},... | collective-permute-start | bytes 24584 | tf_op jit(solution)/shard_map/ppermute | solution.py:718
  35.8 6.2 %collective-permute-start.10 = (f32[16,128]{1,0:T(8,128)S(1)}, f32[16,128]{1,0:T(8,128)S(1)}, u32[]{:S(2)}, u32[]{:S(2)}) collective-permute-start(f32[16,128]{1,0:T(8,128)S(1)} %get-tuple-element.44), channel_id=1, source_target_pairs={{0,1},{1,2},{2,3},{3,0},{4,5},{5,6},{6,7},{7,4},{8,9},{9,10},{10,1... | collective-permute-start | bytes 24584 | tf_op jit(solution)/shard_map/ppermute | solution.py:718
  39.1 4.0 %collective-permute-start.13 = (f32[16,128]{1,0:T(8,128)S(1)}, f32[16,128]{1,0:T(8,128)S(1)}, u32[]{:S(2)}, u32[]{:S(2)}) collective-permute-start(f32[16,128]{1,0:T(8,128)S(1)} %get-tuple-element.45), channel_id=1, source_target_pairs={{0,11},{1,8},{2,9},{3,10},{4,15},{5,12},{6,13},{7,14},{8,3},{9,0},... | collective-permute-start | bytes 24584 | tf_op jit(solution)/shard_map/ppermute | solution.py:718
  39.3 3.7 %collective-permute-start.12 = (f32[16,128]{1,0:T(8,128)S(1)}, f32[16,128]{1,0:T(8,128)S(1)}, u32[]{:S(2)}, u32[]{:S(2)}) collective-permute-start(f32[16,128]{1,0:T(8,128)S(1)} %get-tuple-element.45), channel_id=1, source_target_pairs={{0,3},{1,0},{2,1},{3,2},{4,7},{5,4},{6,5},{7,6},{8,11},{9,8},{10,9... | collective-permute-start | bytes 24584 | tf_op jit(solution)/shard_map/ppermute | solution.py:718
  43.6 3.3 %collective-permute-start.17 = (f32[40,128]{1,0:T(8,128)S(1)}, f32[40,128]{1,0:T(8,128)S(1)}, u32[]{:S(2)}, u32[]{:S(2)}) collective-permute-start(f32[40,128]{1,0:T(8,128)S(1)} %get-tuple-element.53.refs_0_), channel_id=1, source_target_pairs={{0,3},{1,2},{2,1},{3,0},{4,7},{5,6},{6,5},{7,4},{8,11},{9,10},{10,... | collective-permute-start | bytes 61448 | tf_op jit(solution)/shard_map/ppermute | solution.py:882
  45.0 3.8 %collective-permute-start.16 = (f32[40,128]{1,0:T(8,128)S(1)}, f32[40,128]{1,0:T(8,128)S(1)}, u32[]{:S(2)}, u32[]{:S(2)}) collective-permute-start(f32[40,128]{1,0:T(8,128)S(1)} %get-tuple-element.53.refs_0_), channel_id=1, source_target_pairs={{0,2},{1,3},{2,0},{3,1},{4,6},{5,7},{6,4},{7,5},{8,10},{9,11},{10,... | collective-permute-start | bytes 61448 | tf_op jit(solution)/shard_map/ppermute | solution.py:882
  46.3 2.5 %collective-permute-start.15 = (f32[40,128]{1,0:T(8,128)S(1)}, f32[40,128]{1,0:T(8,128)S(1)}, u32[]{:S(2)}, u32[]{:S(2)}) collective-permute-start(f32[40,128]{1,0:T(8,128)S(1)} %get-tuple-element.53.refs_0_), channel_id=1, source_target_pairs={{0,1},{1,0},{2,3},{3,2},{4,5},{5,4},{6,7},{7,6},{8,9},{9,8},{10,11... | collective-permute-start | bytes 61448 | tf_op jit(solution)/shard_map/ppermute | solution.py:882
  (4 other events, 5.2 us)
